TPU v7x, 32 devices: a whole 2x2x4 slice. The times are simulated.
32 devices in a mesh: section: 4 (over y, core), shard: 8 (over z, x).
Axes of the slice: x: 2, y: 2, z: 4, core: 2. Of those that a mesh axis runs over, the one named last changes fastest.
Arguments:
- activations: bfloat16 [4, 8, 32, 8192], P('section', None, None, 'shard'), may hold values from -6 to 6
- top_grad: bfloat16 [8, 32, 8192], P(None, None, 'shard'), may hold values from -6 to 6
- projection: bfloat16 [4, 8192, 8192], P('section', None, 'shard'), may hold values from -0.03125 to 0.03125
- basis_out: bfloat16 [4, 8192, 4096], P('section', None, 'shard'), may hold values from -0.0625 to 0.0625
- basis_in: bfloat16 [4, 8192, 4096], P('section', 'shard'), may hold values from -0.0625 to 0.0625
Outputs:
- eigenvalues: float32 [4, 4096, 4096], P('section', 'shard')
All inputs are finite; a program needn't handle non-finite values.
Results may differ from a plain program's by a relative error of at most 0.007.
Values may be sent and summed in bfloat16 or wider, within the bound.
No kernel may reach another device: no remote copies, remote signals or barrier semaphores. Data moves between devices by JAX's collectives and lax.ppermute only.
A program may use at most 128 MiB of HBM per device.

v0:
```python
import jax
import jax.numpy as jnp
from jax import lax
from jax.sharding import PartitionSpec as P

MICRO = 8


def passed_along(block, axis, distance):
    devices = range(lax.axis_size(axis))
    route = [(i - distance, i) for i in devices if i - distance in devices]
    return lax.ppermute(block, axis, route)


def per_device(activations, top_grad, projection, basis_out, basis_in):
    section_idx = lax.axis_index("section")
    last_section = lax.axis_size("section") - 1
    at_top = section_idx == last_section
    weight_cols = projection[0]
    out_cols = basis_out[0]
    seq_len = top_grad.shape[1]
    feat_loc = top_grad.shape[2]
    eig_rows = out_cols.shape[1]
    scale = 1.0 / jnp.sqrt(jnp.float32(seq_len))
    partial_rot = jnp.einsum(
        "msd,de->mse", activations[0], basis_in[0], preferred_element_type=jnp.float32
    )
    rot_in = lax.psum(partial_rot, "shard").astype(jnp.bfloat16)

    def absorb(piece):
        through = jnp.dot(piece, weight_cols, preferred_element_type=jnp.float32)
        rotated = jnp.dot(piece, out_cols, preferred_element_type=jnp.float32)
        return (through, rotated)

    def chain_step(step_index, current):
        micro_idx = step_index - (last_section - section_idx)
        active = jnp.logical_and(micro_idx >= 0, micro_idx < MICRO)
        micro_safe = jnp.clip(micro_idx, 0, MICRO - 1)
        through, rotated = absorb(lax.all_gather(current, "shard", axis=1, tiled=True))
        lower = (current.astype(jnp.float32) + through).astype(jnp.bfloat16)
        received = passed_along(lower, "section", -1)
        next_index = jnp.minimum(step_index + 1, MICRO - 1).astype(jnp.int32)
        next_top = lax.dynamic_index_in_dim(top_grad, next_index, 0, keepdims=False)
        following = jnp.where(at_top, next_top, received)
        return (following, rotated.astype(jnp.bfloat16), active, micro_safe)

    start_grad = jnp.where(at_top, top_grad[0], jnp.zeros((seq_len, feat_loc), jnp.bfloat16))
    total_steps = MICRO + lax.axis_size("section") - 1

    def store_loop(step_index, carry):
        current, stored = carry
        following, rot_out, active, micro_safe = chain_step(step_index, current)
        updated = lax.dynamic_update_index_in_dim(stored, rot_out, micro_safe, 0)
        stored = jnp.where(active, updated, stored)
        return (following, stored)

    start_store = jnp.zeros((MICRO, seq_len, eig_rows), jnp.bfloat16)
    final_grad, stored = lax.fori_loop(0, total_steps, store_loop, (start_grad, start_store))
    product = jnp.einsum("msg,mse->mge", stored, rot_in, preferred_element_type=jnp.float32) * scale
    summed = jnp.sum(product * product, axis=0)
    return (summed / MICRO)[None]


def solution(mesh):
    return jax.shard_map(
        per_device,
        mesh=mesh,
        in_specs=(
            P("section", None, None, "shard"),
            P(None, None, "shard"),
            P("section", None, "shard"),
            P("section", None, "shard"),
            P("section", "shard", None),
        ),
        out_specs=P("section", "shard", None),
        check_vma=False,
    )
```

profile of v0, /device:TPU:0, one launch (start us, length us, event | category | flops | bytes accessed | tf_op | source)
XLA Modules:
  0.0 712.9 jit_solution(4539812220489466830)
XLA Ops:
  0.9 521.4 %while.17 = (s32[]{:T(128)}, bf16[32,1024]{1,0:T(8,128)(2,1)S(1)}, bf16[8,32,512]{2,1,0:T(8,128)(2,1)S(1)}, pred[]{:T(512)}, bf16[8,32,1024]{2,1,0:T(8,128)(2,1)...) while((s32[]{:T(128)}, bf16[32,1024]{1,0:T(8,128)(2,1)S(1)}, ...), condition=%wide.region_1.2_spmd, body=%wide.region_0.0_spmd.sunk | while | flops 805470208 | bytes 27459848 | solution.py:58
  0.9 33.0 %all_gather.10 = bf16[32,8192]{1,0:T(8,128)(2,1)S(1)} all-gather(bf16[32,1024]{1,0:T(8,128)(2,1)S(1)} %get-tuple-element.275), channel_id=1, replica_groups=mesh['section'=4,'shard'=8] {'shard'}, dimensions={1}, use_global_device_ids=true | all-gather | bytes 589824 | tf_op jit(solution)/shard_map/while/body/eval_jaxpr/all_gather | solution.py:39
  34.0 8.8 %fusion.24 = bf16[32,1024]{1,0:T(8,128)(2,1)S(1)} fusion(bf16[32,8192]{1,0:T(8,128)(2,1)S(1)} %all_gather.10, bf16[8192,1024]{1,0:T(8,128)(2,1)} %get-tuple-element.291, bf16[32,1024]{1,0:T(8,128)(2,1)S(1)} %get-tuple-element.275), kind=kOutput, calls=%fused_computation.1.clone.1 | convolution fusion | flops 536969216 | bytes 17432576 | tf_op jit(solution)/shard_map/while/body/eval_jaxpr/dot_general | solution.py:31
  44.0 4.9 fusion.25
  49.8 31.4 %all_gather.10 = bf16[32,8192]{1,0:T(8,128)(2,1)S(1)} all-gather(bf16[32,1024]{1,0:T(8,128)(2,1)S(1)} %get-tuple-element.275), channel_id=1, replica_groups=mesh['section'=4,'shard'=8] {'shard'}, dimensions={1}, use_global_device_ids=true | all-gather | bytes 589824 | tf_op jit(solution)/shard_map/while/body/eval_jaxpr/all_gather | solution.py:39
  81.2 8.8 %fusion.24 = bf16[32,1024]{1,0:T(8,128)(2,1)S(1)} fusion(bf16[32,8192]{1,0:T(8,128)(2,1)S(1)} %all_gather.10, bf16[8192,1024]{1,0:T(8,128)(2,1)} %get-tuple-element.291, bf16[32,1024]{1,0:T(8,128)(2,1)S(1)} %get-tuple-element.275), kind=kOutput, calls=%fused_computation.1.clone.1 | convolution fusion | flops 536969216 | bytes 17432576 | tf_op jit(solution)/shard_map/while/body/eval_jaxpr/dot_general | solution.py:31
  91.3 4.9 fusion.25
  97.0 31.4 %all_gather.10 = bf16[32,8192]{1,0:T(8,128)(2,1)S(1)} all-gather(bf16[32,1024]{1,0:T(8,128)(2,1)S(1)} %get-tuple-element.275), channel_id=1, replica_groups=mesh['section'=4,'shard'=8] {'shard'}, dimensions={1}, use_global_device_ids=true | all-gather | bytes 589824 | tf_op jit(solution)/shard_map/while/body/eval_jaxpr/all_gather | solution.py:39
  128.4 8.8 %fusion.24 = bf16[32,1024]{1,0:T(8,128)(2,1)S(1)} fusion(bf16[32,8192]{1,0:T(8,128)(2,1)S(1)} %all_gather.10, bf16[8192,1024]{1,0:T(8,128)(2,1)} %get-tuple-element.291, bf16[32,1024]{1,0:T(8,128)(2,1)S(1)} %get-tuple-element.275), kind=kOutput, calls=%fused_computation.1.clone.1 | convolution fusion | flops 536969216 | bytes 17432576 | tf_op jit(solution)/shard_map/while/body/eval_jaxpr/dot_general | solution.py:31
  138.5 4.9 fusion.25
  144.3 31.3 %all_gather.10 = bf16[32,8192]{1,0:T(8,128)(2,1)S(1)} all-gather(bf16[32,1024]{1,0:T(8,128)(2,1)S(1)} %get-tuple-element.275), channel_id=1, replica_groups=mesh['section'=4,'shard'=8] {'shard'}, dimensions={1}, use_global_device_ids=true | all-gather | bytes 589824 | tf_op jit(solution)/shard_map/while/body/eval_jaxpr/all_gather | solution.py:39
  175.6 8.8 %fusion.24 = bf16[32,1024]{1,0:T(8,128)(2,1)S(1)} fusion(bf16[32,8192]{1,0:T(8,128)(2,1)S(1)} %all_gather.10, bf16[8192,1024]{1,0:T(8,128)(2,1)} %get-tuple-element.291, bf16[32,1024]{1,0:T(8,128)(2,1)S(1)} %get-tuple-element.275), kind=kOutput, calls=%fused_computation.1.clone.1 | convolution fusion | flops 536969216 | bytes 17432576 | tf_op jit(solution)/shard_map/while/body/eval_jaxpr/dot_general | solution.py:31
  191.4 31.3 %all_gather.10 = bf16[32,8192]{1,0:T(8,128)(2,1)S(1)} all-gather(bf16[32,1024]{1,0:T(8,128)(2,1)S(1)} %get-tuple-element.275), channel_id=1, replica_groups=mesh['section'=4,'shard'=8] {'shard'}, dimensions={1}, use_global_device_ids=true | all-gather | bytes 589824 | tf_op jit(solution)/shard_map/while/body/eval_jaxpr/all_gather | solution.py:39
  222.7 8.8 %fusion.24 = bf16[32,1024]{1,0:T(8,128)(2,1)S(1)} fusion(bf16[32,8192]{1,0:T(8,128)(2,1)S(1)} %all_gather.10, bf16[8192,1024]{1,0:T(8,128)(2,1)} %get-tuple-element.291, bf16[32,1024]{1,0:T(8,128)(2,1)S(1)} %get-tuple-element.275), kind=kOutput, calls=%fused_computation.1.clone.1 | convolution fusion | flops 536969216 | bytes 17432576 | tf_op jit(solution)/shard_map/while/body/eval_jaxpr/dot_general | solution.py:31
  232.8 4.9 fusion.25
  238.5 31.3 %all_gather.10 = bf16[32,8192]{1,0:T(8,128)(2,1)S(1)} all-gather(bf16[32,1024]{1,0:T(8,128)(2,1)S(1)} %get-tuple-element.275), channel_id=1, replica_groups=mesh['section'=4,'shard'=8] {'shard'}, dimensions={1}, use_global_device_ids=true | all-gather | bytes 589824 | tf_op jit(solution)/shard_map/while/body/eval_jaxpr/all_gather | solution.py:39
  269.9 8.8 %fusion.24 = bf16[32,1024]{1,0:T(8,128)(2,1)S(1)} fusion(bf16[32,8192]{1,0:T(8,128)(2,1)S(1)} %all_gather.10, bf16[8192,1024]{1,0:T(8,128)(2,1)} %get-tuple-element.291, bf16[32,1024]{1,0:T(8,128)(2,1)S(1)} %get-tuple-element.275), kind=kOutput, calls=%fused_computation.1.clone.1 | convolution fusion | flops 536969216 | bytes 17432576 | tf_op jit(solution)/shard_map/while/body/eval_jaxpr/dot_general | solution.py:31
  285.7 31.4 %all_gather.10 = bf16[32,8192]{1,0:T(8,128)(2,1)S(1)} all-gather(bf16[32,1024]{1,0:T(8,128)(2,1)S(1)} %get-tuple-element.275), channel_id=1, replica_groups=mesh['section'=4,'shard'=8] {'shard'}, dimensions={1}, use_global_device_ids=true | all-gather | bytes 589824 | tf_op jit(solution)/shard_map/while/body/eval_jaxpr/all_gather | solution.py:39
  317.2 8.8 %fusion.24 = bf16[32,1024]{1,0:T(8,128)(2,1)S(1)} fusion(bf16[32,8192]{1,0:T(8,128)(2,1)S(1)} %all_gather.10, bf16[8192,1024]{1,0:T(8,128)(2,1)} %get-tuple-element.291, bf16[32,1024]{1,0:T(8,128)(2,1)S(1)} %get-tuple-element.275), kind=kOutput, calls=%fused_computation.1.clone.1 | convolution fusion | flops 536969216 | bytes 17432576 | tf_op jit(solution)/shard_map/while/body/eval_jaxpr/dot_general | solution.py:31
  327.2 4.9 fusion.25
  333.0 31.3 %all_gather.10 = bf16[32,8192]{1,0:T(8,128)(2,1)S(1)} all-gather(bf16[32,1024]{1,0:T(8,128)(2,1)S(1)} %get-tuple-element.275), channel_id=1, replica_groups=mesh['section'=4,'shard'=8] {'shard'}, dimensions={1}, use_global_device_ids=true | all-gather | bytes 589824 | tf_op jit(solution)/shard_map/while/body/eval_jaxpr/all_gather | solution.py:39
  364.4 8.8 %fusion.24 = bf16[32,1024]{1,0:T(8,128)(2,1)S(1)} fusion(bf16[32,8192]{1,0:T(8,128)(2,1)S(1)} %all_gather.10, bf16[8192,1024]{1,0:T(8,128)(2,1)} %get-tuple-element.291, bf16[32,1024]{1,0:T(8,128)(2,1)S(1)} %get-tuple-element.275), kind=kOutput, calls=%fused_computation.1.clone.1 | convolution fusion | flops 536969216 | bytes 17432576 | tf_op jit(solution)/shard_map/while/body/eval_jaxpr/dot_general | solution.py:31
  380.2 31.7 %all_gather.10 = bf16[32,8192]{1,0:T(8,128)(2,1)S(1)} all-gather(bf16[32,1024]{1,0:T(8,128)(2,1)S(1)} %get-tuple-element.275), channel_id=1, replica_groups=mesh['section'=4,'shard'=8] {'shard'}, dimensions={1}, use_global_device_ids=true | all-gather | bytes 589824 | tf_op jit(solution)/shard_map/while/body/eval_jaxpr/all_gather | solution.py:39
  411.9 8.8 %fusion.24 = bf16[32,1024]{1,0:T(8,128)(2,1)S(1)} fusion(bf16[32,8192]{1,0:T(8,128)(2,1)S(1)} %all_gather.10, bf16[8192,1024]{1,0:T(8,128)(2,1)} %get-tuple-element.291, bf16[32,1024]{1,0:T(8,128)(2,1)S(1)} %get-tuple-element.275), kind=kOutput, calls=%fused_computation.1.clone.1 | convolution fusion | flops 536969216 | bytes 17432576 | tf_op jit(solution)/shard_map/while/body/eval_jaxpr/dot_general | solution.py:31
  427.8 31.5 %all_gather.10 = bf16[32,8192]{1,0:T(8,128)(2,1)S(1)} all-gather(bf16[32,1024]{1,0:T(8,128)(2,1)S(1)} %get-tuple-element.275), channel_id=1, replica_groups=mesh['section'=4,'shard'=8] {'shard'}, dimensions={1}, use_global_device_ids=true | all-gather | bytes 589824 | tf_op jit(solution)/shard_map/while/body/eval_jaxpr/all_gather | solution.py:39
  459.2 8.8 %fusion.24 = bf16[32,1024]{1,0:T(8,128)(2,1)S(1)} fusion(bf16[32,8192]{1,0:T(8,128)(2,1)S(1)} %all_gather.10, bf16[8192,1024]{1,0:T(8,128)(2,1)} %get-tuple-element.291, bf16[32,1024]{1,0:T(8,128)(2,1)S(1)} %get-tuple-element.275), kind=kOutput, calls=%fused_computation.1.clone.1 | convolution fusion | flops 536969216 | bytes 17432576 | tf_op jit(solution)/shard_map/while/body/eval_jaxpr/dot_general | solution.py:31
  475.1 31.4 %all_gather.10 = bf16[32,8192]{1,0:T(8,128)(2,1)S(1)} all-gather(bf16[32,1024]{1,0:T(8,128)(2,1)S(1)} %get-tuple-element.275), channel_id=1, replica_groups=mesh['section'=4,'shard'=8] {'shard'}, dimensions={1}, use_global_device_ids=true | all-gather | bytes 589824 | tf_op jit(solution)/shard_map/while/body/eval_jaxpr/all_gather | solution.py:39
  506.5 8.8 %fusion.24 = bf16[32,1024]{1,0:T(8,128)(2,1)S(1)} fusion(bf16[32,8192]{1,0:T(8,128)(2,1)S(1)} %all_gather.10, bf16[8192,1024]{1,0:T(8,128)(2,1)} %get-tuple-element.291, bf16[32,1024]{1,0:T(8,128)(2,1)S(1)} %get-tuple-element.275), kind=kOutput, calls=%fused_computation.1.clone.1 | convolution fusion | flops 536969216 | bytes 17432576 | tf_op jit(solution)/shard_map/while/body/eval_jaxpr/dot_general | solution.py:31
  516.5 4.9 fusion.25
  522.3 7.7 %fusion.4 = f32[8,32,4096]{2,1,0:T(8,128)} fusion(bf16[1,1024,4096]{2,1,0:T(8,128)(2,1)} %param.11, bf16[1,8,32,1024]{3,2,1,0:T(8,128)(2,1)S(1)} %copy-done), kind=kOutput, calls=%fused_computation.8 | convolution fusion | flops 2147483648 | bytes 13107200 | tf_op jit(solution)/shard_map/msd,de->mse/dot_general | solution.py:25
  530.1 168.4 %all-reduce.1 = bf16[8,32,4096]{2,1,0:T(8,128)(2,1)S(1)} all-reduce(f32[8,32,4096]{2,1,0:T(8,128)} %fusion.4), channel_id=1, replica_groups=mesh['section'=4,'shard'=8] {'shard'}, use_global_device_ids=true, to_apply=%region_2.3 | all-reduce | flops 1048576 | bytes 6291456 | tf_op jit(solution)/shard_map/psum | solution.py:28
  698.5 10.4 %multiply_reduce_fusion = f32[512,4096]{1,0:T(8,128)S(1)} fusion(bf16[8,32,512]{2,1,0:T(8,128)(2,1)S(1)} %get-tuple-element.196, bf16[8,32,4096]{2,1,0:T(8,128)(2,1)S(1)} %all-reduce.1), kind=kOutput, calls=%fused_computation.7 | convolution fusion | flops 1121976320 | bytes 10747904 | tf_op jit(solution)/shard_map/msg,mse->mge/dot_general | solution.py:59
  (43 shorter events, 53.2 us)
Async XLA Ops:
  0.0 522.3 %copy-start = (bf16[1,8,32,1024]{3,2,1,0:T(8,128)(2,1)S(1)}, bf16[1,8,32,1024]{3,2,1,0:T(8,128)(2,1)}, u32[]{:S(2)}) copy-start(bf16[1,8,32,1024]{3,2,1,0:T(8,128)(2,1)} %param.7) | copy-start | bytes 1572868
  42.7 6.2 collective-permute-start
  89.9 6.2 collective-permute-start
  137.2 6.2 collective-permute-start
  184.3 6.2 collective-permute-start
  231.4 6.2 collective-permute-start
  278.6 6.2 collective-permute-start
  325.9 6.2 collective-permute-start
  373.1 6.2 collective-permute-start
  420.7 6.2 collective-permute-start
  468.0 6.2 collective-permute-start
  515.2 6.2 collective-permute-start
where the time goes:
time: 718 us; the launch traced here: 713 us
  blocking collectives  515 us (72%)
  matrix products  168 us (23%)
  other arithmetic  14.3 us (2%)
  starting transfers between devices  14.2 us (2%)
    all_gather x11, blocking collectives, chain_step(): lax.all_gather(current, 'shard', axis=1, tiled=True)  347 us
    psum x1, blocking collectives, per_device(): rot_in = lax.psum(partial_rot, 'shard').astype(jnp.bfloat16)  168 us
    dot_general x11, matrix products, absorb(): through = jnp.dot(piece, weight_cols, preferred_element_type=jnp.float32)  96.3 us
    dot_general x11, matrix products, absorb(): rotated = jnp.dot(piece, out_cols, preferred_element_type=jnp.float32)  54 us
  transfers between devices with their start and end apart: 11, of which 0 were waited for; matrix products, arithmetic and copies ran while one was open for 8% of the time, Pallas kernels for 0%

commit v1 on v0

v1 whole, which is shorter than its diff:
```python
import jax
import jax.numpy as jnp
from jax import lax
from jax.experimental import pallas as pl
from jax.experimental.pallas import tpu as pltpu
from jax.sharding import PartitionSpec as P

VMEM_LIMIT = 48 * 1024 * 1024


def gathered_dot(blocks, weights, base=None):
    parts, rows, depth = blocks.shape
    cols = weights.shape[1]
    group = max(1, min(parts, 1024 // depth))
    steps = parts // group

    def body(*refs):
        if base is None:
            blocks_ref, weights_ref, out_ref, total = refs
        else:
            blocks_ref, weights_ref, base_ref, out_ref, total = refs
        step = pl.program_id(0)

        @pl.when(step == 0)
        def _():
            if base is None:
                total[...] = jnp.zeros_like(total)
            else:
                total[...] = base_ref[...].astype(jnp.float32)

        for j in range(group):
            total[...] += jnp.dot(
                blocks_ref[j],
                weights_ref[j * depth : (j + 1) * depth, :],
                preferred_element_type=jnp.float32,
            )

        @pl.when(step == steps - 1)
        def _():
            out_ref[...] = total[...].astype(jnp.bfloat16)

    whole = pl.BlockSpec((rows, cols), lambda i: (0, 0))
    return pl.pallas_call(
        body,
        grid=(steps,),
        in_specs=[
            pl.BlockSpec((group, rows, depth), lambda i: (i, 0, 0)),
            pl.BlockSpec((group * depth, cols), lambda i: (i, 0)),
        ]
        + ([] if base is None else [whole]),
        out_specs=whole,
        out_shape=jax.ShapeDtypeStruct((rows, cols), jnp.bfloat16),
        scratch_shapes=[pltpu.VMEM((rows, cols), jnp.float32)],
        compiler_params=pltpu.CompilerParams(vmem_limit_bytes=VMEM_LIMIT),
        cost_estimate=pl.CostEstimate(
            flops=2 * parts * rows * depth * cols,
            bytes_accessed=2 * (parts * rows * depth + parts * depth * cols + rows * cols),
            transcendentals=0,
        ),
        name="gathered_dot",
    )(blocks, weights, *([] if base is None else [base]))


def mean_square(rot_out, rot_in, micro, seq):
    runs, rows, width = rot_in.shape
    eig_rows = rot_out.shape[1]

    def body(out_ref_in, in_ref, eig_ref):
        for m in range(micro):
            rows_of = slice(m * seq, (m + 1) * seq)
            product = lax.dot_general(
                out_ref_in[rows_of, :],
                in_ref[0, rows_of, :],
                (((0,), (0,)), ((), ())),
                preferred_element_type=jnp.float32,
            )
            square = product * product
            eig_ref[...] = square if m == 0 else eig_ref[...] + square
        eig_ref[...] *= 1.0 / (seq * micro)

    return pl.pallas_call(
        body,
        grid=(runs,),
        in_specs=[
            pl.BlockSpec((rows, eig_rows), lambda i: (0, 0)),
            pl.BlockSpec((1, rows, width), lambda i: (i, 0, 0)),
        ],
        out_specs=pl.BlockSpec((eig_rows, width), lambda i: (0, i)),
        out_shape=jax.ShapeDtypeStruct((eig_rows, runs * width), jnp.float32),
        compiler_params=pltpu.CompilerParams(vmem_limit_bytes=VMEM_LIMIT),
        cost_estimate=pl.CostEstimate(
            flops=2 * rows * eig_rows * runs * width * 8,
            bytes_accessed=4 * eig_rows * runs * width,
            transcendentals=0,
        ),
        name="mean_square",
    )(rot_out, rot_in)


def per_device(activations, top_grad, projection, basis_out, basis_in):
    sections = lax.axis_size("section")
    shards = lax.axis_size("shard")
    section = lax.axis_index("section")
    micro, seq, feat_loc = top_grad.shape
    rows = micro * seq
    eig_a = basis_in.shape[2]
    weights, out_cols = projection[0], basis_out[0]

    partial_rot = jnp.dot(
        activations[0].reshape(rows, feat_loc), basis_in[0], preferred_element_type=jnp.float32
    ).astype(jnp.bfloat16)
    partial_rot = partial_rot.reshape(rows, shards, eig_a // shards).transpose(1, 0, 2)
    own_rot = lax.psum_scatter(partial_rot, "shard", scatter_dimension=0, tiled=False)
    rot_in = lax.all_gather(own_rot, "shard", axis=0)

    current = top_grad.reshape(rows, feat_loc)
    rot_out = jnp.zeros((rows, out_cols.shape[1]), jnp.bfloat16)
    for step in range(sections):
        active = section == sections - 1 - step
        blocks = lax.all_gather(current, "shard", axis=0)
        if step < sections - 1:
            lower = gathered_dot(blocks, weights, current)
            route = [(sections - 1 - step, sections - 2 - step)]
            received = lax.ppermute(lower, "section", route)
        rot_out = lax.cond(
            active,
            lambda blocks, old: gathered_dot(blocks, out_cols),
            lambda blocks, old: old,
            blocks,
            rot_out,
        )
        if step < sections - 1:
            current = received
    return mean_square(rot_out, rot_in, micro, seq)[None]


def solution(mesh):
    return jax.shard_map(
        per_device,
        mesh=mesh,
        in_specs=(
            P("section", None, None, "shard"),
            P(None, None, "shard"),
            P("section", None, "shard"),
            P("section", None, "shard"),
            P("section", "shard", None),
        ),
        out_specs=P("section", "shard", None),
        check_vma=False,
    )
```

time: 718 us -> 483 us (0.67)
  blocking collectives: 515 us -> 0 us
  waiting for transfers between devices: 0.13 us -> 396 us
  matrix products: 168 us -> 5.72 us
  Pallas kernels: 0 us -> 53.5 us
  other arithmetic: 14.3 us -> 0 us
  between operations: 0.03 us -> 13.6 us
  starting transfers between devices: 14.2 us -> 2.89 us
  local copies, waits for them, and re-layouts: 0.02 us -> 10.4 us
    all_gather x11 -> x0, blocking collectives: 347 us -> none  [chain_step(): lax.all_gather(current, 'shard', axis=1, tiled=True)]
    all_gather x0 -> x5, waiting for transfers between devices: none -> 339 us  [the longest x4 298 us: per_device(): blocks = lax.all_gather(current, 'shard', axis=0)]
    psum x1 -> x0, blocking collectives: 168 us -> none  [per_device(): rot_in = lax.psum(partial_rot, 'shard').astype(jnp.bfloat16)]
    dot_general x24 -> x1, matrix products: 168 us -> 5.72 us  [per_device(): jnp.dot(activations[0].reshape(rows, feat_loc), basis_in[0], preferred_el...]
    reduce_scatter x0 -> x1, waiting for transfers between devices: none -> 54 us  [per_device(): lax.psum_scatter(partial_rot, 'shard', scatter_dimension=0, tiled=False)]
    pallas_call x0 -> x5, Pallas kernels: none -> 53.5 us  [the longest x4 42.3 us: gathered_dot(): pl.pallas_call(body, grid=(steps,), in_specs=[pl.BlockSpec((group, rows,...]
    ppermute x11 -> x3, starting transfers between devices: 14.2 us -> 2.68 us  [per_device(): received = lax.ppermute(lower, 'section', route)]
    select_n x12 -> x0, other arithmetic: 10.3 us -> none  [the longest x11 9.38 us: chain_step(): following = jnp.where(at_top, next_top, received)]
  transfers between devices with their start and end apart: 11 -> 9, of which waited for: 0 -> 7; matrix products, arithmetic and copies ran while one was open for 8% -> 2% of each run, Pallas kernels for 0% -> 4%
where the time goes in v1:
time: 483 us; the launch traced here: 482 us
  waiting for transfers between devices  396 us (82%)
  Pallas kernels  53.5 us (11%)
  between operations  13.6 us (3%)
  local copies, waits for them, and re-layouts  10.4 us (2%)
  matrix products  5.72 us (1%)
    all_gather x4, waiting for transfers between devices, per_device(): blocks = lax.all_gather(current, 'shard', axis=0)  298 us
    reduce_scatter x1, waiting for transfers between devices, per_device(): lax.psum_scatter(partial_rot, 'shard', scatter_dimension=0, tiled=False)  54 us
    pallas_call x4, Pallas kernels, gathered_dot(): pl.pallas_call(body, grid=(steps,), in_specs=[pl.BlockSpec((group, rows,...  42.3 us
    all_gather x1, waiting for transfers between devices, per_device(): rot_in = lax.all_gather(own_rot, 'shard', axis=0)  41.3 us
    pallas_call x1, Pallas kernels, mean_square(): pl.pallas_call(body, grid=(runs,), in_specs=[pl.BlockSpec((rows, eig_rows...  11.2 us
  transfers between devices with their start and end apart: 9, of which 7 were waited for; matrix products, arithmetic and copies ran while one was open for 2% of the time, Pallas kernels for 4%

profile of v1, /device:TPU:0, one launch (start us, length us, event | category | flops | bytes accessed | tf_op | source)
XLA Modules:
  0.0 482.5 jit_solution(11810289361275628063)
XLA Ops:
  6.5 0.7 all-gather.9.cloned.1.call-update
  7.3 0.0 all-gather.13.cloned.1.call-start
  7.3 78.3 %all-gather.9.cloned.1.call-done.refs_0_ = bf16[8,256,1024]{2,1,0:T(8,128)(2,1)} async-done(((bf16[1,256,1024]{2,1,0:T(8,128)(2,1)}), bf16[8,256,1024]{2,1,0:T(8,128)(2,1)}) %all-gather.9.cloned.1.call-update) | async-done | bytes 4194320 | tf_op jit(solution)/shard_map/all_gather | solution.py:120
  85.6 1.0 copy-done.2
  86.7 11.3 %gathered_dot.11 = bf16[256,1024]{1,0:T(8,128)(2,1)S(1)} custom-call(bf16[8,256,1024]{2,1,0:T(8,128)(2,1)} %all-gather.9.cloned.1.call-done.refs_0_, bf16[8192,1024]{1,0:T(8,128)(2,1)} %bitcast.21, bf16[256,1024]{1,0:T(8,128)(2,1)S(1)} %bitcast.20), custom_call_target="tpu_custom_call" | custom-call | flops 4294967296 | bytes 21495808 | tf_op jit(solution)/shard_map/gathered_dot/pallas_call | solution.py:43
  98.0 0.7 collective-permute-start
  98.7 0.8 copy-done.5
  99.5 0.0 all-gather.13.cloned.1.call-update
  99.5 0.0 all-gather.15.cloned.1.call-start
  99.6 74.9 %all-gather.13.cloned.1.call-done = bf16[2048,1024]{1,0:T(8,128)(2,1)} async-done(((bf16[256,1024]{1,0:T(8,128)(2,1)}), bf16[2048,1024]{1,0:T(8,128)(2,1)}) %all-gather.13.cloned.1.call-update) | async-done | bytes 4194320 | tf_op jit(solution)/shard_map/all_gather | solution.py:120
  174.4 1.0 copy-done.6
  175.5 11.3 %gathered_dot.12 = bf16[256,1024]{1,0:T(8,128)(2,1)S(1)} custom-call(bf16[8,256,1024]{2,1,0:T(8,128)(2,1)} %bitcast.28, bf16[8192,1024]{1,0:T(8,128)(2,1)} %bitcast.22, bf16[256,1024]{1,0:T(8,128)(2,1)S(1)} %copy-done.6), custom_call_target="tpu_custom_call" | custom-call | flops 4294967296 | bytes 21495808 | tf_op jit(solution)/shard_map/gathered_dot/pallas_call | solution.py:43
  186.8 0.7 collective-permute-start.1
  187.5 0.8 copy-done.3
  188.4 0.0 reduce-scatter.2.cloned.1.call-start
  188.4 5.7 %fusion.2 = bf16[256,4096]{1,0:T(8,128)(2,1)S(1)} fusion(bf16[256,1024]{1,0:T(8,128)(2,1)S(1)} %bitcast.18, bf16[1,1024,4096]{2,1,0:T(8,128)(2,1)} %param.17), kind=kOutput, calls=%fused_computation.2 | convolution fusion | flops 2148532224 | bytes 11010048 | tf_op jit(solution)/shard_map/dot_general | solution.py:109
  194.2 2.5 copy.8
  196.7 0.0 all-gather.17.cloned.1.call-start
  196.7 72.0 %all-gather.15.cloned.1.call-done = bf16[2048,1024]{1,0:T(8,128)(2,1)} async-done(((bf16[256,1024]{1,0:T(8,128)(2,1)}), bf16[2048,1024]{1,0:T(8,128)(2,1)}) %all-gather.15.cloned.1.call-update) | async-done | bytes 4194320 | tf_op jit(solution)/shard_map/all_gather | solution.py:120
  268.7 11.4 %gathered_dot.13 = bf16[256,1024]{1,0:T(8,128)(2,1)S(1)} custom-call(bf16[8,256,1024]{2,1,0:T(8,128)(2,1)} %bitcast.30, bf16[8192,1024]{1,0:T(8,128)(2,1)} %bitcast.23, bf16[256,1024]{1,0:T(8,128)(2,1)S(1)} %copy-done.4), custom_call_target="tpu_custom_call" | custom-call | flops 4294967296 | bytes 21495808 | tf_op jit(solution)/shard_map/gathered_dot/pallas_call | solution.py:43
  280.1 1.3 collective-permute-start.2
  281.4 2.5 collective-permute-done.2
  283.9 0.8 copy-done.8
  284.7 0.0 all-gather.11.cloned.1.call-start
  284.8 54.0 %reduce-scatter.2.cloned.1.call-done = bf16[1,256,512]{1,2,0:T(8,128)(2,1)} async-done(((bf16[8,256,512]{1,2,0:T(8,128)(2,1)}), bf16[1,256,512]{1,2,0:T(8,128)(2,1)}) %reduce-scatter.2.cloned.1.call-update) | async-done | bytes 262160 | tf_op jit(solution)/shard_map/reduce_scatter | solution.py:113
  338.8 1.8 copy.9
  340.7 72.5 %all-gather.17.cloned.1.call-done = bf16[2048,1024]{1,0:T(8,128)(2,1)} async-done(((bf16[256,1024]{1,0:T(8,128)(2,1)}), bf16[2048,1024]{1,0:T(8,128)(2,1)}) %all-gather.17.cloned.1.call-update) | async-done | bytes 4194320 | tf_op jit(solution)/shard_map/all_gather | solution.py:120
  413.2 8.2 %conditional.7 = (bf16[256,512]{1,0:T(8,128)(2,1)S(1)}) conditional(s32[]{:T(128)} %convert_element_type.15, bf16[256,512]{1,0:T(8,128)(2,1)S(1)} %get-tuple-element.46, (bf16[8,256,1024]{2,1,0:T(8,128)(2,1)}, bf16[8192,512]{1,0:T(8,128)(2,1)}) %tuple.60), branch_computations={%region_6.0_spmd, %region_7.0_spmd} | conditional | flops 2147483648 | bytes 12845064 | solution.py:125
  413.2 8.2 %gathered_dot.10 = bf16[256,512]{1,0:T(8,128)(2,1)S(1)} custom-call(bf16[8,256,1024]{2,1,0:T(8,128)(2,1)} %get-tuple-element.42.refs_0_, bf16[8192,512]{1,0:T(8,128)(2,1)} %get-tuple-element.43.refs_1_), custom_call_target="tpu_custom_call" | custom-call | flops 2147483648 | bytes 12845056 | tf_op jit(solution)/shard_map/cond/branch_1_fun/gathered_dot/pallas_call | solution.py:43
  421.4 41.3 %all-gather.11.cloned.1.call-done.in_ref = bf16[8,256,512]{2,1,0:T(8,128)(2,1)} async-done(((bf16[1,256,512]{2,1,0:T(8,128)(2,1)}), bf16[8,256,512]{2,1,0:T(8,128)(2,1)}) %all-gather.11.cloned.1.call-update) | async-done | bytes 2097168 | tf_op jit(solution)/shard_map/all_gather | solution.py:114
  462.8 1.6 copy-done.7
  464.4 11.2 %mean_square.1 = f32[512,4096]{1,0:T(8,128)} custom-call(bf16[256,512]{1,0:T(8,128)(2,1)S(1)} %get-tuple-element.47.out_ref_in, bf16[8,256,512]{2,1,0:T(8,128)(2,1)S(1)} %copy-done.7), custom_call_target="tpu_custom_call" | custom-call | flops 8589934592 | bytes 8388608 | tf_op jit(solution)/shard_map/mean_square/pallas_call | solution.py:81
  (23 shorter events, 0.2 us)
Async XLA Ops:
  6.5 181.9 %copy-start = (bf16[1,8,32,1024]{3,2,1,0:T(8,128)(2,1)S(1)}, bf16[1,8,32,1024]{3,2,1,0:T(8,128)(2,1)}, u32[]{:S(2)}) copy-start(bf16[1,8,32,1024]{3,2,1,0:T(8,128)(2,1)} %param.13) | copy-start | bytes 1572868
  6.5 79.1 %all-gather.9.cloned.1.call-start = ((), (), s32[]{:S(2)}) async-start(), calls=%async_computation.1 | async-start | bytes 4718592 | tf_op jit(solution)/shard_map/all_gather | solution.py:120
  7.3 167.2 %all-gather.13.cloned.1.call-start = ((), (), s32[]{:S(2)}) async-start(), calls=%async_computation.4 | async-start | bytes 4718592 | tf_op jit(solution)/shard_map/all_gather | solution.py:120
  85.6 1.0 copy-start.2
  98.0 0.7 collective-permute-start
  98.7 0.8 copy-start.5
  99.5 169.2 %all-gather.15.cloned.1.call-start = ((), (), s32[]{:S(2)}) async-start(), calls=%async_computation.5 | async-start | bytes 4718592 | tf_op jit(solution)/shard_map/all_gather | solution.py:120
  174.4 1.0 copy-start.6
  186.8 0.7 collective-permute-start.1
  187.5 0.8 copy-start.3
  188.4 150.4 %reduce-scatter.2.cloned.1.call-start = ((), (), s32[]{:S(2)}) async-start(), calls=%async_computation.2 | async-start | bytes 2359296 | tf_op jit(solution)/shard_map/reduce_scatter | solution.py:113
  194.2 74.5 %copy-start.4 = (bf16[256,1024]{1,0:T(8,128)(2,1)S(1)}, bf16[256,1024]{1,0:T(8,128)(2,1)}, u32[]{:S(2)}) copy-start(bf16[256,1024]{1,0:T(8,128)(2,1)} %copy-done.3) | copy-start | bytes 1572868
  196.7 216.5 %all-gather.17.cloned.1.call-start = ((), (), s32[]{:S(2)}) async-start(), calls=%async_computation.6 | async-start | bytes 4718592 | tf_op jit(solution)/shard_map/all_gather | solution.py:120
  280.1 3.8 collective-permute-start.2
  283.9 0.8 copy-start.8
  284.7 178.0 %all-gather.11.cloned.1.call-start = ((), (), s32[]{:S(2)}) async-start(), calls=%async_computation.3 | async-start | bytes 2359296 | tf_op jit(solution)/shard_map/all_gather | solution.py:114
  462.8 1.6 copy-start.7
  464.4 11.3 %copy-start.1 = (bf16[1,8,32,1024]{3,2,1,0:T(8,128)(2,1)S(1)}, bf16[1,8,32,1024]{3,2,1,0:T(8,128)(2,1)}, u32[]{:S(2)}) copy-start(bf16[1,8,32,1024]{3,2,1,0:T(8,128)(2,1)} %param.13) | copy-start | bytes 1572868
Sparse Core Ops, SparseCore 0:
  9.5 76.0 all-gather.8
  99.6 74.7 all-gather.12
  188.5 80.1 all-gather.14
  272.1 66.6 reduce-scatter.1
  340.7 72.4 all-gather.16
  415.2 47.5 all-gather.10

commit v2 on v1

v2 whole, which is shorter than its diff:
```python
import jax
import jax.numpy as jnp
from jax import lax
from jax.experimental import pallas as pl
from jax.experimental.pallas import tpu as pltpu
from jax.sharding import PartitionSpec as P

DOT_VMEM = 20 * 1024 * 1024
SQUARE_VMEM = 32 * 1024 * 1024


def blocks_dot(blocks, sources, weights, base, last):
    rows, depth = blocks[0].shape
    cols = weights.shape[1]
    count = len(blocks)
    halves = 2 if depth % 256 == 0 else 1
    tile = depth // halves

    def body(sources_ref, *refs):
        block_refs, rest = refs[:count], refs[count:]
        if base is None:
            weights_ref, out_ref, total = rest
        else:
            weights_ref, base_ref, out_ref, total = rest
        which, half = pl.program_id(0), pl.program_id(1)

        @pl.when((which == 0) & (half == 0))
        def _():
            if base is None:
                total[...] = jnp.zeros_like(total)
            else:
                total[...] = base_ref[...].astype(jnp.float32)

        for i in range(count):
            for j in range(halves):

                @pl.when((which == i) & (half == j))
                def _():
                    total[...] += jnp.dot(
                        block_refs[i][:, j * tile : (j + 1) * tile],
                        weights_ref[...],
                        preferred_element_type=jnp.float32,
                    )

        @pl.when((which == count - 1) & (half == halves - 1))
        def _():
            out_ref[...] = total[...].astype(out_ref.dtype)

    def whole(shape):
        return pl.BlockSpec(shape, lambda i, j, s: (0, 0))

    out_type = jnp.bfloat16 if last else jnp.float32
    return pl.pallas_call(
        body,
        grid_spec=pltpu.PrefetchScalarGridSpec(
            num_scalar_prefetch=1,
            grid=(count, halves),
            in_specs=[whole((rows, depth))] * count
            + [pl.BlockSpec((tile, cols), lambda i, j, s: (s[i] * halves + j, 0))]
            + ([] if base is None else [whole((rows, cols))]),
            out_specs=whole((rows, cols)),
            scratch_shapes=[pltpu.VMEM((rows, cols), jnp.float32)],
        ),
        out_shape=jax.ShapeDtypeStruct((rows, cols), out_type),
        compiler_params=pltpu.CompilerParams(vmem_limit_bytes=DOT_VMEM),
        cost_estimate=pl.CostEstimate(
            flops=2 * count * rows * depth * cols,
            bytes_accessed=2 * count * (rows + cols) * depth,
            transcendentals=0,
        ),
        name="blocks_dot",
    )(jnp.stack(sources).astype(jnp.int32), *blocks, weights, *([] if base is None else [base]))


def gather_blocks(own, section, shards, inner):
    def swapped(block, flip):
        here = [section * shards + i for i in range(shards)]
        there = [section * shards + (i ^ flip) for i in range(shards)]
        return lax.ppermute(block, ("section", "shard"), list(zip(here, there)))

    got = {(0, 0): own}
    for dz in range(1, shards // inner):
        got[dz, 0] = swapped(own, dz * inner)
    for dz in range(shards // inner):
        for dx in range(1, inner):
            got[dz, dx] = swapped(got[dz, 0], dx)
    return got


def mean_square(rot_out, rot_in, micro, seq):
    runs, rows, width = rot_in.shape
    eig_rows = rot_out.shape[1]

    def body(out_ref_in, in_ref, eig_ref):
        for m in range(micro):
            rows_of = slice(m * seq, (m + 1) * seq)
            product = lax.dot_general(
                out_ref_in[rows_of, :],
                in_ref[0, rows_of, :],
                (((0,), (0,)), ((), ())),
                preferred_element_type=jnp.float32,
            )
            square = product * product
            eig_ref[...] = square if m == 0 else eig_ref[...] + square
        eig_ref[...] *= 1.0 / (seq * micro)

    return pl.pallas_call(
        body,
        grid=(runs,),
        in_specs=[
            pl.BlockSpec((rows, eig_rows), lambda i: (0, 0)),
            pl.BlockSpec((1, rows, width), lambda i: (i, 0, 0)),
        ],
        out_specs=pl.BlockSpec((eig_rows, width), lambda i: (0, i)),
        out_shape=jax.ShapeDtypeStruct((eig_rows, runs * width), jnp.float32),
        compiler_params=pltpu.CompilerParams(vmem_limit_bytes=SQUARE_VMEM),
        cost_estimate=pl.CostEstimate(
            flops=2 * rows * eig_rows * runs * width * 8,
            bytes_accessed=4 * eig_rows * runs * width,
            transcendentals=0,
        ),
        name="mean_square",
    )(rot_out, rot_in)


def per_device(activations, top_grad, projection, basis_out, basis_in):
    sections = lax.axis_size("section")
    shards = lax.axis_size("shard")
    section = lax.axis_index("section")
    micro, seq, feat_loc = top_grad.shape
    rows = micro * seq
    eig_a = basis_in.shape[2]
    weights, out_cols = projection[0], basis_out[0]

    partial_rot = jnp.dot(
        activations[0].reshape(rows, feat_loc), basis_in[0], preferred_element_type=jnp.float32
    ).astype(jnp.bfloat16)
    partial_rot = partial_rot.reshape(rows, shards, eig_a // shards).transpose(1, 0, 2)
    own_rot = lax.psum_scatter(partial_rot, "shard", scatter_dimension=0, tiled=False)
    rot_in = lax.all_gather(own_rot, "shard", axis=0)

    inner = 1
    while 2 * (2 * inner) ** 2 <= shards:
        inner *= 2
    shard = lax.axis_index("shard")
    current = top_grad.reshape(rows, feat_loc)
    rot_out = None
    for step in range(sections):
        turn = sections - 1 - step
        blocks = gather_blocks(current, turn, shards, inner)
        source = {(dz, dx): shard ^ (dz * inner + dx) for dz, dx in blocks}
        groups = [[(dz, dx) for dx in range(inner)] for dz in range(shards // inner)]
        final = turn == 0
        total = None if final else current
        for n, group in enumerate(groups):
            total = blocks_dot(
                [blocks[g] for g in group],
                [source[g] for g in group],
                out_cols if final else weights,
                total,
                n == len(groups) - 1,
            )
        if final:
            rot_out = total if rot_out is None else jnp.where(section == 0, total, rot_out)
            break
        received = lax.ppermute(total, "section", [(turn, turn - 1)])
        flat = list(blocks.values())
        rot_out = lax.cond(
            section == turn,
            lambda *a: blocks_dot(a[1:], list(source.values()), out_cols, None, True),
            lambda *a: a[0],
            jnp.zeros((rows, out_cols.shape[1]), jnp.bfloat16) if rot_out is None else rot_out,
            *flat,
        )
        current = received
    return mean_square(rot_out, rot_in, micro, seq)[None]


def solution(mesh):
    return jax.shard_map(
        per_device,
        mesh=mesh,
        in_specs=(
            P("section", None, None, "shard"),
            P(None, None, "shard"),
            P("section", None, "shard"),
            P("section", None, "shard"),
            P("section", "shard", None),
        ),
        out_specs=P("section", "shard", None),
        check_vma=False,
    )
```

time: 483 us -> 291 us (0.60)
  waiting for transfers between devices: 396 us -> 132 us
  starting transfers between devices: 2.89 us -> 55.7 us
  local copies, waits for them, and re-layouts: 10.4 us -> 28.1 us
    all_gather x4 -> x0, waiting for transfers between devices: 298 us -> none  [per_device(): blocks = lax.all_gather(current, 'shard', axis=0)]
    ppermute x3 -> x31, waiting for transfers between devices: 2.51 us -> 88.7 us  [the longest x3 77.2 us: per_device(): received = lax.ppermute(total, 'section', [(turn, turn - 1)])]
    ppermute x3 -> x31, starting transfers between devices: 2.68 us -> 55.6 us  [the longest x28 52.9 us: swapped(): return lax.ppermute(block, ('section', 'shard'), list(zip(here, there)))]
    all_gather x1, waiting for transfers between devices: 41.3 us -> 0.02 us  [per_device(): rot_in = lax.all_gather(own_rot, 'shard', axis=0)]
    unnamed x18 -> x66, local copies, waits for them, and re-layouts: 6.12 us -> 23.8 us
    reduce_scatter x1, waiting for transfers between devices: 54 us -> 42.8 us  [per_device(): lax.psum_scatter(partial_rot, 'shard', scatter_dimension=0, tiled=False)]
    pallas_call x4 -> x16, Pallas kernels: 42.3 us -> 42.1 us  [blocks_dot(): pl.pallas_call(body, grid_spec=pltpu.PrefetchScalarGridSpec(num_scalar_pr...]
  transfers between devices with their start and end apart: 9 -> 33, of which waited for: 7 -> 4; matrix products, arithmetic and copies ran while one was open for 2% -> 1% of each run, Pallas kernels for 4% -> 15%
where the time goes in v2:
time: 291 us; the launch traced here: 289 us
  waiting for transfers between devices  132 us (45%)
  starting transfers between devices  55.7 us (19%)
  Pallas kernels  53.3 us (18%)
  local copies, waits for them, and re-layouts  28.1 us (10%)
  between operations  14.4 us (5%)
  matrix products  5.77 us (2%)
    ppermute x3, waiting for transfers between devices, per_device(): received = lax.ppermute(total, 'section', [(turn, turn - 1)])  77.2 us
    ppermute x28, starting transfers between devices, swapped(): return lax.ppermute(block, ('section', 'shard'), list(zip(here, there)))  52.9 us
    reduce_scatter x1, waiting for transfers between devices, per_device(): lax.psum_scatter(partial_rot, 'shard', scatter_dimension=0, tiled=False)  42.8 us
    pallas_call x16, Pallas kernels, blocks_dot(): pl.pallas_call(body, grid_spec=pltpu.PrefetchScalarGridSpec(num_scalar_pr...  42.1 us
    unnamed x66, local copies, waits for them, and re-layouts  23.8 us
    ppermute x28, waiting for transfers between devices, swapped(): return lax.ppermute(block, ('section', 'shard'), list(zip(here, there)))  11.5 us
    pallas_call x1, Pallas kernels, mean_square(): pl.pallas_call(body, grid=(runs,), in_specs=[pl.BlockSpec((rows, eig_rows...  11.2 us
  transfers between devices with their start and end apart: 33, of which 4 were waited for; matrix products, arithmetic and copies ran while one was open for 1% of the time, Pallas kernels for 15%

profile of v2, /device:TPU:0, one launch (start us, length us, event | category | flops | bytes accessed | tf_op | source)
XLA Modules:
  0.0 289.4 jit_solution(6482783368612594490)
XLA Ops:
  7.6 5.8 %fusion.2 = bf16[256,4096]{1,0:T(8,128)(2,1)S(1)} fusion(bf16[256,1024]{1,0:T(8,128)(2,1)S(1)} %bitcast.46, bf16[1,1024,4096]{2,1,0:T(8,128)(2,1)} %param.15), kind=kOutput, calls=%fused_computation.2 | convolution fusion | flops 2148532224 | bytes 11010048 | tf_op jit(solution)/shard_map/dot_general | solution.py:135
  13.4 2.5 copy.8
  21.2 6.1 %copy-done.2 = bf16[1,8192,1024]{2,1,0:T(8,128)(2,1)S(1)} copy-done((bf16[1,8192,1024]{2,1,0:T(8,128)(2,1)S(1)}, bf16[1,8192,1024]{2,1,0:T(8,128)(2,1)}, u32[]{:S(2)}) %copy-start.2) | copy-done | bytes 16777240
  27.3 2.4 blocks_dot.22.refs_3_
  29.8 3.3 %copy-done.3 = bf16[1,8192,1024]{2,1,0:T(8,128)(2,1)S(1)} copy-done((bf16[1,8192,1024]{2,1,0:T(8,128)(2,1)S(1)}, bf16[1,8192,1024]{2,1,0:T(8,128)(2,1)}, u32[]{:S(2)}) %copy-start.3) | copy-done | bytes 16777240
  33.1 2.4 blocks_dot.23.refs_3_
  35.6 2.4 blocks_dot.24.refs_3_
  38.1 2.4 blocks_dot.25
  46.4 2.4 blocks_dot.26.refs_3_
  48.9 2.4 blocks_dot.27.refs_3_
  51.4 2.4 blocks_dot.28.refs_3_
  53.9 2.4 blocks_dot.29
  57.0 42.8 %reduce-scatter.2.cloned.1.call-done = bf16[1,256,512]{1,2,0:T(8,128)(2,1)} async-done(((bf16[8,256,512]{1,2,0:T(8,128)(2,1)}), bf16[1,256,512]{1,2,0:T(8,128)(2,1)}) %reduce-scatter.2.cloned.1.call-update) | async-done | bytes 262160 | tf_op jit(solution)/shard_map/reduce_scatter | solution.py:139
  106.7 5.8 %copy-done.4 = bf16[1,8192,1024]{2,1,0:T(8,128)(2,1)S(1)} copy-done((bf16[1,8192,1024]{2,1,0:T(8,128)(2,1)S(1)}, bf16[1,8192,1024]{2,1,0:T(8,128)(2,1)}, u32[]{:S(2)}) %copy-start.4) | copy-done | bytes 16777240
  112.4 2.4 blocks_dot.30.refs_3_
  114.9 5.8 %copy-done.5 = bf16[1,8192,1024]{2,1,0:T(8,128)(2,1)S(1)} copy-done((bf16[1,8192,1024]{2,1,0:T(8,128)(2,1)S(1)}, bf16[1,8192,1024]{2,1,0:T(8,128)(2,1)}, u32[]{:S(2)}) %copy-start.5) | copy-done | bytes 16777240
  120.7 2.4 blocks_dot.31.refs_3_
  123.2 2.4 blocks_dot.32.refs_3_
  125.6 2.4 blocks_dot.33
  129.4 77.2 %collective-permute-done.23.refs_0_ = bf16[256,1024]{1,0:T(8,128)(2,1)S(1)} collective-permute-done((bf16[256,1024]{1,0:T(8,128)(2,1)S(1)}, bf16[256,1024]{1,0:T(8,128)(2,1)S(1)}, u32[]{:S(2)}, u32[]{:S(2)}) %collective-permute-start.23) | collective-permute-done | bytes 524320 | tf_op jit(solution)/shard_map/ppermute | solution.py:166
  206.6 20.6 %collective-permute-start.28 = (bf16[256,1024]{1,0:T(8,128)(2,1)S(1)}, bf16[256,1024]{1,0:T(8,128)(2,1)S(1)}, u32[]{:S(2)}, u32[]{:S(2)}) collective-permute-start(bf16[256,1024]{1,0:T(8,128)(2,1)S(1)} %collective-permute-done.23.refs_0_), channel_id=1, source_target_pairs={{0,2},{1,3},{2,0},{3,1},{4,6},{5,7},{6,4},{7,5}} | collective-permute-start | bytes 1572872 | tf_op jit(solution)/shard_map/ppermute | solution.py:79
  227.2 2.5 collective-permute-start.26
  229.7 3.7 %collective-permute-start.24 = (bf16[256,1024]{1,0:T(8,128)(2,1)S(1)}, bf16[256,1024]{1,0:T(8,128)(2,1)S(1)}, u32[]{:S(2)}, u32[]{:S(2)}) collective-permute-start(bf16[256,1024]{1,0:T(8,128)(2,1)S(1)} %collective-permute-done.23.refs_0_), channel_id=1, source_target_pairs={{0,6},{1,7},{2,4},{3,5},{4,2},{5,3},{6,0},{7,1}} | collective-permute-start | bytes 1572872 | tf_op jit(solution)/shard_map/ppermute | solution.py:79
  233.4 2.6 collective-permute-start.30
  237.2 3.0 %collective-permute-start.29 = (bf16[256,1024]{1,0:T(8,128)(2,1)S(1)}, bf16[256,1024]{1,0:T(8,128)(2,1)}, u32[]{:S(2)}, u32[]{:S(2)}) collective-permute-start(bf16[256,1024]{1,0:T(8,128)(2,1)S(1)} %collective-permute-done.28.refs_0_), channel_id=1, source_target_pairs={{0,1},{1,0},{2,3},{3,2},{4,5},{5,4},{6,7},{7,6}} | collective-permute-start | bytes 1572872 | tf_op jit(solution)/shard_map/ppermute | solution.py:79
  240.1 10.3 %collective-permute-done.26.refs_0_ = bf16[256,1024]{1,0:T(8,128)(2,1)S(1)} collective-permute-done((bf16[256,1024]{1,0:T(8,128)(2,1)S(1)}, bf16[256,1024]{1,0:T(8,128)(2,1)S(1)}, u32[]{:S(2)}, u32[]{:S(2)}) %collective-permute-start.26) | collective-permute-done | bytes 524320 | tf_op jit(solution)/shard_map/ppermute | solution.py:79
  250.4 2.2 collective-permute-start.27
  252.6 3.6 %collective-permute-start.25 = (bf16[256,1024]{1,0:T(8,128)(2,1)S(1)}, bf16[256,1024]{1,0:T(8,128)(2,1)S(1)}, u32[]{:S(2)}, u32[]{:S(2)}) collective-permute-start(bf16[256,1024]{1,0:T(8,128)(2,1)S(1)} %collective-permute-done.24.refs_0_), channel_id=1, source_target_pairs={{0,1},{1,0},{2,3},{3,2},{4,5},{5,4},{6,7},{7,6}} | collective-permute-start | bytes 1572872 | tf_op jit(solution)/shard_map/ppermute | solution.py:79
  256.6 4.0 %blocks_dot.34.refs_3_ = f32[256,512]{1,0:T(8,128)S(1)} custom-call(s32[2]{0:T(128)S(1)} %pad_add_fusion.3.sources_ref, bf16[256,1024]{1,0:T(8,128)(2,1)S(1)} %collective-permute-done.23.refs_0_, bf16[256,1024]{1,0:T(8,128)(2,1)S(1)} %collective-permute-done.30.refs_1_, bf16[8192,512]{1,0:T(8,128)(2,1)} %bitcast.62), custom_call_target="tpu_custom_call" | custom-call | flops 536870912 | bytes 3145728 | tf_op jit(solution)/shard_map/blocks_dot/pallas_call | solution.py:53
  260.6 4.1 %blocks_dot.35.refs_3_ = f32[256,512]{1,0:T(8,128)S(1)} custom-call(s32[2]{0:T(128)S(1)} %pad_add_fusion.2.sources_ref, bf16[256,1024]{1,0:T(8,128)(2,1)S(1)} %collective-permute-done.28.refs_0_, bf16[256,1024]{1,0:T(8,128)(2,1)} %collective-permute-done.29.refs_1_, bf16[8192,512]{1,0:T(8,128)(2,1)} %bitcast.63, f32[256,512]{1,0:T(8,128)S(1)} %blocks_dot.34.refs_3_), custom_call_target="tpu_custom_call" | custom-call | flops 536870912 | bytes 3145728 | tf_op jit(solution)/shard_map/blocks_dot/pallas_call | solution.py:53
  264.8 2.9 %blocks_dot.36.refs_3_ = f32[256,512]{1,0:T(8,128)S(1)} custom-call(s32[2]{0:T(128)S(1)} %pad_add_fusion.1.sources_ref, bf16[256,1024]{1,0:T(8,128)(2,1)S(1)} %collective-permute-done.26.refs_0_, bf16[256,1024]{1,0:T(8,128)(2,1)} %collective-permute-done.27.refs_1_, bf16[8192,512]{1,0:T(8,128)(2,1)S(1)} %bitcast.66, f32[256,512]{1,0:T(8,128)S(1)} %blocks_dot.35.refs_3_), custom_call_target="tpu_custom_call" | custom-call | flops 536870912 | bytes 3145728 | tf_op jit(solution)/shard_map/blocks_dot/pallas_call | solution.py:53
  271.4 11.2 %mean_square.1 = f32[512,4096]{1,0:T(8,128)} custom-call(bf16[256,512]{1,0:T(8,128)(2,1)S(1)} %broadcast_select_fusion.out_ref_in, bf16[8,256,512]{2,1,0:T(8,128)(2,1)S(1)} %copy-done.6), custom_call_target="tpu_custom_call" | custom-call | flops 8589934592 | bytes 8388608 | tf_op jit(solution)/shard_map/mean_square/pallas_call | solution.py:107
  (132 shorter events, 25.9 us)
Async XLA Ops:
  6.5 93.3 %reduce-scatter.2.cloned.1.call-start = ((), (), s32[]{:S(2)}) async-start(), calls=%async_computation.1 | async-start | bytes 2359296 | tf_op jit(solution)/shard_map/reduce_scatter | solution.py:139
  15.8 253.9 %all-gather.2.cloned.1.call-start = ((), (), s32[]{:S(2)}) async-start(), calls=%async_computation.2 | async-start | bytes 2359296 | tf_op jit(solution)/shard_map/all_gather | solution.py:140
  15.9 2.8 collective-permute-start.4
  16.6 2.9 %collective-permute-start.2 = (bf16[256,1024]{1,0:T(8,128)(2,1)S(1)}, bf16[256,1024]{1,0:T(8,128)(2,1)S(1)}, u32[]{:S(2)}, u32[]{:S(2)}) collective-permute-start(bf16[256,1024]{1,0:T(8,128)(2,1)S(1)} %bitcast.71), channel_id=1, source_target_pairs={{24,28},{25,29},{26,30},{27,31},{28,24},{29,25},{30,26},{31,27}} | collective-permute-start | bytes 1572872 | tf_op jit(solution)/shard_map/ppermute | solution.py:79
  17.3 3.0 %collective-permute-start = (bf16[256,1024]{1,0:T(8,128)(2,1)S(1)}, bf16[256,1024]{1,0:T(8,128)(2,1)S(1)}, u32[]{:S(2)}, u32[]{:S(2)}) collective-permute-start(bf16[256,1024]{1,0:T(8,128)(2,1)S(1)} %bitcast.72), channel_id=1, source_target_pairs={{24,30},{25,31},{26,28},{27,29},{28,26},{29,27},{30,24},{31,25}} | collective-permute-start | bytes 1572872 | tf_op jit(solution)/shard_map/ppermute | solution.py:79
  18.0 3.1 %collective-permute-start.6 = (bf16[256,1024]{1,0:T(8,128)(2,1)S(1)}, bf16[256,1024]{1,0:T(8,128)(2,1)S(1)}, u32[]{:S(2)}, u32[]{:S(2)}) collective-permute-start(bf16[256,1024]{1,0:T(8,128)(2,1)S(1)} %bitcast.73), channel_id=1, source_target_pairs={{24,25},{25,24},{26,27},{27,26},{28,29},{29,28},{30,31},{31,30}} | collective-permute-start | bytes 1572872 | tf_op jit(solution)/shard_map/ppermute | solution.py:79
  18.7 11.0 %collective-permute-start.5 = (bf16[256,1024]{1,0:T(8,128)(2,1)S(1)}, bf16[256,1024]{1,0:T(8,128)(2,1)S(1)}, u32[]{:S(2)}, u32[]{:S(2)}) collective-permute-start(bf16[256,1024]{1,0:T(8,128)(2,1)S(1)} %collective-permute-done.4.refs_0_), channel_id=1, source_target_pairs={{24,25},{25,24},{26,27},{27,26},{28,29},{29,28},{30,31},{31,30}} | collective-permute-start | bytes 1572872 | tf_op jit(solution)/shard_map/ppermute | solution.py:79
  19.5 16.0 %collective-permute-start.3 = (bf16[256,1024]{1,0:T(8,128)(2,1)S(1)}, bf16[256,1024]{1,0:T(8,128)(2,1)S(1)}, u32[]{:S(2)}, u32[]{:S(2)}) collective-permute-start(bf16[256,1024]{1,0:T(8,128)(2,1)S(1)} %collective-permute-done.2.refs_0_), channel_id=1, source_target_pairs={{24,25},{25,24},{26,27},{27,26},{28,29},{29,28},{30,31},{31,30}} | collective-permute-start | bytes 1572872 | tf_op jit(solution)/shard_map/ppermute | solution.py:79
  20.3 17.7 %collective-permute-start.1 = (bf16[256,1024]{1,0:T(8,128)(2,1)S(1)}, bf16[256,1024]{1,0:T(8,128)(2,1)S(1)}, u32[]{:S(2)}, u32[]{:S(2)}) collective-permute-start(bf16[256,1024]{1,0:T(8,128)(2,1)S(1)} %collective-permute-done.refs_0_), channel_id=1, source_target_pairs={{24,25},{25,24},{26,27},{27,26},{28,29},{29,28},{30,31},{31,30}} | collective-permute-start | bytes 1572872 | tf_op jit(solution)/shard_map/ppermute | solution.py:79
  41.2 2.8 collective-permute-start.12
  41.9 2.8 collective-permute-start.10
  42.7 2.9 collective-permute-start.8
  43.4 3.1 %collective-permute-start.14 = (bf16[256,1024]{1,0:T(8,128)(2,1)S(1)}, bf16[256,1024]{1,0:T(8,128)(2,1)S(1)}, u32[]{:S(2)}, u32[]{:S(2)}) collective-permute-start(bf16[256,1024]{1,0:T(8,128)(2,1)S(1)} %collective-permute-done.7.refs_0_.refs_3_), channel_id=1, source_target_pairs={{16,17},{17,16},{18,19},{19,18},{20,21},{21,20},{22,23},{23,22}} | collective-permute-start | bytes 1572872 | tf_op jit(solution)/shard_map/ppermute | solution.py:79
  44.1 4.8 %collective-permute-start.13 = (bf16[256,1024]{1,0:T(8,128)(2,1)S(1)}, bf16[256,1024]{1,0:T(8,128)(2,1)S(1)}, u32[]{:S(2)}, u32[]{:S(2)}) collective-permute-start(bf16[256,1024]{1,0:T(8,128)(2,1)S(1)} %collective-permute-done.12.refs_0_), channel_id=1, source_target_pairs={{16,17},{17,16},{18,19},{19,18},{20,21},{21,20},{22,23},{23,22}} | collective-permute-start | bytes 1572872 | tf_op jit(solution)/shard_map/ppermute | solution.py:79
  44.8 6.6 %collective-permute-start.11 = (bf16[256,1024]{1,0:T(8,128)(2,1)S(1)}, bf16[256,1024]{1,0:T(8,128)(2,1)S(1)}, u32[]{:S(2)}, u32[]{:S(2)}) collective-permute-start(bf16[256,1024]{1,0:T(8,128)(2,1)S(1)} %collective-permute-done.10.refs_0_), channel_id=1, source_target_pairs={{16,17},{17,16},{18,19},{19,18},{20,21},{21,20},{22,23},{23,22}} | collective-permute-start | bytes 1572872 | tf_op jit(solution)/shard_map/ppermute | solution.py:79
  45.5 8.3 %collective-permute-start.9 = (bf16[256,1024]{1,0:T(8,128)(2,1)S(1)}, bf16[256,1024]{1,0:T(8,128)(2,1)S(1)}, u32[]{:S(2)}, u32[]{:S(2)}) collective-permute-start(bf16[256,1024]{1,0:T(8,128)(2,1)S(1)} %collective-permute-done.8.refs_0_), channel_id=1, source_target_pairs={{16,17},{17,16},{18,19},{19,18},{20,21},{21,20},{22,23},{23,22}} | collective-permute-start | bytes 1572872 | tf_op jit(solution)/shard_map/ppermute | solution.py:79
  56.3 45.3 %collective-permute-start.15 = (bf16[256,1024]{1,0:T(8,128)(2,1)S(1)}, bf16[256,1024]{1,0:T(8,128)(2,1)S(1)}, u32[]{:S(2)}, u32[]{:S(2)}) collective-permute-start(bf16[256,1024]{1,0:T(8,128)(2,1)S(1)} %blocks_dot.29), channel_id=1, source_target_pairs={{16,8},{17,9},{18,10},{19,11},{20,12},{21,13},{22,14},{23,15}} | collective-permute-start | bytes 1572872 | tf_op jit(solution)/shard_map/ppermute | solution.py:166
  101.7 2.8 collective-permute-start.20
  102.4 2.8 collective-permute-start.18
  103.1 2.9 collective-permute-start.16
  103.8 2.9 collective-permute-start.22
  104.5 10.4 %collective-permute-start.21 = (bf16[256,1024]{1,0:T(8,128)(2,1)S(1)}, bf16[256,1024]{1,0:T(8,128)(2,1)S(1)}, u32[]{:S(2)}, u32[]{:S(2)}) collective-permute-start(bf16[256,1024]{1,0:T(8,128)(2,1)S(1)} %collective-permute-done.20.refs_0_), channel_id=1, source_target_pairs={{8,9},{9,8},{10,11},{11,10},{12,13},{13,12},{14,15},{15,14}} | collective-permute-start | bytes 1572872 | tf_op jit(solution)/shard_map/ppermute | solution.py:79
  105.2 17.9 %collective-permute-start.19 = (bf16[256,1024]{1,0:T(8,128)(2,1)S(1)}, bf16[256,1024]{1,0:T(8,128)(2,1)S(1)}, u32[]{:S(2)}, u32[]{:S(2)}) collective-permute-start(bf16[256,1024]{1,0:T(8,128)(2,1)S(1)} %collective-permute-done.18.refs_0_), channel_id=1, source_target_pairs={{8,9},{9,8},{10,11},{11,10},{12,13},{13,12},{14,15},{15,14}} | collective-permute-start | bytes 1572872 | tf_op jit(solution)/shard_map/ppermute | solution.py:79
  105.9 19.7 %collective-permute-start.17 = (bf16[256,1024]{1,0:T(8,128)(2,1)S(1)}, bf16[256,1024]{1,0:T(8,128)(2,1)S(1)}, u32[]{:S(2)}, u32[]{:S(2)}) collective-permute-start(bf16[256,1024]{1,0:T(8,128)(2,1)S(1)} %collective-permute-done.16.refs_0_), channel_id=1, source_target_pairs={{8,9},{9,8},{10,11},{11,10},{12,13},{13,12},{14,15},{15,14}} | collective-permute-start | bytes 1572872 | tf_op jit(solution)/shard_map/ppermute | solution.py:79
  128.1 78.5 %collective-permute-start.23 = (bf16[256,1024]{1,0:T(8,128)(2,1)S(1)}, bf16[256,1024]{1,0:T(8,128)(2,1)S(1)}, u32[]{:S(2)}, u32[]{:S(2)}) collective-permute-start(bf16[256,1024]{1,0:T(8,128)(2,1)S(1)} %blocks_dot.33), channel_id=1, source_target_pairs={{8,0},{9,1},{10,2},{11,3},{12,4},{13,5},{14,6},{15,7}} | collective-permute-start | bytes 1572872 | tf_op jit(solution)/shard_map/ppermute | solution.py:166
  206.6 30.6 %collective-permute-start.28 = (bf16[256,1024]{1,0:T(8,128)(2,1)S(1)}, bf16[256,1024]{1,0:T(8,128)(2,1)S(1)}, u32[]{:S(2)}, u32[]{:S(2)}) collective-permute-start(bf16[256,1024]{1,0:T(8,128)(2,1)S(1)} %collective-permute-done.23.refs_0_), channel_id=1, source_target_pairs={{0,2},{1,3},{2,0},{3,1},{4,6},{5,7},{6,4},{7,5}} | collective-permute-start | bytes 1572872 | tf_op jit(solution)/shard_map/ppermute | solution.py:79
  227.2 23.3 %collective-permute-start.26 = (bf16[256,1024]{1,0:T(8,128)(2,1)S(1)}, bf16[256,1024]{1,0:T(8,128)(2,1)S(1)}, u32[]{:S(2)}, u32[]{:S(2)}) collective-permute-start(bf16[256,1024]{1,0:T(8,128)(2,1)S(1)} %collective-permute-done.23.refs_0_), channel_id=1, source_target_pairs={{0,4},{1,5},{2,6},{3,7},{4,0},{5,1},{6,2},{7,3}} | collective-permute-start | bytes 1572872 | tf_op jit(solution)/shard_map/ppermute | solution.py:79
  229.7 23.0 %collective-permute-start.24 = (bf16[256,1024]{1,0:T(8,128)(2,1)S(1)}, bf16[256,1024]{1,0:T(8,128)(2,1)S(1)}, u32[]{:S(2)}, u32[]{:S(2)}) collective-permute-start(bf16[256,1024]{1,0:T(8,128)(2,1)S(1)} %collective-permute-done.23.refs_0_), channel_id=1, source_target_pairs={{0,6},{1,7},{2,4},{3,5},{4,2},{5,3},{6,0},{7,1}} | collective-permute-start | bytes 1572872 | tf_op jit(solution)/shard_map/ppermute | solution.py:79
  233.4 23.2 %collective-permute-start.30 = (bf16[256,1024]{1,0:T(8,128)(2,1)S(1)}, bf16[256,1024]{1,0:T(8,128)(2,1)S(1)}, u32[]{:S(2)}, u32[]{:S(2)}) collective-permute-start(bf16[256,1024]{1,0:T(8,128)(2,1)S(1)} %collective-permute-done.23.refs_0_), channel_id=1, source_target_pairs={{0,1},{1,0},{2,3},{3,2},{4,5},{5,4},{6,7},{7,6}} | collective-permute-start | bytes 1572872 | tf_op jit(solution)/shard_map/ppermute | solution.py:79
  237.2 23.4 %collective-permute-start.29 = (bf16[256,1024]{1,0:T(8,128)(2,1)S(1)}, bf16[256,1024]{1,0:T(8,128)(2,1)}, u32[]{:S(2)}, u32[]{:S(2)}) collective-permute-start(bf16[256,1024]{1,0:T(8,128)(2,1)S(1)} %collective-permute-done.28.refs_0_), channel_id=1, source_target_pairs={{0,1},{1,0},{2,3},{3,2},{4,5},{5,4},{6,7},{7,6}} | collective-permute-start | bytes 1572872 | tf_op jit(solution)/shard_map/ppermute | solution.py:79
  250.4 14.3 %collective-permute-start.27 = (bf16[256,1024]{1,0:T(8,128)(2,1)S(1)}, bf16[256,1024]{1,0:T(8,128)(2,1)}, u32[]{:S(2)}, u32[]{:S(2)}) collective-permute-start(bf16[256,1024]{1,0:T(8,128)(2,1)S(1)} %collective-permute-done.26.refs_0_), channel_id=1, source_target_pairs={{0,1},{1,0},{2,3},{3,2},{4,5},{5,4},{6,7},{7,6}} | collective-permute-start | bytes 1572872 | tf_op jit(solution)/shard_map/ppermute | solution.py:79
  252.6 15.1 %collective-permute-start.25 = (bf16[256,1024]{1,0:T(8,128)(2,1)S(1)}, bf16[256,1024]{1,0:T(8,128)(2,1)S(1)}, u32[]{:S(2)}, u32[]{:S(2)}) collective-permute-start(bf16[256,1024]{1,0:T(8,128)(2,1)S(1)} %collective-permute-done.24.refs_0_), channel_id=1, source_target_pairs={{0,1},{1,0},{2,3},{3,2},{4,5},{5,4},{6,7},{7,6}} | collective-permute-start | bytes 1572872 | tf_op jit(solution)/shard_map/ppermute | solution.py:79
  (34 other events, 229.6 us)
Sparse Core Ops, SparseCore 0:
  16.0 83.8 reduce-scatter.1
  101.9 96.9 all-gather.1

commit v3 on v0

v3 whole, which is shorter than its diff:
```python
import jax
import jax.numpy as jnp
from jax import lax
from jax.experimental import pallas as pl
from jax.experimental.pallas import tpu as pltpu
from jax.sharding import PartitionSpec as P

DOT_VMEM = 50 * 1024 * 1024
SQUARE_VMEM = 40 * 1024 * 1024


def tile_dot(blocks, weights, picks, bases, out_type, cols, by_rows):
    rows, depth = blocks[0].shape
    count = len(blocks)
    width = 256 if cols % 256 == 0 else cols
    tiles = cols // width

    def body(picks_ref, *refs):
        total = None
        for block_ref, weight_ref in zip(refs[:count], refs[count : 2 * count]):
            part = jnp.dot(block_ref[...], weight_ref[...], preferred_element_type=jnp.float32)
            total = part if total is None else total + part
        for base_ref in refs[2 * count : -1]:
            total = total + base_ref[...].astype(jnp.float32)
        refs[-1][...] = total.astype(out_type)

    def weight_spec(i):
        if by_rows:
            return pl.BlockSpec((depth, width), lambda j, picked: (picked[i], j))
        return pl.BlockSpec((depth, width), lambda j, picked: (0, picked[i] * tiles + j))

    tile = pl.BlockSpec((rows, width), lambda j, picked: (0, j))
    whole = pl.BlockSpec((rows, depth), lambda j, picked: (0, 0))
    return pl.pallas_call(
        body,
        grid_spec=pltpu.PrefetchScalarGridSpec(
            num_scalar_prefetch=1,
            grid=(tiles,),
            in_specs=[whole] * count + [weight_spec(i) for i in range(count)] + [tile] * len(bases),
            out_specs=tile,
        ),
        out_shape=jax.ShapeDtypeStruct((rows, cols), out_type),
        compiler_params=pltpu.CompilerParams(vmem_limit_bytes=DOT_VMEM),
        cost_estimate=pl.CostEstimate(
            flops=2 * count * rows * depth * cols,
            bytes_accessed=2 * count * (rows + cols) * depth,
            transcendentals=0,
        ),
        name="tile_dot",
    )(jnp.stack(picks).astype(jnp.int32), *blocks, *[weights] * count, *bases)


def dot_if(active, blocks, weights, picks, bases, out_type, cols, by_rows):
    count = len(blocks)

    def run(*args):
        blocks, bases = args[:count], args[count:]
        return tile_dot(blocks, weights, picks, bases, out_type, cols, by_rows)

    def skip(*args):
        return jnp.zeros((args[0].shape[0], cols), out_type)

    return lax.cond(active, run, skip, *blocks, *bases)


def mean_square(rot_out, blocks, picks, micro, seq):
    count = len(blocks)
    rows, width = blocks[0].shape
    eig_rows = rot_out.shape[1]

    def body(picks_ref, out_ref_in, *refs):
        block_refs, eig_ref, block = refs[:count], refs[count], refs[count + 1]
        for i in range(count):

            @pl.when(pl.program_id(0) == i)
            def _():
                block[...] = block_refs[i][...]

        for m in range(micro):
            rows_of = slice(m * seq, (m + 1) * seq)
            product = lax.dot_general(
                out_ref_in[rows_of, :],
                block[rows_of, :],
                (((0,), (0,)), ((), ())),
                preferred_element_type=jnp.float32,
            )
            square = product * product
            eig_ref[...] = square if m == 0 else eig_ref[...] + square
        eig_ref[...] *= 1.0 / (seq * micro)

    return pl.pallas_call(
        body,
        grid_spec=pltpu.PrefetchScalarGridSpec(
            num_scalar_prefetch=1,
            grid=(count,),
            in_specs=[pl.BlockSpec((rows, eig_rows), lambda i, picked: (0, 0))]
            + [pl.BlockSpec((rows, width), lambda i, picked: (0, 0))] * count,
            out_specs=pl.BlockSpec((eig_rows, width), lambda i, picked: (0, picked[i])),
            scratch_shapes=[pltpu.VMEM((rows, width), jnp.bfloat16)],
        ),
        out_shape=jax.ShapeDtypeStruct((eig_rows, count * width), jnp.float32),
        compiler_params=pltpu.CompilerParams(vmem_limit_bytes=SQUARE_VMEM),
        cost_estimate=pl.CostEstimate(
            flops=16 * rows * eig_rows * count * width,
            bytes_accessed=4 * eig_rows * count * width,
            transcendentals=0,
        ),
        name="mean_square",
    )(jnp.stack(picks).astype(jnp.int32), rot_out, *blocks)


def per_device(activations, top_grad, projection, basis_out, basis_in):
    sections = lax.axis_size("section")
    shards = lax.axis_size("shard")
    section, shard = lax.axis_index("section"), lax.axis_index("shard")
    micro, seq, feat_loc = top_grad.shape
    rows = micro * seq
    width = basis_in.shape[2] // shards
    weights, out_cols, in_cols = projection[0], basis_out[0], basis_in[0]
    inputs = activations[0].reshape(rows, feat_loc)
    top = top_grad.reshape(rows, feat_loc)

    inner = 1
    while 2 * (2 * inner) ** 2 <= shards:
        inner *= 2
    outer = shards // inner
    steps = [(dz, dx) for dz in range(outer) for dx in range(inner)]
    picks = {(dz, dx): shard ^ (dz * inner + dx) for dz, dx in steps}

    def moved(block, flip, pairs):
        route = [(a * shards + i, b * shards + (i ^ flip)) for a, b in pairs for i in range(shards)]
        return lax.ppermute(block, ("section", "shard"), route)

    def spread(block, pairs):
        stays = all(a == b for a, b in pairs)
        sent = {0: block if stays else moved(block, 0, pairs)}
        dz = 1
        while dz < outer:
            sent[dz] = moved(block, dz * inner, pairs)
            dz *= 2
        return sent

    def gather(sent, among):
        pairs = [(a, a) for a in among]
        got = {}
        for dz in range(outer):
            low = dz & -dz
            if low == dz:
                got[dz, 0] = sent[dz]
            else:
                got[dz, 0] = moved(got[dz ^ low, 0], low * inner, pairs)
            for dx in range(1, inner):
                low_x = dx & -dx
                got[dz, dx] = moved(got[dz, dx ^ low_x], low_x, pairs)
        return got

    groups = [[(dz, dx) for dx in range(inner)] for dz in range(outer)]
    if inner > 1:
        groups = groups[:-1] + [groups[-1][:-1], groups[-1][-1:]]

    def chain(sent, turns, rot_out):
        for turn in turns:
            mine = section == turn
            got = gather(sent, [turn])
            got[0, 0], rot_out = lax.optimization_barrier((got[0, 0], rot_out))
            final = turn == 0
            matrix = out_cols if final else weights
            bases = [] if final else [got[0, 0]]
            for n, group in enumerate(groups):
                total = dot_if(
                    mine,
                    [got[g] for g in group],
                    matrix,
                    [picks[g] for g in group],
                    bases,
                    jnp.bfloat16 if n == len(groups) - 1 else jnp.float32,
                    matrix.shape[1],
                    True,
                )
                bases = [total]
            if final:
                return jnp.where(mine, total, rot_out)
            sent = spread(total, [(turn, turn - 1)])
            rot_out = lax.cond(
                mine,
                lambda old, *blocks: tile_dot(
                    blocks,
                    out_cols,
                    [picks[g] for g in steps],
                    [],
                    jnp.bfloat16,
                    out_cols.shape[1],
                    True,
                ),
                lambda old, *blocks: old,
                rot_out,
                *[got[g] for g in steps],
            )
        return sent, rot_out

    def rotate_in(inputs, among):
        pairs = [(a, a) for a in among]
        mine = (section >= min(among)) & (section <= max(among))

        def product(dz, dx, bases):
            return dot_if(
                mine, [inputs], in_cols, [picks[dz, dx]], bases, jnp.bfloat16, width, False
            )

        crossed = {
            dz: [moved(product(dz, dx, []), dx, pairs) for dx in range(1, inner)]
            for dz in [*range(1, outer), 0]
        }
        arrived = [
            moved(product(dz, 0, crossed[dz]), dz * inner, pairs) for dz in range(1, outer)
        ]
        own = product(0, 0, crossed[0] + arrived)
        got = gather(spread(own, pairs), among)
        return [got[g] for g in steps]

    half = sections // 2
    upper = list(range(sections - 1, half - 1, -1))
    lower = list(range(half - 1, -1, -1))
    sent = spread(top, [(upper[0], upper[0])])
    rot_out = jnp.zeros((rows, out_cols.shape[1]), jnp.bfloat16)
    sent, rot_out = chain(sent, upper, rot_out)
    low_rot_in = rotate_in(inputs, lower)
    sent, low_rot_in, inputs = lax.optimization_barrier((sent, low_rot_in, inputs))
    rot_out = chain(sent, lower, rot_out)
    high_rot_in = rotate_in(inputs, upper)
    eigenvalues = lax.cond(
        section >= half,
        lambda rot_out, low, high: mean_square(rot_out, high, [picks[g] for g in steps], micro, seq),
        lambda rot_out, low, high: mean_square(rot_out, low, [picks[g] for g in steps], micro, seq),
        rot_out,
        low_rot_in,
        high_rot_in,
    )
    return eigenvalues[None]


def solution(mesh):
    return jax.shard_map(
        per_device,
        mesh=mesh,
        in_specs=(
            P("section", None, None, "shard"),
            P(None, None, "shard"),
            P("section", None, "shard"),
            P("section", None, "shard"),
            P("section", "shard", None),
        ),
        out_specs=P("section", "shard", None),
        check_vma=False,
    )
```

time: 718 us -> 360 us (0.50)
  the two profiles are of different devices: /device:TPU:0 before, /device:TPU:4 now
where the time goes in v3:
time: 360 us; the launch traced here: 358 us
  starting transfers between devices  226 us (63%)
  Pallas kernels  60.7 us (17%)
  waiting for transfers between devices  54 us (15%)
  local copies, waits for them, and re-layouts  15.6 us (4%)
    ppermute x59, starting transfers between devices, moved(): return lax.ppermute(block, ('section', 'shard'), route)  226 us
    ppermute x59, waiting for transfers between devices, moved(): return lax.ppermute(block, ('section', 'shard'), route)  54 us
    pallas_call x14, Pallas kernels, tile_dot(): pl.pallas_call(body, grid_spec=pltpu.PrefetchScalarGridSpec(num_scalar_pr...  47.3 us
    pallas_call x1, Pallas kernels, mean_square(): pl.pallas_call(body, grid_spec=pltpu.PrefetchScalarGridSpec(num_scalar_pr...  13.4 us
    unnamed x34, local copies, waits for them, and re-layouts  8.17 us
    another operation x24, local copies, waits for them, and re-layouts  7.24 us
  transfers between devices with their start and end apart: 59, of which 11 were waited for; matrix products, arithmetic and copies ran while one was open for 2% of the time, Pallas kernels for 13%

profile of v3, /device:TPU:4, one launch (start us, length us, event | category | flops | bytes accessed | tf_op | source)
XLA Modules:
  0.0 358.0 jit_solution(6666720725591809900)
XLA Ops:
  0.0 6.7 %collective-permute-start = (bf16[256,1024]{1,0:T(8,128)(2,1)}, bf16[256,1024]{1,0:T(8,128)(2,1)S(1)}, u32[]{:S(2)}, u32[]{:S(2)}) collective-permute-start(bf16[256,1024]{1,0:T(8,128)(2,1)} %bitcast.150), channel_id=1, source_target_pairs={{24,28},{25,29},{26,30},{27,31},{28,24},{29,25},{30,26},{31,27}} | collective-permute-start | bytes 1572872 | tf_op jit(solution)/shard_map/ppermute | solution.py:132
  6.7 6.8 %collective-permute-start.4 = (bf16[256,1024]{1,0:T(8,128)(2,1)}, bf16[256,1024]{1,0:T(8,128)(2,1)S(1)}, u32[]{:S(2)}, u32[]{:S(2)}) collective-permute-start(bf16[256,1024]{1,0:T(8,128)(2,1)} %bitcast.151), channel_id=1, source_target_pairs={{24,26},{25,27},{26,24},{27,25},{28,30},{29,31},{30,28},{31,29}} | collective-permute-start | bytes 1572872 | tf_op jit(solution)/shard_map/ppermute | solution.py:132
  13.4 13.4 %collective-permute-start.1 = (bf16[256,1024]{1,0:T(8,128)(2,1)S(1)}, bf16[256,1024]{1,0:T(8,128)(2,1)}, u32[]{:S(2)}, u32[]{:S(2)}) collective-permute-start(bf16[256,1024]{1,0:T(8,128)(2,1)S(1)} %collective-permute-done), channel_id=1, source_target_pairs={{24,26},{25,27},{26,24},{27,25},{28,30},{29,31},{30,28},{31,29}} | collective-permute-start | bytes 1572872 | tf_op jit(solution)/shard_map/ppermute | solution.py:132
  26.9 7.2 %collective-permute-start.6 = (bf16[256,1024]{1,0:T(8,128)(2,1)}, bf16[256,1024]{1,0:T(8,128)(2,1)}, u32[]{:S(2)}, u32[]{:S(2)}) collective-permute-start(bf16[256,1024]{1,0:T(8,128)(2,1)} %bitcast.152), channel_id=1, source_target_pairs={{24,25},{25,24},{26,27},{27,26},{28,29},{29,28},{30,31},{31,30}} | collective-permute-start | bytes 1572872 | tf_op jit(solution)/shard_map/ppermute | solution.py:132
  34.0 6.4 %collective-permute-start.5 = (bf16[256,1024]{1,0:T(8,128)(2,1)S(1)}, bf16[256,1024]{1,0:T(8,128)(2,1)S(1)}, u32[]{:S(2)}, u32[]{:S(2)}) collective-permute-start(bf16[256,1024]{1,0:T(8,128)(2,1)S(1)} %collective-permute-done.4), channel_id=1, source_target_pairs={{24,25},{25,24},{26,27},{27,26},{28,29},{29,28},{30,31},{31,30}} | collective-permute-start | bytes 1572872 | tf_op jit(solution)/shard_map/ppermute | solution.py:132
  47.0 31.0 %collective-permute-start.23 = (bf16[256,512]{1,0:T(8,128)(2,1)S(1)}, bf16[256,512]{1,0:T(8,128)(2,1)S(1)}, u32[]{:S(2)}, u32[]{:S(2)}) collective-permute-start(bf16[256,512]{1,0:T(8,128)(2,1)S(1)} %get-tuple-element.929), channel_id=1, source_target_pairs={{8,9},{9,8},{10,11},{11,10},{12,13},{13,12},{14,15},{15,14},{0,1},... | collective-permute-start | bytes 786440 | tf_op jit(solution)/shard_map/ppermute | solution.py:132
  89.0 17.3 %collective-permute-start.24 = (bf16[256,512]{1,0:T(8,128)(2,1)}, bf16[256,512]{1,0:T(8,128)(2,1)}, u32[]{:S(2)}, u32[]{:S(2)}) collective-permute-start(bf16[256,512]{1,0:T(8,128)(2,1)} %get-tuple-element.930), channel_id=1, source_target_pairs={{8,14},{9,15},{10,12},{11,13},{12,10},{13,11},{14,8},{15,9},{0,6},... | collective-permute-start | bytes 786440 | tf_op jit(solution)/shard_map/ppermute | solution.py:132
  126.5 4.8 %conditional.46 = (f32[256,1024]{1,0:T(8,128)S(1)}) conditional(s32[]{:T(128)} %convert_element_type.17, () %tuple.269, (s32[]{:T(128)}, s32[]{:T(128)}, bf16[256,1024]{1,0:T(8,128)(2,1)S(1)}, bf16[256,1024]{1,0:T(8,128)(2,1)}, bf16[8192,1024]{1,0:T(8,128)(2,1)}) %tuple.421), branch_computations={%region_12.0_spmd, %region_13.0_spmd} | conditional | flops 1073741824 | bytes 5242904 | solution.py:63
  126.6 4.7 %tile_dot.45 = f32[256,1024]{1,0:T(8,128)S(1)} custom-call(s32[2]{0:T(128)S(1)} %pad_add_fusion.3.picks_ref, bf16[256,1024]{1,0:T(8,128)(2,1)S(1)} %get-tuple-element.667.refs_0_.refs_4_, bf16[256,1024]{1,0:T(8,128)(2,1)} %get-tuple-element.668.refs_1_, bf16[8192,1024]{1,0:T(8,128)(2,1)} %get-tuple-element.669.refs_2_.refs_3_, ...), custom_call_target="tpu_custom_call" | custom-call | flops 1073741824 | bytes 5242880 | tf_op jit(solution)/shard_map/cond/branch_1_fun/tile_dot/pallas_call | solution.py:34
  131.4 35.1 %collective-permute-start.30 = (bf16[256,512]{1,0:T(8,128)(2,1)}, bf16[256,512]{1,0:T(8,128)(2,1)}, u32[]{:S(2)}, u32[]{:S(2)}) collective-permute-start(bf16[256,512]{1,0:T(8,128)(2,1)} %collective-permute-done.28), channel_id=1, source_target_pairs={{8,10},{9,11},{10,8},{11,9},{12,14},{13,15},{14,12},{15,13},{0,2},... | collective-permute-start | bytes 786440 | tf_op jit(solution)/shard_map/ppermute | solution.py:132
  166.4 5.8 %conditional.47 = (f32[256,1024]{1,0:T(8,128)}) conditional(s32[]{:T(128)} %convert_element_type.17, () %tuple.268, (s32[]{:T(128)}, s32[]{:T(128)}, bf16[256,1024]{1,0:T(8,128)(2,1)}, bf16[256,1024]{1,0:T(8,128)(2,1)}, bf16[8192,1024]{1,0:T(8,128)(2,1)}, /*index=5*/f32[256,1024]{1,0:T(8,128)S(1)}) %tuple.422), branch_computations={%region_14.0_spmd, %region_15.0_spmd} | conditional | flops 1073741824 | bytes 5242904 | solution.py:63
  166.5 5.7 %tile_dot.46 = f32[256,1024]{1,0:T(8,128)} custom-call(s32[2]{0:T(128)S(1)} %pad_add_fusion.4.picks_ref, bf16[256,1024]{1,0:T(8,128)(2,1)} %get-tuple-element.672.refs_0_, bf16[256,1024]{1,0:T(8,128)(2,1)} %get-tuple-element.673.refs_1_, bf16[8192,1024]{1,0:T(8,128)(2,1)} %get-tuple-element.674.refs_2_.refs_3_, ...), custom_call_target="tpu_custom_call" | custom-call | flops 1073741824 | bytes 5242880 | tf_op jit(solution)/shard_map/cond/branch_1_fun/tile_dot/pallas_call | solution.py:34
  173.6 5.1 %conditional.48 = (f32[256,1024]{1,0:T(8,128)S(1)}) conditional(s32[]{:T(128)} %convert_element_type.17, () %tuple.267, (s32[]{:T(128)}, s32[]{:T(128)}, bf16[256,1024]{1,0:T(8,128)(2,1)S(1)}, bf16[256,1024]{1,0:T(8,128)(2,1)}, bf16[8192,1024]{1,0:T(8,128)(2,1)}, /*index=5*/f32[256,1024]{1,0:T(8,128)}) %tuple.423), branch_computations={%region_16.0_spmd, %region_17.0_spmd} | conditional | flops 1073741824 | bytes 5242904 | solution.py:63
  173.6 5.0 %tile_dot.47 = f32[256,1024]{1,0:T(8,128)S(1)} custom-call(s32[2]{0:T(128)S(1)} %pad_add_fusion.5.picks_ref, bf16[256,1024]{1,0:T(8,128)(2,1)S(1)} %get-tuple-element.678.refs_0_, bf16[256,1024]{1,0:T(8,128)(2,1)} %get-tuple-element.679.refs_1_, bf16[8192,1024]{1,0:T(8,128)(2,1)} %get-tuple-element.680.refs_2_.refs_3_, ...), custom_call_target="tpu_custom_call" | custom-call | flops 1073741824 | bytes 5242880 | tf_op jit(solution)/shard_map/cond/branch_1_fun/tile_dot/pallas_call | solution.py:34
  178.7 4.4 %conditional.49 = (f32[256,1024]{1,0:T(8,128)}) conditional(s32[]{:T(128)} %convert_element_type.17, () %tuple.266, (s32[]{:T(128)}, bf16[256,1024]{1,0:T(8,128)(2,1)}, bf16[8192,1024]{1,0:T(8,128)(2,1)}, f32[256,1024]{1,0:T(8,128)S(1)}) %tuple.424), branch_computations={%region_18.0_spmd, %region_19.0_spmd} | conditional | flops 536870912 | bytes 2621448 | solution.py:63
  178.7 4.3 %tile_dot.48 = f32[256,1024]{1,0:T(8,128)} custom-call(s32[1]{0:T(128)} %bitcast.22.picks_ref, bf16[256,1024]{1,0:T(8,128)(2,1)} %get-tuple-element.683.refs_0_, bf16[8192,1024]{1,0:T(8,128)(2,1)} %get-tuple-element.684.refs_1_, f32[256,1024]{1,0:T(8,128)S(1)} %get-tuple-element.685.refs_2_), custom_call_target="tpu_custom_call" | custom-call | flops 536870912 | bytes 2621440 | tf_op jit(solution)/shard_map/cond/branch_1_fun/tile_dot/pallas_call | solution.py:34
  183.0 3.5 conditional.50
  183.0 3.5 tile_dot.49
  194.6 7.6 %collective-permute-done.16 = bf16[256,1024]{1,0:T(8,128)(2,1)} collective-permute-done((bf16[256,1024]{1,0:T(8,128)(2,1)S(1)}, bf16[256,1024]{1,0:T(8,128)(2,1)}, u32[]{:S(2)}, u32[]{:S(2)}) %collective-permute-start.16) | collective-permute-done | bytes 524320 | tf_op jit(solution)/shard_map/ppermute | solution.py:132
  202.2 5.5 %collective-permute-done.15 = bf16[256,1024]{1,0:T(8,128)(2,1)S(1)} collective-permute-done((bf16[256,1024]{1,0:T(8,128)(2,1)S(1)}, bf16[256,1024]{1,0:T(8,128)(2,1)S(1)}, u32[]{:S(2)}, u32[]{:S(2)}) %collective-permute-start.15) | collective-permute-done | bytes 524320 | tf_op jit(solution)/shard_map/ppermute | solution.py:132
  220.0 7.2 %conditional.59 = (bf16[256,512]{1,0:T(8,128)(2,1)S(1)}) conditional(s32[]{:T(128)} %convert_element_type.17, bf16[256,512]{1,0:T(8,128)(2,1)S(1)} %get-tuple-element.918, (s32[]{:T(128)}, s32[]{:T(128)}, s32[]{:T(128)}, s32[]{:T(128)}, s32[]{:T(128)}, /*index=5*/s32[]{:T(128)}, s32[]{:T(128)}, s32[]{:T(128)}, bf16[256,1024]{1,0:T(8,128)(2,1)S(1)}, ...), branch_computations={%region_38.0_spmd, %region_39.0_spmd} | conditional | flops 2147483648 | bytes 12582984 | solution.py:184
  220.3 6.9 %tile_dot.58 = bf16[256,512]{1,0:T(8,128)(2,1)S(1)} custom-call(s32[8]{0:T(128)S(1)} %stack.257.picks_ref, bf16[256,1024]{1,0:T(8,128)(2,1)S(1)} %get-tuple-element.729.refs_0_, bf16[256,1024]{1,0:T(8,128)(2,1)} %get-tuple-element.730.refs_1_, bf16[256,1024]{1,0:T(8,128)(2,1)} %get-tuple-element.731.refs_2_, bf16[256,1024]{1,0:T(8,128)(2,1)} %get-tuple-element.732.refs_3_, ...), custom_call_target="tpu_custom_call" | custom-call | flops 2147483648 | bytes 12582912 | tf_op jit(solution)/shard_map/cond/branch_1_fun/tile_dot/pallas_call | solution.py:34
  246.9 12.2 %collective-permute-start.51 = (bf16[256,512]{1,0:T(8,128)(2,1)}, bf16[256,512]{1,0:T(8,128)(2,1)S(1)}, u32[]{:S(2)}, u32[]{:S(2)}) collective-permute-start(bf16[256,512]{1,0:T(8,128)(2,1)} %copy-done.13), channel_id=1, source_target_pairs={{24,30},{25,31},{26,28},{27,29},{28,26},{29,27},{30,24},{31,25},{1... | collective-permute-start | bytes 786440 | tf_op jit(solution)/shard_map/ppermute | solution.py:132
  261.5 4.3 %collective-permute-start.49 = (bf16[256,512]{1,0:T(8,128)(2,1)}, bf16[256,512]{1,0:T(8,128)(2,1)}, u32[]{:S(2)}, u32[]{:S(2)}) collective-permute-start(bf16[256,512]{1,0:T(8,128)(2,1)} %get-tuple-element.948), channel_id=1, source_target_pairs={{24,28},{25,29},{26,30},{27,31},{28,24},{29,25},{30,26},{31,27},{1... | collective-permute-start | bytes 786440 | tf_op jit(solution)/shard_map/ppermute | solution.py:132
  268.2 3.4 collective-permute-start.47
  275.3 9.9 %collective-permute-done.49 = bf16[256,512]{1,0:T(8,128)(2,1)} collective-permute-done((bf16[256,512]{1,0:T(8,128)(2,1)}, bf16[256,512]{1,0:T(8,128)(2,1)}, u32[]{:S(2)}, u32[]{:S(2)}) %collective-permute-start.49) | collective-permute-done | bytes 262176 | tf_op jit(solution)/shard_map/ppermute | solution.py:132
  289.6 3.9 %collective-permute-start.53 = (bf16[256,512]{1,0:T(8,128)(2,1)}, bf16[256,512]{1,0:T(8,128)(2,1)}, u32[]{:S(2)}, u32[]{:S(2)}) collective-permute-start(bf16[256,512]{1,0:T(8,128)(2,1)} %get-tuple-element.951), channel_id=1, source_target_pairs={{24,26},{25,27},{26,24},{27,25},{28,30},{29,31},{30,28},{31,29},{1... | collective-permute-start | bytes 786440 | tf_op jit(solution)/shard_map/ppermute | solution.py:132
  294.9 8.7 %collective-permute-done.55 = bf16[256,512]{1,0:T(8,128)(2,1)} collective-permute-done((bf16[256,512]{1,0:T(8,128)(2,1)}, bf16[256,512]{1,0:T(8,128)(2,1)}, u32[]{:S(2)}, u32[]{:S(2)}) %collective-permute-start.55) | collective-permute-done | bytes 262176 | tf_op jit(solution)/shard_map/ppermute | solution.py:132
  307.5 7.9 %collective-permute-done.57 = bf16[256,512]{1,0:T(8,128)(2,1)} collective-permute-done((bf16[256,512]{1,0:T(8,128)(2,1)}, bf16[256,512]{1,0:T(8,128)(2,1)}, u32[]{:S(2)}, u32[]{:S(2)}) %collective-permute-start.57) | collective-permute-done | bytes 262176 | tf_op jit(solution)/shard_map/ppermute | solution.py:132
  332.3 5.6 %collective-permute-done.54 = bf16[256,512]{1,0:T(8,128)(2,1)} collective-permute-done((bf16[256,512]{1,0:T(8,128)(2,1)}, bf16[256,512]{1,0:T(8,128)(2,1)}, u32[]{:S(2)}, u32[]{:S(2)}) %collective-permute-start.54) | collective-permute-done | bytes 262176 | tf_op jit(solution)/shard_map/ppermute | solution.py:132
  341.1 13.5 %conditional.79 = (f32[1,512,4096]{2,1,0:T(8,128)S(1)}) conditional(s32[]{:T(128)} %convert_element_type.14, (s32[]{:T(128)}, s32[]{:T(128)}, s32[]{:T(128)}, s32[]{:T(128)}, s32[]{:T(128)}, /*index=5*/s32[]{:T(128)}, s32[]{:T(128)}, s32[]{:T(128)}, bf16[256,512]{1,0:T(8,128)(2,1)S(1)}, bf16[256,512]{1,0:T(8,128)(2,1)}, ...), branch_computations={%region_78.79_spmd, %region_79.80_spmd} | conditional | flops 8589934592 | bytes 8388680 | solution.py:231
  341.2 13.4 %mean_square.3 = f32[512,4096]{1,0:T(8,128)S(1)} custom-call(s32[8]{0:T(128)S(1)} %stack.314.picks_ref, bf16[256,512]{1,0:T(8,128)(2,1)S(1)} %get-tuple-element.861.out_ref_in, bf16[256,512]{1,0:T(8,128)(2,1)} %get-tuple-element.862.refs_0_, bf16[256,512]{1,0:T(8,128)(2,1)} %get-tuple-element.863.refs_1_, bf16[256,512]{1,0:T(8,128)(2,1)} %get-tuple-element.864.refs_2_, ...), custom_call_target="tpu_custom_call" | custom-call | flops 8589934592 | bytes 8388608 | tf_op jit(solution)/shard_map/cond/branch_1_fun/mean_square/pallas_call | solution.py:91
  (205 shorter events, 144.8 us)
Async XLA Ops:
  6.7 27.4 %collective-permute-start.4 = (bf16[256,1024]{1,0:T(8,128)(2,1)}, bf16[256,1024]{1,0:T(8,128)(2,1)S(1)}, u32[]{:S(2)}, u32[]{:S(2)}) collective-permute-start(bf16[256,1024]{1,0:T(8,128)(2,1)} %bitcast.151), channel_id=1, source_target_pairs={{24,26},{25,27},{26,24},{27,25},{28,30},{29,31},{30,28},{31,29}} | collective-permute-start | bytes 1572872 | tf_op jit(solution)/shard_map/ppermute | solution.py:132
  13.4 28.5 %collective-permute-start.1 = (bf16[256,1024]{1,0:T(8,128)(2,1)S(1)}, bf16[256,1024]{1,0:T(8,128)(2,1)}, u32[]{:S(2)}, u32[]{:S(2)}) collective-permute-start(bf16[256,1024]{1,0:T(8,128)(2,1)S(1)} %collective-permute-done), channel_id=1, source_target_pairs={{24,26},{25,27},{26,24},{27,25},{28,30},{29,31},{30,28},{31,29}} | collective-permute-start | bytes 1572872 | tf_op jit(solution)/shard_map/ppermute | solution.py:132
  45.6 40.9 %collective-permute-start.7 = (bf16[256,1024]{1,0:T(8,128)(2,1)}, bf16[256,1024]{1,0:T(8,128)(2,1)S(1)}, u32[]{:S(2)}, u32[]{:S(2)}) collective-permute-start(bf16[256,1024]{1,0:T(8,128)(2,1)} %get-tuple-element.917), channel_id=1, source_target_pairs={{24,20},{25,21},{26,22},{27,23},{28,16},{29,17},{30,18},{31,19}} | collective-permute-start | bytes 1572872 | tf_op jit(solution)/shard_map/ppermute | solution.py:132
  47.0 35.2 %collective-permute-start.23 = (bf16[256,512]{1,0:T(8,128)(2,1)S(1)}, bf16[256,512]{1,0:T(8,128)(2,1)S(1)}, u32[]{:S(2)}, u32[]{:S(2)}) collective-permute-start(bf16[256,512]{1,0:T(8,128)(2,1)S(1)} %get-tuple-element.929), channel_id=1, source_target_pairs={{8,9},{9,8},{10,11},{11,10},{12,13},{13,12},{14,15},{15,14},{0,1},... | collective-permute-start | bytes 786440 | tf_op jit(solution)/shard_map/ppermute | solution.py:132
  80.8 29.0 %collective-permute-start.13 = (bf16[256,1024]{1,0:T(8,128)(2,1)}, bf16[256,1024]{1,0:T(8,128)(2,1)S(1)}, u32[]{:S(2)}, u32[]{:S(2)}) collective-permute-start(bf16[256,1024]{1,0:T(8,128)(2,1)} %get-tuple-element.917), channel_id=1, source_target_pairs={{24,16},{25,17},{26,18},{27,19},{28,20},{29,21},{30,22},{31,23}} | collective-permute-start | bytes 1572872 | tf_op jit(solution)/shard_map/ppermute | solution.py:132
  82.2 31.1 %collective-permute-start.11 = (bf16[256,1024]{1,0:T(8,128)(2,1)}, bf16[256,1024]{1,0:T(8,128)(2,1)}, u32[]{:S(2)}, u32[]{:S(2)}) collective-permute-start(bf16[256,1024]{1,0:T(8,128)(2,1)} %get-tuple-element.917), channel_id=1, source_target_pairs={{24,18},{25,19},{26,16},{27,17},{28,22},{29,23},{30,20},{31,21}} | collective-permute-start | bytes 1572872 | tf_op jit(solution)/shard_map/ppermute | solution.py:132
  84.2 22.8 %collective-permute-start.18 = (bf16[256,512]{1,0:T(8,128)(2,1)}, bf16[256,512]{1,0:T(8,128)(2,1)S(1)}, u32[]{:S(2)}, u32[]{:S(2)}) collective-permute-start(bf16[256,512]{1,0:T(8,128)(2,1)} %copy-done.12), channel_id=1, source_target_pairs={{8,9},{9,8},{10,11},{11,10},{12,13},{13,12},{14,15},{15,14},{0,1},... | collective-permute-start | bytes 786440 | tf_op jit(solution)/shard_map/ppermute | solution.py:132
  86.6 32.5 %collective-permute-start.8 = (bf16[256,1024]{1,0:T(8,128)(2,1)S(1)}, bf16[256,1024]{1,0:T(8,128)(2,1)}, u32[]{:S(2)}, u32[]{:S(2)}) collective-permute-start(bf16[256,1024]{1,0:T(8,128)(2,1)S(1)} %collective-permute-done.7), channel_id=1, source_target_pairs={{16,18},{17,19},{18,16},{19,17},{20,22},{21,23},{22,20},{23,21}} | collective-permute-start | bytes 1572872 | tf_op jit(solution)/shard_map/ppermute | solution.py:132
  89.0 20.1 %collective-permute-start.24 = (bf16[256,512]{1,0:T(8,128)(2,1)}, bf16[256,512]{1,0:T(8,128)(2,1)}, u32[]{:S(2)}, u32[]{:S(2)}) collective-permute-start(bf16[256,512]{1,0:T(8,128)(2,1)} %get-tuple-element.930), channel_id=1, source_target_pairs={{8,14},{9,15},{10,12},{11,13},{12,10},{13,11},{14,8},{15,9},{0,6},... | collective-permute-start | bytes 786440 | tf_op jit(solution)/shard_map/ppermute | solution.py:132
  113.2 18.1 %collective-permute-start.12 = (bf16[256,1024]{1,0:T(8,128)(2,1)}, bf16[256,1024]{1,0:T(8,128)(2,1)}, u32[]{:S(2)}, u32[]{:S(2)}) collective-permute-start(bf16[256,1024]{1,0:T(8,128)(2,1)} %collective-permute-done.11), channel_id=1, source_target_pairs={{16,17},{17,16},{18,19},{19,18},{20,21},{21,20},{22,23},{23,22}} | collective-permute-start | bytes 1572872 | tf_op jit(solution)/shard_map/ppermute | solution.py:132
  115.7 56.5 %collective-permute-start.10 = (bf16[256,1024]{1,0:T(8,128)(2,1)S(1)}, bf16[256,1024]{1,0:T(8,128)(2,1)}, u32[]{:S(2)}, u32[]{:S(2)}) collective-permute-start(bf16[256,1024]{1,0:T(8,128)(2,1)S(1)} %collective-permute-done.7), channel_id=1, source_target_pairs={{16,17},{17,16},{18,19},{19,18},{20,21},{21,20},{22,23},{23,22}} | collective-permute-start | bytes 1572872 | tf_op jit(solution)/shard_map/ppermute | solution.py:132
  119.1 63.9 %collective-permute-start.9 = (bf16[256,1024]{1,0:T(8,128)(2,1)}, bf16[256,1024]{1,0:T(8,128)(2,1)}, u32[]{:S(2)}, u32[]{:S(2)}) collective-permute-start(bf16[256,1024]{1,0:T(8,128)(2,1)} %collective-permute-done.8), channel_id=1, source_target_pairs={{16,17},{17,16},{18,19},{19,18},{20,21},{21,20},{22,23},{23,22}} | collective-permute-start | bytes 1572872 | tf_op jit(solution)/shard_map/ppermute | solution.py:132
  123.7 64.9 %collective-permute-start.26 = (bf16[256,512]{1,0:T(8,128)(2,1)}, bf16[256,512]{1,0:T(8,128)(2,1)}, u32[]{:S(2)}, u32[]{:S(2)}) collective-permute-start(bf16[256,512]{1,0:T(8,128)(2,1)} %get-tuple-element.931), channel_id=1, source_target_pairs={{8,10},{9,11},{10,8},{11,9},{12,14},{13,15},{14,12},{15,13},{0,2},... | collective-permute-start | bytes 786440 | tf_op jit(solution)/shard_map/ppermute | solution.py:132
  125.1 65.6 %collective-permute-start.25 = (bf16[256,512]{1,0:T(8,128)(2,1)}, bf16[256,512]{1,0:T(8,128)(2,1)}, u32[]{:S(2)}, u32[]{:S(2)}) collective-permute-start(bf16[256,512]{1,0:T(8,128)(2,1)} %get-tuple-element.931), channel_id=1, source_target_pairs={{8,9},{9,8},{10,11},{11,10},{12,13},{13,12},{14,15},{15,14},{0,1},... | collective-permute-start | bytes 786440 | tf_op jit(solution)/shard_map/ppermute | solution.py:132
  131.4 60.7 %collective-permute-start.30 = (bf16[256,512]{1,0:T(8,128)(2,1)}, bf16[256,512]{1,0:T(8,128)(2,1)}, u32[]{:S(2)}, u32[]{:S(2)}) collective-permute-start(bf16[256,512]{1,0:T(8,128)(2,1)} %collective-permute-done.28), channel_id=1, source_target_pairs={{8,10},{9,11},{10,8},{11,9},{12,14},{13,15},{14,12},{15,13},{0,2},... | collective-permute-start | bytes 786440 | tf_op jit(solution)/shard_map/ppermute | solution.py:132
  172.2 20.6 %collective-permute-start.29 = (bf16[256,512]{1,0:T(8,128)(2,1)}, bf16[256,512]{1,0:T(8,128)(2,1)}, u32[]{:S(2)}, u32[]{:S(2)}) collective-permute-start(bf16[256,512]{1,0:T(8,128)(2,1)} %collective-permute-done.28), channel_id=1, source_target_pairs={{8,9},{9,8},{10,11},{11,10},{12,13},{13,12},{14,15},{15,14},{0,1},... | collective-permute-start | bytes 786440 | tf_op jit(solution)/shard_map/ppermute | solution.py:132
  209.2 18.1 %collective-permute-start.36 = (bf16[256,1024]{1,0:T(8,128)(2,1)S(1)}, bf16[256,1024]{1,0:T(8,128)(2,1)}, u32[]{:S(2)}, u32[]{:S(2)}) collective-permute-start(bf16[256,1024]{1,0:T(8,128)(2,1)S(1)} %collective-permute-done.15), channel_id=1, source_target_pairs={{8,9},{9,8},{10,11},{11,10},{12,13},{13,12},{14,15},{15,14}} | collective-permute-start | bytes 1572872 | tf_op jit(solution)/shard_map/ppermute | solution.py:132
  216.6 27.7 %collective-permute-start.50 = (bf16[256,512]{1,0:T(8,128)(2,1)}, bf16[256,512]{1,0:T(8,128)(2,1)}, u32[]{:S(2)}, u32[]{:S(2)}) collective-permute-start(bf16[256,512]{1,0:T(8,128)(2,1)} %get-tuple-element.949), channel_id=1, source_target_pairs={{24,25},{25,24},{26,27},{27,26},{28,29},{29,28},{30,31},{31,30},{1... | collective-permute-start | bytes 786440 | tf_op jit(solution)/shard_map/ppermute | solution.py:132
  229.5 44.3 %collective-permute-start.37 = (bf16[256,1024]{1,0:T(8,128)(2,1)}, bf16[256,1024]{1,0:T(8,128)(2,1)S(1)}, u32[]{:S(2)}, u32[]{:S(2)}) collective-permute-start(bf16[256,1024]{1,0:T(8,128)(2,1)} %get-tuple-element.937), channel_id=1, source_target_pairs={{8,4},{9,5},{10,6},{11,7},{12,0},{13,1},{14,2},{15,3}} | collective-permute-start | bytes 1572872 | tf_op jit(solution)/shard_map/ppermute | solution.py:132
  231.9 27.1 %collective-permute-start.48 = (bf16[256,512]{1,0:T(8,128)(2,1)S(1)}, bf16[256,512]{1,0:T(8,128)(2,1)S(1)}, u32[]{:S(2)}, u32[]{:S(2)}) collective-permute-start(bf16[256,512]{1,0:T(8,128)(2,1)S(1)} %get-tuple-element.947), channel_id=1, source_target_pairs={{24,25},{25,24},{26,27},{27,26},{28,29},{29,28},{30,31},{31,30},{1... | collective-permute-start | bytes 786440 | tf_op jit(solution)/shard_map/ppermute | solution.py:132
  236.1 29.6 %collective-permute-start.46 = (bf16[256,512]{1,0:T(8,128)(2,1)S(1)}, bf16[256,512]{1,0:T(8,128)(2,1)S(1)}, u32[]{:S(2)}, u32[]{:S(2)}) collective-permute-start(bf16[256,512]{1,0:T(8,128)(2,1)S(1)} %get-tuple-element.945), channel_id=1, source_target_pairs={{24,25},{25,24},{26,27},{27,26},{28,29},{29,28},{30,31},{31,30},{1... | collective-permute-start | bytes 786440 | tf_op jit(solution)/shard_map/ppermute | solution.py:132
  241.9 29.7 %collective-permute-start.45 = (bf16[256,512]{1,0:T(8,128)(2,1)}, bf16[256,512]{1,0:T(8,128)(2,1)S(1)}, u32[]{:S(2)}, u32[]{:S(2)}) collective-permute-start(bf16[256,512]{1,0:T(8,128)(2,1)} %get-tuple-element.944), channel_id=1, source_target_pairs={{24,25},{25,24},{26,27},{27,26},{28,29},{29,28},{30,31},{31,30},{1... | collective-permute-start | bytes 786440 | tf_op jit(solution)/shard_map/ppermute | solution.py:132
  246.9 26.3 %collective-permute-start.51 = (bf16[256,512]{1,0:T(8,128)(2,1)}, bf16[256,512]{1,0:T(8,128)(2,1)S(1)}, u32[]{:S(2)}, u32[]{:S(2)}) collective-permute-start(bf16[256,512]{1,0:T(8,128)(2,1)} %copy-done.13), channel_id=1, source_target_pairs={{24,30},{25,31},{26,28},{27,29},{28,26},{29,27},{30,24},{31,25},{1... | collective-permute-start | bytes 786440 | tf_op jit(solution)/shard_map/ppermute | solution.py:132
  261.5 23.7 %collective-permute-start.49 = (bf16[256,512]{1,0:T(8,128)(2,1)}, bf16[256,512]{1,0:T(8,128)(2,1)}, u32[]{:S(2)}, u32[]{:S(2)}) collective-permute-start(bf16[256,512]{1,0:T(8,128)(2,1)} %get-tuple-element.948), channel_id=1, source_target_pairs={{24,28},{25,29},{26,30},{27,31},{28,24},{29,25},{30,26},{31,27},{1... | collective-permute-start | bytes 786440 | tf_op jit(solution)/shard_map/ppermute | solution.py:132
  268.2 17.0 %collective-permute-start.47 = (bf16[256,512]{1,0:T(8,128)(2,1)}, bf16[256,512]{1,0:T(8,128)(2,1)}, u32[]{:S(2)}, u32[]{:S(2)}) collective-permute-start(bf16[256,512]{1,0:T(8,128)(2,1)} %get-tuple-element.946), channel_id=1, source_target_pairs={{24,26},{25,27},{26,24},{27,25},{28,30},{29,31},{30,28},{31,29},{1... | collective-permute-start | bytes 786440 | tf_op jit(solution)/shard_map/ppermute | solution.py:132
  271.6 21.8 %collective-permute-start.43 = (bf16[256,1024]{1,0:T(8,128)(2,1)}, bf16[256,1024]{1,0:T(8,128)(2,1)}, u32[]{:S(2)}, u32[]{:S(2)}) collective-permute-start(bf16[256,1024]{1,0:T(8,128)(2,1)} %get-tuple-element.937), channel_id=1, source_target_pairs={{8,0},{9,1},{10,2},{11,3},{12,4},{13,5},{14,6},{15,7}} | collective-permute-start | bytes 1572872 | tf_op jit(solution)/shard_map/ppermute | solution.py:132
  273.1 21.1 %collective-permute-start.41 = (bf16[256,1024]{1,0:T(8,128)(2,1)}, bf16[256,1024]{1,0:T(8,128)(2,1)S(1)}, u32[]{:S(2)}, u32[]{:S(2)}) collective-permute-start(bf16[256,1024]{1,0:T(8,128)(2,1)} %get-tuple-element.937), channel_id=1, source_target_pairs={{8,2},{9,3},{10,0},{11,1},{12,6},{13,7},{14,4},{15,5}} | collective-permute-start | bytes 1572872 | tf_op jit(solution)/shard_map/ppermute | solution.py:132
  273.8 30.4 %collective-permute-start.38 = (bf16[256,1024]{1,0:T(8,128)(2,1)S(1)}, bf16[256,1024]{1,0:T(8,128)(2,1)}, u32[]{:S(2)}, u32[]{:S(2)}) collective-permute-start(bf16[256,1024]{1,0:T(8,128)(2,1)S(1)} %collective-permute-done.37), channel_id=1, source_target_pairs={{0,2},{1,3},{2,0},{3,1},{4,6},{5,7},{6,4},{7,5}} | collective-permute-start | bytes 1572872 | tf_op jit(solution)/shard_map/ppermute | solution.py:132
  293.5 25.2 %collective-permute-start.44 = (bf16[256,1024]{1,0:T(8,128)(2,1)}, bf16[256,1024]{1,0:T(8,128)(2,1)S(1)}, u32[]{:S(2)}, u32[]{:S(2)}) collective-permute-start(bf16[256,1024]{1,0:T(8,128)(2,1)} %collective-permute-done.43), channel_id=1, source_target_pairs={{0,1},{1,0},{2,3},{3,2},{4,5},{5,4},{6,7},{7,6}} | collective-permute-start | bytes 1572872 | tf_op jit(solution)/shard_map/ppermute | solution.py:132
  294.2 27.0 %collective-permute-start.42 = (bf16[256,1024]{1,0:T(8,128)(2,1)S(1)}, bf16[256,1024]{1,0:T(8,128)(2,1)S(1)}, u32[]{:S(2)}, u32[]{:S(2)}) collective-permute-start(bf16[256,1024]{1,0:T(8,128)(2,1)S(1)} %collective-permute-done.41), channel_id=1, source_target_pairs={{0,1},{1,0},{2,3},{3,2},{4,5},{5,4},{6,7},{7,6}} | collective-permute-start | bytes 1572872 | tf_op jit(solution)/shard_map/ppermute | solution.py:132
  303.5 21.1 %collective-permute-start.40 = (bf16[256,1024]{1,0:T(8,128)(2,1)S(1)}, bf16[256,1024]{1,0:T(8,128)(2,1)S(1)}, u32[]{:S(2)}, u32[]{:S(2)}) collective-permute-start(bf16[256,1024]{1,0:T(8,128)(2,1)S(1)} %collective-permute-done.37), channel_id=1, source_target_pairs={{0,1},{1,0},{2,3},{3,2},{4,5},{5,4},{6,7},{7,6}} | collective-permute-start | bytes 1572872 | tf_op jit(solution)/shard_map/ppermute | solution.py:132
  304.2 25.0 %collective-permute-start.39 = (bf16[256,1024]{1,0:T(8,128)(2,1)}, bf16[256,1024]{1,0:T(8,128)(2,1)S(1)}, u32[]{:S(2)}, u32[]{:S(2)}) collective-permute-start(bf16[256,1024]{1,0:T(8,128)(2,1)} %collective-permute-done.38), channel_id=1, source_target_pairs={{0,1},{1,0},{2,3},{3,2},{4,5},{5,4},{6,7},{7,6}} | collective-permute-start | bytes 1572872 | tf_op jit(solution)/shard_map/ppermute | solution.py:132
  (44 other events, 459.9 us)

commit v4 on v0

v4 whole, which is shorter than its diff:
```python
import jax
import jax.numpy as jnp
from jax import lax
from jax.experimental import pallas as pl
from jax.experimental.pallas import tpu as pltpu
from jax.sharding import PartitionSpec as P

DOT_VMEM = 10 * 1024 * 1024
VMEM = pl.BlockSpec(memory_space=pltpu.VMEM)
SMEM = pl.BlockSpec(memory_space=pltpu.SMEM)
ANY = pl.BlockSpec(memory_space=pl.ANY)


def scalars(*values):
    return jnp.stack([jnp.asarray(v).astype(jnp.int32) for v in values])


def params():
    return pltpu.CompilerParams(vmem_limit_bytes=DOT_VMEM)


def cost(flops, moved):
    return pl.CostEstimate(flops=flops, bytes_accessed=moved, transcendentals=0)


def resident(active, weights, picks, by_rows):
    count = len(picks)
    shape = list(weights.shape)
    shape[0 if by_rows else 1] //= count
    run = shape[0 if by_rows else 1]

    def body(at, weights_ref, out_ref, sems):
        def copy(i):
            part = pl.ds(pl.multiple_of(at[1 + i] * run, run), run)
            source = weights_ref.at[part, :] if by_rows else weights_ref.at[:, part]
            return pltpu.make_async_copy(source, out_ref.at[i], sems.at[i])

        @pl.when(at[0] == 1)
        def _():
            for i in range(count):
                copy(i).start()
            for i in range(count):
                copy(i).wait()

    return pl.pallas_call(
        body,
        in_specs=[SMEM, ANY],
        out_specs=VMEM,
        out_shape=jax.ShapeDtypeStruct((count, *shape), weights.dtype),
        scratch_shapes=[pltpu.SemaphoreType.DMA((count,))],
        compiler_params=params(),
        cost_estimate=cost(0, 2 * weights.size),
        name="resident",
    )(scalars(active, *picks), weights)


def block_dot(active, blocks, weights, wanted, base, out_type):
    _, rows, depth = blocks[0].shape
    cols = weights.shape[2]
    width = 256 if cols % 256 == 0 else cols
    count = len(blocks)

    def body(active_ref, *refs):
        block_refs, weights_ref = refs[:count], refs[count]
        base_ref, out_ref = (None if base is None else refs[count + 1]), refs[-1]

        @pl.when(active_ref[0] == 1)
        def _():
            def tile(j, _):
                here = pl.ds(pl.multiple_of(j * width, width), width)
                total = None if base is None else base_ref[:, here].astype(jnp.float32)
                for a, i, w in wanted:
                    part = jnp.dot(
                        block_refs[a][i],
                        weights_ref[w, :, here],
                        preferred_element_type=jnp.float32,
                    )
                    total = part if total is None else total + part
                out_ref[:, here] = total.astype(out_type)
                return 0

            lax.fori_loop(0, cols // width, tile, 0)

    return pl.pallas_call(
        body,
        in_specs=[SMEM] + [VMEM] * (count + 1 + (base is not None)),
        out_specs=VMEM,
        out_shape=jax.ShapeDtypeStruct((rows, cols), out_type),
        compiler_params=params(),
        cost_estimate=cost(2 * len(wanted) * rows * depth * cols, rows * cols),
        name="block_dot",
    )(scalars(active), *blocks, weights, *([] if base is None else [base]))


def rotate_more(active, old, blocks, weights, wanted):
    _, rows, depth = blocks[0].shape
    cols = weights.shape[2]
    width = 256 if cols % 256 == 0 else cols
    count = len(blocks)

    def body(active_ref, *refs):
        block_refs, weights_ref, old_ref, out_ref = refs[:count], refs[count], refs[-2], refs[-1]

        @pl.when(active_ref[0] == 0)
        def _():
            out_ref[...] = old_ref[...]

        @pl.when(active_ref[0] == 1)
        def _():
            def tile(j, _):
                here = pl.ds(pl.multiple_of(j * width, width), width)
                total = None
                for a, i, w in wanted:
                    part = jnp.dot(
                        block_refs[a][i],
                        weights_ref[w, :, here],
                        preferred_element_type=jnp.float32,
                    )
                    total = part if total is None else total + part
                out_ref[:, here] = total.astype(out_ref.dtype)
                return 0

            lax.fori_loop(0, cols // width, tile, 0)

    return pl.pallas_call(
        body,
        in_specs=[SMEM] + [VMEM] * (count + 2),
        out_specs=VMEM,
        out_shape=jax.ShapeDtypeStruct((rows, cols), old.dtype),
        compiler_params=params(),
        cost_estimate=cost(2 * len(wanted) * rows * depth * cols, rows * cols),
        name="rotate_more",
    )(scalars(active), *blocks, weights, old)


def partials(active, inputs, weights, wanted, arrived, out_types, joined):
    rows, depth = inputs.shape
    width = weights.shape[2]
    count = len(arrived)

    def body(active_ref, inputs_ref, weights_ref, *refs):
        arrived_refs, out_refs = refs[:count], refs[count:]

        @pl.when(active_ref[0] == 1)
        def _():
            for n, (w, adds) in enumerate(wanted):
                total = jnp.dot(
                    inputs_ref[...], weights_ref[w], preferred_element_type=jnp.float32
                )
                for a, i in adds:
                    total = total + arrived_refs[a][i].astype(jnp.float32)
                out_ref = out_refs[0] if joined else out_refs[n]
                out_ref[n if joined else 0] = total.astype(out_ref.dtype)

    if joined:
        shapes = [jax.ShapeDtypeStruct((len(wanted), rows, width), out_types[0])]
    else:
        shapes = [jax.ShapeDtypeStruct((1, rows, width), t) for t in out_types]
    return pl.pallas_call(
        body,
        in_specs=[SMEM] + [VMEM] * (2 + count),
        out_specs=[VMEM] * len(shapes),
        out_shape=shapes,
        compiler_params=params(),
        cost_estimate=cost(2 * len(wanted) * rows * depth * width, rows * width),
        name="partials",
    )(scalars(active), inputs, weights, *arrived)


def mean_square(upper, rot_out, low, high, runs, picks, micro, seq):
    _, rows, width = low[0].shape
    eig_rows = rot_out.shape[1]
    count = len(runs)
    tall = 128 if eig_rows % 128 == 0 else eig_rows
    wide = 256 if width % 256 == 0 else width
    across = width // wide

    def body(at, rot_ref, *refs):
        low_refs, high_refs = refs[: len(low)], refs[len(low) : 2 * len(low)]
        eig_ref, turned, block, result, sems = refs[2 * len(low) :]
        for m in range(micro):
            turned[m] = rot_ref[m * seq : (m + 1) * seq, :].T

        def copy(n):
            columns = pl.ds(pl.multiple_of(at[1 + n] * width, width), width)
            return pltpu.make_async_copy(result.at[n % 2], eig_ref.at[:, columns], sems.at[n % 2])

        for n, (a, i) in enumerate(runs):

            @pl.when(at[0] == 1)
            def _():
                block[...] = high_refs[a][i]

            @pl.when(at[0] == 0)
            def _():
                block[...] = low_refs[a][i]

            if n >= 2:
                copy(n - 2).wait()

            def tile(t, _):
                down = pl.ds(pl.multiple_of((t // across) * tall, tall), tall)
                here = pl.ds(pl.multiple_of((t % across) * wide, wide), wide)
                total = None
                for m in range(micro):
                    product = jnp.dot(
                        turned[m, down, :],
                        block[m * seq : (m + 1) * seq, here],
                        preferred_element_type=jnp.float32,
                    )
                    square = product * product
                    total = square if total is None else total + square
                result[n % 2, down, here] = total * (1.0 / (seq * micro))
                return 0

            lax.fori_loop(0, (eig_rows // tall) * across, tile, 0)
            copy(n).start()
        for n in range(max(0, count - 2), count):
            copy(n).wait()

    return pl.pallas_call(
        body,
        in_specs=[SMEM] + [VMEM] * (1 + 2 * len(low)),
        out_specs=ANY,
        out_shape=jax.ShapeDtypeStruct((eig_rows, count * width), jnp.float32),
        scratch_shapes=[
            pltpu.VMEM((micro, eig_rows, seq), rot_out.dtype),
            pltpu.VMEM((rows, width), rot_out.dtype),
            pltpu.VMEM((2, eig_rows, width), jnp.float32),
            pltpu.SemaphoreType.DMA((2,)),
        ],
        compiler_params=params(),
        cost_estimate=cost(16 * rows * eig_rows * count * width, 4 * eig_rows * count * width),
        name="mean_square",
    )(scalars(upper, *picks), rot_out, *low, *high)


def per_device(activations, top_grad, projection, basis_out, basis_in):
    sections = lax.axis_size("section")
    shards = lax.axis_size("shard")
    section, shard = lax.axis_index("section"), lax.axis_index("shard")
    micro, seq, feat_loc = top_grad.shape
    rows = micro * seq
    inputs = activations[0].reshape(rows, feat_loc)
    top = top_grad.reshape(1, rows, feat_loc)
    half = sections // 2

    inner = 1
    while 2 * (2 * inner) ** 2 <= shards:
        inner *= 2
    outer = shards // inner
    picks = [shard ^ part for part in range(shards)]

    def moved(block, flip, pairs):
        route = [(a * shards + i, b * shards + (i ^ flip)) for a, b in pairs for i in range(shards)]
        return lax.ppermute(block, ("section", "shard"), route)

    def spread(block, pairs):
        stays = all(a == b for a, b in pairs)
        sent = {0: block if stays else moved(block, 0, pairs)}
        dz = 1
        while dz < outer:
            sent[dz] = moved(block, dz * inner, pairs)
            dz *= 2
        return sent

    def along_outer(sent, pairs):
        got = dict(sent)
        for dz in range(outer):
            low = dz & -dz
            if dz not in got:
                got[dz] = moved(got[dz ^ low], low * inner, pairs)
        return got

    def along_inner(blocks, pairs):
        return {dx: moved(blocks, dx, pairs) for dx in range(1, inner)}

    def chain(sent, turns, rot_out, weights, out_cols):
        for turn in turns:
            mine = section == turn
            pairs = [(turn, turn)]
            matrix = out_cols if turn == 0 else weights
            sent[0], rot_out = lax.optimization_barrier((sent[0], rot_out))
            total = None if turn == 0 else sent[0].reshape(rows, feat_loc)
            every = []
            batches = [[0]] + ([list(range(1, outer - 1))] if outer > 2 else []) + [[outer - 1]]
            got = along_outer(sent, pairs)
            for n, batch in enumerate(batches):
                near = [got[dz] for dz in batch]
                if n == len(batches) - 1 and total is not None:
                    near[0], total = lax.optimization_barrier((near[0], total))
                joined = near[0] if len(near) == 1 else jnp.concatenate(near)
                far = along_inner(joined, pairs)
                own = [(joined, [(i, dz * inner) for i, dz in enumerate(batch)])]
                other = [(far[dx], [(i, dz * inner + dx) for i, dz in enumerate(batch)]) for dx in far]
                every += own + other
                last = n == len(batches) - 1
                for part, group in enumerate([own, other] if last or n else [own + other]):
                    if not group:
                        continue
                    final = last and (part == 1 or not other)
                    total = block_dot(
                        mine,
                        [a for a, _ in group],
                        matrix,
                        [(k, i, w) for k, (_, uses) in enumerate(group) for i, w in uses],
                        total,
                        jnp.bfloat16 if final else jnp.float32,
                    )
            if turn == 0:
                return jnp.where(mine, total, rot_out)
            sent = spread(total.reshape(1, rows, feat_loc), [(turn, turn - 1)])
            rot_out = rotate_more(
                mine,
                rot_out,
                [a for a, _ in every],
                out_cols,
                [(k, i, w) for k, (_, uses) in enumerate(every) for i, w in uses],
            )
        return sent, rot_out

    def rotate_in(inputs, among):
        pairs = [(a, a) for a in among]
        mine = (section >= min(among)) & (section <= max(among))
        in_cols = resident(mine, basis_in[0], picks, False)
        first = list(range(1, 1 + outer // 2))
        second = list(range(1 + outer // 2, outer)) + [0]
        crossed = {}
        for batch in (first, second):
            crossed[batch[0]] = []
            for dx in range(1, inner):
                (sent,) = partials(
                    mine,
                    inputs,
                    in_cols,
                    [(dz * inner + dx, []) for dz in batch],
                    [],
                    [jnp.bfloat16],
                    True,
                )
                crossed[batch[0]].append(moved(sent, dx, pairs))
        arrived = []
        for batch in (first, second):
            sums = partials(
                mine,
                inputs,
                in_cols,
                [
                    (dz * inner, [(a, n) for a in range(inner - 1)])
                    for n, dz in enumerate(batch)
                ],
                crossed[batch[0]],
                [jnp.bfloat16 if dz else jnp.float32 for dz in batch],
                False,
            )
            arrived += [moved(s, dz * inner, pairs) for s, dz in zip(sums, batch) if dz]
        own = sums[-1]
        for other in arrived:
            own = own + other.astype(jnp.float32)
        got = along_outer(spread(own.astype(jnp.bfloat16), pairs), pairs)
        arrays, runs = [], {}
        for batch in (list(range(outer // 2)), list(range(outer // 2, outer))):
            near = jnp.concatenate([got[dz] for dz in batch])
            for dx, blocks in {0: near, **along_inner(near, pairs)}.items():
                for i, dz in enumerate(batch):
                    runs[dz * inner + dx] = (len(arrays), i)
                arrays.append(blocks)
        return arrays, [runs[n] for n in range(shards)]

    upper = list(range(sections - 1, half - 1, -1))
    lower = list(range(half - 1, -1, -1))
    weights = resident(True, projection[0], picks, True)
    out_cols = resident(True, basis_out[0], picks, True)
    rot_out = jnp.zeros((rows, basis_out.shape[2]), jnp.bfloat16)

    sent = spread(top, [(upper[0], upper[0])])
    sent, rot_out = chain(sent, upper, rot_out, weights, out_cols)
    low, runs = rotate_in(inputs, lower)
    sent, low, inputs = lax.optimization_barrier((sent, low, inputs))
    rot_out = chain(sent, lower, rot_out, weights, out_cols)
    high, runs = rotate_in(inputs, upper)
    return mean_square(section >= half, rot_out, low, high, runs, picks, micro, seq)[None]


def solution(mesh):
    return jax.shard_map(
        per_device,
        mesh=mesh,
        in_specs=(
            P("section", None, None, "shard"),
            P(None, None, "shard"),
            P("section", None, "shard"),
            P("section", None, "shard"),
            P("section", "shard", None),
        ),
        out_specs=P("section", "shard", None),
        check_vma=False,
    )
```

time: 718 us -> 281 us (0.39)
  blocking collectives: 515 us -> 0 us
  matrix products: 168 us -> 0 us
  waiting for transfers between devices: 0.13 us -> 97.6 us
  starting transfers between devices: 14.2 us -> 83.2 us
  Pallas kernels: 0 us -> 48.7 us
  local copies, waits for them, and re-layouts: 0.02 us -> 45.4 us
  other arithmetic: 14.3 us -> 2.63 us
    all_gather x11 -> x0, blocking collectives: 347 us -> none  [chain_step(): lax.all_gather(current, 'shard', axis=1, tiled=True)]
    dot_general x24 -> x0, matrix products: 168 us -> none  [the longest x11 96.3 us: absorb(): through = jnp.dot(piece, weight_cols, preferred_element_type=jnp.float32)]
    psum x1 -> x0, blocking collectives: 168 us -> none  [per_device(): rot_in = lax.psum(partial_rot, 'shard').astype(jnp.bfloat16)]
    ppermute x11 -> x47, waiting for transfers between devices: 0.13 us -> 97.6 us  [moved(): return lax.ppermute(block, ('section', 'shard'), route)]
    ppermute x11 -> x47, starting transfers between devices: 14.2 us -> 83.2 us  [moved(): return lax.ppermute(block, ('section', 'shard'), route)]
    pallas_call x0 -> x36, Pallas kernels: none -> 48.7 us  [the longest x1 20.5 us: mean_square(): pl.pallas_call(body, in_specs=[SMEM] + [VMEM] * (1 + 2 * len(low)), out_s...]
    unnamed x2 -> x98, local copies, waits for them, and re-layouts: 0.01 us -> 40.7 us
    select_n x12 -> x1, other arithmetic: 10.3 us -> 0.03 us  [chain(): return jnp.where(mine, total, rot_out)]
  transfers between devices with their start and end apart: 11 -> 47, of which waited for: 0 -> 11; matrix products, arithmetic and copies ran while one was open for 8% -> 3% of each run, Pallas kernels for 0% -> 10%
where the time goes in v4:
time: 281 us; the launch traced here: 279 us
  waiting for transfers between devices  97.6 us (35%)
  starting transfers between devices  83.2 us (30%)
  Pallas kernels  48.7 us (17%)
  local copies, waits for them, and re-layouts  45.4 us (16%)
    ppermute x47, waiting for transfers between devices, moved(): return lax.ppermute(block, ('section', 'shard'), route)  97.6 us
    ppermute x47, starting transfers between devices, moved(): return lax.ppermute(block, ('section', 'shard'), route)  83.2 us
    unnamed x98, local copies, waits for them, and re-layouts  40.7 us
    pallas_call x1, Pallas kernels, mean_square(): pl.pallas_call(body, in_specs=[SMEM] + [VMEM] * (1 + 2 * len(low)), out_s...  20.5 us
    pallas_call x20, Pallas kernels, block_dot(): pl.pallas_call(body, in_specs=[SMEM] + [VMEM] * (count + 1 + (base is not...  14.2 us
  transfers between devices with their start and end apart: 47, of which 11 were waited for; matrix products, arithmetic and copies ran while one was open for 3% of the time, Pallas kernels for 10%

profile of v4, /device:TPU:0, one launch (start us, length us, event | category | flops | bytes accessed | tf_op | source)
XLA Modules:
  0.0 278.9 jit_solution(5173490059441081105)
XLA Ops:
  6.3 5.8 %copy-done.9 = bf16[1,8192,1024]{2,1,0:T(8,128)(2,1)S(1)} copy-done((bf16[1,8192,1024]{2,1,0:T(8,128)(2,1)S(1)}, bf16[1,8192,1024]{2,1,0:T(8,128)(2,1)}, u32[]{:S(2)}) %copy-start.9) | copy-done | bytes 16777240
  24.1 3.4 %copy-done.7 = bf16[1,1024,4096]{2,1,0:T(8,128)(2,1)S(1)} copy-done((bf16[1,1024,4096]{2,1,0:T(8,128)(2,1)S(1)}, bf16[1,1024,4096]{2,1,0:T(8,128)(2,1)}, u32[]{:S(2)}) %copy-start.7) | copy-done | bytes 8388632
  27.5 2.0 resident.6.weights_ref
  30.2 5.1 %collective-permute-start.16 = (bf16[2,256,512]{2,1,0:T(8,128)(2,1)S(1)}, bf16[2,256,512]{2,1,0:T(8,128)(2,1)S(1)}, u32[]{:S(2)}, u32[]{:S(2)}) collective-permute-start(bf16[2,256,512]{2,1,0:T(8,128)(2,1)S(1)} %partials.8), channel_id=1, source_target_pairs={{8,9},{9,8},{10,11},{11,10},{12,13},{13,12},{14,15},{15,14},{0,1},... | collective-permute-start | bytes 1572872 | tf_op jit(solution)/shard_map/ppermute | solution.py:256
  36.1 2.1 collective-permute-start.17
  44.7 3.5 %collective-permute-done.16.refs_0_ = bf16[2,256,512]{2,1,0:T(8,128)(2,1)S(1)} collective-permute-done((bf16[2,256,512]{2,1,0:T(8,128)(2,1)S(1)}, bf16[2,256,512]{2,1,0:T(8,128)(2,1)S(1)}, u32[]{:S(2)}, u32[]{:S(2)}) %collective-permute-start.16) | collective-permute-done | bytes 524320 | tf_op jit(solution)/shard_map/ppermute | solution.py:256
  49.7 5.9 %collective-permute-start.20 = (bf16[1,256,512]{2,1,0:T(8,128)(2,1)}, bf16[1,256,512]{2,1,0:T(8,128)(2,1)}, u32[]{:S(2)}, u32[]{:S(2)}) collective-permute-start(bf16[1,256,512]{2,1,0:T(8,128)(2,1)} %get-tuple-element.47), channel_id=1, source_target_pairs={{8,14},{9,15},{10,12},{11,13},{12,10},{13,11},{14,8},{15,9},{0,6},... | collective-permute-start | bytes 786440 | tf_op jit(solution)/shard_map/ppermute | solution.py:256
  55.6 3.0 %collective-permute-done.17.refs_0_ = bf16[2,256,512]{2,1,0:T(8,128)(2,1)S(1)} collective-permute-done((bf16[2,256,512]{2,1,0:T(8,128)(2,1)S(1)}, bf16[2,256,512]{2,1,0:T(8,128)(2,1)S(1)}, u32[]{:S(2)}, u32[]{:S(2)}) %collective-permute-start.17) | collective-permute-done | bytes 524320 | tf_op jit(solution)/shard_map/ppermute | solution.py:256
  60.2 4.6 %collective-permute-start.19 = (bf16[1,256,512]{2,1,0:T(8,128)(2,1)}, bf16[1,256,512]{2,1,0:T(8,128)(2,1)}, u32[]{:S(2)}, u32[]{:S(2)}) collective-permute-start(bf16[1,256,512]{2,1,0:T(8,128)(2,1)} %get-tuple-element.46), channel_id=1, source_target_pairs={{8,12},{9,13},{10,14},{11,15},{12,8},{13,9},{14,10},{15,11},{0,4},... | collective-permute-start | bytes 786440 | tf_op jit(solution)/shard_map/ppermute | solution.py:256
  64.8 3.5 %collective-permute-start.18 = (bf16[1,256,512]{2,1,0:T(8,128)(2,1)}, bf16[1,256,512]{2,1,0:T(8,128)(2,1)}, u32[]{:S(2)}, u32[]{:S(2)}) collective-permute-start(bf16[1,256,512]{2,1,0:T(8,128)(2,1)} %get-tuple-element.45), channel_id=1, source_target_pairs={{8,10},{9,11},{10,8},{11,9},{12,14},{13,15},{14,12},{15,13},{0,2},... | collective-permute-start | bytes 786440 | tf_op jit(solution)/shard_map/ppermute | solution.py:256
  70.9 5.7 %collective-permute-done.19 = bf16[1,256,512]{2,1,0:T(8,128)(2,1)} collective-permute-done((bf16[1,256,512]{2,1,0:T(8,128)(2,1)}, bf16[1,256,512]{2,1,0:T(8,128)(2,1)}, u32[]{:S(2)}, u32[]{:S(2)}) %collective-permute-start.19) | collective-permute-done | bytes 262176 | tf_op jit(solution)/shard_map/ppermute | solution.py:256
  76.6 2.2 collective-permute-done.18
  82.1 4.5 %collective-permute-start.23 = (bf16[1,256,512]{2,1,0:T(8,128)(2,1)S(1)}, bf16[1,256,512]{2,1,0:T(8,128)(2,1)S(1)}, u32[]{:S(2)}, u32[]{:S(2)}) collective-permute-start(bf16[1,256,512]{2,1,0:T(8,128)(2,1)S(1)} %add_convert_fusion.1), channel_id=1, source_target_pairs={{8,12},{9,13},{10,14},{11,15},{12,8},{13,9},{14,10},{15,11},{0,4},... | collective-permute-start | bytes 786440 | tf_op jit(solution)/shard_map/ppermute | solution.py:256
  86.7 5.9 %copy-done.1 = bf16[8,1024,1024]{2,1,0:T(8,128)(2,1)S(1)} copy-done((bf16[8,1024,1024]{2,1,0:T(8,128)(2,1)S(1)}, bf16[8,1024,1024]{2,1,0:T(8,128)(2,1)}, u32[]{:S(2)}) %copy-start.1) | copy-done | bytes 16777240
  97.5 2.2 collective-permute-start.24
  99.7 3.5 %collective-permute-start.22 = (bf16[2,256,512]{2,1,0:T(8,128)(2,1)S(1)}, bf16[2,256,512]{2,1,0:T(8,128)(2,1)S(1)}, u32[]{:S(2)}, u32[]{:S(2)}) collective-permute-start(bf16[2,256,512]{2,1,0:T(8,128)(2,1)S(1)} %pad_maximum_fusion.refs_0_), channel_id=1, source_target_pairs={{8,9},{9,8},{10,11},{11,10},{12,13},{13,12},{14,15},{15,14},{0,1},... | collective-permute-start | bytes 1572872 | tf_op jit(solution)/shard_map/ppermute | solution.py:256
  103.3 2.7 collective-permute-done.24
  106.0 3.5 %collective-permute-start.25 = (bf16[2,256,512]{2,1,0:T(8,128)(2,1)S(1)}, bf16[2,256,512]{2,1,0:T(8,128)(2,1)S(1)}, u32[]{:S(2)}, u32[]{:S(2)}) collective-permute-start(bf16[2,256,512]{2,1,0:T(8,128)(2,1)S(1)} %constant_dynamic-update-slice_fusion.4.refs_2_), channel_id=1, source_target_pairs={{8,9},{9,8},{10,11},{11,10},{12,13},{13,12},{14,15},{15,14},{0,1},... | collective-permute-start | bytes 1572872 | tf_op jit(solution)/shard_map/ppermute | solution.py:256
  113.0 3.5 %collective-permute-done.22.refs_1_ = bf16[2,256,512]{2,1,0:T(8,128)(2,1)S(1)} collective-permute-done((bf16[2,256,512]{2,1,0:T(8,128)(2,1)S(1)}, bf16[2,256,512]{2,1,0:T(8,128)(2,1)S(1)}, u32[]{:S(2)}, u32[]{:S(2)}) %collective-permute-start.22) | collective-permute-done | bytes 524320 | tf_op jit(solution)/shard_map/ppermute | solution.py:256
  116.5 8.5 %collective-permute-done.25.refs_3_ = bf16[2,256,512]{2,1,0:T(8,128)(2,1)S(1)} collective-permute-done((bf16[2,256,512]{2,1,0:T(8,128)(2,1)S(1)}, bf16[2,256,512]{2,1,0:T(8,128)(2,1)S(1)}, u32[]{:S(2)}, u32[]{:S(2)}) %collective-permute-start.25) | collective-permute-done | bytes 524320 | tf_op jit(solution)/shard_map/ppermute | solution.py:256
  132.9 6.0 %copy-done.2 = bf16[8,1024,1024]{2,1,0:T(8,128)(2,1)S(1)} copy-done((bf16[8,1024,1024]{2,1,0:T(8,128)(2,1)S(1)}, bf16[8,1024,1024]{2,1,0:T(8,128)(2,1)}, u32[]{:S(2)}) %copy-start.2) | copy-done | bytes 16777240
  145.5 3.4 %copy-done.8 = bf16[1,1024,4096]{2,1,0:T(8,128)(2,1)S(1)} copy-done((bf16[1,1024,4096]{2,1,0:T(8,128)(2,1)S(1)}, bf16[1,1024,4096]{2,1,0:T(8,128)(2,1)}, u32[]{:S(2)}) %copy-start.8) | copy-done | bytes 8388632
  152.3 58.3 %collective-permute-done.32 = bf16[1,256,1024]{2,1,0:T(8,128)(2,1)} collective-permute-done((bf16[1,256,1024]{2,1,0:T(8,128)(2,1)}, bf16[1,256,1024]{2,1,0:T(8,128)(2,1)}, u32[]{:S(2)}, u32[]{:S(2)}) %collective-permute-start.32) | collective-permute-done | bytes 524320 | tf_op jit(solution)/shard_map/ppermute | solution.py:256
  214.4 3.1 %collective-permute-start.33 = (bf16[2,256,1024]{2,1,0:T(8,128)(2,1)S(1)}, bf16[2,256,1024]{2,1,0:T(8,128)(2,1)}, u32[]{:S(2)}, u32[]{:S(2)}) collective-permute-start(bf16[2,256,1024]{2,1,0:T(8,128)(2,1)S(1)} %constant_dynamic-update-slice_fusion.8.refs_0_), channel_id=1, source_target_pairs={{0,1},{1,0},{2,3},{3,2},{4,5},{5,4},{6,7},{7,6}} | collective-permute-start | bytes 3145736 | tf_op jit(solution)/shard_map/ppermute | solution.py:256
  221.3 3.0 %collective-permute-start.35 = (bf16[1,256,1024]{2,1,0:T(8,128)(2,1)}, bf16[1,256,1024]{2,1,0:T(8,128)(2,1)S(1)}, u32[]{:S(2)}, u32[]{:S(2)}) collective-permute-start(bf16[1,256,1024]{2,1,0:T(8,128)(2,1)} %collective-permute-done.34.refs_0_), channel_id=1, source_target_pairs={{0,1},{1,0},{2,3},{3,2},{4,5},{5,4},{6,7},{7,6}} | collective-permute-start | bytes 1572872 | tf_op jit(solution)/shard_map/ppermute | solution.py:256
  229.9 7.1 %collective-permute-done.35.refs_1_ = bf16[1,256,1024]{2,1,0:T(8,128)(2,1)S(1)} collective-permute-done((bf16[1,256,1024]{2,1,0:T(8,128)(2,1)}, bf16[1,256,1024]{2,1,0:T(8,128)(2,1)S(1)}, u32[]{:S(2)}, u32[]{:S(2)}) %collective-permute-start.35) | collective-permute-done | bytes 524320 | tf_op jit(solution)/shard_map/ppermute | solution.py:256
  237.0 3.4 %copy-done.4 = bf16[8,1024,512]{2,1,0:T(8,128)(2,1)S(1)} copy-done((bf16[8,1024,512]{2,1,0:T(8,128)(2,1)S(1)}, bf16[8,1024,512]{2,1,0:T(8,128)(2,1)}, u32[]{:S(2)}) %copy-start.4) | copy-done | bytes 8388632
  240.4 1.9 block_dot.35.refs_2_
  243.3 2.2 block_dot.37.refs_2_
  245.5 2.8 %collective-permute-start.36 = (bf16[1,256,1024]{2,1,0:T(8,128)(2,1)S(1)}, bf16[1,256,1024]{2,1,0:T(8,128)(2,1)S(1)}, u32[]{:S(2)}, u32[]{:S(2)}) collective-permute-start(bf16[1,256,1024]{2,1,0:T(8,128)(2,1)S(1)} %collective-permute-done.31.refs_0_), channel_id=1, source_target_pairs={{0,1},{1,0},{2,3},{3,2},{4,5},{5,4},{6,7},{7,6}} | collective-permute-start | bytes 1572872 | tf_op jit(solution)/shard_map/ppermute | solution.py:256
  253.3 3.4 %copy-done.5 = bf16[8,1024,512]{2,1,0:T(8,128)(2,1)S(1)} copy-done((bf16[8,1024,512]{2,1,0:T(8,128)(2,1)S(1)}, bf16[8,1024,512]{2,1,0:T(8,128)(2,1)}, u32[]{:S(2)}) %copy-start.5) | copy-done | bytes 8388632
  258.2 20.5 %mean_square.1 = f32[512,4096]{1,0:T(8,128)} custom-call(s32[9]{0:T(128)S(1)} %stack.63.at, bf16[256,512]{1,0:T(8,128)(2,1)S(1)} %broadcast_select_fusion.rot_ref, bf16[2,256,512]{2,1,0:T(8,128)(2,1)S(1)} %copy-done.27, bf16[2,256,512]{2,1,0:T(8,128)(2,1)S(1)} %copy-done.31, bf16[2,256,512]{2,1,0:T(8,128)(2,1)S(1)} %copy-done.29, ...), custom_call_target="tpu_custom_call" | custom-call | flops 8589934592 | bytes 8388608 | tf_op jit(solution)/shard_map/mean_square/pallas_call | solution.py:221
  (216 shorter events, 81.5 us)
Async XLA Ops:
  4.7 11.5 %collective-permute-start.1 = (bf16[1,256,1024]{2,1,0:T(8,128)(2,1)}, bf16[1,256,1024]{2,1,0:T(8,128)(2,1)}, u32[]{:S(2)}, u32[]{:S(2)}) collective-permute-start(bf16[1,256,1024]{2,1,0:T(8,128)(2,1)} %collective-permute-done), channel_id=1, source_target_pairs={{24,26},{25,27},{26,24},{27,25},{28,30},{29,31},{30,28},{31,29}} | collective-permute-start | bytes 1572872 | tf_op jit(solution)/shard_map/ppermute | solution.py:256
  21.1 18.5 %collective-permute-start.8 = (bf16[1,256,1024]{2,1,0:T(8,128)(2,1)}, bf16[1,256,1024]{2,1,0:T(8,128)(2,1)}, u32[]{:S(2)}, u32[]{:S(2)}) collective-permute-start(bf16[1,256,1024]{2,1,0:T(8,128)(2,1)} %bitcast.16), channel_id=1, source_target_pairs={{24,18},{25,19},{26,16},{27,17},{28,22},{29,23},{30,20},{31,21}} | collective-permute-start | bytes 1572872 | tf_op jit(solution)/shard_map/ppermute | solution.py:256
  22.6 18.1 %collective-permute-start.6 = (bf16[1,256,1024]{2,1,0:T(8,128)(2,1)}, bf16[1,256,1024]{2,1,0:T(8,128)(2,1)}, u32[]{:S(2)}, u32[]{:S(2)}) collective-permute-start(bf16[1,256,1024]{2,1,0:T(8,128)(2,1)} %bitcast.16), channel_id=1, source_target_pairs={{24,20},{25,21},{26,22},{27,23},{28,16},{29,17},{30,18},{31,19}} | collective-permute-start | bytes 1572872 | tf_op jit(solution)/shard_map/ppermute | solution.py:256
  30.2 18.0 %collective-permute-start.16 = (bf16[2,256,512]{2,1,0:T(8,128)(2,1)S(1)}, bf16[2,256,512]{2,1,0:T(8,128)(2,1)S(1)}, u32[]{:S(2)}, u32[]{:S(2)}) collective-permute-start(bf16[2,256,512]{2,1,0:T(8,128)(2,1)S(1)} %partials.8), channel_id=1, source_target_pairs={{8,9},{9,8},{10,11},{11,10},{12,13},{13,12},{14,15},{15,14},{0,1},... | collective-permute-start | bytes 1572872 | tf_op jit(solution)/shard_map/ppermute | solution.py:256
  36.1 22.5 %collective-permute-start.17 = (bf16[2,256,512]{2,1,0:T(8,128)(2,1)S(1)}, bf16[2,256,512]{2,1,0:T(8,128)(2,1)S(1)}, u32[]{:S(2)}, u32[]{:S(2)}) collective-permute-start(bf16[2,256,512]{2,1,0:T(8,128)(2,1)S(1)} %partials.10), channel_id=1, source_target_pairs={{8,9},{9,8},{10,11},{11,10},{12,13},{13,12},{14,15},{15,14},{0,1},... | collective-permute-start | bytes 1572872 | tf_op jit(solution)/shard_map/ppermute | solution.py:256
  38.2 31.3 %collective-permute-start.10 = (bf16[1,256,1024]{2,1,0:T(8,128)(2,1)}, bf16[1,256,1024]{2,1,0:T(8,128)(2,1)}, u32[]{:S(2)}, u32[]{:S(2)}) collective-permute-start(bf16[1,256,1024]{2,1,0:T(8,128)(2,1)} %bitcast.16), channel_id=1, source_target_pairs={{24,16},{25,17},{26,18},{27,19},{28,20},{29,21},{30,22},{31,23}} | collective-permute-start | bytes 1572872 | tf_op jit(solution)/shard_map/ppermute | solution.py:256
  41.8 52.1 %collective-permute-start.9 = (bf16[2,256,1024]{2,1,0:T(8,128)(2,1)S(1)}, bf16[2,256,1024]{2,1,0:T(8,128)(2,1)}, u32[]{:S(2)}, u32[]{:S(2)}) collective-permute-start(bf16[2,256,1024]{2,1,0:T(8,128)(2,1)S(1)} %constant_dynamic-update-slice_fusion.2.refs_0_.refs_2_), channel_id=1, source_target_pairs={{16,17},{17,16},{18,19},{19,18},{20,21},{21,20},{22,23},{23,22}} | collective-permute-start | bytes 3145736 | tf_op jit(solution)/shard_map/ppermute | solution.py:256
  49.7 20.5 %collective-permute-start.20 = (bf16[1,256,512]{2,1,0:T(8,128)(2,1)}, bf16[1,256,512]{2,1,0:T(8,128)(2,1)}, u32[]{:S(2)}, u32[]{:S(2)}) collective-permute-start(bf16[1,256,512]{2,1,0:T(8,128)(2,1)} %get-tuple-element.47), channel_id=1, source_target_pairs={{8,14},{9,15},{10,12},{11,13},{12,10},{13,11},{14,8},{15,9},{0,6},... | collective-permute-start | bytes 786440 | tf_op jit(solution)/shard_map/ppermute | solution.py:256
  60.2 16.4 %collective-permute-start.19 = (bf16[1,256,512]{2,1,0:T(8,128)(2,1)}, bf16[1,256,512]{2,1,0:T(8,128)(2,1)}, u32[]{:S(2)}, u32[]{:S(2)}) collective-permute-start(bf16[1,256,512]{2,1,0:T(8,128)(2,1)} %get-tuple-element.46), channel_id=1, source_target_pairs={{8,12},{9,13},{10,14},{11,15},{12,8},{13,9},{14,10},{15,11},{0,4},... | collective-permute-start | bytes 786440 | tf_op jit(solution)/shard_map/ppermute | solution.py:256
  64.8 14.0 %collective-permute-start.18 = (bf16[1,256,512]{2,1,0:T(8,128)(2,1)}, bf16[1,256,512]{2,1,0:T(8,128)(2,1)}, u32[]{:S(2)}, u32[]{:S(2)}) collective-permute-start(bf16[1,256,512]{2,1,0:T(8,128)(2,1)} %get-tuple-element.45), channel_id=1, source_target_pairs={{8,10},{9,11},{10,8},{11,9},{12,14},{13,15},{14,12},{15,13},{0,2},... | collective-permute-start | bytes 786440 | tf_op jit(solution)/shard_map/ppermute | solution.py:256
  69.5 17.2 %collective-permute-start.11 = (bf16[1,256,1024]{2,1,0:T(8,128)(2,1)}, bf16[1,256,1024]{2,1,0:T(8,128)(2,1)S(1)}, u32[]{:S(2)}, u32[]{:S(2)}) collective-permute-start(bf16[1,256,1024]{2,1,0:T(8,128)(2,1)} %collective-permute-done.10.refs_0_), channel_id=1, source_target_pairs={{16,17},{17,16},{18,19},{19,18},{20,21},{21,20},{22,23},{23,22}} | collective-permute-start | bytes 1572872 | tf_op jit(solution)/shard_map/ppermute | solution.py:256
  70.2 25.1 %collective-permute-start.7 = (bf16[1,256,1024]{2,1,0:T(8,128)(2,1)}, bf16[1,256,1024]{2,1,0:T(8,128)(2,1)S(1)}, u32[]{:S(2)}, u32[]{:S(2)}) collective-permute-start(bf16[1,256,1024]{2,1,0:T(8,128)(2,1)} %collective-permute-done.6), channel_id=1, source_target_pairs={{16,18},{17,19},{18,16},{19,17},{20,22},{21,23},{22,20},{23,21}} | collective-permute-start | bytes 1572872 | tf_op jit(solution)/shard_map/ppermute | solution.py:256
  80.2 19.5 %collective-permute-start.21 = (bf16[1,256,512]{2,1,0:T(8,128)(2,1)S(1)}, bf16[1,256,512]{2,1,0:T(8,128)(2,1)S(1)}, u32[]{:S(2)}, u32[]{:S(2)}) collective-permute-start(bf16[1,256,512]{2,1,0:T(8,128)(2,1)S(1)} %add_convert_fusion.1), channel_id=1, source_target_pairs={{8,10},{9,11},{10,8},{11,9},{12,14},{13,15},{14,12},{15,13},{0,2},... | collective-permute-start | bytes 786440 | tf_op jit(solution)/shard_map/ppermute | solution.py:256
  82.1 15.4 %collective-permute-start.23 = (bf16[1,256,512]{2,1,0:T(8,128)(2,1)S(1)}, bf16[1,256,512]{2,1,0:T(8,128)(2,1)S(1)}, u32[]{:S(2)}, u32[]{:S(2)}) collective-permute-start(bf16[1,256,512]{2,1,0:T(8,128)(2,1)S(1)} %add_convert_fusion.1), channel_id=1, source_target_pairs={{8,12},{9,13},{10,14},{11,15},{12,8},{13,9},{14,10},{15,11},{0,4},... | collective-permute-start | bytes 786440 | tf_op jit(solution)/shard_map/ppermute | solution.py:256
  95.2 14.4 %collective-permute-start.12 = (bf16[1,256,1024]{2,1,0:T(8,128)(2,1)S(1)}, bf16[1,256,1024]{2,1,0:T(8,128)(2,1)S(1)}, u32[]{:S(2)}, u32[]{:S(2)}) collective-permute-start(bf16[1,256,1024]{2,1,0:T(8,128)(2,1)S(1)} %collective-permute-done.7.refs_0_.refs_4_), channel_id=1, source_target_pairs={{16,17},{17,16},{18,19},{19,18},{20,21},{21,20},{22,23},{23,22}} | collective-permute-start | bytes 1572872 | tf_op jit(solution)/shard_map/ppermute | solution.py:256
  99.7 16.8 %collective-permute-start.22 = (bf16[2,256,512]{2,1,0:T(8,128)(2,1)S(1)}, bf16[2,256,512]{2,1,0:T(8,128)(2,1)S(1)}, u32[]{:S(2)}, u32[]{:S(2)}) collective-permute-start(bf16[2,256,512]{2,1,0:T(8,128)(2,1)S(1)} %pad_maximum_fusion.refs_0_), channel_id=1, source_target_pairs={{8,9},{9,8},{10,11},{11,10},{12,13},{13,12},{14,15},{15,14},{0,1},... | collective-permute-start | bytes 1572872 | tf_op jit(solution)/shard_map/ppermute | solution.py:256
  106.0 18.9 %collective-permute-start.25 = (bf16[2,256,512]{2,1,0:T(8,128)(2,1)S(1)}, bf16[2,256,512]{2,1,0:T(8,128)(2,1)S(1)}, u32[]{:S(2)}, u32[]{:S(2)}) collective-permute-start(bf16[2,256,512]{2,1,0:T(8,128)(2,1)S(1)} %constant_dynamic-update-slice_fusion.4.refs_2_), channel_id=1, source_target_pairs={{8,9},{9,8},{10,11},{11,10},{12,13},{13,12},{14,15},{15,14},{0,1},... | collective-permute-start | bytes 1572872 | tf_op jit(solution)/shard_map/ppermute | solution.py:256
  109.7 16.1 %collective-permute-start.13 = (bf16[1,256,1024]{2,1,0:T(8,128)(2,1)S(1)}, bf16[1,256,1024]{2,1,0:T(8,128)(2,1)S(1)}, u32[]{:S(2)}, u32[]{:S(2)}) collective-permute-start(bf16[1,256,1024]{2,1,0:T(8,128)(2,1)S(1)} %bitcast.54), channel_id=1, source_target_pairs={{16,8},{17,9},{18,10},{19,11},{20,12},{21,13},{22,14},{23,15}} | collective-permute-start | bytes 1572872 | tf_op jit(solution)/shard_map/ppermute | solution.py:256
  110.5 15.3 %collective-permute-start.14 = (bf16[1,256,1024]{2,1,0:T(8,128)(2,1)S(1)}, bf16[1,256,1024]{2,1,0:T(8,128)(2,1)S(1)}, u32[]{:S(2)}, u32[]{:S(2)}) collective-permute-start(bf16[1,256,1024]{2,1,0:T(8,128)(2,1)S(1)} %bitcast.55), channel_id=1, source_target_pairs={{16,10},{17,11},{18,8},{19,9},{20,14},{21,15},{22,12},{23,13}} | collective-permute-start | bytes 1572872 | tf_op jit(solution)/shard_map/ppermute | solution.py:256
  111.4 14.4 %collective-permute-start.15 = (bf16[1,256,1024]{2,1,0:T(8,128)(2,1)S(1)}, bf16[1,256,1024]{2,1,0:T(8,128)(2,1)}, u32[]{:S(2)}, u32[]{:S(2)}) collective-permute-start(bf16[1,256,1024]{2,1,0:T(8,128)(2,1)S(1)} %bitcast.56), channel_id=1, source_target_pairs={{16,12},{17,13},{18,14},{19,15},{20,8},{21,9},{22,10},{23,11}} | collective-permute-start | bytes 1572872 | tf_op jit(solution)/shard_map/ppermute | solution.py:256
  126.9 11.9 %collective-permute-start.27 = (bf16[2,256,1024]{2,1,0:T(8,128)(2,1)S(1)}, bf16[2,256,1024]{2,1,0:T(8,128)(2,1)}, u32[]{:S(2)}, u32[]{:S(2)}) collective-permute-start(bf16[2,256,1024]{2,1,0:T(8,128)(2,1)S(1)} %constant_dynamic-update-slice_fusion.6.refs_0_.refs_2_), channel_id=1, source_target_pairs={{8,9},{9,8},{10,11},{11,10},{12,13},{13,12},{14,15},{15,14}} | collective-permute-start | bytes 3145736 | tf_op jit(solution)/shard_map/ppermute | solution.py:256
  142.8 67.7 %collective-permute-start.32 = (bf16[1,256,1024]{2,1,0:T(8,128)(2,1)}, bf16[1,256,1024]{2,1,0:T(8,128)(2,1)}, u32[]{:S(2)}, u32[]{:S(2)}) collective-permute-start(bf16[1,256,1024]{2,1,0:T(8,128)(2,1)} %bitcast.24), channel_id=1, source_target_pairs={{8,2},{9,3},{10,0},{11,1},{12,6},{13,7},{14,4},{15,5}} | collective-permute-start | bytes 1572872 | tf_op jit(solution)/shard_map/ppermute | solution.py:256
  144.1 69.2 %collective-permute-start.30 = (bf16[1,256,1024]{2,1,0:T(8,128)(2,1)}, bf16[1,256,1024]{2,1,0:T(8,128)(2,1)}, u32[]{:S(2)}, u32[]{:S(2)}) collective-permute-start(bf16[1,256,1024]{2,1,0:T(8,128)(2,1)} %bitcast.24), channel_id=1, source_target_pairs={{8,4},{9,5},{10,6},{11,7},{12,0},{13,1},{14,2},{15,3}} | collective-permute-start | bytes 1572872 | tf_op jit(solution)/shard_map/ppermute | solution.py:256
  149.6 67.9 %collective-permute-start.37 = (bf16[2,256,512]{2,1,0:T(8,128)(2,1)S(1)}, bf16[2,256,512]{2,1,0:T(8,128)(2,1)S(1)}, u32[]{:S(2)}, u32[]{:S(2)}) collective-permute-start(bf16[2,256,512]{2,1,0:T(8,128)(2,1)S(1)} %partials.12), channel_id=1, source_target_pairs={{24,25},{25,24},{26,27},{27,26},{28,29},{29,28},{30,31},{31,30},{1... | collective-permute-start | bytes 1572872 | tf_op jit(solution)/shard_map/ppermute | solution.py:256
  150.3 68.1 %collective-permute-start.38 = (bf16[2,256,512]{2,1,0:T(8,128)(2,1)S(1)}, bf16[2,256,512]{2,1,0:T(8,128)(2,1)S(1)}, u32[]{:S(2)}, u32[]{:S(2)}) collective-permute-start(bf16[2,256,512]{2,1,0:T(8,128)(2,1)S(1)} %partials.14), channel_id=1, source_target_pairs={{24,25},{25,24},{26,27},{27,26},{28,29},{29,28},{30,31},{31,30},{1... | collective-permute-start | bytes 1572872 | tf_op jit(solution)/shard_map/ppermute | solution.py:256
  151.0 70.4 %collective-permute-start.34 = (bf16[1,256,1024]{2,1,0:T(8,128)(2,1)}, bf16[1,256,1024]{2,1,0:T(8,128)(2,1)}, u32[]{:S(2)}, u32[]{:S(2)}) collective-permute-start(bf16[1,256,1024]{2,1,0:T(8,128)(2,1)} %bitcast.24), channel_id=1, source_target_pairs={{8,0},{9,1},{10,2},{11,3},{12,4},{13,5},{14,6},{15,7}} | collective-permute-start | bytes 1572872 | tf_op jit(solution)/shard_map/ppermute | solution.py:256
  214.4 28.8 %collective-permute-start.33 = (bf16[2,256,1024]{2,1,0:T(8,128)(2,1)S(1)}, bf16[2,256,1024]{2,1,0:T(8,128)(2,1)}, u32[]{:S(2)}, u32[]{:S(2)}) collective-permute-start(bf16[2,256,1024]{2,1,0:T(8,128)(2,1)S(1)} %constant_dynamic-update-slice_fusion.8.refs_0_), channel_id=1, source_target_pairs={{0,1},{1,0},{2,3},{3,2},{4,5},{5,4},{6,7},{7,6}} | collective-permute-start | bytes 3145736 | tf_op jit(solution)/shard_map/ppermute | solution.py:256
  221.3 15.6 %collective-permute-start.35 = (bf16[1,256,1024]{2,1,0:T(8,128)(2,1)}, bf16[1,256,1024]{2,1,0:T(8,128)(2,1)S(1)}, u32[]{:S(2)}, u32[]{:S(2)}) collective-permute-start(bf16[1,256,1024]{2,1,0:T(8,128)(2,1)} %collective-permute-done.34.refs_0_), channel_id=1, source_target_pairs={{0,1},{1,0},{2,3},{3,2},{4,5},{5,4},{6,7},{7,6}} | collective-permute-start | bytes 1572872 | tf_op jit(solution)/shard_map/ppermute | solution.py:256
  224.4 21.1 %collective-permute-start.31 = (bf16[1,256,1024]{2,1,0:T(8,128)(2,1)}, bf16[1,256,1024]{2,1,0:T(8,128)(2,1)S(1)}, u32[]{:S(2)}, u32[]{:S(2)}) collective-permute-start(bf16[1,256,1024]{2,1,0:T(8,128)(2,1)} %collective-permute-done.30), channel_id=1, source_target_pairs={{0,2},{1,3},{2,0},{3,1},{4,6},{5,7},{6,4},{7,5}} | collective-permute-start | bytes 1572872 | tf_op jit(solution)/shard_map/ppermute | solution.py:256
  227.9 20.4 %collective-permute-start.42 = (bf16[1,256,512]{2,1,0:T(8,128)(2,1)S(1)}, bf16[1,256,512]{2,1,0:T(8,128)(2,1)}, u32[]{:S(2)}, u32[]{:S(2)}) collective-permute-start(bf16[1,256,512]{2,1,0:T(8,128)(2,1)S(1)} %add_convert_fusion), channel_id=1, source_target_pairs={{24,26},{25,27},{26,24},{27,25},{28,30},{29,31},{30,28},{31,29},{1... | collective-permute-start | bytes 786440 | tf_op jit(solution)/shard_map/ppermute | solution.py:256
  229.2 22.5 %collective-permute-start.45 = (bf16[1,256,512]{2,1,0:T(8,128)(2,1)}, bf16[1,256,512]{2,1,0:T(8,128)(2,1)S(1)}, u32[]{:S(2)}, u32[]{:S(2)}) collective-permute-start(bf16[1,256,512]{2,1,0:T(8,128)(2,1)} %collective-permute-done.44), channel_id=1, source_target_pairs={{24,26},{25,27},{26,24},{27,25},{28,30},{29,31},{30,28},{31,29},{1... | collective-permute-start | bytes 786440 | tf_op jit(solution)/shard_map/ppermute | solution.py:256
  245.5 11.9 %collective-permute-start.36 = (bf16[1,256,1024]{2,1,0:T(8,128)(2,1)S(1)}, bf16[1,256,1024]{2,1,0:T(8,128)(2,1)S(1)}, u32[]{:S(2)}, u32[]{:S(2)}) collective-permute-start(bf16[1,256,1024]{2,1,0:T(8,128)(2,1)S(1)} %collective-permute-done.31.refs_0_), channel_id=1, source_target_pairs={{0,1},{1,0},{2,3},{3,2},{4,5},{5,4},{6,7},{7,6}} | collective-permute-start | bytes 1572872 | tf_op jit(solution)/shard_map/ppermute | solution.py:256
  (61 other events, 483.8 us)

commit v5 on v0

v5 whole, which is shorter than its diff:
```python
import jax
import jax.numpy as jnp
from jax import lax
from jax.experimental import pallas as pl
from jax.experimental.pallas import tpu as pltpu
from jax.sharding import PartitionSpec as P

DOT_VMEM = 24 * 1024 * 1024
VMEM = pl.BlockSpec(memory_space=pltpu.VMEM)
SMEM = pl.BlockSpec(memory_space=pltpu.SMEM)
HBM = pl.BlockSpec(memory_space=pltpu.HBM)


def scalars(*values):
    return jnp.stack([jnp.asarray(v).astype(jnp.int32) for v in values])


def params():
    return pltpu.CompilerParams(vmem_limit_bytes=DOT_VMEM)


def cost(flops, moved):
    return pl.CostEstimate(flops=flops, bytes_accessed=moved, transcendentals=0)


def in_hbm(array):
    return pltpu.with_memory_space_constraint(array, pltpu.HBM)


def run_of(ref, axis, at, length):
    part = pl.ds(pl.multiple_of(at * length, length), length)
    return ref.at[part, :] if axis == 0 else ref.at[:, part]


def resident(weights, picks):
    count = len(picks)
    depth, cols = weights.shape[0] // count, weights.shape[1]

    def body(at, weights_ref, out_ref, sems):
        def copy(i):
            return pltpu.make_async_copy(
                run_of(weights_ref, 0, at[i], depth), out_ref.at[i], sems.at[i]
            )

        for i in range(count):
            copy(i).start()
        for i in range(count):
            copy(i).wait()

    return pl.pallas_call(
        body,
        in_specs=[SMEM, HBM],
        out_specs=VMEM,
        out_shape=jax.ShapeDtypeStruct((count, depth, cols), weights.dtype),
        scratch_shapes=[pltpu.SemaphoreType.DMA((count,))],
        compiler_params=params(),
        cost_estimate=cost(0, 2 * weights.size),
        name="resident",
    )(scalars(*picks), in_hbm(weights))


def block_dot(active, blocks, weights, wanted, base, out_type):
    rows, depth = blocks[0].shape
    cols = weights.shape[2]
    width = 256 if cols % 256 == 0 else cols
    count = len(blocks)

    def body(active_ref, weights_ref, base_ref, *refs):
        @pl.when(active_ref[0] == 1)
        def _():
            def tile(j, _):
                here = pl.ds(pl.multiple_of(j * width, width), width)
                total = base_ref[:, here].astype(jnp.float32)
                for block_ref, w in zip(refs[:count], wanted):
                    total += jnp.dot(
                        block_ref[...], weights_ref[w, :, here], preferred_element_type=jnp.float32
                    )
                refs[count][:, here] = total.astype(out_type)
                return 0

            lax.fori_loop(0, cols // width, tile, 0)

    return pl.pallas_call(
        body,
        in_specs=[SMEM] + [VMEM] * (count + 2),
        out_specs=VMEM,
        out_shape=jax.ShapeDtypeStruct((rows, cols), out_type),
        compiler_params=params(),
        cost_estimate=cost(2 * count * rows * depth * cols, rows * cols),
        name="block_dot",
    )(scalars(active), weights, base, *blocks)


def stream_dot(active, blocks, weights, picks, base, out_type, kept):
    rows, depth = blocks[0].shape
    cols = weights.shape[1]
    count = len(blocks)

    def body(at, weights_ref, base_ref, *refs):
        block_refs, (out_ref, runs, sems) = refs[:count], refs[count:]

        def copy(k):
            return pltpu.make_async_copy(
                run_of(weights_ref, 0, at[1 + k], depth), runs.at[k], sems.at[k]
            )

        @pl.when(at[0] == 1)
        def _():
            for k in range(count):
                copy(k).start()
            total = None if kept else base_ref[...]
            for k in range(count):
                copy(k).wait()
                part = jnp.dot(block_refs[k][...], runs[k], preferred_element_type=jnp.float32)
                total = part if total is None else total + part
            out_ref[...] = total.astype(out_type)

    return pl.pallas_call(
        body,
        in_specs=[SMEM, HBM] + [VMEM] * (count + 1),
        out_specs=VMEM,
        out_shape=jax.ShapeDtypeStruct((rows, cols), out_type),
        scratch_shapes=[
            pltpu.VMEM((count, depth, cols), weights.dtype),
            pltpu.SemaphoreType.DMA((count,)),
        ],
        input_output_aliases={2: 0} if kept else {},
        compiler_params=params(),
        cost_estimate=cost(2 * count * rows * depth * cols, 2 * count * depth * cols),
        name="stream_dot",
    )(scalars(active, *picks), in_hbm(weights), base, *blocks)


def partials(active, inputs, weights, picks, inner):
    rows, depth = inputs.shape
    count = len(picks)
    width = weights.shape[1] // count

    def body(at, weights_ref, inputs_ref, *refs):
        out_refs, (runs, sems) = refs[:inner], refs[inner:]
        order = [n for dx in [*range(1, inner), 0] for n in range(dx, count, inner)]

        def copy(n):
            return pltpu.make_async_copy(
                run_of(weights_ref, 1, at[1 + n], width), runs.at[n], sems.at[n]
            )

        @pl.when(at[0] == 1)
        def _():
            for n in order:
                copy(n).start()
            for n in order:
                copy(n).wait()
                total = jnp.dot(inputs_ref[...], runs[n], preferred_element_type=jnp.float32)
                out_ref = out_refs[n % inner]
                out_ref[n // inner] = total.astype(out_ref.dtype)

    return pl.pallas_call(
        body,
        in_specs=[SMEM, HBM, VMEM],
        out_specs=[VMEM] * inner,
        out_shape=[
            jax.ShapeDtypeStruct((count // inner, rows, width), jnp.bfloat16 if dx else jnp.float32)
            for dx in range(inner)
        ],
        scratch_shapes=[
            pltpu.VMEM((count, depth, width), weights.dtype),
            pltpu.SemaphoreType.DMA((count,)),
        ],
        compiler_params=params(),
        cost_estimate=cost(2 * rows * weights.size, 2 * weights.size),
        name="partials",
    )(scalars(active, *picks), in_hbm(weights), inputs)


def added(active, own, arrived):
    count, rows, width = own.shape

    def body(active_ref, own_ref, *refs):
        arrived_refs, out_refs = refs[: len(arrived)], refs[len(arrived) :]

        @pl.when(active_ref[0] == 1)
        def _():
            for n in range(count):
                total = own_ref[n]
                for ref in arrived_refs:
                    total = total + ref[n].astype(jnp.float32)
                out_refs[n][...] = total.astype(out_refs[n].dtype)

    return pl.pallas_call(
        body,
        in_specs=[SMEM] + [VMEM] * (1 + len(arrived)),
        out_specs=[VMEM] * count,
        out_shape=[
            jax.ShapeDtypeStruct((rows, width), jnp.bfloat16 if n else jnp.float32)
            for n in range(count)
        ],
        compiler_params=params(),
        cost_estimate=cost(own.size, 8 * own.size),
        name="added",
    )(scalars(active), own, *arrived)


def mean_square(upper, rot_out, low, high, picks, micro, seq):
    _, rows, width = low[0].shape
    eig_rows = rot_out.shape[1]
    count, inner = len(picks), len(low)

    def body(at, rot_ref, *refs):
        low_refs, high_refs = refs[:inner], refs[inner : 2 * inner]
        eig_ref, turned, block, result, sems = refs[2 * inner :]
        for m in range(micro):
            turned[m] = rot_ref[m * seq : (m + 1) * seq, :].T

        def copy(n):
            return pltpu.make_async_copy(
                result.at[n % 2], run_of(eig_ref, 1, at[1 + n], width), sems.at[n % 2]
            )

        def squared(m):
            product = jnp.dot(
                turned[m], block[m * seq : (m + 1) * seq, :], preferred_element_type=jnp.float32
            )
            return product * product

        for n in range(count):

            @pl.when(at[0] == 1)
            def _():
                block[...] = high_refs[n % inner][n // inner]

            @pl.when(at[0] == 0)
            def _():
                block[...] = low_refs[n % inner][n // inner]

            if n >= 2:
                copy(n - 2).wait()
            for m in range(0, micro, 2):
                pair = squared(m) + squared(m + 1) if m + 1 < micro else squared(m)
                result[n % 2] = pair if m == 0 else result[n % 2] + pair
            result[n % 2] = result[n % 2] * (1.0 / (seq * micro))
            copy(n).start()
        for n in range(max(0, count - 2), count):
            copy(n).wait()

    return pl.pallas_call(
        body,
        in_specs=[SMEM] + [VMEM] * (1 + 2 * inner),
        out_specs=HBM,
        out_shape=jax.ShapeDtypeStruct((eig_rows, count * width), jnp.float32),
        scratch_shapes=[
            pltpu.VMEM((micro, eig_rows, seq), rot_out.dtype),
            pltpu.VMEM((rows, width), rot_out.dtype),
            pltpu.VMEM((2, eig_rows, width), jnp.float32),
            pltpu.SemaphoreType.DMA((2,)),
        ],
        compiler_params=params(),
        cost_estimate=cost(16 * rows * eig_rows * count * width, 4 * eig_rows * count * width),
        name="mean_square",
    )(scalars(upper, *picks), rot_out, *low, *high)


def per_device(activations, top_grad, projection, basis_out, basis_in):
    sections = lax.axis_size("section")
    shards = lax.axis_size("shard")
    section, shard = lax.axis_index("section"), lax.axis_index("shard")
    micro, seq, feat_loc = top_grad.shape
    rows = micro * seq
    inputs = activations[0].reshape(rows, feat_loc)
    top = top_grad.reshape(rows, feat_loc)
    out_cols = basis_out[0]
    half = sections // 2

    inner = 1
    while 2 * (2 * inner) ** 2 <= shards:
        inner *= 2
    outer = shards // inner
    picks = [shard ^ part for part in range(shards)]

    def moved(block, flip, pairs):
        route = [(a * shards + i, b * shards + (i ^ flip)) for a, b in pairs for i in range(shards)]
        return lax.ppermute(block, ("section", "shard"), route)

    def spread(block, pairs):
        powers = [1 << p for p in range(outer.bit_length() - 1)]
        near = {dz: moved(block, dz * inner, pairs) for dz in reversed(powers)}
        return near, {dx: moved(block, dx, pairs) for dx in range(1, inner)}

    def along_outer(near, pairs):
        got = dict(near)
        for dz in range(outer):
            low = dz & -dz
            if dz not in got:
                got[dz] = moved(got[dz ^ low], low * inner, pairs)
        return got

    def handed_down(grad, turn):
        own = moved(grad, 0, [(turn + 1, turn)])
        if turn % 2 == 0:
            near, side = spread(grad, [(turn + 1, turn)])
        else:
            near, side = spread(own, [(turn, turn)])
        return {0: own, **near}, side

    def chain(sent, turns, rot_out, weights):
        for turn in turns:
            mine = section == turn
            near, side = sent
            got = along_outer(near, [(turn, turn)])
            base, rot_out = lax.optimization_barrier((near[0], rot_out))

            def product(dots, base, last):
                blocks, parts = [b for b, _ in dots], [p for _, p in dots]
                out_type = jnp.bfloat16 if last else jnp.float32
                if turn == 0:
                    at = [picks[p] for p in parts]
                    return stream_dot(mine, blocks, out_cols, at, base, out_type, False)
                return block_dot(mine, blocks, weights, parts, base, out_type)

            if turn == 0:
                base = jnp.zeros((rows, out_cols.shape[1]), jnp.float32)
                base, rot_out = lax.optimization_barrier((base, rot_out))
            blocks = {(0, 0): near[0], **{(0, dx): block for dx, block in side.items()}}
            totals = [product([(b, dx) for (_, dx), b in blocks.items()], base, outer == 1)]
            for dz in range(1, outer + 1):
                if dz < outer:
                    block, _ = lax.optimization_barrier((got[dz], totals[max(0, dz - 2)]))
                    blocks[dz, 0] = got[dz]
                    for dx in range(1, inner):
                        blocks[dz, dx] = moved(block, dx, [(turn, turn)])
                if dz > 1:
                    dots = [(blocks[dz - 1, dx], (dz - 1) * inner + dx) for dx in range(inner)]
                    if dz == outer - 1:
                        dots.append((blocks[dz, 0], dz * inner))
                    if dz == outer and outer > 2 and inner > 1:
                        dots = dots[1:]
                    totals.append(product(dots, totals[-1], dz == outer))
            if turn == 0:
                return jnp.where(mine, totals[-1], rot_out)
            sent = handed_down(totals[-1], turn - 1)
            parts = list(blocks)
            rot_out = stream_dot(
                mine,
                [blocks[p] for p in parts],
                out_cols,
                [picks[dz * inner + dx] for dz, dx in parts],
                rot_out,
                jnp.bfloat16,
                True,
            )
        return sent, rot_out

    def rotate_in(inputs, among):
        pairs = [(a, a) for a in among]
        mine = (section >= min(among)) & (section <= max(among))
        own, *others = partials(mine, inputs, basis_in[0], picks, inner)
        arrived = [moved(other, 1 + n, pairs) for n, other in enumerate(others)]
        own, *sums = added(mine, own, arrived)
        for dz, part in enumerate(sums, 1):
            own = own + moved(part, dz * inner, pairs).astype(jnp.float32)
        own = own.astype(jnp.bfloat16)
        powers = [1 << p for p in range(outer.bit_length() - 1)]
        near = {0: own, **{dz: moved(own, dz * inner, pairs) for dz in reversed(powers)}}
        got = along_outer(near, pairs)
        column = jnp.stack([got[dz] for dz in range(outer)])
        return [column] + [moved(column, dx, pairs) for dx in range(1, inner)]

    upper = list(range(sections - 1, half - 1, -1))
    lower = list(range(half - 1, -1, -1))
    rot_out = jnp.zeros((rows, out_cols.shape[1]), jnp.bfloat16)

    near, side = spread(top, [(upper[0], upper[0])])
    weights = resident(projection[0], picks)
    sent, rot_out = chain(({0: top, **near}, side), upper, rot_out, weights)
    low = rotate_in(inputs, lower)
    sent, low, inputs = lax.optimization_barrier((sent, low, inputs))
    rot_out = chain(sent, lower, rot_out, weights)
    high = rotate_in(inputs, upper)
    return mean_square(section >= half, rot_out, low, high, picks, micro, seq)[None]


def solution(mesh):
    return jax.shard_map(
        per_device,
        mesh=mesh,
        in_specs=(
            P("section", None, None, "shard"),
            P(None, None, "shard"),
            P("section", None, "shard"),
            P("section", None, "shard"),
            P("section", "shard", None),
        ),
        out_specs=P("section", "shard", None),
        check_vma=False,
    )
```

time: 718 us -> 255 us (0.36)
  blocking collectives: 515 us -> 0 us
  matrix products: 168 us -> 0 us
  waiting for transfers between devices: 0.13 us -> 83.8 us
  starting transfers between devices: 14.2 us -> 73.6 us
  Pallas kernels: 0 us -> 53.7 us
  local copies, waits for them, and re-layouts: 0.02 us -> 38 us
  other arithmetic: 14.3 us -> 3.58 us
    all_gather x11 -> x0, blocking collectives: 347 us -> none  [chain_step(): lax.all_gather(current, 'shard', axis=1, tiled=True)]
    dot_general x24 -> x0, matrix products: 168 us -> none  [the longest x11 96.3 us: absorb(): through = jnp.dot(piece, weight_cols, preferred_element_type=jnp.float32)]
    psum x1 -> x0, blocking collectives: 168 us -> none  [per_device(): rot_in = lax.psum(partial_rot, 'shard').astype(jnp.bfloat16)]
    ppermute x11 -> x47, waiting for transfers between devices: 0.13 us -> 83.8 us  [moved(): return lax.ppermute(block, ('section', 'shard'), route)]
    ppermute x11 -> x47, starting transfers between devices: 14.2 us -> 73.6 us  [moved(): return lax.ppermute(block, ('section', 'shard'), route)]
    pallas_call x0 -> x25, Pallas kernels: none -> 53.7 us  [the longest x7 15.3 us: stream_dot(): pl.pallas_call(body, in_specs=[SMEM, HBM] + [VMEM] * (count + 1), out_spe...]
    unnamed x2 -> x72, local copies, waits for them, and re-layouts: 0.01 us -> 37.3 us
    select_n x12 -> x1, other arithmetic: 10.3 us -> 0.03 us  [chain(): return jnp.where(mine, totals[-1], rot_out)]
  transfers between devices with their start and end apart: 11 -> 47, of which waited for: 0 -> 10; matrix products, arithmetic and copies ran while one was open for 8% -> 2% of each run, Pallas kernels for 0% -> 15%
where the time goes in v5:
time: 255 us; the launch traced here: 254 us
  waiting for transfers between devices  83.8 us (33%)
  starting transfers between devices  73.6 us (29%)
  Pallas kernels  53.7 us (21%)
  local copies, waits for them, and re-layouts  38 us (15%)
  other arithmetic  3.58 us (1%)
    ppermute x47, waiting for transfers between devices, moved(): return lax.ppermute(block, ('section', 'shard'), route)  83.8 us
    ppermute x47, starting transfers between devices, moved(): return lax.ppermute(block, ('section', 'shard'), route)  73.6 us
    unnamed x72, local copies, waits for them, and re-layouts  37.3 us
    pallas_call x7, Pallas kernels, stream_dot(): pl.pallas_call(body, in_specs=[SMEM, HBM] + [VMEM] * (count + 1), out_spe...  15.3 us
    pallas_call x1, Pallas kernels, mean_square(): pl.pallas_call(body, in_specs=[SMEM] + [VMEM] * (1 + 2 * inner), out_spec...  13.7 us
    pallas_call x2, Pallas kernels, partials(): pl.pallas_call(body, in_specs=[SMEM, HBM, VMEM], out_specs=[VMEM] * inner...  8.61 us
    pallas_call x12, Pallas kernels, block_dot(): pl.pallas_call(body, in_specs=[SMEM] + [VMEM] * (count + 2), out_specs=VM...  6.98 us
    pallas_call x1, Pallas kernels, resident(): pl.pallas_call(body, in_specs=[SMEM, HBM], out_specs=VMEM, out_shape=jax....  6.47 us
  transfers between devices with their start and end apart: 47, of which 10 were waited for; matrix products, arithmetic and copies ran while one was open for 2% of the time, Pallas kernels for 15%

profile of v5, /device:TPU:0, one launch (start us, length us, event | category | flops | bytes accessed | tf_op | source)
XLA Modules:
  0.0 253.7 jit_solution(16252711656739727863)
XLA Ops:
  2.2 6.5 %resident.1.weights_ref = bf16[8,1024,1024]{2,1,0:T(8,128)(2,1)S(1)} custom-call(s32[8]{0:T(128)S(1)} %stack.107.at, bf16[8192,1024]{1,0:T(8,128)(2,1)} %bitcast.48), custom_call_target="tpu_custom_call" | custom-call | bytes 16777216 | tf_op jit(solution)/shard_map/resident/pallas_call | solution.py:50
  8.7 5.8 %copy-done = bf16[8,1024,1024]{2,1,0:T(8,128)(2,1)} copy-done((bf16[8,1024,1024]{2,1,0:T(8,128)(2,1)}, bf16[8,1024,1024]{2,1,0:T(8,128)(2,1)S(1)}, u32[]{:S(2)}) %copy-start) | copy-done | bytes 16777240
  18.4 5.8 %copy-done.1 = bf16[8,1024,1024]{2,1,0:T(8,128)(2,1)S(1)} copy-done((bf16[8,1024,1024]{2,1,0:T(8,128)(2,1)S(1)}, bf16[8,1024,1024]{2,1,0:T(8,128)(2,1)}, u32[]{:S(2)}) %copy-start.1) | copy-done | bytes 16777240
  26.3 7.0 %partials.2 = (f32[4,256,512]{2,1,0:T(8,128)S(1)}, bf16[4,256,512]{2,1,0:T(8,128)(2,1)}) custom-call(s32[9]{0:T(128)S(1)} %stack.224.at, bf16[1024,4096]{1,0:T(8,128)(2,1)} %bitcast.46, bf16[256,1024]{1,0:T(8,128)(2,1)S(1)} %bitcast.37), custom_call_target="tpu_custom_call" | custom-call | flops 2147483648 | bytes 8388608 | tf_op jit(solution)/shard_map/partials/pallas_call | solution.py:158
  33.3 4.8 %collective-permute-start.19 = (bf16[4,256,512]{2,1,0:T(8,128)(2,1)}, bf16[4,256,512]{2,1,0:T(8,128)(2,1)}, u32[]{:S(2)}, u32[]{:S(2)}) collective-permute-start(bf16[4,256,512]{2,1,0:T(8,128)(2,1)} %get-tuple-element.55), channel_id=1, source_target_pairs={{8,9},{9,8},{10,11},{11,10},{12,13},{13,12},{14,15},{15,14},{0,1},... | collective-permute-start | bytes 3145736 | tf_op jit(solution)/shard_map/ppermute | solution.py:282
  43.3 18.3 %collective-permute-done.19.refs_0_ = bf16[4,256,512]{2,1,0:T(8,128)(2,1)} collective-permute-done((bf16[4,256,512]{2,1,0:T(8,128)(2,1)}, bf16[4,256,512]{2,1,0:T(8,128)(2,1)}, u32[]{:S(2)}, u32[]{:S(2)}) %collective-permute-start.19) | collective-permute-done | bytes 1048608 | tf_op jit(solution)/shard_map/ppermute | solution.py:282
  64.6 3.7 %collective-permute-start.20 = (bf16[256,512]{1,0:T(8,128)(2,1)S(1)}, bf16[256,512]{1,0:T(8,128)(2,1)S(1)}, u32[]{:S(2)}, u32[]{:S(2)}) collective-permute-start(bf16[256,512]{1,0:T(8,128)(2,1)S(1)} %get-tuple-element.57), channel_id=1, source_target_pairs={{8,10},{9,11},{10,8},{11,9},{12,14},{13,15},{14,12},{15,13},{0,2},... | collective-permute-start | bytes 786440 | tf_op jit(solution)/shard_map/ppermute | solution.py:282
  68.3 4.5 %collective-permute-start.21 = (bf16[256,512]{1,0:T(8,128)(2,1)S(1)}, bf16[256,512]{1,0:T(8,128)(2,1)S(1)}, u32[]{:S(2)}, u32[]{:S(2)}) collective-permute-start(bf16[256,512]{1,0:T(8,128)(2,1)S(1)} %get-tuple-element.58), channel_id=1, source_target_pairs={{8,12},{9,13},{10,14},{11,15},{12,8},{13,9},{14,10},{15,11},{0,4},... | collective-permute-start | bytes 786440 | tf_op jit(solution)/shard_map/ppermute | solution.py:282
  72.9 1.9 collective-permute-start.22
  82.2 5.8 %copy-done.3 = bf16[8,1024,1024]{2,1,0:T(8,128)(2,1)S(1)} copy-done((bf16[8,1024,1024]{2,1,0:T(8,128)(2,1)S(1)}, bf16[8,1024,1024]{2,1,0:T(8,128)(2,1)}, u32[]{:S(2)}) %copy-start.3) | copy-done | bytes 16777240
  89.4 1.8 collective-permute-done.21
  91.3 7.2 %collective-permute-start.24 = (bf16[256,512]{1,0:T(8,128)(2,1)S(1)}, bf16[256,512]{1,0:T(8,128)(2,1)S(1)}, u32[]{:S(2)}, u32[]{:S(2)}) collective-permute-start(bf16[256,512]{1,0:T(8,128)(2,1)S(1)} %add_convert_fusion.1), channel_id=1, source_target_pairs={{8,12},{9,13},{10,14},{11,15},{12,8},{13,9},{14,10},{15,11},{0,4},... | collective-permute-start | bytes 786440 | tf_op jit(solution)/shard_map/ppermute | solution.py:282
  99.3 1.9 collective-permute-start.23
  101.2 8.0 %collective-permute-done.24 = bf16[256,512]{1,0:T(8,128)(2,1)S(1)} collective-permute-done((bf16[256,512]{1,0:T(8,128)(2,1)S(1)}, bf16[256,512]{1,0:T(8,128)(2,1)S(1)}, u32[]{:S(2)}, u32[]{:S(2)}) %collective-permute-start.24) | collective-permute-done | bytes 262176 | tf_op jit(solution)/shard_map/ppermute | solution.py:282
  109.1 1.9 collective-permute-start.25
  112.6 5.6 %collective-permute-done.25 = bf16[256,512]{1,0:T(8,128)(2,1)S(1)} collective-permute-done((bf16[256,512]{1,0:T(8,128)(2,1)S(1)}, bf16[256,512]{1,0:T(8,128)(2,1)S(1)}, u32[]{:S(2)}, u32[]{:S(2)}) %collective-permute-start.25) | collective-permute-done | bytes 262176 | tf_op jit(solution)/shard_map/ppermute | solution.py:282
  119.3 3.4 %collective-permute-start.26 = (bf16[4,256,512]{2,1,0:T(8,128)(2,1)}, bf16[4,256,512]{2,1,0:T(8,128)(2,1)}, u32[]{:S(2)}, u32[]{:S(2)}) collective-permute-start(bf16[4,256,512]{2,1,0:T(8,128)(2,1)} %pad_maximum_fusion.refs_0_), channel_id=1, source_target_pairs={{8,9},{9,8},{10,11},{11,10},{12,13},{13,12},{14,15},{15,14},{0,1},... | collective-permute-start | bytes 3145736 | tf_op jit(solution)/shard_map/ppermute | solution.py:282
  129.8 17.8 %collective-permute-done.26.refs_1_ = bf16[4,256,512]{2,1,0:T(8,128)(2,1)} collective-permute-done((bf16[4,256,512]{2,1,0:T(8,128)(2,1)}, bf16[4,256,512]{2,1,0:T(8,128)(2,1)}, u32[]{:S(2)}, u32[]{:S(2)}) %collective-permute-start.26) | collective-permute-done | bytes 1048608 | tf_op jit(solution)/shard_map/ppermute | solution.py:282
  151.8 5.8 %copy-done.4 = bf16[8,1024,1024]{2,1,0:T(8,128)(2,1)S(1)} copy-done((bf16[8,1024,1024]{2,1,0:T(8,128)(2,1)S(1)}, bf16[8,1024,1024]{2,1,0:T(8,128)(2,1)}, u32[]{:S(2)}) %copy-start.4) | copy-done | bytes 16777240
  161.2 1.8 block_dot.21.base_ref
  178.1 21.8 %collective-permute-done.31.refs_0_ = bf16[256,1024]{1,0:T(8,128)(2,1)} collective-permute-done((bf16[256,1024]{1,0:T(8,128)(2,1)}, bf16[256,1024]{1,0:T(8,128)(2,1)}, u32[]{:S(2)}, u32[]{:S(2)}) %collective-permute-start.31) | collective-permute-done | bytes 524320 | tf_op jit(solution)/shard_map/ppermute | solution.py:282
  203.6 3.2 %stream_dot.10.base_ref = f32[256,512]{1,0:T(8,128)S(1)} custom-call(s32[3]{0:T(128)S(1)} %pad_add_fusion.3.at, bf16[8192,512]{1,0:T(8,128)(2,1)} %bitcast.42, f32[256,512]{1,0:T(8,128)S(1)} %broadcast_in_dim.9.base_ref, bf16[256,1024]{1,0:T(8,128)(2,1)} %collective-permute-done.31.refs_0_, bf16[256,1024]{1,0:T(8,128)(2,1)} %collective-permute-done.32.refs_1_), custom_call_target="tpu_custom_call" | custom-call | flops 536870912 | bytes 2097152 | tf_op jit(solution)/shard_map/stream_dot/pallas_call | solution.py:118
  206.9 3.2 %collective-permute-start.34 = (bf16[256,1024]{1,0:T(8,128)(2,1)}, bf16[256,1024]{1,0:T(8,128)(2,1)S(1)}, u32[]{:S(2)}, u32[]{:S(2)}) collective-permute-start(bf16[256,1024]{1,0:T(8,128)(2,1)} %collective-permute-done.33.refs_0_), channel_id=1, source_target_pairs={{0,1},{1,0},{2,3},{3,2},{4,5},{5,4},{6,7},{7,6}} | collective-permute-start | bytes 1572872 | tf_op jit(solution)/shard_map/ppermute | solution.py:282
  210.1 4.7 %collective-permute-done.35.refs_0_ = bf16[256,1024]{1,0:T(8,128)(2,1)S(1)} collective-permute-done((bf16[256,1024]{1,0:T(8,128)(2,1)}, bf16[256,1024]{1,0:T(8,128)(2,1)S(1)}, u32[]{:S(2)}, u32[]{:S(2)}) %collective-permute-start.35) | collective-permute-done | bytes 524320 | tf_op jit(solution)/shard_map/ppermute | solution.py:282
  214.7 1.9 collective-permute-start.37
  219.5 3.2 %collective-permute-start.36 = (bf16[256,1024]{1,0:T(8,128)(2,1)S(1)}, bf16[256,1024]{1,0:T(8,128)(2,1)S(1)}, u32[]{:S(2)}, u32[]{:S(2)}) collective-permute-start(bf16[256,1024]{1,0:T(8,128)(2,1)S(1)} %collective-permute-done.35.refs_0_), channel_id=1, source_target_pairs={{0,1},{1,0},{2,3},{3,2},{4,5},{5,4},{6,7},{7,6}} | collective-permute-start | bytes 1572872 | tf_op jit(solution)/shard_map/ppermute | solution.py:282
  222.8 3.1 %stream_dot.11.base_ref = f32[256,512]{1,0:T(8,128)S(1)} custom-call(s32[3]{0:T(128)S(1)} %pad_add_fusion.2.at, bf16[8192,512]{1,0:T(8,128)(2,1)} %bitcast.43, f32[256,512]{1,0:T(8,128)S(1)} %stream_dot.10.base_ref, bf16[256,1024]{1,0:T(8,128)(2,1)} %collective-permute-done.33.refs_0_, bf16[256,1024]{1,0:T(8,128)(2,1)S(1)} %collective-permute-done.34.refs_1_), custom_call_target="tpu_custom_call" | custom-call | flops 536870912 | bytes 2097152 | tf_op jit(solution)/shard_map/stream_dot/pallas_call | solution.py:118
  225.8 3.2 %collective-permute-start.38 = (bf16[256,1024]{1,0:T(8,128)(2,1)S(1)}, bf16[256,1024]{1,0:T(8,128)(2,1)}, u32[]{:S(2)}, u32[]{:S(2)}) collective-permute-start(bf16[256,1024]{1,0:T(8,128)(2,1)S(1)} %collective-permute-done.37.refs_2_), channel_id=1, source_target_pairs={{0,1},{1,0},{2,3},{3,2},{4,5},{5,4},{6,7},{7,6}} | collective-permute-start | bytes 1572872 | tf_op jit(solution)/shard_map/ppermute | solution.py:282
  230.5 2.9 %stream_dot.12.base_ref = f32[256,512]{1,0:T(8,128)S(1)} custom-call(s32[4]{0:T(128)S(1)} %pad_add_fusion.1.at, bf16[8192,512]{1,0:T(8,128)(2,1)} %bitcast.44, f32[256,512]{1,0:T(8,128)S(1)} %stream_dot.11.base_ref, bf16[256,1024]{1,0:T(8,128)(2,1)S(1)} %collective-permute-done.35.refs_0_, bf16[256,1024]{1,0:T(8,128)(2,1)S(1)} %collective-permute-done.36.refs_1_, ...), custom_call_target="tpu_custom_call" | custom-call | flops 805306368 | bytes 3145728 | tf_op jit(solution)/shard_map/stream_dot/pallas_call | solution.py:118
  233.4 3.6 %collective-permute-done.38.refs_0_ = bf16[256,1024]{1,0:T(8,128)(2,1)} collective-permute-done((bf16[256,1024]{1,0:T(8,128)(2,1)S(1)}, bf16[256,1024]{1,0:T(8,128)(2,1)}, u32[]{:S(2)}, u32[]{:S(2)}) %collective-permute-start.38) | collective-permute-done | bytes 524320 | tf_op jit(solution)/shard_map/ppermute | solution.py:282
  237.0 2.7 %stream_dot.13 = bf16[256,512]{1,0:T(8,128)(2,1)S(1)} custom-call(s32[2]{0:T(128)S(1)} %pad_add_fusion.at, bf16[8192,512]{1,0:T(8,128)(2,1)} %bitcast.45, f32[256,512]{1,0:T(8,128)S(1)} %stream_dot.12.base_ref, bf16[256,1024]{1,0:T(8,128)(2,1)} %collective-permute-done.38.refs_0_), custom_call_target="tpu_custom_call" | custom-call | flops 268435456 | bytes 1048576 | tf_op jit(solution)/shard_map/stream_dot/pallas_call | solution.py:118
  239.8 13.7 %mean_square.1 = f32[512,4096]{1,0:T(8,128)} custom-call(s32[9]{0:T(128)S(1)} %stack.98.at, bf16[256,512]{1,0:T(8,128)(2,1)S(1)} %broadcast_select_fusion.rot_ref, bf16[4,256,512]{2,1,0:T(8,128)(2,1)} %pad_maximum_fusion.refs_0_, bf16[4,256,512]{2,1,0:T(8,128)(2,1)} %collective-permute-done.26.refs_1_, bf16[4,256,512]{2,1,0:T(8,128)(2,1)S(1)} %pad_maximum_fusion.1.refs_2_, ...), custom_call_target="tpu_custom_call" | custom-call | flops 8589934592 | bytes 8388608 | tf_op jit(solution)/shard_map/mean_square/pallas_call | solution.py:246
  (178 shorter events, 66.1 us)
Async XLA Ops:
  0.7 14.0 %collective-permute-start.1 = (bf16[256,1024]{1,0:T(8,128)(2,1)}, bf16[256,1024]{1,0:T(8,128)(2,1)S(1)}, u32[]{:S(2)}, u32[]{:S(2)}) collective-permute-start(bf16[256,1024]{1,0:T(8,128)(2,1)} %bitcast.32), channel_id=1, source_target_pairs={{24,26},{25,27},{26,24},{27,25},{28,30},{29,31},{30,28},{31,29}} | collective-permute-start | bytes 1572872 | tf_op jit(solution)/shard_map/ppermute | solution.py:282
  1.4 14.0 %collective-permute-start.3 = (bf16[256,1024]{1,0:T(8,128)(2,1)}, bf16[256,1024]{1,0:T(8,128)(2,1)S(1)}, u32[]{:S(2)}, u32[]{:S(2)}) collective-permute-start(bf16[256,1024]{1,0:T(8,128)(2,1)} %bitcast.33), channel_id=1, source_target_pairs={{24,28},{25,29},{26,30},{27,31},{28,24},{29,25},{30,26},{31,27}} | collective-permute-start | bytes 1572872 | tf_op jit(solution)/shard_map/ppermute | solution.py:282
  16.9 21.2 %collective-permute-start.4 = (bf16[256,1024]{1,0:T(8,128)(2,1)S(1)}, bf16[256,1024]{1,0:T(8,128)(2,1)S(1)}, u32[]{:S(2)}, u32[]{:S(2)}) collective-permute-start(bf16[256,1024]{1,0:T(8,128)(2,1)S(1)} %collective-permute-done.3.refs_0_.refs_4_), channel_id=1, source_target_pairs={{24,25},{25,24},{26,27},{27,26},{28,29},{29,28},{30,31},{31,30}} | collective-permute-start | bytes 1572872 | tf_op jit(solution)/shard_map/ppermute | solution.py:282
  25.3 14.2 %collective-permute-start.6 = (bf16[256,1024]{1,0:T(8,128)(2,1)}, bf16[256,1024]{1,0:T(8,128)(2,1)S(1)}, u32[]{:S(2)}, u32[]{:S(2)}) collective-permute-start(bf16[256,1024]{1,0:T(8,128)(2,1)} %collective-permute-done.5.refs_2_.refs_6_), channel_id=1, source_target_pairs={{24,25},{25,24},{26,27},{27,26},{28,29},{29,28},{30,31},{31,30}} | collective-permute-start | bytes 1572872 | tf_op jit(solution)/shard_map/ppermute | solution.py:282
  33.3 28.3 %collective-permute-start.19 = (bf16[4,256,512]{2,1,0:T(8,128)(2,1)}, bf16[4,256,512]{2,1,0:T(8,128)(2,1)}, u32[]{:S(2)}, u32[]{:S(2)}) collective-permute-start(bf16[4,256,512]{2,1,0:T(8,128)(2,1)} %get-tuple-element.55), channel_id=1, source_target_pairs={{8,9},{9,8},{10,11},{11,10},{12,13},{13,12},{14,15},{15,14},{0,1},... | collective-permute-start | bytes 3145736 | tf_op jit(solution)/shard_map/ppermute | solution.py:282
  40.4 27.9 %collective-permute-start.8 = (bf16[256,1024]{1,0:T(8,128)(2,1)}, bf16[256,1024]{1,0:T(8,128)(2,1)S(1)}, u32[]{:S(2)}, u32[]{:S(2)}) collective-permute-start(bf16[256,1024]{1,0:T(8,128)(2,1)} %block_dot.15), channel_id=1, source_target_pairs={{24,17},{25,16},{26,19},{27,18},{28,21},{29,20},{30,23},{31,22}} | collective-permute-start | bytes 1572872 | tf_op jit(solution)/shard_map/ppermute | solution.py:282
  41.1 31.7 %collective-permute-start.7 = (bf16[256,1024]{1,0:T(8,128)(2,1)}, bf16[256,1024]{1,0:T(8,128)(2,1)S(1)}, u32[]{:S(2)}, u32[]{:S(2)}) collective-permute-start(bf16[256,1024]{1,0:T(8,128)(2,1)} %block_dot.15), channel_id=1, source_target_pairs={{24,16},{25,17},{26,18},{27,19},{28,20},{29,21},{30,22},{31,23}} | collective-permute-start | bytes 1572872 | tf_op jit(solution)/shard_map/ppermute | solution.py:282
  41.8 46.2 %collective-permute-start.9 = (bf16[256,1024]{1,0:T(8,128)(2,1)}, bf16[256,1024]{1,0:T(8,128)(2,1)S(1)}, u32[]{:S(2)}, u32[]{:S(2)}) collective-permute-start(bf16[256,1024]{1,0:T(8,128)(2,1)} %block_dot.15), channel_id=1, source_target_pairs={{24,18},{25,19},{26,16},{27,17},{28,22},{29,23},{30,20},{31,21}} | collective-permute-start | bytes 1572872 | tf_op jit(solution)/shard_map/ppermute | solution.py:282
  42.5 46.2 %collective-permute-start.11 = (bf16[256,1024]{1,0:T(8,128)(2,1)}, bf16[256,1024]{1,0:T(8,128)(2,1)S(1)}, u32[]{:S(2)}, u32[]{:S(2)}) collective-permute-start(bf16[256,1024]{1,0:T(8,128)(2,1)} %block_dot.15), channel_id=1, source_target_pairs={{24,20},{25,21},{26,22},{27,23},{28,16},{29,17},{30,18},{31,19}} | collective-permute-start | bytes 1572872 | tf_op jit(solution)/shard_map/ppermute | solution.py:282
  64.6 24.8 %collective-permute-start.20 = (bf16[256,512]{1,0:T(8,128)(2,1)S(1)}, bf16[256,512]{1,0:T(8,128)(2,1)S(1)}, u32[]{:S(2)}, u32[]{:S(2)}) collective-permute-start(bf16[256,512]{1,0:T(8,128)(2,1)S(1)} %get-tuple-element.57), channel_id=1, source_target_pairs={{8,10},{9,11},{10,8},{11,9},{12,14},{13,15},{14,12},{15,13},{0,2},... | collective-permute-start | bytes 786440 | tf_op jit(solution)/shard_map/ppermute | solution.py:282
  68.3 22.8 %collective-permute-start.21 = (bf16[256,512]{1,0:T(8,128)(2,1)S(1)}, bf16[256,512]{1,0:T(8,128)(2,1)S(1)}, u32[]{:S(2)}, u32[]{:S(2)}) collective-permute-start(bf16[256,512]{1,0:T(8,128)(2,1)S(1)} %get-tuple-element.58), channel_id=1, source_target_pairs={{8,12},{9,13},{10,14},{11,15},{12,8},{13,9},{14,10},{15,11},{0,4},... | collective-permute-start | bytes 786440 | tf_op jit(solution)/shard_map/ppermute | solution.py:282
  72.9 18.3 %collective-permute-start.22 = (bf16[256,512]{1,0:T(8,128)(2,1)S(1)}, bf16[256,512]{1,0:T(8,128)(2,1)S(1)}, u32[]{:S(2)}, u32[]{:S(2)}) collective-permute-start(bf16[256,512]{1,0:T(8,128)(2,1)S(1)} %get-tuple-element.59), channel_id=1, source_target_pairs={{8,14},{9,15},{10,12},{11,13},{12,10},{13,11},{14,8},{15,9},{0,6},... | collective-permute-start | bytes 786440 | tf_op jit(solution)/shard_map/ppermute | solution.py:282
  88.0 23.1 %collective-permute-start.10 = (bf16[256,1024]{1,0:T(8,128)(2,1)S(1)}, bf16[256,1024]{1,0:T(8,128)(2,1)S(1)}, u32[]{:S(2)}, u32[]{:S(2)}) collective-permute-start(bf16[256,1024]{1,0:T(8,128)(2,1)S(1)} %collective-permute-done.9.refs_0_.refs_2_), channel_id=1, source_target_pairs={{16,17},{17,16},{18,19},{19,18},{20,21},{21,20},{22,23},{23,22}} | collective-permute-start | bytes 1572872 | tf_op jit(solution)/shard_map/ppermute | solution.py:282
  88.7 23.2 %collective-permute-start.13 = (bf16[256,1024]{1,0:T(8,128)(2,1)S(1)}, bf16[256,1024]{1,0:T(8,128)(2,1)S(1)}, u32[]{:S(2)}, u32[]{:S(2)}) collective-permute-start(bf16[256,1024]{1,0:T(8,128)(2,1)S(1)} %collective-permute-done.11.refs_0_.refs_4_), channel_id=1, source_target_pairs={{16,18},{17,19},{18,16},{19,17},{20,22},{21,23},{22,20},{23,21}} | collective-permute-start | bytes 1572872 | tf_op jit(solution)/shard_map/ppermute | solution.py:282
  91.3 17.8 %collective-permute-start.24 = (bf16[256,512]{1,0:T(8,128)(2,1)S(1)}, bf16[256,512]{1,0:T(8,128)(2,1)S(1)}, u32[]{:S(2)}, u32[]{:S(2)}) collective-permute-start(bf16[256,512]{1,0:T(8,128)(2,1)S(1)} %add_convert_fusion.1), channel_id=1, source_target_pairs={{8,12},{9,13},{10,14},{11,15},{12,8},{13,9},{14,10},{15,11},{0,4},... | collective-permute-start | bytes 786440 | tf_op jit(solution)/shard_map/ppermute | solution.py:282
  98.6 24.2 %collective-permute-start.12 = (bf16[256,1024]{1,0:T(8,128)(2,1)S(1)}, bf16[256,1024]{1,0:T(8,128)(2,1)S(1)}, u32[]{:S(2)}, u32[]{:S(2)}) collective-permute-start(bf16[256,1024]{1,0:T(8,128)(2,1)S(1)} %collective-permute-done.11.refs_0_.refs_4_), channel_id=1, source_target_pairs={{16,17},{17,16},{18,19},{19,18},{20,21},{21,20},{22,23},{23,22}} | collective-permute-start | bytes 1572872 | tf_op jit(solution)/shard_map/ppermute | solution.py:282
  99.3 13.3 %collective-permute-start.23 = (bf16[256,512]{1,0:T(8,128)(2,1)S(1)}, bf16[256,512]{1,0:T(8,128)(2,1)S(1)}, u32[]{:S(2)}, u32[]{:S(2)}) collective-permute-start(bf16[256,512]{1,0:T(8,128)(2,1)S(1)} %add_convert_fusion.1), channel_id=1, source_target_pairs={{8,10},{9,11},{10,8},{11,9},{12,14},{13,15},{14,12},{15,13},{0,2},... | collective-permute-start | bytes 786440 | tf_op jit(solution)/shard_map/ppermute | solution.py:282
  111.9 11.7 %collective-permute-start.14 = (bf16[256,1024]{1,0:T(8,128)(2,1)S(1)}, bf16[256,1024]{1,0:T(8,128)(2,1)S(1)}, u32[]{:S(2)}, u32[]{:S(2)}) collective-permute-start(bf16[256,1024]{1,0:T(8,128)(2,1)S(1)} %collective-permute-done.13.refs_2_.refs_6_), channel_id=1, source_target_pairs={{16,17},{17,16},{18,19},{19,18},{20,21},{21,20},{22,23},{23,22}} | collective-permute-start | bytes 1572872 | tf_op jit(solution)/shard_map/ppermute | solution.py:282
  119.3 28.3 %collective-permute-start.26 = (bf16[4,256,512]{2,1,0:T(8,128)(2,1)}, bf16[4,256,512]{2,1,0:T(8,128)(2,1)}, u32[]{:S(2)}, u32[]{:S(2)}) collective-permute-start(bf16[4,256,512]{2,1,0:T(8,128)(2,1)} %pad_maximum_fusion.refs_0_), channel_id=1, source_target_pairs={{8,9},{9,8},{10,11},{11,10},{12,13},{13,12},{14,15},{15,14},{0,1},... | collective-permute-start | bytes 3145736 | tf_op jit(solution)/shard_map/ppermute | solution.py:282
  125.2 22.4 %collective-permute-start.18 = (bf16[256,1024]{1,0:T(8,128)(2,1)S(1)}, bf16[256,1024]{1,0:T(8,128)(2,1)}, u32[]{:S(2)}, u32[]{:S(2)}) collective-permute-start(bf16[256,1024]{1,0:T(8,128)(2,1)S(1)} %collective-permute-done.15.base_ref.refs_0_), channel_id=1, source_target_pairs={{8,9},{9,8},{10,11},{11,10},{12,13},{13,12},{14,15},{15,14}} | collective-permute-start | bytes 1572872 | tf_op jit(solution)/shard_map/ppermute | solution.py:282
  126.6 21.0 %collective-permute-start.17 = (bf16[256,1024]{1,0:T(8,128)(2,1)S(1)}, bf16[256,1024]{1,0:T(8,128)(2,1)}, u32[]{:S(2)}, u32[]{:S(2)}) collective-permute-start(bf16[256,1024]{1,0:T(8,128)(2,1)S(1)} %collective-permute-done.15.base_ref.refs_0_), channel_id=1, source_target_pairs={{8,12},{9,13},{10,14},{11,15},{12,8},{13,9},{14,10},{15,11}} | collective-permute-start | bytes 1572872 | tf_op jit(solution)/shard_map/ppermute | solution.py:282
  128.1 19.5 %collective-permute-start.16 = (bf16[256,1024]{1,0:T(8,128)(2,1)S(1)}, bf16[256,1024]{1,0:T(8,128)(2,1)}, u32[]{:S(2)}, u32[]{:S(2)}) collective-permute-start(bf16[256,1024]{1,0:T(8,128)(2,1)S(1)} %collective-permute-done.15.base_ref.refs_0_), channel_id=1, source_target_pairs={{8,10},{9,11},{10,8},{11,9},{12,14},{13,15},{14,12},{15,13}} | collective-permute-start | bytes 1572872 | tf_op jit(solution)/shard_map/ppermute | solution.py:282
  149.3 14.5 %collective-permute-start.39 = (bf16[4,256,512]{2,1,0:T(8,128)(2,1)}, bf16[4,256,512]{2,1,0:T(8,128)(2,1)}, u32[]{:S(2)}, u32[]{:S(2)}) collective-permute-start(bf16[4,256,512]{2,1,0:T(8,128)(2,1)} %get-tuple-element.80), channel_id=1, source_target_pairs={{24,25},{25,24},{26,27},{27,26},{28,29},{29,28},{30,31},{31,30},{1... | collective-permute-start | bytes 3145736 | tf_op jit(solution)/shard_map/ppermute | solution.py:282
  170.5 36.3 %collective-permute-start.33 = (bf16[256,1024]{1,0:T(8,128)(2,1)}, bf16[256,1024]{1,0:T(8,128)(2,1)}, u32[]{:S(2)}, u32[]{:S(2)}) collective-permute-start(bf16[256,1024]{1,0:T(8,128)(2,1)} %block_dot.23), channel_id=1, source_target_pairs={{8,2},{9,3},{10,0},{11,1},{12,6},{13,7},{14,4},{15,5}} | collective-permute-start | bytes 1572872 | tf_op jit(solution)/shard_map/ppermute | solution.py:282
  171.8 31.7 %collective-permute-start.32 = (bf16[256,1024]{1,0:T(8,128)(2,1)}, bf16[256,1024]{1,0:T(8,128)(2,1)}, u32[]{:S(2)}, u32[]{:S(2)}) collective-permute-start(bf16[256,1024]{1,0:T(8,128)(2,1)} %block_dot.23), channel_id=1, source_target_pairs={{8,1},{9,0},{10,3},{11,2},{12,5},{13,4},{14,7},{15,6}} | collective-permute-start | bytes 1572872 | tf_op jit(solution)/shard_map/ppermute | solution.py:282
  173.1 26.8 %collective-permute-start.31 = (bf16[256,1024]{1,0:T(8,128)(2,1)}, bf16[256,1024]{1,0:T(8,128)(2,1)}, u32[]{:S(2)}, u32[]{:S(2)}) collective-permute-start(bf16[256,1024]{1,0:T(8,128)(2,1)} %block_dot.23), channel_id=1, source_target_pairs={{8,0},{9,1},{10,2},{11,3},{12,4},{13,5},{14,6},{15,7}} | collective-permute-start | bytes 1572872 | tf_op jit(solution)/shard_map/ppermute | solution.py:282
  175.3 25.3 %collective-permute-start.44 = (bf16[256,512]{1,0:T(8,128)(2,1)}, bf16[256,512]{1,0:T(8,128)(2,1)}, u32[]{:S(2)}, u32[]{:S(2)}) collective-permute-start(bf16[256,512]{1,0:T(8,128)(2,1)} %add_convert_fusion), channel_id=1, source_target_pairs={{24,28},{25,29},{26,30},{27,31},{28,24},{29,25},{30,26},{31,27},{1... | collective-permute-start | bytes 786440 | tf_op jit(solution)/shard_map/ppermute | solution.py:282
  176.7 38.1 %collective-permute-start.35 = (bf16[256,1024]{1,0:T(8,128)(2,1)}, bf16[256,1024]{1,0:T(8,128)(2,1)S(1)}, u32[]{:S(2)}, u32[]{:S(2)}) collective-permute-start(bf16[256,1024]{1,0:T(8,128)(2,1)} %block_dot.23), channel_id=1, source_target_pairs={{8,4},{9,5},{10,6},{11,7},{12,0},{13,1},{14,2},{15,3}} | collective-permute-start | bytes 1572872 | tf_op jit(solution)/shard_map/ppermute | solution.py:282
  199.9 16.8 %collective-permute-start.43 = (bf16[256,512]{1,0:T(8,128)(2,1)}, bf16[256,512]{1,0:T(8,128)(2,1)S(1)}, u32[]{:S(2)}, u32[]{:S(2)}) collective-permute-start(bf16[256,512]{1,0:T(8,128)(2,1)} %add_convert_fusion), channel_id=1, source_target_pairs={{24,26},{25,27},{26,24},{27,25},{28,30},{29,31},{30,28},{31,29},{1... | collective-permute-start | bytes 786440 | tf_op jit(solution)/shard_map/ppermute | solution.py:282
  200.6 16.1 %collective-permute-start.45 = (bf16[256,512]{1,0:T(8,128)(2,1)}, bf16[256,512]{1,0:T(8,128)(2,1)S(1)}, u32[]{:S(2)}, u32[]{:S(2)}) collective-permute-start(bf16[256,512]{1,0:T(8,128)(2,1)} %collective-permute-done.44), channel_id=1, source_target_pairs={{24,26},{25,27},{26,24},{27,25},{28,30},{29,31},{30,28},{31,29},{1... | collective-permute-start | bytes 786440 | tf_op jit(solution)/shard_map/ppermute | solution.py:282
  206.9 15.9 %collective-permute-start.34 = (bf16[256,1024]{1,0:T(8,128)(2,1)}, bf16[256,1024]{1,0:T(8,128)(2,1)S(1)}, u32[]{:S(2)}, u32[]{:S(2)}) collective-permute-start(bf16[256,1024]{1,0:T(8,128)(2,1)} %collective-permute-done.33.refs_0_), channel_id=1, source_target_pairs={{0,1},{1,0},{2,3},{3,2},{4,5},{5,4},{6,7},{7,6}} | collective-permute-start | bytes 1572872 | tf_op jit(solution)/shard_map/ppermute | solution.py:282
  217.8 22.0 %collective-permute-start.46 = (bf16[4,256,512]{2,1,0:T(8,128)(2,1)S(1)}, bf16[4,256,512]{2,1,0:T(8,128)(2,1)}, u32[]{:S(2)}, u32[]{:S(2)}) collective-permute-start(bf16[4,256,512]{2,1,0:T(8,128)(2,1)S(1)} %pad_maximum_fusion.1.refs_2_), channel_id=1, source_target_pairs={{24,25},{25,24},{26,27},{27,26},{28,29},{29,28},{30,31},{31,30},{1... | collective-permute-start | bytes 3145736 | tf_op jit(solution)/shard_map/ppermute | solution.py:282
  (51 other events, 351.1 us)

commit v6 on v5

v6 whole, which is shorter than its diff:
```python
import jax
import jax.numpy as jnp
from jax import lax
from jax.experimental import pallas as pl
from jax.experimental.pallas import tpu as pltpu
from jax.sharding import PartitionSpec as P

DOT_VMEM = 24 * 1024 * 1024
VMEM = pl.BlockSpec(memory_space=pltpu.VMEM)
SMEM = pl.BlockSpec(memory_space=pltpu.SMEM)
HBM = pl.BlockSpec(memory_space=pltpu.HBM)


def scalars(*values):
    return jnp.stack([jnp.asarray(v).astype(jnp.int32) for v in values])


def params():
    return pltpu.CompilerParams(vmem_limit_bytes=DOT_VMEM)


def cost(flops, moved):
    return pl.CostEstimate(flops=flops, bytes_accessed=moved, transcendentals=0)


def in_hbm(array):
    return pltpu.with_memory_space_constraint(array, pltpu.HBM)


def run_of(ref, axis, at, length):
    part = pl.ds(pl.multiple_of(at * length, length), length)
    return ref.at[part, :] if axis == 0 else ref.at[:, part]


def stream_dot(active, blocks, matrices, picks, bases, out_types):
    rows, depth = blocks[0].shape
    count, kinds = len(blocks), len(matrices)
    shapes = [m.shape[1] for m in matrices]
    given = [base for base in bases if base is not None]

    def body(at, *refs):
        refs = list(refs)

        def take(n):
            taken, refs[:n] = refs[:n], []
            return taken

        matrix_refs, block_refs = take(kinds), take(count)
        base_refs = [None if base is None else take(1)[0] for base in bases]
        out_refs, run_refs, total_refs, (sems,) = take(kinds), take(kinds), take(kinds), refs

        def copy(k, m):
            return pltpu.make_async_copy(
                run_of(matrix_refs[m], 0, at[1 + k], depth), run_refs[m].at[k], sems.at[m, k]
            )

        @pl.when(at[0] == 1)
        def _():
            for k in range(count):
                for m in range(kinds):
                    copy(k, m).start()
            for k in range(count):
                for m in range(kinds):
                    copy(k, m).wait()
                    width = 256 if shapes[m] % 256 == 0 else shapes[m]

                    def tile(j, _):
                        here = pl.ds(pl.multiple_of(j * width, width), width)
                        total = jnp.dot(
                            block_refs[k][...],
                            run_refs[m][k, :, here],
                            preferred_element_type=jnp.float32,
                        )
                        if k:
                            total += total_refs[m][:, here]
                        elif base_refs[m] is not None:
                            total += base_refs[m][:, here].astype(jnp.float32)
                        if k < count - 1:
                            total_refs[m][:, here] = total
                        else:
                            out_refs[m][:, here] = total.astype(out_types[m])
                        return 0

                    lax.fori_loop(0, shapes[m] // width, tile, 0)

    return pl.pallas_call(
        body,
        in_specs=[SMEM] + [HBM] * kinds + [VMEM] * (count + len(given)),
        out_specs=[VMEM] * kinds,
        out_shape=[jax.ShapeDtypeStruct((rows, n), t) for n, t in zip(shapes, out_types)],
        scratch_shapes=[pltpu.VMEM((count, depth, n), m.dtype) for n, m in zip(shapes, matrices)]
        + [pltpu.VMEM((rows, n), jnp.float32) for n in shapes]
        + [pltpu.SemaphoreType.DMA((kinds, count))],
        compiler_params=params(),
        cost_estimate=cost(
            2 * count * rows * depth * sum(shapes), 2 * count * depth * sum(shapes)
        ),
        name="stream_dot",
    )(scalars(active, *picks), *[in_hbm(m) for m in matrices], *blocks, *given)


def partials(active, inputs, weights, picks, inner):
    rows, depth = inputs.shape
    count = len(picks)
    width = weights.shape[1] // count

    def body(at, weights_ref, inputs_ref, *refs):
        out_refs, (runs, sems) = refs[:inner], refs[inner:]
        order = [n for dx in [*range(1, inner), 0] for n in range(dx, count, inner)]

        def copy(n):
            return pltpu.make_async_copy(
                run_of(weights_ref, 1, at[1 + n], width), runs.at[n], sems.at[n]
            )

        @pl.when(at[0] == 1)
        def _():
            for n in order:
                copy(n).start()
            for n in order:
                copy(n).wait()
                total = jnp.dot(inputs_ref[...], runs[n], preferred_element_type=jnp.float32)
                out_ref = out_refs[n % inner]
                out_ref[n // inner] = total.astype(out_ref.dtype)

    return pl.pallas_call(
        body,
        in_specs=[SMEM, HBM, VMEM],
        out_specs=[VMEM] * inner,
        out_shape=[
            jax.ShapeDtypeStruct((count // inner, rows, width), jnp.bfloat16 if dx else jnp.float32)
            for dx in range(inner)
        ],
        scratch_shapes=[
            pltpu.VMEM((count, depth, width), weights.dtype),
            pltpu.SemaphoreType.DMA((count,)),
        ],
        compiler_params=params(),
        cost_estimate=cost(2 * rows * weights.size, 2 * weights.size),
        name="partials",
    )(scalars(active, *picks), in_hbm(weights), inputs)


def added(active, own, arrived):
    count, rows, width = own.shape

    def body(active_ref, own_ref, *refs):
        arrived_refs, out_refs = refs[: len(arrived)], refs[len(arrived) :]

        @pl.when(active_ref[0] == 1)
        def _():
            for n in range(count):
                total = own_ref[n]
                for ref in arrived_refs:
                    total = total + ref[n].astype(jnp.float32)
                out_refs[n][...] = total.astype(out_refs[n].dtype)

    return pl.pallas_call(
        body,
        in_specs=[SMEM] + [VMEM] * (1 + len(arrived)),
        out_specs=[VMEM] * count,
        out_shape=[
            jax.ShapeDtypeStruct((rows, width), jnp.bfloat16 if n else jnp.float32)
            for n in range(count)
        ],
        compiler_params=params(),
        cost_estimate=cost(own.size, 8 * own.size),
        name="added",
    )(scalars(active), own, *arrived)


def mean_square(section, half, rot_outs, low, high, picks, micro, seq):
    _, rows, width = low[0].shape
    eig_rows = rot_outs[0].shape[1]
    count, inner, sections = len(picks), len(low), len(rot_outs)

    def body(at, *refs):
        rot_refs, refs = refs[:sections], refs[sections:]
        low_refs, high_refs = refs[:inner], refs[inner : 2 * inner]
        eig_ref, rot, block, result, sems = refs[2 * inner :]
        for s in range(sections):

            @pl.when(at[0] == s)
            def _():
                rot[...] = rot_refs[s][...]

        def copy(n):
            return pltpu.make_async_copy(
                result.at[n % 2], run_of(eig_ref, 1, at[1 + n], width), sems.at[n % 2]
            )

        for n in range(count):

            @pl.when(at[0] >= half)
            def _():
                block[...] = high_refs[n % inner][n // inner]

            @pl.when(at[0] < half)
            def _():
                block[...] = low_refs[n % inner][n // inner]

            if n >= 2:
                copy(n - 2).wait()
            for m in range(micro):
                rows_of = slice(m * seq, (m + 1) * seq)
                product = lax.dot_general(
                    rot[rows_of, :],
                    block[rows_of, :],
                    (((0,), (0,)), ((), ())),
                    preferred_element_type=jnp.float32,
                )
                square = product * product
                result[n % 2] = square if m == 0 else result[n % 2] + square
            result[n % 2] = result[n % 2] * (1.0 / (seq * micro))
            copy(n).start()
        for n in range(max(0, count - 2), count):
            copy(n).wait()

    return pl.pallas_call(
        body,
        in_specs=[SMEM] + [VMEM] * (sections + 2 * inner),
        out_specs=HBM,
        out_shape=jax.ShapeDtypeStruct((eig_rows, count * width), jnp.float32),
        scratch_shapes=[
            pltpu.VMEM((rows, eig_rows), rot_outs[0].dtype),
            pltpu.VMEM((rows, width), rot_outs[0].dtype),
            pltpu.VMEM((2, eig_rows, width), jnp.float32),
            pltpu.SemaphoreType.DMA((2,)),
        ],
        compiler_params=params(),
        cost_estimate=cost(16 * rows * eig_rows * count * width, 4 * eig_rows * count * width),
        name="mean_square",
    )(scalars(section, *picks), *rot_outs, *low, *high)


def per_device(activations, top_grad, projection, basis_out, basis_in):
    sections = lax.axis_size("section")
    shards = lax.axis_size("shard")
    section, shard = lax.axis_index("section"), lax.axis_index("shard")
    micro, seq, feat_loc = top_grad.shape
    rows = micro * seq
    inputs = activations[0].reshape(rows, feat_loc)
    top = top_grad.reshape(rows, feat_loc)
    weights, out_cols = projection[0], basis_out[0]
    half = sections // 2

    inner = 1
    while 2 * (2 * inner) ** 2 <= shards:
        inner *= 2
    outer = shards // inner
    picks = [shard ^ part for part in range(shards)]

    def moved(block, flip, pairs):
        route = [(a * shards + i, b * shards + (i ^ flip)) for a, b in pairs for i in range(shards)]
        return lax.ppermute(block, ("section", "shard"), route)

    def spread(block, pairs):
        powers = [1 << p for p in range(outer.bit_length() - 1)]
        near = {dz: moved(block, dz * inner, pairs) for dz in reversed(powers)}
        return near, {dx: moved(block, dx, pairs) for dx in range(1, inner)}

    def along_outer(near, pairs):
        got = dict(near)
        for dz in range(outer):
            low = dz & -dz
            if dz not in got:
                got[dz] = moved(got[dz ^ low], low * inner, pairs)
        return got

    def handed_down(grad, turn):
        own = moved(grad, 0, [(turn + 1, turn)])
        if turn % 2 == 0:
            near, side = spread(grad, [(turn + 1, turn)])
        else:
            near, side = spread(own, [(turn, turn)])
        return {0: own, **near}, side

    def relay(turn, sent, first=None):
        mine = section == turn
        near, side = sent
        got = along_outer(near, [(turn, turn)])
        matrices = [out_cols] if turn == 0 else [weights, out_cols]
        bases = [None] if turn == 0 else [near[0], None]

        def products(dots, bases, last):
            return stream_dot(
                mine,
                [block for block, _ in dots],
                matrices,
                [picks[part] for _, part in dots],
                bases,
                [jnp.bfloat16 if last else jnp.float32] * len(matrices),
            )

        blocks = {(0, 0): near[0], **{(0, dx): block for dx, block in side.items()}}
        if first is not None:
            blocks[0, 0], first = lax.optimization_barrier((near[0], first))
        dots = [(block, dx) for (_, dx), block in blocks.items()]
        totals = [products(dots, bases, outer == 1)]
        for dz in range(1, outer + 1):
            if dz < outer:
                block, _ = lax.optimization_barrier((got[dz], totals[max(0, dz - 2)][0]))
                blocks[dz, 0] = got[dz]
                for dx in range(1, inner):
                    blocks[dz, dx] = moved(block, dx, [(turn, turn)])
            if dz > 1:
                dots = [(blocks[dz - 1, dx], (dz - 1) * inner + dx) for dx in range(inner)]
                if dz == outer - 1:
                    dots.append((blocks[dz, 0], dz * inner))
                if dz == outer and outer > 2 and inner > 1:
                    dots = dots[1:]
                totals.append(products(dots, totals[-1], dz == outer))
        return totals[-1]

    def rotate_begin(inputs, among):
        pairs = [(a, a) for a in among]
        own, *others = partials(in_turn(among), inputs, basis_in[0], picks, inner)
        return own, others, [moved(other, 1 + n, pairs) for n, other in enumerate(others)]

    def rotate_end(own, arrived, among):
        pairs = [(a, a) for a in among]
        own, *sums = added(in_turn(among), own, arrived)
        for dz, part in enumerate(sums, 1):
            own = own + moved(part, dz * inner, pairs).astype(jnp.float32)
        own = own.astype(jnp.bfloat16)
        powers = [1 << p for p in range(outer.bit_length() - 1)]
        near = {0: own, **{dz: moved(own, dz * inner, pairs) for dz in reversed(powers)}}
        got = along_outer(near, pairs)
        return jnp.stack([got[dz] for dz in range(outer)])

    def in_turn(among):
        return (section >= min(among)) & (section <= max(among))

    def all_columns(column, among):
        return [column] + [moved(column, dx, [(a, a) for a in among]) for dx in range(1, inner)]

    upper = list(range(sections - 1, half - 1, -1))
    lower = list(range(half - 1, -1, -1))
    rot_outs = [None] * sections

    low_own, low_others, low_arrived = rotate_begin(inputs, lower)
    near, side = spread(top, [(upper[0], upper[0])])
    sent = {0: top, **near}, side
    for turn in upper:
        grad, rot_outs[turn] = relay(turn, sent, low_others if turn == upper[0] else None)
        if turn != upper[-1]:
            sent = handed_down(grad, turn - 1)
    low = rotate_end(low_own, low_arrived, lower)
    grad, low = lax.optimization_barrier((grad, low))
    sent = handed_down(grad, lower[0])
    low = all_columns(low, lower)
    inputs, _ = lax.optimization_barrier((inputs, sent[0][0]))
    high_own, _, high_arrived = rotate_begin(inputs, upper)
    for turn in lower:
        *grad, rot_outs[turn] = relay(turn, sent)
        if turn != 0:
            sent = handed_down(grad[0], turn - 1)
    high = all_columns(rotate_end(high_own, high_arrived, upper), upper)
    return mean_square(section, half, rot_outs, low, high, picks, micro, seq)[None]


def solution(mesh):
    return jax.shard_map(
        per_device,
        mesh=mesh,
        in_specs=(
            P("section", None, None, "shard"),
            P(None, None, "shard"),
            P("section", None, "shard"),
            P("section", None, "shard"),
            P("section", "shard", None),
        ),
        out_specs=P("section", "shard", None),
        check_vma=False,
    )
```

time: 255 us -> 247 us (0.969)
  local copies, waits for them, and re-layouts: 38 us -> 2.72 us
  waiting for transfers between devices: 83.8 us -> 118 us
  Pallas kernels: 53.7 us -> 46 us
    unnamed x72 -> x14, local copies, waits for them, and re-layouts: 37.3 us -> 2.47 us
    ppermute x47, waiting for transfers between devices: 83.8 us -> 118 us  [moved(): return lax.ppermute(block, ('section', 'shard'), route)]
    pallas_call x21 -> x17, Pallas kernels: 42.5 us -> 37.4 us  [the longest x16 24.2 us: stream_dot(): pl.pallas_call(body, in_specs=[SMEM] + [HBM] * kinds + [VMEM] * (count +...]
  transfers between devices with their start and end apart: 47 -> 47, of which waited for: 10 -> 8; matrix products, arithmetic and copies ran while one was open for 2% -> 2% of each run, Pallas kernels for 15% -> 13%
where the time goes in v6:
time: 247 us; the launch traced here: 245 us
  waiting for transfers between devices  118 us (48%)
  starting transfers between devices  73.7 us (30%)
  Pallas kernels  46 us (19%)
  other arithmetic  3.66 us (1%)
  local copies, waits for them, and re-layouts  2.72 us (1%)
    ppermute x47, waiting for transfers between devices, moved(): return lax.ppermute(block, ('section', 'shard'), route)  118 us
    ppermute x47, starting transfers between devices, moved(): return lax.ppermute(block, ('section', 'shard'), route)  73.7 us
    pallas_call x16, Pallas kernels, stream_dot(): pl.pallas_call(body, in_specs=[SMEM] + [HBM] * kinds + [VMEM] * (count +...  24.2 us
    pallas_call x1, Pallas kernels, mean_square(): pl.pallas_call(body, in_specs=[SMEM] + [VMEM] * (sections + 2 * inner), o...  13.2 us
    pallas_call x2, Pallas kernels, partials(): pl.pallas_call(body, in_specs=[SMEM, HBM, VMEM], out_specs=[VMEM] * inner...  7.14 us
  transfers between devices with their start and end apart: 47, of which 8 were waited for; matrix products, arithmetic and copies ran while one was open for 2% of the time, Pallas kernels for 13%

profile of v6, /device:TPU:0, one launch (start us, length us, event | category | flops | bytes accessed | tf_op | source)
XLA Modules:
  0.0 245.2 jit_solution(16873291439195416698)
XLA Ops:
  0.0 1.6 collective-permute-start.3
  2.3 1.5 collective-permute-start
  4.9 6.3 %partials.2 = (f32[4,256,512]{2,1,0:T(8,128)S(1)}, bf16[4,256,512]{2,1,0:T(8,128)(2,1)}) custom-call(s32[9]{0:T(128)S(1)} %stack.236.at, bf16[1024,4096]{1,0:T(8,128)(2,1)} %bitcast.64, bf16[256,1024]{1,0:T(8,128)(2,1)S(1)} %bitcast.34), custom_call_target="tpu_custom_call" | custom-call | flops 2147483648 | bytes 8388608 | tf_op jit(solution)/shard_map/partials/pallas_call | solution.py:126
  15.9 4.8 %collective-permute-start.15 = (bf16[4,256,512]{2,1,0:T(8,128)(2,1)}, bf16[4,256,512]{2,1,0:T(8,128)(2,1)}, u32[]{:S(2)}, u32[]{:S(2)}) collective-permute-start(bf16[4,256,512]{2,1,0:T(8,128)(2,1)} %get-tuple-element.57), channel_id=1, source_target_pairs={{8,9},{9,8},{10,11},{11,10},{12,13},{13,12},{14,15},{15,14},{0,1},... | collective-permute-start | bytes 3145736 | tf_op jit(solution)/shard_map/ppermute | solution.py:255
  23.4 1.5 collective-permute-start.11
  26.3 1.5 collective-permute-start.7
  27.8 16.5 %collective-permute-done.15.refs_0_ = bf16[4,256,512]{2,1,0:T(8,128)(2,1)} collective-permute-done((bf16[4,256,512]{2,1,0:T(8,128)(2,1)}, bf16[4,256,512]{2,1,0:T(8,128)(2,1)}, u32[]{:S(2)}, u32[]{:S(2)}) %collective-permute-start.15) | collective-permute-done | bytes 1048608 | tf_op jit(solution)/shard_map/ppermute | solution.py:255
  45.6 3.7 %collective-permute-start.16 = (bf16[256,512]{1,0:T(8,128)(2,1)S(1)}, bf16[256,512]{1,0:T(8,128)(2,1)S(1)}, u32[]{:S(2)}, u32[]{:S(2)}) collective-permute-start(bf16[256,512]{1,0:T(8,128)(2,1)S(1)} %get-tuple-element.81), channel_id=1, source_target_pairs={{8,10},{9,11},{10,8},{11,9},{12,14},{13,15},{14,12},{15,13},{0,2},... | collective-permute-start | bytes 786440 | tf_op jit(solution)/shard_map/ppermute | solution.py:255
  49.4 4.5 %collective-permute-start.17 = (bf16[256,512]{1,0:T(8,128)(2,1)S(1)}, bf16[256,512]{1,0:T(8,128)(2,1)S(1)}, u32[]{:S(2)}, u32[]{:S(2)}) collective-permute-start(bf16[256,512]{1,0:T(8,128)(2,1)S(1)} %get-tuple-element.82), channel_id=1, source_target_pairs={{8,12},{9,13},{10,14},{11,15},{12,8},{13,9},{14,10},{15,11},{0,4},... | collective-permute-start | bytes 786440 | tf_op jit(solution)/shard_map/ppermute | solution.py:255
  53.9 1.9 collective-permute-start.18
  58.5 13.8 %collective-permute-done.17 = bf16[256,512]{1,0:T(8,128)(2,1)S(1)} collective-permute-done((bf16[256,512]{1,0:T(8,128)(2,1)S(1)}, bf16[256,512]{1,0:T(8,128)(2,1)S(1)}, u32[]{:S(2)}, u32[]{:S(2)}) %collective-permute-start.17) | collective-permute-done | bytes 262176 | tf_op jit(solution)/shard_map/ppermute | solution.py:255
  72.4 7.2 %collective-permute-start.20 = (bf16[256,512]{1,0:T(8,128)(2,1)S(1)}, bf16[256,512]{1,0:T(8,128)(2,1)S(1)}, u32[]{:S(2)}, u32[]{:S(2)}) collective-permute-start(bf16[256,512]{1,0:T(8,128)(2,1)S(1)} %add_convert_fusion.1), channel_id=1, source_target_pairs={{8,12},{9,13},{10,14},{11,15},{12,8},{13,9},{14,10},{15,11},{0,4},... | collective-permute-start | bytes 786440 | tf_op jit(solution)/shard_map/ppermute | solution.py:255
  80.4 1.9 collective-permute-start.19
  82.3 7.9 %collective-permute-done.20 = bf16[256,512]{1,0:T(8,128)(2,1)S(1)} collective-permute-done((bf16[256,512]{1,0:T(8,128)(2,1)S(1)}, bf16[256,512]{1,0:T(8,128)(2,1)S(1)}, u32[]{:S(2)}, u32[]{:S(2)}) %collective-permute-start.20) | collective-permute-done | bytes 262176 | tf_op jit(solution)/shard_map/ppermute | solution.py:255
  90.2 1.9 collective-permute-start.21
  93.6 5.7 %collective-permute-done.21 = bf16[256,512]{1,0:T(8,128)(2,1)S(1)} collective-permute-done((bf16[256,512]{1,0:T(8,128)(2,1)S(1)}, bf16[256,512]{1,0:T(8,128)(2,1)S(1)}, u32[]{:S(2)}, u32[]{:S(2)}) %collective-permute-start.21) | collective-permute-done | bytes 262176 | tf_op jit(solution)/shard_map/ppermute | solution.py:255
  104.0 1.5 collective-permute-start.23
  124.7 54.7 %collective-permute-done.34.refs_2_ = bf16[256,1024]{1,0:T(8,128)(2,1)S(1)} collective-permute-done((bf16[256,1024]{1,0:T(8,128)(2,1)S(1)}, bf16[256,1024]{1,0:T(8,128)(2,1)S(1)}, u32[]{:S(2)}, u32[]{:S(2)}) %collective-permute-start.34) | collective-permute-done | bytes 524320 | tf_op jit(solution)/shard_map/ppermute | solution.py:255
  180.9 2.4 collective-permute-start.38
  183.3 3.0 %stream_dot.28.refs_3_ = f32[256,512]{1,0:T(8,128)S(1)} custom-call(s32[3]{0:T(128)S(1)} %add_add_fusion.10.at, bf16[8192,512]{1,0:T(8,128)(2,1)} %bitcast.60, bf16[256,1024]{1,0:T(8,128)(2,1)S(1)} %collective-permute-done.33.refs_1_, bf16[256,1024]{1,0:T(8,128)(2,1)S(1)} %collective-permute-done.34.refs_2_), custom_call_target="tpu_custom_call" | custom-call | flops 536870912 | bytes 2097152 | tf_op jit(solution)/shard_map/stream_dot/pallas_call | solution.py:86
  186.4 3.4 %collective-permute-start.35 = (bf16[256,1024]{1,0:T(8,128)(2,1)}, bf16[256,1024]{1,0:T(8,128)(2,1)S(1)}, u32[]{:S(2)}, u32[]{:S(2)}) collective-permute-start(bf16[256,1024]{1,0:T(8,128)(2,1)} %collective-permute-done.32.refs_1_), channel_id=1, source_target_pairs={{0,1},{1,0},{2,3},{3,2},{4,5},{5,4},{6,7},{7,6}} | collective-permute-start | bytes 1572872 | tf_op jit(solution)/shard_map/ppermute | solution.py:255
  189.8 1.7 collective-permute-done.30.refs_1_
  191.4 2.0 collective-permute-start.31
  194.8 1.7 collective-permute-start.46
  196.5 3.2 %collective-permute-start.37 = (bf16[256,1024]{1,0:T(8,128)(2,1)S(1)}, bf16[256,1024]{1,0:T(8,128)(2,1)}, u32[]{:S(2)}, u32[]{:S(2)}) collective-permute-start(bf16[256,1024]{1,0:T(8,128)(2,1)S(1)} %collective-permute-done.30.refs_1_), channel_id=1, source_target_pairs={{0,1},{1,0},{2,3},{3,2},{4,5},{5,4},{6,7},{7,6}} | collective-permute-start | bytes 1572872 | tf_op jit(solution)/shard_map/ppermute | solution.py:255
  199.8 14.1 %collective-permute-done.35.refs_2_ = bf16[256,1024]{1,0:T(8,128)(2,1)S(1)} collective-permute-done((bf16[256,1024]{1,0:T(8,128)(2,1)}, bf16[256,1024]{1,0:T(8,128)(2,1)S(1)}, u32[]{:S(2)}, u32[]{:S(2)}) %collective-permute-start.35) | collective-permute-done | bytes 524320 | tf_op jit(solution)/shard_map/ppermute | solution.py:255
  213.9 3.5 %stream_dot.29.refs_4_ = f32[256,512]{1,0:T(8,128)S(1)} custom-call(s32[3]{0:T(128)S(1)} %add_add_fusion.9.at, bf16[8192,512]{1,0:T(8,128)(2,1)} %bitcast.61, bf16[256,1024]{1,0:T(8,128)(2,1)} %collective-permute-done.32.refs_1_, bf16[256,1024]{1,0:T(8,128)(2,1)S(1)} %collective-permute-done.35.refs_2_, f32[256,512]{1,0:T(8,128)S(1)} %stream_dot.28.refs_3_), custom_call_target="tpu_custom_call" | custom-call | flops 536870912 | bytes 2097152 | tf_op jit(solution)/shard_map/stream_dot/pallas_call | solution.py:86
  217.4 3.0 %collective-permute-start.36 = (bf16[256,1024]{1,0:T(8,128)(2,1)}, bf16[256,1024]{1,0:T(8,128)(2,1)}, u32[]{:S(2)}, u32[]{:S(2)}) collective-permute-start(bf16[256,1024]{1,0:T(8,128)(2,1)} %collective-permute-done.31.refs_3_), channel_id=1, source_target_pairs={{0,1},{1,0},{2,3},{3,2},{4,5},{5,4},{6,7},{7,6}} | collective-permute-start | bytes 1572872 | tf_op jit(solution)/shard_map/ppermute | solution.py:255
  220.7 4.4 %stream_dot.30.refs_2_ = f32[256,512]{1,0:T(8,128)S(1)} custom-call(s32[4]{0:T(128)S(1)} %add_add_fusion.11.at, bf16[8192,512]{1,0:T(8,128)(2,1)} %bitcast.62, bf16[256,1024]{1,0:T(8,128)(2,1)S(1)} %collective-permute-done.30.refs_1_, bf16[256,1024]{1,0:T(8,128)(2,1)} %collective-permute-done.37.refs_2_, bf16[256,1024]{1,0:T(8,128)(2,1)} %collective-permute-done.31.refs_3_, ...), custom_call_target="tpu_custom_call" | custom-call | flops 805306368 | bytes 3145728 | tf_op jit(solution)/shard_map/stream_dot/pallas_call | solution.py:86
  225.0 3.8 %collective-permute-done.36.refs_1_ = bf16[256,1024]{1,0:T(8,128)(2,1)} collective-permute-done((bf16[256,1024]{1,0:T(8,128)(2,1)}, bf16[256,1024]{1,0:T(8,128)(2,1)}, u32[]{:S(2)}, u32[]{:S(2)}) %collective-permute-start.36) | collective-permute-done | bytes 524320 | tf_op jit(solution)/shard_map/ppermute | solution.py:255
  228.8 2.9 %stream_dot.31.refs_0_ = bf16[256,512]{1,0:T(8,128)(2,1)S(1)} custom-call(s32[2]{0:T(128)S(1)} %pad_add_fusion.at, bf16[8192,512]{1,0:T(8,128)(2,1)} %bitcast.63, bf16[256,1024]{1,0:T(8,128)(2,1)} %collective-permute-done.36.refs_1_, f32[256,512]{1,0:T(8,128)S(1)} %stream_dot.30.refs_2_), custom_call_target="tpu_custom_call" | custom-call | flops 268435456 | bytes 1048576 | tf_op jit(solution)/shard_map/stream_dot/pallas_call | solution.py:86
  231.8 13.2 %mean_square.1 = f32[512,4096]{1,0:T(8,128)} custom-call(s32[9]{0:T(128)S(1)} %stack.219.at, bf16[256,512]{1,0:T(8,128)(2,1)S(1)} %stream_dot.31.refs_0_, bf16[256,512]{1,0:T(8,128)(2,1)S(1)} %copy-done.6, bf16[256,512]{1,0:T(8,128)(2,1)S(1)} %copy-done.4, bf16[256,512]{1,0:T(8,128)(2,1)S(1)} %get-tuple-element.100.refs_3_, ...), custom_call_target="tpu_custom_call" | custom-call | flops 8589934592 | bytes 8388608 | tf_op jit(solution)/shard_map/mean_square/pallas_call | solution.py:219
  (120 shorter events, 43.5 us)
Async XLA Ops:
  0.0 11.3 %collective-permute-start.3 = (bf16[256,1024]{1,0:T(8,128)(2,1)}, bf16[256,1024]{1,0:T(8,128)(2,1)}, u32[]{:S(2)}, u32[]{:S(2)}) collective-permute-start(bf16[256,1024]{1,0:T(8,128)(2,1)} %bitcast.29), channel_id=1, source_target_pairs={{24,25},{25,24},{26,27},{27,26},{28,29},{29,28},{30,31},{31,30}} | collective-permute-start | bytes 1572872 | tf_op jit(solution)/shard_map/ppermute | solution.py:255
  1.6 10.8 %collective-permute-start.2 = (bf16[256,1024]{1,0:T(8,128)(2,1)}, bf16[256,1024]{1,0:T(8,128)(2,1)S(1)}, u32[]{:S(2)}, u32[]{:S(2)}) collective-permute-start(bf16[256,1024]{1,0:T(8,128)(2,1)} %bitcast.30), channel_id=1, source_target_pairs={{24,26},{25,27},{26,24},{27,25},{28,30},{29,31},{30,28},{31,29}} | collective-permute-start | bytes 1572872 | tf_op jit(solution)/shard_map/ppermute | solution.py:255
  2.3 10.8 %collective-permute-start = (bf16[256,1024]{1,0:T(8,128)(2,1)}, bf16[256,1024]{1,0:T(8,128)(2,1)}, u32[]{:S(2)}, u32[]{:S(2)}) collective-permute-start(bf16[256,1024]{1,0:T(8,128)(2,1)} %bitcast.31), channel_id=1, source_target_pairs={{24,28},{25,29},{26,30},{27,31},{28,24},{29,25},{30,26},{31,27}} | collective-permute-start | bytes 1572872 | tf_op jit(solution)/shard_map/ppermute | solution.py:255
  13.8 7.1 %collective-permute-start.6 = (bf16[256,1024]{1,0:T(8,128)(2,1)}, bf16[256,1024]{1,0:T(8,128)(2,1)S(1)}, u32[]{:S(2)}, u32[]{:S(2)}) collective-permute-start(bf16[256,1024]{1,0:T(8,128)(2,1)} %collective-permute-done.refs_2_), channel_id=1, source_target_pairs={{24,25},{25,24},{26,27},{27,26},{28,29},{29,28},{30,31},{31,30}} | collective-permute-start | bytes 1572872 | tf_op jit(solution)/shard_map/ppermute | solution.py:255
  15.9 28.3 %collective-permute-start.15 = (bf16[4,256,512]{2,1,0:T(8,128)(2,1)}, bf16[4,256,512]{2,1,0:T(8,128)(2,1)}, u32[]{:S(2)}, u32[]{:S(2)}) collective-permute-start(bf16[4,256,512]{2,1,0:T(8,128)(2,1)} %get-tuple-element.57), channel_id=1, source_target_pairs={{8,9},{9,8},{10,11},{11,10},{12,13},{13,12},{14,15},{15,14},{0,1},... | collective-permute-start | bytes 3145736 | tf_op jit(solution)/shard_map/ppermute | solution.py:255
  23.4 25.9 %collective-permute-start.11 = (bf16[256,1024]{1,0:T(8,128)(2,1)}, bf16[256,1024]{1,0:T(8,128)(2,1)}, u32[]{:S(2)}, u32[]{:S(2)}) collective-permute-start(bf16[256,1024]{1,0:T(8,128)(2,1)} %get-tuple-element.68), channel_id=1, source_target_pairs={{24,17},{25,16},{26,19},{27,18},{28,21},{29,20},{30,23},{31,22}} | collective-permute-start | bytes 1572872 | tf_op jit(solution)/shard_map/ppermute | solution.py:255
  24.9 29.0 %collective-permute-start.10 = (bf16[256,1024]{1,0:T(8,128)(2,1)}, bf16[256,1024]{1,0:T(8,128)(2,1)S(1)}, u32[]{:S(2)}, u32[]{:S(2)}) collective-permute-start(bf16[256,1024]{1,0:T(8,128)(2,1)} %get-tuple-element.68), channel_id=1, source_target_pairs={{24,16},{25,17},{26,18},{27,19},{28,20},{29,21},{30,22},{31,23}} | collective-permute-start | bytes 1572872 | tf_op jit(solution)/shard_map/ppermute | solution.py:255
  25.6 31.4 %collective-permute-start.9 = (bf16[256,1024]{1,0:T(8,128)(2,1)}, bf16[256,1024]{1,0:T(8,128)(2,1)S(1)}, u32[]{:S(2)}, u32[]{:S(2)}) collective-permute-start(bf16[256,1024]{1,0:T(8,128)(2,1)} %get-tuple-element.68), channel_id=1, source_target_pairs={{24,18},{25,19},{26,16},{27,17},{28,22},{29,23},{30,20},{31,21}} | collective-permute-start | bytes 1572872 | tf_op jit(solution)/shard_map/ppermute | solution.py:255
  26.3 31.4 %collective-permute-start.7 = (bf16[256,1024]{1,0:T(8,128)(2,1)}, bf16[256,1024]{1,0:T(8,128)(2,1)}, u32[]{:S(2)}, u32[]{:S(2)}) collective-permute-start(bf16[256,1024]{1,0:T(8,128)(2,1)} %get-tuple-element.68), channel_id=1, source_target_pairs={{24,20},{25,21},{26,22},{27,23},{28,16},{29,17},{30,18},{31,19}} | collective-permute-start | bytes 1572872 | tf_op jit(solution)/shard_map/ppermute | solution.py:255
  45.6 12.8 %collective-permute-start.16 = (bf16[256,512]{1,0:T(8,128)(2,1)S(1)}, bf16[256,512]{1,0:T(8,128)(2,1)S(1)}, u32[]{:S(2)}, u32[]{:S(2)}) collective-permute-start(bf16[256,512]{1,0:T(8,128)(2,1)S(1)} %get-tuple-element.81), channel_id=1, source_target_pairs={{8,10},{9,11},{10,8},{11,9},{12,14},{13,15},{14,12},{15,13},{0,2},... | collective-permute-start | bytes 786440 | tf_op jit(solution)/shard_map/ppermute | solution.py:255
  49.4 22.9 %collective-permute-start.17 = (bf16[256,512]{1,0:T(8,128)(2,1)S(1)}, bf16[256,512]{1,0:T(8,128)(2,1)S(1)}, u32[]{:S(2)}, u32[]{:S(2)}) collective-permute-start(bf16[256,512]{1,0:T(8,128)(2,1)S(1)} %get-tuple-element.82), channel_id=1, source_target_pairs={{8,12},{9,13},{10,14},{11,15},{12,8},{13,9},{14,10},{15,11},{0,4},... | collective-permute-start | bytes 786440 | tf_op jit(solution)/shard_map/ppermute | solution.py:255
  53.9 18.3 %collective-permute-start.18 = (bf16[256,512]{1,0:T(8,128)(2,1)S(1)}, bf16[256,512]{1,0:T(8,128)(2,1)S(1)}, u32[]{:S(2)}, u32[]{:S(2)}) collective-permute-start(bf16[256,512]{1,0:T(8,128)(2,1)S(1)} %get-tuple-element.83), channel_id=1, source_target_pairs={{8,14},{9,15},{10,12},{11,13},{12,10},{13,11},{14,8},{15,9},{0,6},... | collective-permute-start | bytes 786440 | tf_op jit(solution)/shard_map/ppermute | solution.py:255
  57.0 35.1 %collective-permute-start.12 = (bf16[256,1024]{1,0:T(8,128)(2,1)S(1)}, bf16[256,1024]{1,0:T(8,128)(2,1)S(1)}, u32[]{:S(2)}, u32[]{:S(2)}) collective-permute-start(bf16[256,1024]{1,0:T(8,128)(2,1)S(1)} %collective-permute-done.9.refs_2_), channel_id=1, source_target_pairs={{16,17},{17,16},{18,19},{19,18},{20,21},{21,20},{22,23},{23,22}} | collective-permute-start | bytes 1572872 | tf_op jit(solution)/shard_map/ppermute | solution.py:255
  57.7 35.0 %collective-permute-start.8 = (bf16[256,1024]{1,0:T(8,128)(2,1)}, bf16[256,1024]{1,0:T(8,128)(2,1)S(1)}, u32[]{:S(2)}, u32[]{:S(2)}) collective-permute-start(bf16[256,1024]{1,0:T(8,128)(2,1)} %collective-permute-done.7.refs_2_), channel_id=1, source_target_pairs={{16,18},{17,19},{18,16},{19,17},{20,22},{21,23},{22,20},{23,21}} | collective-permute-start | bytes 1572872 | tf_op jit(solution)/shard_map/ppermute | solution.py:255
  72.4 17.8 %collective-permute-start.20 = (bf16[256,512]{1,0:T(8,128)(2,1)S(1)}, bf16[256,512]{1,0:T(8,128)(2,1)S(1)}, u32[]{:S(2)}, u32[]{:S(2)}) collective-permute-start(bf16[256,512]{1,0:T(8,128)(2,1)S(1)} %add_convert_fusion.1), channel_id=1, source_target_pairs={{8,12},{9,13},{10,14},{11,15},{12,8},{13,9},{14,10},{15,11},{0,4},... | collective-permute-start | bytes 786440 | tf_op jit(solution)/shard_map/ppermute | solution.py:255
  79.6 19.8 %collective-permute-start.14 = (bf16[256,1024]{1,0:T(8,128)(2,1)}, bf16[256,1024]{1,0:T(8,128)(2,1)S(1)}, u32[]{:S(2)}, u32[]{:S(2)}) collective-permute-start(bf16[256,1024]{1,0:T(8,128)(2,1)} %collective-permute-done.7.refs_2_), channel_id=1, source_target_pairs={{16,17},{17,16},{18,19},{19,18},{20,21},{21,20},{22,23},{23,22}} | collective-permute-start | bytes 1572872 | tf_op jit(solution)/shard_map/ppermute | solution.py:255
  80.4 13.2 %collective-permute-start.19 = (bf16[256,512]{1,0:T(8,128)(2,1)S(1)}, bf16[256,512]{1,0:T(8,128)(2,1)S(1)}, u32[]{:S(2)}, u32[]{:S(2)}) collective-permute-start(bf16[256,512]{1,0:T(8,128)(2,1)S(1)} %add_convert_fusion.1), channel_id=1, source_target_pairs={{8,10},{9,11},{10,8},{11,9},{12,14},{13,15},{14,12},{15,13},{0,2},... | collective-permute-start | bytes 786440 | tf_op jit(solution)/shard_map/ppermute | solution.py:255
  90.2 9.1 %collective-permute-start.21 = (bf16[256,512]{1,0:T(8,128)(2,1)S(1)}, bf16[256,512]{1,0:T(8,128)(2,1)S(1)}, u32[]{:S(2)}, u32[]{:S(2)}) collective-permute-start(bf16[256,512]{1,0:T(8,128)(2,1)S(1)} %collective-permute-done.20), channel_id=1, source_target_pairs={{8,10},{9,11},{10,8},{11,9},{12,14},{13,15},{14,12},{15,13},{0,2},... | collective-permute-start | bytes 786440 | tf_op jit(solution)/shard_map/ppermute | solution.py:255
  92.7 7.8 %collective-permute-start.13 = (bf16[256,1024]{1,0:T(8,128)(2,1)S(1)}, bf16[256,1024]{1,0:T(8,128)(2,1)S(1)}, u32[]{:S(2)}, u32[]{:S(2)}) collective-permute-start(bf16[256,1024]{1,0:T(8,128)(2,1)S(1)} %collective-permute-done.8.refs_4_), channel_id=1, source_target_pairs={{16,17},{17,16},{18,19},{19,18},{20,21},{21,20},{22,23},{23,22}} | collective-permute-start | bytes 1572872 | tf_op jit(solution)/shard_map/ppermute | solution.py:255
  112.1 7.7 %collective-permute-start.41 = (bf16[256,512]{1,0:T(8,128)(2,1)S(1)}, bf16[256,512]{1,0:T(8,128)(2,1)S(1)}, u32[]{:S(2)}, u32[]{:S(2)}) collective-permute-start(bf16[256,512]{1,0:T(8,128)(2,1)S(1)} %get-tuple-element.107), channel_id=1, source_target_pairs={{24,28},{25,29},{26,30},{27,31},{28,24},{29,25},{30,26},{31,27},{1... | collective-permute-start | bytes 786440 | tf_op jit(solution)/shard_map/ppermute | solution.py:255
  115.9 63.5 %collective-permute-start.34 = (bf16[256,1024]{1,0:T(8,128)(2,1)S(1)}, bf16[256,1024]{1,0:T(8,128)(2,1)S(1)}, u32[]{:S(2)}, u32[]{:S(2)}) collective-permute-start(bf16[256,1024]{1,0:T(8,128)(2,1)S(1)} %get-tuple-element.94), channel_id=1, source_target_pairs={{8,1},{9,0},{10,3},{11,2},{12,5},{13,4},{14,7},{15,6}} | collective-permute-start | bytes 1572872 | tf_op jit(solution)/shard_map/ppermute | solution.py:255
  117.2 63.7 %collective-permute-start.33 = (bf16[256,1024]{1,0:T(8,128)(2,1)S(1)}, bf16[256,1024]{1,0:T(8,128)(2,1)S(1)}, u32[]{:S(2)}, u32[]{:S(2)}) collective-permute-start(bf16[256,1024]{1,0:T(8,128)(2,1)S(1)} %get-tuple-element.94), channel_id=1, source_target_pairs={{8,0},{9,1},{10,2},{11,3},{12,4},{13,5},{14,6},{15,7}} | collective-permute-start | bytes 1572872 | tf_op jit(solution)/shard_map/ppermute | solution.py:255
  118.5 67.8 %collective-permute-start.32 = (bf16[256,1024]{1,0:T(8,128)(2,1)S(1)}, bf16[256,1024]{1,0:T(8,128)(2,1)}, u32[]{:S(2)}, u32[]{:S(2)}) collective-permute-start(bf16[256,1024]{1,0:T(8,128)(2,1)S(1)} %get-tuple-element.94), channel_id=1, source_target_pairs={{8,2},{9,3},{10,0},{11,1},{12,6},{13,7},{14,4},{15,5}} | collective-permute-start | bytes 1572872 | tf_op jit(solution)/shard_map/ppermute | solution.py:255
  120.7 70.8 %collective-permute-start.30 = (bf16[256,1024]{1,0:T(8,128)(2,1)S(1)}, bf16[256,1024]{1,0:T(8,128)(2,1)S(1)}, u32[]{:S(2)}, u32[]{:S(2)}) collective-permute-start(bf16[256,1024]{1,0:T(8,128)(2,1)S(1)} %get-tuple-element.94), channel_id=1, source_target_pairs={{8,4},{9,5},{10,6},{11,7},{12,0},{13,1},{14,2},{15,3}} | collective-permute-start | bytes 1572872 | tf_op jit(solution)/shard_map/ppermute | solution.py:255
  123.4 70.1 %collective-permute-start.43 = (bf16[256,512]{1,0:T(8,128)(2,1)}, bf16[256,512]{1,0:T(8,128)(2,1)}, u32[]{:S(2)}, u32[]{:S(2)}) collective-permute-start(bf16[256,512]{1,0:T(8,128)(2,1)} %add_convert_fusion), channel_id=1, source_target_pairs={{24,26},{25,27},{26,24},{27,25},{28,30},{29,31},{30,28},{31,29},{1... | collective-permute-start | bytes 786440 | tf_op jit(solution)/shard_map/ppermute | solution.py:255
  179.4 14.0 %collective-permute-start.45 = (bf16[256,512]{1,0:T(8,128)(2,1)}, bf16[256,512]{1,0:T(8,128)(2,1)}, u32[]{:S(2)}, u32[]{:S(2)}) collective-permute-start(bf16[256,512]{1,0:T(8,128)(2,1)} %collective-permute-done.44), channel_id=1, source_target_pairs={{24,26},{25,27},{26,24},{27,25},{28,30},{29,31},{30,28},{31,29},{1... | collective-permute-start | bytes 786440 | tf_op jit(solution)/shard_map/ppermute | solution.py:255
  180.9 50.9 %collective-permute-start.38 = (bf16[4,256,512]{2,1,0:T(8,128)(2,1)S(1)}, bf16[4,256,512]{2,1,0:T(8,128)(2,1)}, u32[]{:S(2)}, u32[]{:S(2)}) collective-permute-start(bf16[4,256,512]{2,1,0:T(8,128)(2,1)S(1)} %pad_maximum_fusion.refs_4_), channel_id=1, source_target_pairs={{8,9},{9,8},{10,11},{11,10},{12,13},{13,12},{14,15},{15,14},{0,1},... | collective-permute-start | bytes 3145736 | tf_op jit(solution)/shard_map/ppermute | solution.py:255
  186.4 27.5 %collective-permute-start.35 = (bf16[256,1024]{1,0:T(8,128)(2,1)}, bf16[256,1024]{1,0:T(8,128)(2,1)S(1)}, u32[]{:S(2)}, u32[]{:S(2)}) collective-permute-start(bf16[256,1024]{1,0:T(8,128)(2,1)} %collective-permute-done.32.refs_1_), channel_id=1, source_target_pairs={{0,1},{1,0},{2,3},{3,2},{4,5},{5,4},{6,7},{7,6}} | collective-permute-start | bytes 1572872 | tf_op jit(solution)/shard_map/ppermute | solution.py:255
  191.4 26.0 %collective-permute-start.31 = (bf16[256,1024]{1,0:T(8,128)(2,1)S(1)}, bf16[256,1024]{1,0:T(8,128)(2,1)}, u32[]{:S(2)}, u32[]{:S(2)}) collective-permute-start(bf16[256,1024]{1,0:T(8,128)(2,1)S(1)} %collective-permute-done.30.refs_1_), channel_id=1, source_target_pairs={{0,2},{1,3},{2,0},{3,1},{4,6},{5,7},{6,4},{7,5}} | collective-permute-start | bytes 1572872 | tf_op jit(solution)/shard_map/ppermute | solution.py:255
  194.8 37.0 %collective-permute-start.46 = (bf16[4,256,512]{2,1,0:T(8,128)(2,1)S(1)}, bf16[4,256,512]{2,1,0:T(8,128)(2,1)}, u32[]{:S(2)}, u32[]{:S(2)}) collective-permute-start(bf16[4,256,512]{2,1,0:T(8,128)(2,1)S(1)} %pad_maximum_fusion.1.refs_6_), channel_id=1, source_target_pairs={{24,25},{25,24},{26,27},{27,26},{28,29},{29,28},{30,31},{31,30},{1... | collective-permute-start | bytes 3145736 | tf_op jit(solution)/shard_map/ppermute | solution.py:255
  196.5 24.2 %collective-permute-start.37 = (bf16[256,1024]{1,0:T(8,128)(2,1)S(1)}, bf16[256,1024]{1,0:T(8,128)(2,1)}, u32[]{:S(2)}, u32[]{:S(2)}) collective-permute-start(bf16[256,1024]{1,0:T(8,128)(2,1)S(1)} %collective-permute-done.30.refs_1_), channel_id=1, source_target_pairs={{0,1},{1,0},{2,3},{3,2},{4,5},{5,4},{6,7},{7,6}} | collective-permute-start | bytes 1572872 | tf_op jit(solution)/shard_map/ppermute | solution.py:255
  217.4 11.4 %collective-permute-start.36 = (bf16[256,1024]{1,0:T(8,128)(2,1)}, bf16[256,1024]{1,0:T(8,128)(2,1)}, u32[]{:S(2)}, u32[]{:S(2)}) collective-permute-start(bf16[256,1024]{1,0:T(8,128)(2,1)} %collective-permute-done.31.refs_3_), channel_id=1, source_target_pairs={{0,1},{1,0},{2,3},{3,2},{4,5},{5,4},{6,7},{7,6}} | collective-permute-start | bytes 1572872 | tf_op jit(solution)/shard_map/ppermute | solution.py:255
  (22 other events, 99.6 us)

commit v7 on v6

v7 whole, which is shorter than its diff:
```python
import jax
import jax.numpy as jnp
from jax import lax
from jax.experimental import pallas as pl
from jax.experimental.pallas import tpu as pltpu
from jax.sharding import PartitionSpec as P

VMEM = pl.BlockSpec(memory_space=pltpu.VMEM)
SMEM = pl.BlockSpec(memory_space=pltpu.SMEM)
HBM = pl.BlockSpec(memory_space=pltpu.HBM)


def params(megabytes):
    return pltpu.CompilerParams(vmem_limit_bytes=megabytes * 1024 * 1024)


def in_hbm(array):
    return pltpu.with_memory_space_constraint(array, pltpu.HBM)


def run_of(ref, axis, at, length):
    part = pl.ds(pl.multiple_of(at * length, length), length)
    return ref.at[part, :] if axis == 0 else ref.at[:, part]


def resident(at, weights):
    count = at.shape[0] - 1
    depth, cols = weights.shape[0] // count, weights.shape[1]

    def body(at, weights_ref, out_ref, sems):
        def copy(i):
            return pltpu.make_async_copy(
                run_of(weights_ref, 0, at[1 + i], depth), out_ref.at[i], sems.at[i]
            )

        for i in range(count):
            copy(i).start()
        for i in range(count):
            copy(i).wait()

    return pl.pallas_call(
        body,
        in_specs=[SMEM, HBM],
        out_specs=VMEM,
        out_shape=jax.ShapeDtypeStruct((count, depth, cols), weights.dtype),
        scratch_shapes=[pltpu.SemaphoreType.DMA((count,))],
        compiler_params=params(4),
        name="resident",
    )(at, in_hbm(weights))


def block_dot(at, turn, blocks, weights, parts, base, out_type):
    rows, depth = blocks[0].shape
    cols = weights.shape[2]
    width = 256 if cols % 256 == 0 else cols
    count = len(blocks)

    def body(at, weights_ref, base_ref, *refs):
        @pl.when(at[0] == turn)
        def _():
            def tile(j, _):
                here = pl.ds(pl.multiple_of(j * width, width), width)
                total = base_ref[:, here].astype(jnp.float32)
                for block_ref, part in zip(refs[:count], parts):
                    total += jnp.dot(
                        block_ref[...],
                        weights_ref[part, :, here],
                        preferred_element_type=jnp.float32,
                    )
                refs[count][:, here] = total.astype(out_type)
                return 0

            lax.fori_loop(0, cols // width, tile, 0)

    return pl.pallas_call(
        body,
        in_specs=[SMEM] + [VMEM] * (count + 2),
        out_specs=VMEM,
        out_shape=jax.ShapeDtypeStruct((rows, cols), out_type),
        compiler_params=params(4),
        name="block_dot",
    )(at, weights, base, *blocks)


def stream_dot(at, turn, blocks, weights, parts, base, out_type):
    rows, depth = blocks[0].shape
    cols = weights.shape[1]
    count = len(blocks)

    def body(at, weights_ref, *refs):
        block_refs, (out_ref, runs, sems) = refs[:count], refs[-3:]

        def copy(k):
            return pltpu.make_async_copy(
                run_of(weights_ref, 0, at[1 + parts[k]], depth), runs.at[k], sems.at[k]
            )

        @pl.when(at[0] == turn)
        def _():
            for k in range(count):
                copy(k).start()
            total = None if base is None else refs[count][...]
            for k in range(count):
                copy(k).wait()
                part = jnp.dot(block_refs[k][...], runs[k], preferred_element_type=jnp.float32)
                total = part if total is None else total + part
            out_ref[...] = total.astype(out_type)

    return pl.pallas_call(
        body,
        in_specs=[SMEM, HBM] + [VMEM] * (count + (base is not None)),
        out_specs=VMEM,
        out_shape=jax.ShapeDtypeStruct((rows, cols), out_type),
        scratch_shapes=[
            pltpu.VMEM((count, depth, cols), weights.dtype),
            pltpu.SemaphoreType.DMA((count,)),
        ],
        compiler_params=params(14),
        name="stream_dot",
    )(at, in_hbm(weights), *blocks, *([] if base is None else [base]))


def partials(at, among, inputs, weights, inner):
    rows, depth = inputs.shape
    count = at.shape[0] - 1
    width = weights.shape[1] // count

    def body(at, weights_ref, inputs_ref, *refs):
        out_refs, (runs, sems) = refs[:inner], refs[inner:]
        order = [n for dx in [*range(1, inner), 0] for n in range(dx, count, inner)]

        def copy(n):
            return pltpu.make_async_copy(
                run_of(weights_ref, 1, at[1 + n], width), runs.at[n], sems.at[n]
            )

        @pl.when((at[0] >= min(among)) & (at[0] <= max(among)))
        def _():
            for n in order:
                copy(n).start()
            for n in order:
                copy(n).wait()
                total = jnp.dot(inputs_ref[...], runs[n], preferred_element_type=jnp.float32)
                out_ref = out_refs[n % inner]
                out_ref[n // inner] = total.astype(out_ref.dtype)

    return pl.pallas_call(
        body,
        in_specs=[SMEM, HBM, VMEM],
        out_specs=[VMEM] * inner,
        out_shape=[
            jax.ShapeDtypeStruct((count // inner, rows, width), jnp.bfloat16 if dx else jnp.float32)
            for dx in range(inner)
        ],
        scratch_shapes=[
            pltpu.VMEM((count, depth, width), weights.dtype),
            pltpu.SemaphoreType.DMA((count,)),
        ],
        compiler_params=params(14),
        name="partials",
    )(at, in_hbm(weights), inputs)


def added(at, among, own, arrived):
    count, rows, width = own.shape

    def body(at, own_ref, *refs):
        arrived_refs, out_refs = refs[: len(arrived)], refs[len(arrived) :]

        @pl.when((at[0] >= min(among)) & (at[0] <= max(among)))
        def _():
            for n in range(count):
                total = own_ref[n]
                for ref in arrived_refs:
                    total = total + ref[n].astype(jnp.float32)
                out_refs[n][...] = total.astype(out_refs[n].dtype)

    return pl.pallas_call(
        body,
        in_specs=[SMEM] + [VMEM] * (1 + len(arrived)),
        out_specs=[VMEM] * count,
        out_shape=[
            jax.ShapeDtypeStruct((rows, width), jnp.bfloat16 if n else jnp.float32)
            for n in range(count)
        ],
        compiler_params=params(4),
        name="added",
    )(at, own, *arrived)


def mean_square(at, half, rot_outs, low, high, micro, seq):
    _, rows, width = low[0].shape
    eig_rows = rot_outs[0].shape[1]
    count, inner, sections = at.shape[0] - 1, len(low), len(rot_outs)

    def body(at, *refs):
        rot_refs, refs = refs[:sections], refs[sections:]
        low_refs, high_refs = refs[:inner], refs[inner : 2 * inner]
        eig_ref, rot, block, result, sems = refs[2 * inner :]
        for s in range(sections):

            @pl.when(at[0] == s)
            def _():
                rot[...] = rot_refs[s][...]

        def copy(n):
            return pltpu.make_async_copy(
                result.at[n % 2], run_of(eig_ref, 1, at[1 + n], width), sems.at[n % 2]
            )

        for n in range(count):

            @pl.when(at[0] >= half)
            def _():
                block[...] = high_refs[n % inner][n // inner]

            @pl.when(at[0] < half)
            def _():
                block[...] = low_refs[n % inner][n // inner]

            if n >= 2:
                copy(n - 2).wait()
            for m in range(micro):
                rows_of = slice(m * seq, (m + 1) * seq)
                product = lax.dot_general(
                    rot[rows_of, :],
                    block[rows_of, :],
                    (((0,), (0,)), ((), ())),
                    preferred_element_type=jnp.float32,
                )
                square = product * product
                total = square if m == 0 else result[n % 2] + square
                result[n % 2] = total if m < micro - 1 else total * (1.0 / (seq * micro))
            copy(n).start()
        for n in range(max(0, count - 2), count):
            copy(n).wait()

    return pl.pallas_call(
        body,
        in_specs=[SMEM] + [VMEM] * (sections + 2 * inner),
        out_specs=HBM,
        out_shape=jax.ShapeDtypeStruct((eig_rows, count * width), jnp.float32),
        scratch_shapes=[
            pltpu.VMEM((rows, eig_rows), rot_outs[0].dtype),
            pltpu.VMEM((rows, width), rot_outs[0].dtype),
            pltpu.VMEM((2, eig_rows, width), jnp.float32),
            pltpu.SemaphoreType.DMA((2,)),
        ],
        compiler_params=params(14),
        name="mean_square",
    )(at, *rot_outs, *low, *high)


def per_device(activations, top_grad, projection, basis_out, basis_in):
    sections = lax.axis_size("section")
    shards = lax.axis_size("shard")
    micro, seq, feat_loc = top_grad.shape
    rows = micro * seq
    inputs = activations[0].reshape(rows, feat_loc)
    top = top_grad.reshape(rows, feat_loc)
    weights, out_cols = projection[0], basis_out[0]
    half = sections // 2

    inner = 1
    while 2 * (2 * inner) ** 2 <= shards:
        inner *= 2
    outer = shards // inner
    shard = lax.axis_index("shard")
    at = jnp.stack(
        [jnp.int32(lax.axis_index("section"))] + [jnp.int32(shard ^ p) for p in range(shards)]
    )

    def moved(block, flip, pairs):
        route = [(a * shards + i, b * shards + (i ^ flip)) for a, b in pairs for i in range(shards)]
        return lax.ppermute(block, ("section", "shard"), route)

    def spread(block, pairs):
        powers = [1 << p for p in range(outer.bit_length() - 1)]
        near = {dz: moved(block, dz * inner, pairs) for dz in reversed(powers)}
        return near, {dx: moved(block, dx, pairs) for dx in range(1, inner)}

    def along_outer(near, pairs):
        got = dict(near)
        for dz in range(outer):
            low = dz & -dz
            if dz not in got:
                got[dz] = moved(got[dz ^ low], low * inner, pairs)
        return got

    def handed_down(grad, turn):
        own = moved(grad, 0, [(turn + 1, turn)])
        if turn % 2 == 0:
            near, side = spread(grad, [(turn + 1, turn)])
        else:
            near, side = spread(own, [(turn, turn)])
        return {0: own, **near}, side

    def relay(turn, sent, before, within):
        near, side = sent
        got = along_outer(near, [(turn, turn)])
        start, *_ = lax.optimization_barrier((near[0], *before))

        def products(dots, base, last):
            blocks, parts = [block for block, _ in dots], [part for _, part in dots]
            out_type = jnp.bfloat16 if last else jnp.float32
            if turn == 0:
                return stream_dot(at, turn, blocks, out_cols, parts, base, out_type)
            return block_dot(at, turn, blocks, weights, parts, base, out_type)

        blocks = {(0, 0): start, **{(0, dx): block for dx, block in side.items()}}
        dots = [(block, dx) for (_, dx), block in blocks.items()]
        totals = [products(dots, None if turn == 0 else start, outer == 1)]
        for dz in range(1, outer + 1):
            if dz < outer:
                block, *_ = lax.optimization_barrier(
                    (got[dz], totals[max(0, dz - 2)], *(within if dz == outer - 1 else []))
                )
                blocks[dz, 0] = got[dz]
                for dx in range(1, inner):
                    blocks[dz, dx] = moved(block, dx, [(turn, turn)])
            if dz > 1:
                dots = [(blocks[dz - 1, dx], (dz - 1) * inner + dx) for dx in range(inner)]
                if dz == outer - 1:
                    dots.append((blocks[dz, 0], dz * inner))
                if dz == outer and outer > 2 and inner > 1:
                    dots = dots[1:]
                totals.append(products(dots, totals[-1], dz == outer))
        return totals[-1], blocks

    def rotated(turn, blocks):
        parts = [dz * inner + dx for dz, dx in blocks]
        return stream_dot(at, turn, list(blocks.values()), out_cols, parts, None, jnp.bfloat16)

    def rotate_begin(inputs, among):
        pairs = [(a, a) for a in among]
        own, *others = partials(at, among, inputs, basis_in[0], inner)
        return own, others, [moved(other, 1 + n, pairs) for n, other in enumerate(others)]

    def summed(sums, among):
        pairs = [(a, a) for a in among]
        own = sums[0]
        for dz, part in enumerate(sums[1:], 1):
            own = own + moved(part, dz * inner, pairs).astype(jnp.float32)
        return own.astype(jnp.bfloat16)

    def outer_columns(own, among):
        pairs = [(a, a) for a in among]
        powers = [1 << p for p in range(outer.bit_length() - 1)]
        near = {0: own, **{dz: moved(own, dz * inner, pairs) for dz in reversed(powers)}}
        got = along_outer(near, pairs)
        return jnp.stack([got[dz] for dz in range(outer)])

    def all_columns(column, among):
        return [column] + [moved(column, dx, [(a, a) for a in among]) for dx in range(1, inner)]

    upper = list(range(sections - 1, half - 1, -1))
    lower = list(range(half - 1, -1, -1))
    rot_outs = [None] * sections

    low_own, low_others, low_arrived = rotate_begin(inputs, lower)
    near, side = spread(top, [(upper[0], upper[0])])
    weights = resident(at, weights)
    sums = added(at, lower, low_own, low_arrived)
    low = summed(sums, lower)
    sent, before, within = ({0: top, **near}, side), low_others, sums
    for turn in upper:
        grad, blocks = relay(turn, sent, before, within)
        within = []
        if turn != upper[-1]:
            sent = handed_down(grad, turn - 1)
            rot_outs[turn] = rotated(turn, blocks)
            before = [rot_outs[turn], low]
    low = outer_columns(low, lower)
    grad, low = lax.optimization_barrier((grad, low))
    sent = handed_down(grad, lower[0])
    low = all_columns(low, lower)
    rot_outs[upper[-1]] = rotated(upper[-1], blocks)
    inputs, _ = lax.optimization_barrier((inputs, sent[0][0]))
    high_own, _, high_arrived = rotate_begin(inputs, upper)
    before = [rot_outs[upper[-1]], *low]
    for turn in lower:
        grad, blocks = relay(turn, sent, before, [])
        if turn != 0:
            sent = handed_down(grad, turn - 1)
            rot_outs[turn] = rotated(turn, blocks)
            before = [rot_outs[turn]]
    rot_outs[0] = grad
    sums = added(at, upper, high_own, high_arrived)
    high = all_columns(outer_columns(summed(sums, upper), upper), upper)
    return mean_square(at, half, rot_outs, low, high, micro, seq)[None]


def solution(mesh):
    return jax.shard_map(
        per_device,
        mesh=mesh,
        in_specs=(
            P("section", None, None, "shard"),
            P(None, None, "shard"),
            P("section", None, "shard"),
            P("section", None, "shard"),
            P("section", "shard", None),
        ),
        out_specs=P("section", "shard", None),
        check_vma=False,
    )
```

time: 247 us -> 209 us (0.85)
  waiting for transfers between devices: 118 us -> 94.1 us
  starting transfers between devices: 73.7 us -> 66.5 us
  other arithmetic: 3.66 us -> 0.56 us
    ppermute x47, waiting for transfers between devices: 118 us -> 94.1 us  [moved(): return lax.ppermute(block, ('section', 'shard'), route)]
    ppermute x47, starting transfers between devices: 73.7 us -> 66.5 us  [moved(): return lax.ppermute(block, ('section', 'shard'), route)]
    pallas_call x16 -> x20, Pallas kernels: 24.2 us -> 25.4 us  [the longest x7 12.3 us: stream_dot(): pl.pallas_call(body, in_specs=[SMEM, HBM] + [VMEM] * (count + (base is no...]
  transfers between devices with their start and end apart: 47 -> 47, of which waited for: 8 -> 11; matrix products, arithmetic and copies ran while one was open for 2% -> 0% of each run, Pallas kernels for 13% -> 16%
where the time goes in v7:
time: 209 us; the launch traced here: 208 us
  waiting for transfers between devices  94.1 us (45%)
  starting transfers between devices  66.5 us (32%)
  Pallas kernels  45 us (22%)
    ppermute x47, waiting for transfers between devices, moved(): return lax.ppermute(block, ('section', 'shard'), route)  94.1 us
    ppermute x47, starting transfers between devices, moved(): return lax.ppermute(block, ('section', 'shard'), route)  66.5 us
    pallas_call x7, Pallas kernels, stream_dot(): pl.pallas_call(body, in_specs=[SMEM, HBM] + [VMEM] * (count + (base is no...  12.3 us
    pallas_call x1, Pallas kernels, mean_square(): pl.pallas_call(body, in_specs=[SMEM] + [VMEM] * (sections + 2 * inner), o...  12.2 us
    pallas_call x12, Pallas kernels, block_dot(): pl.pallas_call(body, in_specs=[SMEM] + [VMEM] * (count + 2), out_specs=VM...  6.61 us
    pallas_call x1, Pallas kernels, resident(): pl.pallas_call(body, in_specs=[SMEM, HBM], out_specs=VMEM, out_shape=jax....  6.47 us
    pallas_call x2, Pallas kernels, partials(): pl.pallas_call(body, in_specs=[SMEM, HBM, VMEM], out_specs=[VMEM] * inner...  6.16 us
  transfers between devices with their start and end apart: 47, of which 11 were waited for; matrix products, arithmetic and copies ran while one was open for 0% of the time, Pallas kernels for 16%

profile of v7, /device:TPU:0, one launch (start us, length us, event | category | flops | bytes accessed | tf_op | source)
XLA Modules:
  0.0 208.4 jit_solution(5684765667984313820)
XLA Ops:
  2.7 5.4 %partials.2 = (f32[4,256,512]{2,1,0:T(8,128)S(1)}, bf16[4,256,512]{2,1,0:T(8,128)(2,1)S(1)}) custom-call(s32[9]{0:T(128)S(1)} %stack.69.at, bf16[1024,4096]{1,0:T(8,128)(2,1)} %bitcast.38, bf16[256,1024]{1,0:T(8,128)(2,1)S(1)} %bitcast.29), custom_call_target="tpu_custom_call" | custom-call | tf_op jit(solution)/shard_map/partials/pallas_call | solution.py:147
  8.0 4.8 %collective-permute-start.6 = (bf16[4,256,512]{2,1,0:T(8,128)(2,1)S(1)}, bf16[4,256,512]{2,1,0:T(8,128)(2,1)S(1)}, u32[]{:S(2)}, u32[]{:S(2)}) collective-permute-start(bf16[4,256,512]{2,1,0:T(8,128)(2,1)S(1)} %get-tuple-element.36), channel_id=1, source_target_pairs={{8,9},{9,8},{10,11},{11,10},{12,13},{13,12},{14,15},{15,14},{0,1},... | collective-permute-start | bytes 3145736 | tf_op jit(solution)/shard_map/ppermute | solution.py:275
  13.6 6.5 %resident.1.weights_ref = bf16[8,1024,1024]{2,1,0:T(8,128)(2,1)S(1)} custom-call(s32[9]{0:T(128)S(1)} %stack.69.at, bf16[8192,1024]{1,0:T(8,128)(2,1)} %bitcast.40), custom_call_target="tpu_custom_call" | custom-call | tf_op jit(solution)/shard_map/resident/pallas_call | solution.py:41
  23.3 12.7 %collective-permute-done.6.refs_0_ = bf16[4,256,512]{2,1,0:T(8,128)(2,1)S(1)} collective-permute-done((bf16[4,256,512]{2,1,0:T(8,128)(2,1)S(1)}, bf16[4,256,512]{2,1,0:T(8,128)(2,1)S(1)}, u32[]{:S(2)}, u32[]{:S(2)}) %collective-permute-start.6) | collective-permute-done | bytes 1048608 | tf_op jit(solution)/shard_map/ppermute | solution.py:275
  37.5 3.7 %collective-permute-start.9 = (bf16[256,512]{1,0:T(8,128)(2,1)S(1)}, bf16[256,512]{1,0:T(8,128)(2,1)S(1)}, u32[]{:S(2)}, u32[]{:S(2)}) collective-permute-start(bf16[256,512]{1,0:T(8,128)(2,1)S(1)} %get-tuple-element.42), channel_id=1, source_target_pairs={{8,10},{9,11},{10,8},{11,9},{12,14},{13,15},{14,12},{15,13},{0,2},... | collective-permute-start | bytes 786440 | tf_op jit(solution)/shard_map/ppermute | solution.py:275
  41.2 4.5 %collective-permute-start.10 = (bf16[256,512]{1,0:T(8,128)(2,1)S(1)}, bf16[256,512]{1,0:T(8,128)(2,1)S(1)}, u32[]{:S(2)}, u32[]{:S(2)}) collective-permute-start(bf16[256,512]{1,0:T(8,128)(2,1)S(1)} %get-tuple-element.43), channel_id=1, source_target_pairs={{8,12},{9,13},{10,14},{11,15},{12,8},{13,9},{14,10},{15,11},{0,4},... | collective-permute-start | bytes 786440 | tf_op jit(solution)/shard_map/ppermute | solution.py:275
  45.7 1.9 collective-permute-start.11
  50.9 13.2 %collective-permute-done.10 = bf16[256,512]{1,0:T(8,128)(2,1)S(1)} collective-permute-done((bf16[256,512]{1,0:T(8,128)(2,1)S(1)}, bf16[256,512]{1,0:T(8,128)(2,1)S(1)}, u32[]{:S(2)}, u32[]{:S(2)}) %collective-permute-start.10) | collective-permute-done | bytes 262176 | tf_op jit(solution)/shard_map/ppermute | solution.py:275
  67.5 6.5 %collective-permute-start.20 = (bf16[256,512]{1,0:T(8,128)(2,1)S(1)}, bf16[256,512]{1,0:T(8,128)(2,1)S(1)}, u32[]{:S(2)}, u32[]{:S(2)}) collective-permute-start(bf16[256,512]{1,0:T(8,128)(2,1)S(1)} %add_convert_fusion.1), channel_id=1, source_target_pairs={{8,12},{9,13},{10,14},{11,15},{12,8},{13,9},{14,10},{15,11},{0,4},... | collective-permute-start | bytes 786440 | tf_op jit(solution)/shard_map/ppermute | solution.py:275
  76.0 1.9 collective-permute-start.19
  78.0 6.7 %collective-permute-done.20 = bf16[256,512]{1,0:T(8,128)(2,1)S(1)} collective-permute-done((bf16[256,512]{1,0:T(8,128)(2,1)S(1)}, bf16[256,512]{1,0:T(8,128)(2,1)S(1)}, u32[]{:S(2)}, u32[]{:S(2)}) %collective-permute-start.20) | collective-permute-done | bytes 262176 | tf_op jit(solution)/shard_map/ppermute | solution.py:275
  84.6 1.9 collective-permute-start.21
  86.5 2.9 %collective-permute-done.19 = bf16[256,512]{1,0:T(8,128)(2,1)S(1)} collective-permute-done((bf16[256,512]{1,0:T(8,128)(2,1)S(1)}, bf16[256,512]{1,0:T(8,128)(2,1)S(1)}, u32[]{:S(2)}, u32[]{:S(2)}) %collective-permute-start.19) | collective-permute-done | bytes 262176 | tf_op jit(solution)/shard_map/ppermute | solution.py:275
  89.5 5.0 %collective-permute-done.21 = bf16[256,512]{1,0:T(8,128)(2,1)S(1)} collective-permute-done((bf16[256,512]{1,0:T(8,128)(2,1)S(1)}, bf16[256,512]{1,0:T(8,128)(2,1)S(1)}, u32[]{:S(2)}, u32[]{:S(2)}) %collective-permute-start.21) | collective-permute-done | bytes 262176 | tf_op jit(solution)/shard_map/ppermute | solution.py:275
  95.7 3.4 %collective-permute-start.23 = (bf16[4,256,512]{2,1,0:T(8,128)(2,1)S(1)}, bf16[4,256,512]{2,1,0:T(8,128)(2,1)S(1)}, u32[]{:S(2)}, u32[]{:S(2)}) collective-permute-start(bf16[4,256,512]{2,1,0:T(8,128)(2,1)S(1)} %pad_maximum_fusion.refs_4_), channel_id=1, source_target_pairs={{8,9},{9,8},{10,11},{11,10},{12,13},{13,12},{14,15},{15,14},{0,1},... | collective-permute-start | bytes 3145736 | tf_op jit(solution)/shard_map/ppermute | solution.py:275
  104.2 19.6 %collective-permute-done.23.refs_5_ = bf16[4,256,512]{2,1,0:T(8,128)(2,1)S(1)} collective-permute-done((bf16[4,256,512]{2,1,0:T(8,128)(2,1)S(1)}, bf16[4,256,512]{2,1,0:T(8,128)(2,1)S(1)}, u32[]{:S(2)}, u32[]{:S(2)}) %collective-permute-start.23) | collective-permute-done | bytes 1048608 | tf_op jit(solution)/shard_map/ppermute | solution.py:275
  131.5 1.3 collective-permute-start.35
  132.8 1.3 collective-permute-start.34
  138.2 20.0 %collective-permute-done.34.refs_0_ = bf16[256,1024]{1,0:T(8,128)(2,1)S(1)} collective-permute-done((bf16[256,1024]{1,0:T(8,128)(2,1)S(1)}, bf16[256,1024]{1,0:T(8,128)(2,1)S(1)}, u32[]{:S(2)}, u32[]{:S(2)}) %collective-permute-start.34) | collective-permute-done | bytes 524320 | tf_op jit(solution)/shard_map/ppermute | solution.py:275
  159.5 3.2 %collective-permute-done.35.refs_1_ = bf16[256,1024]{1,0:T(8,128)(2,1)S(1)} collective-permute-done((bf16[256,1024]{1,0:T(8,128)(2,1)S(1)}, bf16[256,1024]{1,0:T(8,128)(2,1)S(1)}, u32[]{:S(2)}, u32[]{:S(2)}) %collective-permute-start.35) | collective-permute-done | bytes 524320 | tf_op jit(solution)/shard_map/ppermute | solution.py:275
  162.7 2.8 %stream_dot.10.refs_2_ = f32[256,512]{1,0:T(8,128)S(1)} custom-call(s32[9]{0:T(128)S(1)} %stack.69.at, bf16[8192,512]{1,0:T(8,128)(2,1)} %bitcast.34, bf16[256,1024]{1,0:T(8,128)(2,1)S(1)} %collective-permute-done.34.refs_0_, bf16[256,1024]{1,0:T(8,128)(2,1)S(1)} %collective-permute-done.35.refs_1_), custom_call_target="tpu_custom_call" | custom-call | tf_op jit(solution)/shard_map/stream_dot/pallas_call | solution.py:109
  165.5 3.5 %collective-permute-done.33.refs_0_ = bf16[256,1024]{1,0:T(8,128)(2,1)S(1)} collective-permute-done((bf16[256,1024]{1,0:T(8,128)(2,1)S(1)}, bf16[256,1024]{1,0:T(8,128)(2,1)S(1)}, u32[]{:S(2)}, u32[]{:S(2)}) %collective-permute-start.33) | collective-permute-done | bytes 524320 | tf_op jit(solution)/shard_map/ppermute | solution.py:275
  169.1 2.5 %collective-permute-start.36 = (bf16[256,1024]{1,0:T(8,128)(2,1)S(1)}, bf16[256,1024]{1,0:T(8,128)(2,1)S(1)}, u32[]{:S(2)}, u32[]{:S(2)}) collective-permute-start(bf16[256,1024]{1,0:T(8,128)(2,1)S(1)} %collective-permute-done.33.refs_0_), channel_id=1, source_target_pairs={{0,1},{1,0},{2,3},{3,2},{4,5},{5,4},{6,7},{7,6}} | collective-permute-start | bytes 1572872 | tf_op jit(solution)/shard_map/ppermute | solution.py:275
  171.6 1.9 collective-permute-start.32
  174.4 3.3 %collective-permute-start.38 = (bf16[256,1024]{1,0:T(8,128)(2,1)S(1)}, bf16[256,1024]{1,0:T(8,128)(2,1)S(1)}, u32[]{:S(2)}, u32[]{:S(2)}) collective-permute-start(bf16[256,1024]{1,0:T(8,128)(2,1)S(1)} %collective-permute-done.31.refs_0_), channel_id=1, source_target_pairs={{0,1},{1,0},{2,3},{3,2},{4,5},{5,4},{6,7},{7,6}} | collective-permute-start | bytes 1572872 | tf_op jit(solution)/shard_map/ppermute | solution.py:275
  177.8 2.4 %collective-permute-done.36.refs_1_ = bf16[256,1024]{1,0:T(8,128)(2,1)S(1)} collective-permute-done((bf16[256,1024]{1,0:T(8,128)(2,1)S(1)}, bf16[256,1024]{1,0:T(8,128)(2,1)S(1)}, u32[]{:S(2)}, u32[]{:S(2)}) %collective-permute-start.36) | collective-permute-done | bytes 524320 | tf_op jit(solution)/shard_map/ppermute | solution.py:275
  180.2 2.6 %stream_dot.11.refs_3_ = f32[256,512]{1,0:T(8,128)S(1)} custom-call(s32[9]{0:T(128)S(1)} %stack.69.at, bf16[8192,512]{1,0:T(8,128)(2,1)} %bitcast.35, bf16[256,1024]{1,0:T(8,128)(2,1)S(1)} %collective-permute-done.33.refs_0_, bf16[256,1024]{1,0:T(8,128)(2,1)S(1)} %collective-permute-done.36.refs_1_, f32[256,512]{1,0:T(8,128)S(1)} %stream_dot.10.refs_2_), custom_call_target="tpu_custom_call" | custom-call | tf_op jit(solution)/shard_map/stream_dot/pallas_call | solution.py:109
  182.7 3.3 %collective-permute-start.37 = (bf16[256,1024]{1,0:T(8,128)(2,1)S(1)}, bf16[256,1024]{1,0:T(8,128)(2,1)S(1)}, u32[]{:S(2)}, u32[]{:S(2)}) collective-permute-start(bf16[256,1024]{1,0:T(8,128)(2,1)S(1)} %collective-permute-done.32.refs_2_), channel_id=1, source_target_pairs={{0,1},{1,0},{2,3},{3,2},{4,5},{5,4},{6,7},{7,6}} | collective-permute-start | bytes 1572872 | tf_op jit(solution)/shard_map/ppermute | solution.py:275
  186.0 2.9 %stream_dot.12.refs_1_ = f32[256,512]{1,0:T(8,128)S(1)} custom-call(s32[9]{0:T(128)S(1)} %stack.69.at, bf16[8192,512]{1,0:T(8,128)(2,1)} %bitcast.36, bf16[256,1024]{1,0:T(8,128)(2,1)S(1)} %collective-permute-done.31.refs_0_, bf16[256,1024]{1,0:T(8,128)(2,1)S(1)} %collective-permute-done.38.refs_1_, bf16[256,1024]{1,0:T(8,128)(2,1)S(1)} %collective-permute-done.32.refs_2_, ...), custom_call_target="tpu_custom_call" | custom-call | tf_op jit(solution)/shard_map/stream_dot/pallas_call | solution.py:109
  188.9 4.9 %collective-permute-done.37.refs_0_ = bf16[256,1024]{1,0:T(8,128)(2,1)S(1)} collective-permute-done((bf16[256,1024]{1,0:T(8,128)(2,1)S(1)}, bf16[256,1024]{1,0:T(8,128)(2,1)S(1)}, u32[]{:S(2)}, u32[]{:S(2)}) %collective-permute-start.37) | collective-permute-done | bytes 524320 | tf_op jit(solution)/shard_map/ppermute | solution.py:275
  193.8 2.2 %stream_dot.13.refs_0_ = bf16[256,512]{1,0:T(8,128)(2,1)S(1)} custom-call(s32[9]{0:T(128)S(1)} %stack.69.at, bf16[8192,512]{1,0:T(8,128)(2,1)} %bitcast.37, bf16[256,1024]{1,0:T(8,128)(2,1)S(1)} %collective-permute-done.37.refs_0_, f32[256,512]{1,0:T(8,128)S(1)} %stream_dot.12.refs_1_), custom_call_target="tpu_custom_call" | custom-call | tf_op jit(solution)/shard_map/stream_dot/pallas_call | solution.py:109
  196.0 12.2 %mean_square.1 = f32[512,4096]{1,0:T(8,128)} custom-call(s32[9]{0:T(128)S(1)} %stack.69.at, bf16[256,512]{1,0:T(8,128)(2,1)S(1)} %stream_dot.13.refs_0_, bf16[256,512]{1,0:T(8,128)(2,1)S(1)} %stream_dot.9.refs_1_, bf16[256,512]{1,0:T(8,128)(2,1)S(1)} %stream_dot.8.refs_2_, bf16[256,512]{1,0:T(8,128)(2,1)S(1)} %stream_dot.7.refs_3_, ...), custom_call_target="tpu_custom_call" | custom-call | tf_op jit(solution)/shard_map/mean_square/pallas_call | solution.py:238
  (98 shorter events, 36.5 us)
Async XLA Ops:
  0.0 20.6 %collective-permute-start.1 = (bf16[256,1024]{1,0:T(8,128)(2,1)}, bf16[256,1024]{1,0:T(8,128)(2,1)S(1)}, u32[]{:S(2)}, u32[]{:S(2)}) collective-permute-start(bf16[256,1024]{1,0:T(8,128)(2,1)} %bitcast.23), channel_id=1, source_target_pairs={{24,26},{25,27},{26,24},{27,25},{28,30},{29,31},{30,28},{31,29}} | collective-permute-start | bytes 1572872 | tf_op jit(solution)/shard_map/ppermute | solution.py:275
  0.8 19.3 %collective-permute-start = (bf16[256,1024]{1,0:T(8,128)(2,1)}, bf16[256,1024]{1,0:T(8,128)(2,1)S(1)}, u32[]{:S(2)}, u32[]{:S(2)}) collective-permute-start(bf16[256,1024]{1,0:T(8,128)(2,1)} %bitcast.24), channel_id=1, source_target_pairs={{24,25},{25,24},{26,27},{27,26},{28,29},{29,28},{30,31},{31,30}} | collective-permute-start | bytes 1572872 | tf_op jit(solution)/shard_map/ppermute | solution.py:275
  8.0 28.0 %collective-permute-start.6 = (bf16[4,256,512]{2,1,0:T(8,128)(2,1)S(1)}, bf16[4,256,512]{2,1,0:T(8,128)(2,1)S(1)}, u32[]{:S(2)}, u32[]{:S(2)}) collective-permute-start(bf16[4,256,512]{2,1,0:T(8,128)(2,1)S(1)} %get-tuple-element.36), channel_id=1, source_target_pairs={{8,9},{9,8},{10,11},{11,10},{12,13},{13,12},{14,15},{15,14},{0,1},... | collective-permute-start | bytes 3145736 | tf_op jit(solution)/shard_map/ppermute | solution.py:275
  21.4 15.4 %collective-permute-start.5 = (bf16[256,1024]{1,0:T(8,128)(2,1)S(1)}, bf16[256,1024]{1,0:T(8,128)(2,1)S(1)}, u32[]{:S(2)}, u32[]{:S(2)}) collective-permute-start(bf16[256,1024]{1,0:T(8,128)(2,1)S(1)} %collective-permute-done.3.refs_0_.refs_4_), channel_id=1, source_target_pairs={{24,26},{25,27},{26,24},{27,25},{28,30},{29,31},{30,28},{31,29}} | collective-permute-start | bytes 1572872 | tf_op jit(solution)/shard_map/ppermute | solution.py:275
  22.1 25.6 %collective-permute-start.4 = (bf16[256,1024]{1,0:T(8,128)(2,1)S(1)}, bf16[256,1024]{1,0:T(8,128)(2,1)S(1)}, u32[]{:S(2)}, u32[]{:S(2)}) collective-permute-start(bf16[256,1024]{1,0:T(8,128)(2,1)S(1)} %collective-permute-done.3.refs_0_.refs_4_), channel_id=1, source_target_pairs={{24,25},{25,24},{26,27},{27,26},{28,29},{29,28},{30,31},{31,30}} | collective-permute-start | bytes 1572872 | tf_op jit(solution)/shard_map/ppermute | solution.py:275
  36.8 11.4 %collective-permute-start.7 = (bf16[256,1024]{1,0:T(8,128)(2,1)S(1)}, bf16[256,1024]{1,0:T(8,128)(2,1)S(1)}, u32[]{:S(2)}, u32[]{:S(2)}) collective-permute-start(bf16[256,1024]{1,0:T(8,128)(2,1)S(1)} %collective-permute-done.5.refs_2_.refs_6_), channel_id=1, source_target_pairs={{24,25},{25,24},{26,27},{27,26},{28,29},{29,28},{30,31},{31,30}} | collective-permute-start | bytes 1572872 | tf_op jit(solution)/shard_map/ppermute | solution.py:275
  37.5 12.7 %collective-permute-start.9 = (bf16[256,512]{1,0:T(8,128)(2,1)S(1)}, bf16[256,512]{1,0:T(8,128)(2,1)S(1)}, u32[]{:S(2)}, u32[]{:S(2)}) collective-permute-start(bf16[256,512]{1,0:T(8,128)(2,1)S(1)} %get-tuple-element.42), channel_id=1, source_target_pairs={{8,10},{9,11},{10,8},{11,9},{12,14},{13,15},{14,12},{15,13},{0,2},... | collective-permute-start | bytes 786440 | tf_op jit(solution)/shard_map/ppermute | solution.py:275
  41.2 22.8 %collective-permute-start.10 = (bf16[256,512]{1,0:T(8,128)(2,1)S(1)}, bf16[256,512]{1,0:T(8,128)(2,1)S(1)}, u32[]{:S(2)}, u32[]{:S(2)}) collective-permute-start(bf16[256,512]{1,0:T(8,128)(2,1)S(1)} %get-tuple-element.43), channel_id=1, source_target_pairs={{8,12},{9,13},{10,14},{11,15},{12,8},{13,9},{14,10},{15,11},{0,4},... | collective-permute-start | bytes 786440 | tf_op jit(solution)/shard_map/ppermute | solution.py:275
  45.7 19.0 %collective-permute-start.11 = (bf16[256,512]{1,0:T(8,128)(2,1)S(1)}, bf16[256,512]{1,0:T(8,128)(2,1)S(1)}, u32[]{:S(2)}, u32[]{:S(2)}) collective-permute-start(bf16[256,512]{1,0:T(8,128)(2,1)S(1)} %get-tuple-element.44), channel_id=1, source_target_pairs={{8,14},{9,15},{10,12},{11,13},{12,10},{13,11},{14,8},{15,9},{0,6},... | collective-permute-start | bytes 786440 | tf_op jit(solution)/shard_map/ppermute | solution.py:275
  48.8 16.8 %collective-permute-start.8 = (bf16[256,1024]{1,0:T(8,128)(2,1)S(1)}, bf16[256,1024]{1,0:T(8,128)(2,1)S(1)}, u32[]{:S(2)}, u32[]{:S(2)}) collective-permute-start(bf16[256,1024]{1,0:T(8,128)(2,1)S(1)} %block_dot.15), channel_id=1, source_target_pairs={{24,16},{25,17},{26,18},{27,19},{28,20},{29,21},{30,22},{31,23}} | collective-permute-start | bytes 1572872 | tf_op jit(solution)/shard_map/ppermute | solution.py:275
  49.5 16.1 %collective-permute-start.12 = (bf16[256,1024]{1,0:T(8,128)(2,1)S(1)}, bf16[256,1024]{1,0:T(8,128)(2,1)S(1)}, u32[]{:S(2)}, u32[]{:S(2)}) collective-permute-start(bf16[256,1024]{1,0:T(8,128)(2,1)S(1)} %block_dot.15), channel_id=1, source_target_pairs={{24,17},{25,16},{26,19},{27,18},{28,21},{29,20},{30,23},{31,22}} | collective-permute-start | bytes 1572872 | tf_op jit(solution)/shard_map/ppermute | solution.py:275
  50.2 15.9 %collective-permute-start.13 = (bf16[256,1024]{1,0:T(8,128)(2,1)S(1)}, bf16[256,1024]{1,0:T(8,128)(2,1)S(1)}, u32[]{:S(2)}, u32[]{:S(2)}) collective-permute-start(bf16[256,1024]{1,0:T(8,128)(2,1)S(1)} %block_dot.15), channel_id=1, source_target_pairs={{24,18},{25,19},{26,16},{27,17},{28,22},{29,23},{30,20},{31,21}} | collective-permute-start | bytes 1572872 | tf_op jit(solution)/shard_map/ppermute | solution.py:275
  67.5 17.1 %collective-permute-start.20 = (bf16[256,512]{1,0:T(8,128)(2,1)S(1)}, bf16[256,512]{1,0:T(8,128)(2,1)S(1)}, u32[]{:S(2)}, u32[]{:S(2)}) collective-permute-start(bf16[256,512]{1,0:T(8,128)(2,1)S(1)} %add_convert_fusion.1), channel_id=1, source_target_pairs={{8,12},{9,13},{10,14},{11,15},{12,8},{13,9},{14,10},{15,11},{0,4},... | collective-permute-start | bytes 786440 | tf_op jit(solution)/shard_map/ppermute | solution.py:275
  74.0 20.5 %collective-permute-start.16 = (bf16[256,1024]{1,0:T(8,128)(2,1)S(1)}, bf16[256,1024]{1,0:T(8,128)(2,1)S(1)}, u32[]{:S(2)}, u32[]{:S(2)}) collective-permute-start(bf16[256,1024]{1,0:T(8,128)(2,1)S(1)} %collective-permute-done.15.refs_0_.refs_4_), channel_id=1, source_target_pairs={{16,17},{17,16},{18,19},{19,18},{20,21},{21,20},{22,23},{23,22}} | collective-permute-start | bytes 1572872 | tf_op jit(solution)/shard_map/ppermute | solution.py:275
  75.3 19.8 %collective-permute-start.18 = (bf16[256,1024]{1,0:T(8,128)(2,1)S(1)}, bf16[256,1024]{1,0:T(8,128)(2,1)S(1)}, u32[]{:S(2)}, u32[]{:S(2)}) collective-permute-start(bf16[256,1024]{1,0:T(8,128)(2,1)S(1)} %collective-permute-done.17.refs_2_.refs_6_), channel_id=1, source_target_pairs={{16,17},{17,16},{18,19},{19,18},{20,21},{21,20},{22,23},{23,22}} | collective-permute-start | bytes 1572872 | tf_op jit(solution)/shard_map/ppermute | solution.py:275
  76.0 13.5 %collective-permute-start.19 = (bf16[256,512]{1,0:T(8,128)(2,1)S(1)}, bf16[256,512]{1,0:T(8,128)(2,1)S(1)}, u32[]{:S(2)}, u32[]{:S(2)}) collective-permute-start(bf16[256,512]{1,0:T(8,128)(2,1)S(1)} %add_convert_fusion.1), channel_id=1, source_target_pairs={{8,10},{9,11},{10,8},{11,9},{12,14},{13,15},{14,12},{15,13},{0,2},... | collective-permute-start | bytes 786440 | tf_op jit(solution)/shard_map/ppermute | solution.py:275
  95.7 28.0 %collective-permute-start.23 = (bf16[4,256,512]{2,1,0:T(8,128)(2,1)S(1)}, bf16[4,256,512]{2,1,0:T(8,128)(2,1)S(1)}, u32[]{:S(2)}, u32[]{:S(2)}) collective-permute-start(bf16[4,256,512]{2,1,0:T(8,128)(2,1)S(1)} %pad_maximum_fusion.refs_4_), channel_id=1, source_target_pairs={{8,9},{9,8},{10,11},{11,10},{12,13},{13,12},{14,15},{15,14},{0,1},... | collective-permute-start | bytes 3145736 | tf_op jit(solution)/shard_map/ppermute | solution.py:275
  99.9 23.9 %collective-permute-start.24 = (bf16[256,1024]{1,0:T(8,128)(2,1)S(1)}, bf16[256,1024]{1,0:T(8,128)(2,1)S(1)}, u32[]{:S(2)}, u32[]{:S(2)}) collective-permute-start(bf16[256,1024]{1,0:T(8,128)(2,1)S(1)} %collective-permute-done.22.base_ref.refs_0_), channel_id=1, source_target_pairs={{8,9},{9,8},{10,11},{11,10},{12,13},{13,12},{14,15},{15,14}} | collective-permute-start | bytes 1572872 | tf_op jit(solution)/shard_map/ppermute | solution.py:275
  100.6 23.7 %collective-permute-start.25 = (bf16[256,1024]{1,0:T(8,128)(2,1)S(1)}, bf16[256,1024]{1,0:T(8,128)(2,1)S(1)}, u32[]{:S(2)}, u32[]{:S(2)}) collective-permute-start(bf16[256,1024]{1,0:T(8,128)(2,1)S(1)} %collective-permute-done.22.base_ref.refs_0_), channel_id=1, source_target_pairs={{8,10},{9,11},{10,8},{11,9},{12,14},{13,15},{14,12},{15,13}} | collective-permute-start | bytes 1572872 | tf_op jit(solution)/shard_map/ppermute | solution.py:275
  101.3 23.7 %collective-permute-start.27 = (bf16[256,1024]{1,0:T(8,128)(2,1)S(1)}, bf16[256,1024]{1,0:T(8,128)(2,1)S(1)}, u32[]{:S(2)}, u32[]{:S(2)}) collective-permute-start(bf16[256,1024]{1,0:T(8,128)(2,1)S(1)} %collective-permute-done.22.base_ref.refs_0_), channel_id=1, source_target_pairs={{8,12},{9,13},{10,14},{11,15},{12,8},{13,9},{14,10},{15,11}} | collective-permute-start | bytes 1572872 | tf_op jit(solution)/shard_map/ppermute | solution.py:275
  102.8 24.9 %collective-permute-start.39 = (bf16[4,256,512]{2,1,0:T(8,128)(2,1)S(1)}, bf16[4,256,512]{2,1,0:T(8,128)(2,1)S(1)}, u32[]{:S(2)}, u32[]{:S(2)}) collective-permute-start(bf16[4,256,512]{2,1,0:T(8,128)(2,1)S(1)} %get-tuple-element.62), channel_id=1, source_target_pairs={{24,25},{25,24},{26,27},{27,26},{28,29},{29,28},{30,31},{31,30},{1... | collective-permute-start | bytes 3145736 | tf_op jit(solution)/shard_map/ppermute | solution.py:275
  131.5 31.3 %collective-permute-start.35 = (bf16[256,1024]{1,0:T(8,128)(2,1)S(1)}, bf16[256,1024]{1,0:T(8,128)(2,1)S(1)}, u32[]{:S(2)}, u32[]{:S(2)}) collective-permute-start(bf16[256,1024]{1,0:T(8,128)(2,1)S(1)} %block_dot.23), channel_id=1, source_target_pairs={{8,1},{9,0},{10,3},{11,2},{12,5},{13,4},{14,7},{15,6}} | collective-permute-start | bytes 1572872 | tf_op jit(solution)/shard_map/ppermute | solution.py:275
  132.8 25.4 %collective-permute-start.34 = (bf16[256,1024]{1,0:T(8,128)(2,1)S(1)}, bf16[256,1024]{1,0:T(8,128)(2,1)S(1)}, u32[]{:S(2)}, u32[]{:S(2)}) collective-permute-start(bf16[256,1024]{1,0:T(8,128)(2,1)S(1)} %block_dot.23), channel_id=1, source_target_pairs={{8,0},{9,1},{10,2},{11,3},{12,4},{13,5},{14,6},{15,7}} | collective-permute-start | bytes 1572872 | tf_op jit(solution)/shard_map/ppermute | solution.py:275
  134.1 35.0 %collective-permute-start.33 = (bf16[256,1024]{1,0:T(8,128)(2,1)S(1)}, bf16[256,1024]{1,0:T(8,128)(2,1)S(1)}, u32[]{:S(2)}, u32[]{:S(2)}) collective-permute-start(bf16[256,1024]{1,0:T(8,128)(2,1)S(1)} %block_dot.23), channel_id=1, source_target_pairs={{8,2},{9,3},{10,0},{11,1},{12,6},{13,7},{14,4},{15,5}} | collective-permute-start | bytes 1572872 | tf_op jit(solution)/shard_map/ppermute | solution.py:275
  136.2 35.4 %collective-permute-start.31 = (bf16[256,1024]{1,0:T(8,128)(2,1)S(1)}, bf16[256,1024]{1,0:T(8,128)(2,1)S(1)}, u32[]{:S(2)}, u32[]{:S(2)}) collective-permute-start(bf16[256,1024]{1,0:T(8,128)(2,1)S(1)} %block_dot.23), channel_id=1, source_target_pairs={{8,4},{9,5},{10,6},{11,7},{12,0},{13,1},{14,2},{15,3}} | collective-permute-start | bytes 1572872 | tf_op jit(solution)/shard_map/ppermute | solution.py:275
  137.5 36.0 %collective-permute-start.43 = (bf16[256,512]{1,0:T(8,128)(2,1)S(1)}, bf16[256,512]{1,0:T(8,128)(2,1)S(1)}, u32[]{:S(2)}, u32[]{:S(2)}) collective-permute-start(bf16[256,512]{1,0:T(8,128)(2,1)S(1)} %add_convert_fusion), channel_id=1, source_target_pairs={{24,26},{25,27},{26,24},{27,25},{28,30},{29,31},{30,28},{31,29},{1... | collective-permute-start | bytes 786440 | tf_op jit(solution)/shard_map/ppermute | solution.py:275
  158.2 15.3 %collective-permute-start.45 = (bf16[256,512]{1,0:T(8,128)(2,1)S(1)}, bf16[256,512]{1,0:T(8,128)(2,1)S(1)}, u32[]{:S(2)}, u32[]{:S(2)}) collective-permute-start(bf16[256,512]{1,0:T(8,128)(2,1)S(1)} %collective-permute-done.44), channel_id=1, source_target_pairs={{24,26},{25,27},{26,24},{27,25},{28,30},{29,31},{30,28},{31,29},{1... | collective-permute-start | bytes 786440 | tf_op jit(solution)/shard_map/ppermute | solution.py:275
  169.1 11.1 %collective-permute-start.36 = (bf16[256,1024]{1,0:T(8,128)(2,1)S(1)}, bf16[256,1024]{1,0:T(8,128)(2,1)S(1)}, u32[]{:S(2)}, u32[]{:S(2)}) collective-permute-start(bf16[256,1024]{1,0:T(8,128)(2,1)S(1)} %collective-permute-done.33.refs_0_), channel_id=1, source_target_pairs={{0,1},{1,0},{2,3},{3,2},{4,5},{5,4},{6,7},{7,6}} | collective-permute-start | bytes 1572872 | tf_op jit(solution)/shard_map/ppermute | solution.py:275
  171.6 11.1 %collective-permute-start.32 = (bf16[256,1024]{1,0:T(8,128)(2,1)S(1)}, bf16[256,1024]{1,0:T(8,128)(2,1)S(1)}, u32[]{:S(2)}, u32[]{:S(2)}) collective-permute-start(bf16[256,1024]{1,0:T(8,128)(2,1)S(1)} %collective-permute-done.31.refs_0_), channel_id=1, source_target_pairs={{0,2},{1,3},{2,0},{3,1},{4,6},{5,7},{6,4},{7,5}} | collective-permute-start | bytes 1572872 | tf_op jit(solution)/shard_map/ppermute | solution.py:275
  173.7 22.3 %collective-permute-start.46 = (bf16[4,256,512]{2,1,0:T(8,128)(2,1)S(1)}, bf16[4,256,512]{2,1,0:T(8,128)(2,1)S(1)}, u32[]{:S(2)}, u32[]{:S(2)}) collective-permute-start(bf16[4,256,512]{2,1,0:T(8,128)(2,1)S(1)} %pad_maximum_fusion.1.refs_6_), channel_id=1, source_target_pairs={{24,25},{25,24},{26,27},{27,26},{28,29},{29,28},{30,31},{31,30},{1... | collective-permute-start | bytes 3145736 | tf_op jit(solution)/shard_map/ppermute | solution.py:275
  174.4 11.6 %collective-permute-start.38 = (bf16[256,1024]{1,0:T(8,128)(2,1)S(1)}, bf16[256,1024]{1,0:T(8,128)(2,1)S(1)}, u32[]{:S(2)}, u32[]{:S(2)}) collective-permute-start(bf16[256,1024]{1,0:T(8,128)(2,1)S(1)} %collective-permute-done.31.refs_0_), channel_id=1, source_target_pairs={{0,1},{1,0},{2,3},{3,2},{4,5},{5,4},{6,7},{7,6}} | collective-permute-start | bytes 1572872 | tf_op jit(solution)/shard_map/ppermute | solution.py:275
  182.7 11.1 %collective-permute-start.37 = (bf16[256,1024]{1,0:T(8,128)(2,1)S(1)}, bf16[256,1024]{1,0:T(8,128)(2,1)S(1)}, u32[]{:S(2)}, u32[]{:S(2)}) collective-permute-start(bf16[256,1024]{1,0:T(8,128)(2,1)S(1)} %collective-permute-done.32.refs_2_), channel_id=1, source_target_pairs={{0,1},{1,0},{2,3},{3,2},{4,5},{5,4},{6,7},{7,6}} | collective-permute-start | bytes 1572872 | tf_op jit(solution)/shard_map/ppermute | solution.py:275
  (18 other events, 94.3 us)

commit v8 on v7

--- a/solution.py
+++ b/solution.py
@@ -23,7 +23,7 @@
     return ref.at[part, :] if axis == 0 else ref.at[:, part]
 
 
-def resident(at, weights):
+def resident(at, weights, only=None):
     count = at.shape[0] - 1
     depth, cols = weights.shape[0] // count, weights.shape[1]
 
@@ -33,10 +33,12 @@
                 run_of(weights_ref, 0, at[1 + i], depth), out_ref.at[i], sems.at[i]
             )
 
-        for i in range(count):
-            copy(i).start()
-        for i in range(count):
-            copy(i).wait()
+        @pl.when((at[0] == only) if only is not None else (at[0] >= 0))
+        def _():
+            for i in range(count):
+                copy(i).start()
+            for i in range(count):
+                copy(i).wait()
 
     return pl.pallas_call(
         body,
@@ -55,34 +57,35 @@
     width = 256 if cols % 256 == 0 else cols
     count = len(blocks)
 
-    def body(at, weights_ref, base_ref, *refs):
+    def body(at, weights_ref, *refs):
         @pl.when(at[0] == turn)
         def _():
             def tile(j, _):
                 here = pl.ds(pl.multiple_of(j * width, width), width)
-                total = base_ref[:, here].astype(jnp.float32)
+                total = None if base is None else refs[count][:, here].astype(jnp.float32)
                 for block_ref, part in zip(refs[:count], parts):
-                    total += jnp.dot(
+                    product = jnp.dot(
                         block_ref[...],
                         weights_ref[part, :, here],
                         preferred_element_type=jnp.float32,
                     )
-                refs[count][:, here] = total.astype(out_type)
+                    total = product if total is None else total + product
+                refs[-1][:, here] = total.astype(out_type)
                 return 0
 
             lax.fori_loop(0, cols // width, tile, 0)
 
     return pl.pallas_call(
         body,
-        in_specs=[SMEM] + [VMEM] * (count + 2),
+        in_specs=[SMEM] + [VMEM] * (1 + count + (base is not None)),
         out_specs=VMEM,
         out_shape=jax.ShapeDtypeStruct((rows, cols), out_type),
         compiler_params=params(4),
         name="block_dot",
-    )(at, weights, base, *blocks)
-
-
-def stream_dot(at, turn, blocks, weights, parts, base, out_type):
+    )(at, weights, *blocks, *([] if base is None else [base]))
+
+
+def stream_dot(at, turn, blocks, weights, parts, out_type):
     rows, depth = blocks[0].shape
     cols = weights.shape[1]
     count = len(blocks)
@@ -99,7 +102,7 @@
         def _():
             for k in range(count):
                 copy(k).start()
-            total = None if base is None else refs[count][...]
+            total = None
             for k in range(count):
                 copy(k).wait()
                 part = jnp.dot(block_refs[k][...], runs[k], preferred_element_type=jnp.float32)
@@ -108,7 +111,7 @@
 
     return pl.pallas_call(
         body,
-        in_specs=[SMEM, HBM] + [VMEM] * (count + (base is not None)),
+        in_specs=[SMEM, HBM] + [VMEM] * count,
         out_specs=VMEM,
         out_shape=jax.ShapeDtypeStruct((rows, cols), out_type),
         scratch_shapes=[
@@ -117,15 +120,16 @@
         ],
         compiler_params=params(14),
         name="stream_dot",
-    )(at, in_hbm(weights), *blocks, *([] if base is None else [base]))
-
-
-def partials(at, among, inputs, weights, inner):
+    )(at, in_hbm(weights), *blocks)
+
+
+def partials(at, among, inputs, weights, inner, after):
     rows, depth = inputs.shape
     count = at.shape[0] - 1
     width = weights.shape[1] // count
 
     def body(at, weights_ref, inputs_ref, *refs):
+        refs = refs[len(after) :]
         out_refs, (runs, sems) = refs[:inner], refs[inner:]
         order = [n for dx in [*range(1, inner), 0] for n in range(dx, count, inner)]
 
@@ -146,7 +150,7 @@
 
     return pl.pallas_call(
         body,
-        in_specs=[SMEM, HBM, VMEM],
+        in_specs=[SMEM, HBM, VMEM] + [VMEM] * len(after),
         out_specs=[VMEM] * inner,
         out_shape=[
             jax.ShapeDtypeStruct((count // inner, rows, width), jnp.bfloat16 if dx else jnp.float32)
@@ -158,7 +162,7 @@
         ],
         compiler_params=params(14),
         name="partials",
-    )(at, in_hbm(weights), inputs)
+    )(at, in_hbm(weights), inputs, *after)
 
 
 def added(at, among, own, arrived):
@@ -188,15 +192,16 @@
     )(at, own, *arrived)
 
 
-def mean_square(at, half, rot_outs, low, high, micro, seq):
+def mean_square(at, half, rot_outs, low, high, low_runs, high_runs, micro, seq):
     _, rows, width = low[0].shape
     eig_rows = rot_outs[0].shape[1]
-    count, inner, sections = at.shape[0] - 1, len(low), len(rot_outs)
+    count, sections = len(low_runs), len(rot_outs)
 
     def body(at, *refs):
         rot_refs, refs = refs[:sections], refs[sections:]
-        low_refs, high_refs = refs[:inner], refs[inner : 2 * inner]
-        eig_ref, rot, block, result, sems = refs[2 * inner :]
+        low_refs, refs = refs[: len(low)], refs[len(low) :]
+        high_refs, refs = refs[: len(high)], refs[len(high) :]
+        eig_ref, rot, block, result, sems = refs
         for s in range(sections):
 
             @pl.when(at[0] == s)
@@ -212,11 +217,13 @@
 
             @pl.when(at[0] >= half)
             def _():
-                block[...] = high_refs[n % inner][n // inner]
+                a, i = high_runs[n]
+                block[...] = high_refs[a][i]
 
             @pl.when(at[0] < half)
             def _():
-                block[...] = low_refs[n % inner][n // inner]
+                a, i = low_runs[n]
+                block[...] = low_refs[a][i]
 
             if n >= 2:
                 copy(n - 2).wait()
@@ -237,7 +244,7 @@
 
     return pl.pallas_call(
         body,
-        in_specs=[SMEM] + [VMEM] * (sections + 2 * inner),
+        in_specs=[SMEM] + [VMEM] * (sections + len(low) + len(high)),
         out_specs=HBM,
         out_shape=jax.ShapeDtypeStruct((eig_rows, count * width), jnp.float32),
         scratch_shapes=[
@@ -295,7 +302,10 @@
             near, side = spread(own, [(turn, turn)])
         return {0: own, **near}, side
 
-    def relay(turn, sent, before, within):
+    order = [0] + [1 << p for p in reversed(range(outer.bit_length() - 1))]
+    order += [dz for dz in range(outer) if dz not in order]
+
+    def relay(turn, sent, before, within, matrix):
         near, side = sent
         got = along_outer(near, [(turn, turn)])
         start, *_ = lax.optimization_barrier((near[0], *before))
@@ -303,37 +313,38 @@
         def products(dots, base, last):
             blocks, parts = [block for block, _ in dots], [part for _, part in dots]
             out_type = jnp.bfloat16 if last else jnp.float32
-            if turn == 0:
-                return stream_dot(at, turn, blocks, out_cols, parts, base, out_type)
-            return block_dot(at, turn, blocks, weights, parts, base, out_type)
+            return block_dot(at, turn, blocks, matrix, parts, base, out_type)
 
         blocks = {(0, 0): start, **{(0, dx): block for dx, block in side.items()}}
         dots = [(block, dx) for (_, dx), block in blocks.items()]
         totals = [products(dots, None if turn == 0 else start, outer == 1)]
-        for dz in range(1, outer + 1):
-            if dz < outer:
+        for n in range(1, outer + 1):
+            if n < outer:
+                dz = order[n]
+                ties = [totals[0]] + [blocks[order[max(0, n - 2)], dx] for dx in range(1, inner)]
                 block, *_ = lax.optimization_barrier(
-                    (got[dz], totals[max(0, dz - 2)], *(within if dz == outer - 1 else []))
+                    (got[dz], *ties, *(within if n == outer - 1 else []))
                 )
                 blocks[dz, 0] = got[dz]
                 for dx in range(1, inner):
                     blocks[dz, dx] = moved(block, dx, [(turn, turn)])
-            if dz > 1:
-                dots = [(blocks[dz - 1, dx], (dz - 1) * inner + dx) for dx in range(inner)]
-                if dz == outer - 1:
-                    dots.append((blocks[dz, 0], dz * inner))
-                if dz == outer and outer > 2 and inner > 1:
+            if n > 1:
+                dz = order[n - 1]
+                dots = [(blocks[dz, dx], dz * inner + dx) for dx in range(inner)]
+                if n == outer - 1:
+                    dots.append((blocks[order[n], 0], order[n] * inner))
+                if n == outer and outer > 2 and inner > 1:
                     dots = dots[1:]
-                totals.append(products(dots, totals[-1], dz == outer))
+                totals.append(products(dots, totals[-1], n == outer))
         return totals[-1], blocks
 
     def rotated(turn, blocks):
         parts = [dz * inner + dx for dz, dx in blocks]
-        return stream_dot(at, turn, list(blocks.values()), out_cols, parts, None, jnp.bfloat16)
-
-    def rotate_begin(inputs, among):
+        return stream_dot(at, turn, list(blocks.values()), out_cols, parts, jnp.bfloat16)
+
+    def rotate_begin(inputs, among, after=()):
         pairs = [(a, a) for a in among]
-        own, *others = partials(at, among, inputs, basis_in[0], inner)
+        own, *others = partials(at, among, inputs, basis_in[0], inner, after)
         return own, others, [moved(other, 1 + n, pairs) for n, other in enumerate(others)]
 
     def summed(sums, among):
@@ -343,15 +354,16 @@
             own = own + moved(part, dz * inner, pairs).astype(jnp.float32)
         return own.astype(jnp.bfloat16)
 
-    def outer_columns(own, among):
+    def outer_columns(own, among, halves):
         pairs = [(a, a) for a in among]
         powers = [1 << p for p in range(outer.bit_length() - 1)]
         near = {0: own, **{dz: moved(own, dz * inner, pairs) for dz in reversed(powers)}}
         got = along_outer(near, pairs)
-        return jnp.stack([got[dz] for dz in range(outer)])
-
-    def all_columns(column, among):
-        return [column] + [moved(column, dx, [(a, a) for a in among]) for dx in range(1, inner)]
+        return [jnp.stack([got[dz] for dz in some]) for some in halves]
+
+    def all_columns(columns, among):
+        pairs = [(a, a) for a in among]
+        return [[c] + [moved(c, dx, pairs) for dx in range(1, inner)] for c in columns]
 
     upper = list(range(sections - 1, half - 1, -1))
     lower = list(range(half - 1, -1, -1))
@@ -360,34 +372,44 @@
     low_own, low_others, low_arrived = rotate_begin(inputs, lower)
     near, side = spread(top, [(upper[0], upper[0])])
     weights = resident(at, weights)
+    halves = [order]
     sums = added(at, lower, low_own, low_arrived)
     low = summed(sums, lower)
     sent, before, within = ({0: top, **near}, side), low_others, sums
     for turn in upper:
-        grad, blocks = relay(turn, sent, before, within)
-        within = []
+        grad, blocks = relay(turn, sent, before, within, weights)
         if turn != upper[-1]:
             sent = handed_down(grad, turn - 1)
             rot_outs[turn] = rotated(turn, blocks)
-            before = [rot_outs[turn], low]
-    low = outer_columns(low, lower)
+            before, within = [low], [rot_outs[turn]]
+    low = outer_columns(low, lower, halves)
     grad, low = lax.optimization_barrier((grad, low))
     sent = handed_down(grad, lower[0])
+    done = moved(grad[:16, :128], 0, [(upper[-1], a) for a in upper[:1]])
     low = all_columns(low, lower)
     rot_outs[upper[-1]] = rotated(upper[-1], blocks)
-    inputs, _ = lax.optimization_barrier((inputs, sent[0][0]))
-    high_own, _, high_arrived = rotate_begin(inputs, upper)
-    before = [rot_outs[upper[-1]], *low]
+    inputs, *_ = lax.optimization_barrier((inputs, sent[0][0]))
+    last_cols = resident(at, out_cols, 0)
+    high_own, _, high_arrived = rotate_begin(inputs, upper, [done])
+    before, within = [], [rot_outs[upper[-1]], *jax.tree.leaves(low)]
     for turn in lower:
-        grad, blocks = relay(turn, sent, before, [])
+        grad, blocks = relay(turn, sent, before, within, weights if turn else last_cols)
         if turn != 0:
             sent = handed_down(grad, turn - 1)
             rot_outs[turn] = rotated(turn, blocks)
-            before = [rot_outs[turn]]
+            before, within = [], [rot_outs[turn]]
     rot_outs[0] = grad
     sums = added(at, upper, high_own, high_arrived)
-    high = all_columns(outer_columns(summed(sums, upper), upper), upper)
-    return mean_square(at, half, rot_outs, low, high, micro, seq)[None]
+    high = all_columns(outer_columns(summed(sums, upper), upper, [order]), upper)
+
+    def runs(parts):
+        place = {dz: (a, i) for a, some in enumerate(parts) for i, dz in enumerate(some)}
+        return [(place[p // inner][0] * inner + p % inner, place[p // inner][1]) for p in range(shards)]
+
+    low, high = jax.tree.leaves(low), jax.tree.leaves(high)
+    return mean_square(
+        at, half, rot_outs, low, high, runs(halves), runs([order]), micro, seq
+    )[None]
 
 
 def solution(mesh):

time: 209 us -> 230 us (1.10)
  the two profiles are of different devices: /device:TPU:0 before, /device:TPU:22 now
where the time goes in v8:
time: 230 us; the launch traced here: 229 us
  waiting for transfers between devices  101 us (44%)
  starting transfers between devices  75.9 us (33%)
  Pallas kernels  48.9 us (21%)
    ppermute x48, waiting for transfers between devices, moved(): return lax.ppermute(block, ('section', 'shard'), route)  101 us
    ppermute x48, starting transfers between devices, moved(): return lax.ppermute(block, ('section', 'shard'), route)  75.9 us
    pallas_call x16, Pallas kernels, block_dot(): pl.pallas_call(body, in_specs=[SMEM] + [VMEM] * (1 + count + (base is not...  16.2 us
    pallas_call x1, Pallas kernels, mean_square(): pl.pallas_call(body, in_specs=[SMEM] + [VMEM] * (sections + len(low) + le...  12.2 us
    pallas_call x2, Pallas kernels, resident(): pl.pallas_call(body, in_specs=[SMEM, HBM], out_specs=VMEM, out_shape=jax....  7.11 us
    pallas_call x3, Pallas kernels, stream_dot(): pl.pallas_call(body, in_specs=[SMEM, HBM] + [VMEM] * count, out_specs=VME...  6.07 us
    pallas_call x2, Pallas kernels, partials(): pl.pallas_call(body, in_specs=[SMEM, HBM, VMEM] + [VMEM] * len(after), ou...  5.98 us
  transfers between devices with their start and end apart: 48, of which 13 were waited for; matrix products, arithmetic and copies ran while one was open for 0% of the time, Pallas kernels for 15%

profile of v8, /device:TPU:22, one launch (start us, length us, event | category | flops | bytes accessed | tf_op | source)
XLA Modules:
  0.0 228.7 jit_solution(6880938971417964930)
XLA Ops:
  4.7 6.5 %resident.3.weights_ref = bf16[8,1024,1024]{2,1,0:T(8,128)(2,1)S(1)} custom-call(s32[9]{0:T(128)S(1)} %stack.69.at, bf16[8192,1024]{1,0:T(8,128)(2,1)} %bitcast.37), custom_call_target="tpu_custom_call" | custom-call | tf_op jit(solution)/shard_map/resident/pallas_call | solution.py:43
  24.3 21.9 %collective-permute-done.10.refs_0_.refs_2_ = bf16[256,1024]{1,0:T(8,128)(2,1)S(1)} collective-permute-done((bf16[256,1024]{1,0:T(8,128)(2,1)S(1)}, bf16[256,1024]{1,0:T(8,128)(2,1)S(1)}, u32[]{:S(2)}, u32[]{:S(2)}) %collective-permute-start.10) | collective-permute-done | bytes 524320 | tf_op jit(solution)/shard_map/ppermute | solution.py:282
  46.2 7.6 %collective-permute-done.14.refs_1_ = bf16[256,1024]{1,0:T(8,128)(2,1)S(1)} collective-permute-done((bf16[256,1024]{1,0:T(8,128)(2,1)S(1)}, bf16[256,1024]{1,0:T(8,128)(2,1)S(1)}, u32[]{:S(2)}, u32[]{:S(2)}) %collective-permute-start.14) | collective-permute-done | bytes 524320 | tf_op jit(solution)/shard_map/ppermute | solution.py:282
  53.8 2.4 %block_dot.20.refs_2_ = f32[256,1024]{1,0:T(8,128)S(1)} custom-call(s32[9]{0:T(128)S(1)} %stack.69.at, bf16[8,1024,1024]{2,1,0:T(8,128)(2,1)S(1)} %resident.3.weights_ref, bf16[256,1024]{1,0:T(8,128)(2,1)S(1)} %collective-permute-done.10.refs_0_.refs_2_, bf16[256,1024]{1,0:T(8,128)(2,1)S(1)} %collective-permute-done.14.refs_1_, ...), custom_call_target="tpu_custom_call" | custom-call | tf_op jit(solution)/shard_map/block_dot/pallas_call | solution.py:78
  56.6 3.1 %collective-permute-start.15 = (bf16[256,1024]{1,0:T(8,128)(2,1)S(1)}, bf16[256,1024]{1,0:T(8,128)(2,1)S(1)}, u32[]{:S(2)}, u32[]{:S(2)}) collective-permute-start(bf16[256,1024]{1,0:T(8,128)(2,1)S(1)} %collective-permute-done.8.refs_0_.refs_2_), channel_id=1, source_target_pairs={{16,17},{17,16},{18,19},{19,18},{20,21},{21,20},{22,23},{23,22}} | collective-permute-start | bytes 1572872 | tf_op jit(solution)/shard_map/ppermute | solution.py:282
  59.7 7.9 %collective-permute-start.9 = (bf16[256,1024]{1,0:T(8,128)(2,1)S(1)}, bf16[256,1024]{1,0:T(8,128)(2,1)S(1)}, u32[]{:S(2)}, u32[]{:S(2)}) collective-permute-start(bf16[256,1024]{1,0:T(8,128)(2,1)S(1)} %collective-permute-done.8.refs_0_.refs_2_), channel_id=1, source_target_pairs={{16,18},{17,19},{18,16},{19,17},{20,22},{21,23},{22,20},{23,21}} | collective-permute-start | bytes 1572872 | tf_op jit(solution)/shard_map/ppermute | solution.py:282
  69.0 2.7 %collective-permute-start.18 = (bf16[256,1024]{1,0:T(8,128)(2,1)S(1)}, bf16[256,1024]{1,0:T(8,128)(2,1)S(1)}, u32[]{:S(2)}, u32[]{:S(2)}) collective-permute-start(bf16[256,1024]{1,0:T(8,128)(2,1)S(1)} %collective-permute-done.17.refs_0_.refs_4_), channel_id=1, source_target_pairs={{16,17},{17,16},{18,19},{19,18},{20,21},{21,20},{22,23},{23,22}} | collective-permute-start | bytes 1572872 | tf_op jit(solution)/shard_map/ppermute | solution.py:282
  71.7 3.1 %collective-permute-done.9.refs_2_.refs_6_ = bf16[256,1024]{1,0:T(8,128)(2,1)S(1)} collective-permute-done((bf16[256,1024]{1,0:T(8,128)(2,1)S(1)}, bf16[256,1024]{1,0:T(8,128)(2,1)S(1)}, u32[]{:S(2)}, u32[]{:S(2)}) %collective-permute-start.9) | collective-permute-done | bytes 524320 | tf_op jit(solution)/shard_map/ppermute | solution.py:282
  74.8 2.7 %collective-permute-start.16 = (bf16[256,1024]{1,0:T(8,128)(2,1)S(1)}, bf16[256,1024]{1,0:T(8,128)(2,1)S(1)}, u32[]{:S(2)}, u32[]{:S(2)}) collective-permute-start(bf16[256,1024]{1,0:T(8,128)(2,1)S(1)} %collective-permute-done.9.refs_2_.refs_6_), channel_id=1, source_target_pairs={{16,17},{17,16},{18,19},{19,18},{20,21},{21,20},{22,23},{23,22}} | collective-permute-start | bytes 1572872 | tf_op jit(solution)/shard_map/ppermute | solution.py:282
  79.0 2.4 %block_dot.21.refs_3_ = f32[256,1024]{1,0:T(8,128)S(1)} custom-call(s32[9]{0:T(128)S(1)} %stack.69.at, bf16[8,1024,1024]{2,1,0:T(8,128)(2,1)S(1)} %resident.3.weights_ref, bf16[256,1024]{1,0:T(8,128)(2,1)S(1)} %collective-permute-done.8.refs_0_.refs_2_, bf16[256,1024]{1,0:T(8,128)(2,1)S(1)} %collective-permute-done.15.refs_1_.refs_3_, ...), custom_call_target="tpu_custom_call" | custom-call | tf_op jit(solution)/shard_map/block_dot/pallas_call | solution.py:78
  81.5 3.0 %block_dot.22.refs_1_ = f32[256,1024]{1,0:T(8,128)S(1)} custom-call(s32[9]{0:T(128)S(1)} %stack.69.at, bf16[8,1024,1024]{2,1,0:T(8,128)(2,1)S(1)} %resident.3.weights_ref, bf16[256,1024]{1,0:T(8,128)(2,1)S(1)} %collective-permute-done.17.refs_0_.refs_4_, bf16[256,1024]{1,0:T(8,128)(2,1)S(1)} %collective-permute-done.18.refs_1_.refs_5_, ...), custom_call_target="tpu_custom_call" | custom-call | tf_op jit(solution)/shard_map/block_dot/pallas_call | solution.py:78
  84.5 1.4 collective-permute-done.16.refs_0_.refs_7_
  85.8 1.8 block_dot.23
  87.7 3.4 %collective-permute-start.22 = (bf16[256,1024]{1,0:T(8,128)(2,1)S(1)}, bf16[256,1024]{1,0:T(8,128)(2,1)S(1)}, u32[]{:S(2)}, u32[]{:S(2)}) collective-permute-start(bf16[256,1024]{1,0:T(8,128)(2,1)S(1)} %block_dot.23), channel_id=1, source_target_pairs={{16,8},{17,9},{18,10},{19,11},{20,12},{21,13},{22,14},{23,15}} | collective-permute-start | bytes 1572872 | tf_op jit(solution)/shard_map/ppermute | solution.py:282
  91.1 6.6 %collective-permute-done.22.refs_0_.refs_2_ = bf16[256,1024]{1,0:T(8,128)(2,1)S(1)} collective-permute-done((bf16[256,1024]{1,0:T(8,128)(2,1)S(1)}, bf16[256,1024]{1,0:T(8,128)(2,1)S(1)}, u32[]{:S(2)}, u32[]{:S(2)}) %collective-permute-start.22) | collective-permute-done | bytes 524320 | tf_op jit(solution)/shard_map/ppermute | solution.py:282
  102.0 5.4 %partials.3 = (f32[4,256,512]{2,1,0:T(8,128)S(1)}, bf16[4,256,512]{2,1,0:T(8,128)(2,1)S(1)}) custom-call(s32[9]{0:T(128)S(1)} %stack.69.at, bf16[1024,4096]{1,0:T(8,128)(2,1)} %bitcast.36, bf16[256,1024]{1,0:T(8,128)(2,1)S(1)} %bitcast.30, bf16[16,128]{1,0:T(8,128)(2,1)S(1)} %collective-permute-done.39.refs_0_), custom_call_target="tpu_custom_call" | custom-call | tf_op jit(solution)/shard_map/partials/pallas_call | solution.py:151
  107.4 2.4 %collective-permute-start.40 = (bf16[4,256,512]{2,1,0:T(8,128)(2,1)S(1)}, bf16[4,256,512]{2,1,0:T(8,128)(2,1)S(1)}, u32[]{:S(2)}, u32[]{:S(2)}) collective-permute-start(bf16[4,256,512]{2,1,0:T(8,128)(2,1)S(1)} %get-tuple-element.58), channel_id=1, source_target_pairs={{24,25},{25,24},{26,27},{27,26},{28,29},{29,28},{30,31},{31,30},{1... | collective-permute-start | bytes 3145736 | tf_op jit(solution)/shard_map/ppermute | solution.py:282
  112.5 4.8 %stream_dot.4.refs_2_ = bf16[256,512]{1,0:T(8,128)(2,1)S(1)} custom-call(s32[9]{0:T(128)S(1)} %stack.69.at, bf16[8192,512]{1,0:T(8,128)(2,1)} %bitcast.32, bf16[256,1024]{1,0:T(8,128)(2,1)S(1)} %collective-permute-done.10.refs_0_.refs_2_, bf16[256,1024]{1,0:T(8,128)(2,1)S(1)} %collective-permute-done.14.refs_1_, ...), custom_call_target="tpu_custom_call" | custom-call | tf_op jit(solution)/shard_map/stream_dot/pallas_call | solution.py:112
  118.8 15.9 %collective-permute-done.40.refs_0_ = bf16[4,256,512]{2,1,0:T(8,128)(2,1)S(1)} collective-permute-done((bf16[4,256,512]{2,1,0:T(8,128)(2,1)S(1)}, bf16[4,256,512]{2,1,0:T(8,128)(2,1)S(1)}, u32[]{:S(2)}, u32[]{:S(2)}) %collective-permute-start.40) | collective-permute-done | bytes 1048608 | tf_op jit(solution)/shard_map/ppermute | solution.py:282
  135.4 3.2 %collective-permute-start.41 = (bf16[256,512]{1,0:T(8,128)(2,1)S(1)}, bf16[256,512]{1,0:T(8,128)(2,1)S(1)}, u32[]{:S(2)}, u32[]{:S(2)}) collective-permute-start(bf16[256,512]{1,0:T(8,128)(2,1)S(1)} %get-tuple-element.60), channel_id=1, source_target_pairs={{24,26},{25,27},{26,24},{27,25},{28,30},{29,31},{30,28},{31,29},{1... | collective-permute-start | bytes 786440 | tf_op jit(solution)/shard_map/ppermute | solution.py:282
  138.6 5.9 %collective-permute-start.42 = (bf16[256,512]{1,0:T(8,128)(2,1)S(1)}, bf16[256,512]{1,0:T(8,128)(2,1)S(1)}, u32[]{:S(2)}, u32[]{:S(2)}) collective-permute-start(bf16[256,512]{1,0:T(8,128)(2,1)S(1)} %get-tuple-element.61), channel_id=1, source_target_pairs={{24,28},{25,29},{26,30},{27,31},{28,24},{29,25},{30,26},{31,27},{1... | collective-permute-start | bytes 786440 | tf_op jit(solution)/shard_map/ppermute | solution.py:282
  144.5 2.5 %collective-permute-start.43 = (bf16[256,512]{1,0:T(8,128)(2,1)S(1)}, bf16[256,512]{1,0:T(8,128)(2,1)S(1)}, u32[]{:S(2)}, u32[]{:S(2)}) collective-permute-start(bf16[256,512]{1,0:T(8,128)(2,1)S(1)} %get-tuple-element.62), channel_id=1, source_target_pairs={{24,30},{25,31},{26,28},{27,29},{28,26},{29,27},{30,24},{31,25},{1... | collective-permute-start | bytes 786440 | tf_op jit(solution)/shard_map/ppermute | solution.py:282
  150.8 11.5 %collective-permute-done.42 = bf16[256,512]{1,0:T(8,128)(2,1)S(1)} collective-permute-done((bf16[256,512]{1,0:T(8,128)(2,1)S(1)}, bf16[256,512]{1,0:T(8,128)(2,1)S(1)}, u32[]{:S(2)}, u32[]{:S(2)}) %collective-permute-start.42) | collective-permute-done | bytes 262176 | tf_op jit(solution)/shard_map/ppermute | solution.py:282
  162.3 5.3 %collective-permute-done.43 = bf16[256,512]{1,0:T(8,128)(2,1)S(1)} collective-permute-done((bf16[256,512]{1,0:T(8,128)(2,1)S(1)}, bf16[256,512]{1,0:T(8,128)(2,1)S(1)}, u32[]{:S(2)}, u32[]{:S(2)}) %collective-permute-start.43) | collective-permute-done | bytes 262176 | tf_op jit(solution)/shard_map/ppermute | solution.py:282
  167.7 1.9 collective-permute-start.44
  169.7 4.9 %collective-permute-start.45 = (bf16[256,512]{1,0:T(8,128)(2,1)S(1)}, bf16[256,512]{1,0:T(8,128)(2,1)S(1)}, u32[]{:S(2)}, u32[]{:S(2)}) collective-permute-start(bf16[256,512]{1,0:T(8,128)(2,1)S(1)} %add_convert_fusion), channel_id=1, source_target_pairs={{24,26},{25,27},{26,24},{27,25},{28,30},{29,31},{30,28},{31,29},{1... | collective-permute-start | bytes 786440 | tf_op jit(solution)/shard_map/ppermute | solution.py:282
  174.5 5.4 %collective-permute-done.44 = bf16[256,512]{1,0:T(8,128)(2,1)S(1)} collective-permute-done((bf16[256,512]{1,0:T(8,128)(2,1)S(1)}, bf16[256,512]{1,0:T(8,128)(2,1)S(1)}, u32[]{:S(2)}, u32[]{:S(2)}) %collective-permute-start.44) | collective-permute-done | bytes 262176 | tf_op jit(solution)/shard_map/ppermute | solution.py:282
  179.9 5.6 %collective-permute-start.46 = (bf16[256,512]{1,0:T(8,128)(2,1)S(1)}, bf16[256,512]{1,0:T(8,128)(2,1)S(1)}, u32[]{:S(2)}, u32[]{:S(2)}) collective-permute-start(bf16[256,512]{1,0:T(8,128)(2,1)S(1)} %collective-permute-done.44), channel_id=1, source_target_pairs={{24,26},{25,27},{26,24},{27,25},{28,30},{29,31},{30,28},{31,29},{1... | collective-permute-start | bytes 786440 | tf_op jit(solution)/shard_map/ppermute | solution.py:282
  188.9 2.1 collective-permute-done.46
  191.1 2.4 %collective-permute-start.47 = (bf16[4,256,512]{2,1,0:T(8,128)(2,1)S(1)}, bf16[4,256,512]{2,1,0:T(8,128)(2,1)S(1)}, u32[]{:S(2)}, u32[]{:S(2)}) collective-permute-start(bf16[4,256,512]{2,1,0:T(8,128)(2,1)S(1)} %pad_maximum_fusion.1.refs_6_), channel_id=1, source_target_pairs={{24,25},{25,24},{26,27},{27,26},{28,29},{29,28},{30,31},{31,30},{1... | collective-permute-start | bytes 3145736 | tf_op jit(solution)/shard_map/ppermute | solution.py:282
  197.3 19.1 %collective-permute-done.47.refs_7_ = bf16[4,256,512]{2,1,0:T(8,128)(2,1)S(1)} collective-permute-done((bf16[4,256,512]{2,1,0:T(8,128)(2,1)S(1)}, bf16[4,256,512]{2,1,0:T(8,128)(2,1)S(1)}, u32[]{:S(2)}, u32[]{:S(2)}) %collective-permute-start.47) | collective-permute-done | bytes 1048608 | tf_op jit(solution)/shard_map/ppermute | solution.py:282
  216.4 12.2 %mean_square.1 = f32[512,4096]{1,0:T(8,128)} custom-call(s32[9]{0:T(128)S(1)} %stack.69.at, bf16[256,512]{1,0:T(8,128)(2,1)S(1)} %block_dot.31.refs_0_, bf16[256,512]{1,0:T(8,128)(2,1)S(1)} %stream_dot.5.refs_1_, bf16[256,512]{1,0:T(8,128)(2,1)S(1)} %stream_dot.4.refs_2_, bf16[256,512]{1,0:T(8,128)(2,1)S(1)} %stream_dot.3.refs_3_, ...), custom_call_target="tpu_custom_call" | custom-call | tf_op jit(solution)/shard_map/mean_square/pallas_call | solution.py:245
  (102 shorter events, 40.8 us)
Async XLA Ops:
  0.0 11.2 %collective-permute-start.2 = (bf16[256,1024]{1,0:T(8,128)(2,1)}, bf16[256,1024]{1,0:T(8,128)(2,1)S(1)}, u32[]{:S(2)}, u32[]{:S(2)}) collective-permute-start(bf16[256,1024]{1,0:T(8,128)(2,1)} %bitcast.23), channel_id=1, source_target_pairs={{24,25},{25,24},{26,27},{27,26},{28,29},{29,28},{30,31},{31,30}} | collective-permute-start | bytes 1572872 | tf_op jit(solution)/shard_map/ppermute | solution.py:282
  0.8 11.0 %collective-permute-start = (bf16[256,1024]{1,0:T(8,128)(2,1)}, bf16[256,1024]{1,0:T(8,128)(2,1)S(1)}, u32[]{:S(2)}, u32[]{:S(2)}) collective-permute-start(bf16[256,1024]{1,0:T(8,128)(2,1)} %bitcast.24), channel_id=1, source_target_pairs={{24,28},{25,29},{26,30},{27,31},{28,24},{29,25},{30,26},{31,27}} | collective-permute-start | bytes 1572872 | tf_op jit(solution)/shard_map/ppermute | solution.py:282
  3.3 10.6 %collective-permute-start.4 = (bf16[4,256,512]{2,1,0:T(8,128)(2,1)S(1)}, bf16[4,256,512]{2,1,0:T(8,128)(2,1)S(1)}, u32[]{:S(2)}, u32[]{:S(2)}) collective-permute-start(bf16[4,256,512]{2,1,0:T(8,128)(2,1)S(1)} %get-tuple-element.34), channel_id=1, source_target_pairs={{8,9},{9,8},{10,11},{11,10},{12,13},{13,12},{14,15},{15,14},{0,1},... | collective-permute-start | bytes 3145736 | tf_op jit(solution)/shard_map/ppermute | solution.py:282
  4.0 9.2 %collective-permute-start.6 = (bf16[256,1024]{1,0:T(8,128)(2,1)S(1)}, bf16[256,1024]{1,0:T(8,128)(2,1)S(1)}, u32[]{:S(2)}, u32[]{:S(2)}) collective-permute-start(bf16[256,1024]{1,0:T(8,128)(2,1)S(1)} %bitcast.25), channel_id=1, source_target_pairs={{24,26},{25,27},{26,24},{27,25},{28,30},{29,31},{30,28},{31,29}} | collective-permute-start | bytes 1572872 | tf_op jit(solution)/shard_map/ppermute | solution.py:282
  19.0 27.2 %collective-permute-start.10 = (bf16[256,1024]{1,0:T(8,128)(2,1)S(1)}, bf16[256,1024]{1,0:T(8,128)(2,1)S(1)}, u32[]{:S(2)}, u32[]{:S(2)}) collective-permute-start(bf16[256,1024]{1,0:T(8,128)(2,1)S(1)} %block_dot.19), channel_id=1, source_target_pairs={{24,16},{25,17},{26,18},{27,19},{28,20},{29,21},{30,22},{31,23}} | collective-permute-start | bytes 1572872 | tf_op jit(solution)/shard_map/ppermute | solution.py:282
  20.3 33.5 %collective-permute-start.14 = (bf16[256,1024]{1,0:T(8,128)(2,1)S(1)}, bf16[256,1024]{1,0:T(8,128)(2,1)S(1)}, u32[]{:S(2)}, u32[]{:S(2)}) collective-permute-start(bf16[256,1024]{1,0:T(8,128)(2,1)S(1)} %block_dot.19), channel_id=1, source_target_pairs={{24,17},{25,16},{26,19},{27,18},{28,21},{29,20},{30,23},{31,22}} | collective-permute-start | bytes 1572872 | tf_op jit(solution)/shard_map/ppermute | solution.py:282
  21.6 35.1 %collective-permute-start.8 = (bf16[256,1024]{1,0:T(8,128)(2,1)S(1)}, bf16[256,1024]{1,0:T(8,128)(2,1)S(1)}, u32[]{:S(2)}, u32[]{:S(2)}) collective-permute-start(bf16[256,1024]{1,0:T(8,128)(2,1)S(1)} %block_dot.19), channel_id=1, source_target_pairs={{24,20},{25,21},{26,22},{27,23},{28,16},{29,17},{30,18},{31,19}} | collective-permute-start | bytes 1572872 | tf_op jit(solution)/shard_map/ppermute | solution.py:282
  23.0 45.9 %collective-permute-start.17 = (bf16[256,1024]{1,0:T(8,128)(2,1)S(1)}, bf16[256,1024]{1,0:T(8,128)(2,1)S(1)}, u32[]{:S(2)}, u32[]{:S(2)}) collective-permute-start(bf16[256,1024]{1,0:T(8,128)(2,1)S(1)} %block_dot.19), channel_id=1, source_target_pairs={{24,18},{25,19},{26,16},{27,17},{28,22},{29,23},{30,20},{31,21}} | collective-permute-start | bytes 1572872 | tf_op jit(solution)/shard_map/ppermute | solution.py:282
  56.6 15.1 %collective-permute-start.15 = (bf16[256,1024]{1,0:T(8,128)(2,1)S(1)}, bf16[256,1024]{1,0:T(8,128)(2,1)S(1)}, u32[]{:S(2)}, u32[]{:S(2)}) collective-permute-start(bf16[256,1024]{1,0:T(8,128)(2,1)S(1)} %collective-permute-done.8.refs_0_.refs_2_), channel_id=1, source_target_pairs={{16,17},{17,16},{18,19},{19,18},{20,21},{21,20},{22,23},{23,22}} | collective-permute-start | bytes 1572872 | tf_op jit(solution)/shard_map/ppermute | solution.py:282
  59.7 15.0 %collective-permute-start.9 = (bf16[256,1024]{1,0:T(8,128)(2,1)S(1)}, bf16[256,1024]{1,0:T(8,128)(2,1)S(1)}, u32[]{:S(2)}, u32[]{:S(2)}) collective-permute-start(bf16[256,1024]{1,0:T(8,128)(2,1)S(1)} %collective-permute-done.8.refs_0_.refs_2_), channel_id=1, source_target_pairs={{16,18},{17,19},{18,16},{19,17},{20,22},{21,23},{22,20},{23,21}} | collective-permute-start | bytes 1572872 | tf_op jit(solution)/shard_map/ppermute | solution.py:282
  67.6 10.6 %collective-permute-start.19 = (bf16[256,512]{1,0:T(8,128)(2,1)S(1)}, bf16[256,512]{1,0:T(8,128)(2,1)S(1)}, u32[]{:S(2)}, u32[]{:S(2)}) collective-permute-start(bf16[256,512]{1,0:T(8,128)(2,1)S(1)} %add_convert_fusion.1), channel_id=1, source_target_pairs={{8,12},{9,13},{10,14},{11,15},{12,8},{13,9},{14,10},{15,11},{0,4},... | collective-permute-start | bytes 786440 | tf_op jit(solution)/shard_map/ppermute | solution.py:282
  69.0 12.5 %collective-permute-start.18 = (bf16[256,1024]{1,0:T(8,128)(2,1)S(1)}, bf16[256,1024]{1,0:T(8,128)(2,1)S(1)}, u32[]{:S(2)}, u32[]{:S(2)}) collective-permute-start(bf16[256,1024]{1,0:T(8,128)(2,1)S(1)} %collective-permute-done.17.refs_0_.refs_4_), channel_id=1, source_target_pairs={{16,17},{17,16},{18,19},{19,18},{20,21},{21,20},{22,23},{23,22}} | collective-permute-start | bytes 1572872 | tf_op jit(solution)/shard_map/ppermute | solution.py:282
  74.8 11.1 %collective-permute-start.16 = (bf16[256,1024]{1,0:T(8,128)(2,1)S(1)}, bf16[256,1024]{1,0:T(8,128)(2,1)S(1)}, u32[]{:S(2)}, u32[]{:S(2)}) collective-permute-start(bf16[256,1024]{1,0:T(8,128)(2,1)S(1)} %collective-permute-done.9.refs_2_.refs_6_), channel_id=1, source_target_pairs={{16,17},{17,16},{18,19},{19,18},{20,21},{21,20},{22,23},{23,22}} | collective-permute-start | bytes 1572872 | tf_op jit(solution)/shard_map/ppermute | solution.py:282
  87.7 10.1 %collective-permute-start.22 = (bf16[256,1024]{1,0:T(8,128)(2,1)S(1)}, bf16[256,1024]{1,0:T(8,128)(2,1)S(1)}, u32[]{:S(2)}, u32[]{:S(2)}) collective-permute-start(bf16[256,1024]{1,0:T(8,128)(2,1)S(1)} %block_dot.23), channel_id=1, source_target_pairs={{16,8},{17,9},{18,10},{19,11},{20,12},{21,13},{22,14},{23,15}} | collective-permute-start | bytes 1572872 | tf_op jit(solution)/shard_map/ppermute | solution.py:282
  97.7 12.8 %collective-permute-start.25 = (bf16[256,1024]{1,0:T(8,128)(2,1)S(1)}, bf16[256,1024]{1,0:T(8,128)(2,1)S(1)}, u32[]{:S(2)}, u32[]{:S(2)}) collective-permute-start(bf16[256,1024]{1,0:T(8,128)(2,1)S(1)} %collective-permute-done.22.refs_0_.refs_2_), channel_id=1, source_target_pairs={{8,9},{9,8},{10,11},{11,10},{12,13},{13,12},{14,15},{15,14}} | collective-permute-start | bytes 1572872 | tf_op jit(solution)/shard_map/ppermute | solution.py:282
  98.4 12.6 %collective-permute-start.23 = (bf16[256,1024]{1,0:T(8,128)(2,1)S(1)}, bf16[256,1024]{1,0:T(8,128)(2,1)S(1)}, u32[]{:S(2)}, u32[]{:S(2)}) collective-permute-start(bf16[256,1024]{1,0:T(8,128)(2,1)S(1)} %collective-permute-done.22.refs_0_.refs_2_), channel_id=1, source_target_pairs={{8,12},{9,13},{10,14},{11,15},{12,8},{13,9},{14,10},{15,11}} | collective-permute-start | bytes 1572872 | tf_op jit(solution)/shard_map/ppermute | solution.py:282
  99.1 18.9 %collective-permute-start.27 = (bf16[4,256,512]{2,1,0:T(8,128)(2,1)S(1)}, bf16[4,256,512]{2,1,0:T(8,128)(2,1)S(1)}, u32[]{:S(2)}, u32[]{:S(2)}) collective-permute-start(bf16[4,256,512]{2,1,0:T(8,128)(2,1)S(1)} %pad_maximum_fusion.refs_4_), channel_id=1, source_target_pairs={{8,9},{9,8},{10,11},{11,10},{12,13},{13,12},{14,15},{15,14},{0,1},... | collective-permute-start | bytes 3145736 | tf_op jit(solution)/shard_map/ppermute | solution.py:282
  107.4 27.3 %collective-permute-start.40 = (bf16[4,256,512]{2,1,0:T(8,128)(2,1)S(1)}, bf16[4,256,512]{2,1,0:T(8,128)(2,1)S(1)}, u32[]{:S(2)}, u32[]{:S(2)}) collective-permute-start(bf16[4,256,512]{2,1,0:T(8,128)(2,1)S(1)} %get-tuple-element.58), channel_id=1, source_target_pairs={{24,25},{25,24},{26,27},{27,26},{28,29},{29,28},{30,31},{31,30},{1... | collective-permute-start | bytes 3145736 | tf_op jit(solution)/shard_map/ppermute | solution.py:282
  109.8 7.5 %collective-permute-start.29 = (bf16[256,1024]{1,0:T(8,128)(2,1)S(1)}, bf16[256,1024]{1,0:T(8,128)(2,1)S(1)}, u32[]{:S(2)}, u32[]{:S(2)}) collective-permute-start(bf16[256,1024]{1,0:T(8,128)(2,1)S(1)} %collective-permute-done.22.refs_0_.refs_2_), channel_id=1, source_target_pairs={{8,10},{9,11},{10,8},{11,9},{12,14},{13,15},{14,12},{15,13}} | collective-permute-start | bytes 1572872 | tf_op jit(solution)/shard_map/ppermute | solution.py:282
  117.3 30.2 %collective-permute-start.30 = (bf16[256,1024]{1,0:T(8,128)(2,1)S(1)}, bf16[256,1024]{1,0:T(8,128)(2,1)S(1)}, u32[]{:S(2)}, u32[]{:S(2)}) collective-permute-start(bf16[256,1024]{1,0:T(8,128)(2,1)S(1)} %collective-permute-done.29.refs_0_.refs_4_), channel_id=1, source_target_pairs={{8,9},{9,8},{10,11},{11,10},{12,13},{13,12},{14,15},{15,14}} | collective-permute-start | bytes 1572872 | tf_op jit(solution)/shard_map/ppermute | solution.py:282
  118.0 30.0 %collective-permute-start.28 = (bf16[256,1024]{1,0:T(8,128)(2,1)S(1)}, bf16[256,1024]{1,0:T(8,128)(2,1)S(1)}, u32[]{:S(2)}, u32[]{:S(2)}) collective-permute-start(bf16[256,1024]{1,0:T(8,128)(2,1)S(1)} %collective-permute-done.24.refs_2_.refs_6_), channel_id=1, source_target_pairs={{8,9},{9,8},{10,11},{11,10},{12,13},{13,12},{14,15},{15,14}} | collective-permute-start | bytes 1572872 | tf_op jit(solution)/shard_map/ppermute | solution.py:282
  135.4 14.6 %collective-permute-start.41 = (bf16[256,512]{1,0:T(8,128)(2,1)S(1)}, bf16[256,512]{1,0:T(8,128)(2,1)S(1)}, u32[]{:S(2)}, u32[]{:S(2)}) collective-permute-start(bf16[256,512]{1,0:T(8,128)(2,1)S(1)} %get-tuple-element.60), channel_id=1, source_target_pairs={{24,26},{25,27},{26,24},{27,25},{28,30},{29,31},{30,28},{31,29},{1... | collective-permute-start | bytes 786440 | tf_op jit(solution)/shard_map/ppermute | solution.py:282
  138.6 23.7 %collective-permute-start.42 = (bf16[256,512]{1,0:T(8,128)(2,1)S(1)}, bf16[256,512]{1,0:T(8,128)(2,1)S(1)}, u32[]{:S(2)}, u32[]{:S(2)}) collective-permute-start(bf16[256,512]{1,0:T(8,128)(2,1)S(1)} %get-tuple-element.61), channel_id=1, source_target_pairs={{24,28},{25,29},{26,30},{27,31},{28,24},{29,25},{30,26},{31,27},{1... | collective-permute-start | bytes 786440 | tf_op jit(solution)/shard_map/ppermute | solution.py:282
  144.5 23.1 %collective-permute-start.43 = (bf16[256,512]{1,0:T(8,128)(2,1)S(1)}, bf16[256,512]{1,0:T(8,128)(2,1)S(1)}, u32[]{:S(2)}, u32[]{:S(2)}) collective-permute-start(bf16[256,512]{1,0:T(8,128)(2,1)S(1)} %get-tuple-element.62), channel_id=1, source_target_pairs={{24,30},{25,31},{26,28},{27,29},{28,26},{29,27},{30,24},{31,25},{1... | collective-permute-start | bytes 786440 | tf_op jit(solution)/shard_map/ppermute | solution.py:282
  148.6 38.3 %collective-permute-start.34 = (bf16[256,1024]{1,0:T(8,128)(2,1)S(1)}, bf16[256,1024]{1,0:T(8,128)(2,1)S(1)}, u32[]{:S(2)}, u32[]{:S(2)}) collective-permute-start(bf16[256,1024]{1,0:T(8,128)(2,1)S(1)} %block_dot.27), channel_id=1, source_target_pairs={{8,1},{9,0},{10,3},{11,2},{12,5},{13,4},{14,7},{15,6}} | collective-permute-start | bytes 1572872 | tf_op jit(solution)/shard_map/ppermute | solution.py:282
  149.4 36.8 %collective-permute-start.33 = (bf16[256,1024]{1,0:T(8,128)(2,1)S(1)}, bf16[256,1024]{1,0:T(8,128)(2,1)S(1)}, u32[]{:S(2)}, u32[]{:S(2)}) collective-permute-start(bf16[256,1024]{1,0:T(8,128)(2,1)S(1)} %block_dot.27), channel_id=1, source_target_pairs={{8,0},{9,1},{10,2},{11,3},{12,4},{13,5},{14,6},{15,7}} | collective-permute-start | bytes 1572872 | tf_op jit(solution)/shard_map/ppermute | solution.py:282
  150.1 37.4 %collective-permute-start.31 = (bf16[256,1024]{1,0:T(8,128)(2,1)S(1)}, bf16[256,1024]{1,0:T(8,128)(2,1)S(1)}, u32[]{:S(2)}, u32[]{:S(2)}) collective-permute-start(bf16[256,1024]{1,0:T(8,128)(2,1)S(1)} %block_dot.27), channel_id=1, source_target_pairs={{8,4},{9,5},{10,6},{11,7},{12,0},{13,1},{14,2},{15,3}} | collective-permute-start | bytes 1572872 | tf_op jit(solution)/shard_map/ppermute | solution.py:282
  167.7 12.2 %collective-permute-start.44 = (bf16[256,512]{1,0:T(8,128)(2,1)S(1)}, bf16[256,512]{1,0:T(8,128)(2,1)S(1)}, u32[]{:S(2)}, u32[]{:S(2)}) collective-permute-start(bf16[256,512]{1,0:T(8,128)(2,1)S(1)} %add_convert_fusion), channel_id=1, source_target_pairs={{24,28},{25,29},{26,30},{27,31},{28,24},{29,25},{30,26},{31,27},{1... | collective-permute-start | bytes 786440 | tf_op jit(solution)/shard_map/ppermute | solution.py:282
  169.7 19.2 %collective-permute-start.45 = (bf16[256,512]{1,0:T(8,128)(2,1)S(1)}, bf16[256,512]{1,0:T(8,128)(2,1)S(1)}, u32[]{:S(2)}, u32[]{:S(2)}) collective-permute-start(bf16[256,512]{1,0:T(8,128)(2,1)S(1)} %add_convert_fusion), channel_id=1, source_target_pairs={{24,26},{25,27},{26,24},{27,25},{28,30},{29,31},{30,28},{31,29},{1... | collective-permute-start | bytes 786440 | tf_op jit(solution)/shard_map/ppermute | solution.py:282
  179.9 11.0 %collective-permute-start.46 = (bf16[256,512]{1,0:T(8,128)(2,1)S(1)}, bf16[256,512]{1,0:T(8,128)(2,1)S(1)}, u32[]{:S(2)}, u32[]{:S(2)}) collective-permute-start(bf16[256,512]{1,0:T(8,128)(2,1)S(1)} %collective-permute-done.44), channel_id=1, source_target_pairs={{24,26},{25,27},{26,24},{27,25},{28,30},{29,31},{30,28},{31,29},{1... | collective-permute-start | bytes 786440 | tf_op jit(solution)/shard_map/ppermute | solution.py:282
  186.2 8.0 %collective-permute-start.37 = (bf16[256,1024]{1,0:T(8,128)(2,1)S(1)}, bf16[256,1024]{1,0:T(8,128)(2,1)S(1)}, u32[]{:S(2)}, u32[]{:S(2)}) collective-permute-start(bf16[256,1024]{1,0:T(8,128)(2,1)S(1)} %block_dot.27), channel_id=1, source_target_pairs={{8,2},{9,3},{10,0},{11,1},{12,6},{13,7},{14,4},{15,5}} | collective-permute-start | bytes 1572872 | tf_op jit(solution)/shard_map/ppermute | solution.py:282
  191.1 25.3 %collective-permute-start.47 = (bf16[4,256,512]{2,1,0:T(8,128)(2,1)S(1)}, bf16[4,256,512]{2,1,0:T(8,128)(2,1)S(1)}, u32[]{:S(2)}, u32[]{:S(2)}) collective-permute-start(bf16[4,256,512]{2,1,0:T(8,128)(2,1)S(1)} %pad_maximum_fusion.1.refs_6_), channel_id=1, source_target_pairs={{24,25},{25,24},{26,27},{27,26},{28,29},{29,28},{30,31},{31,30},{1... | collective-permute-start | bytes 3145736 | tf_op jit(solution)/shard_map/ppermute | solution.py:282
  (19 other events, 90.8 us)

commit v9 on v8

--- a/solution.py
+++ b/solution.py
@@ -123,13 +123,12 @@
     )(at, in_hbm(weights), *blocks)
 
 
-def partials(at, among, inputs, weights, inner, after):
+def partials(at, among, inputs, weights, inner):
     rows, depth = inputs.shape
     count = at.shape[0] - 1
     width = weights.shape[1] // count
 
     def body(at, weights_ref, inputs_ref, *refs):
-        refs = refs[len(after) :]
         out_refs, (runs, sems) = refs[:inner], refs[inner:]
         order = [n for dx in [*range(1, inner), 0] for n in range(dx, count, inner)]
 
@@ -150,7 +149,7 @@
 
     return pl.pallas_call(
         body,
-        in_specs=[SMEM, HBM, VMEM] + [VMEM] * len(after),
+        in_specs=[SMEM, HBM, VMEM],
         out_specs=[VMEM] * inner,
         out_shape=[
             jax.ShapeDtypeStruct((count // inner, rows, width), jnp.bfloat16 if dx else jnp.float32)
@@ -162,7 +161,7 @@
         ],
         compiler_params=params(14),
         name="partials",
-    )(at, in_hbm(weights), inputs, *after)
+    )(at, in_hbm(weights), inputs)
 
 
 def added(at, among, own, arrived):
@@ -286,19 +285,21 @@
         near = {dz: moved(block, dz * inner, pairs) for dz in reversed(powers)}
         return near, {dx: moved(block, dx, pairs) for dx in range(1, inner)}
 
-    def along_outer(near, pairs):
+    def along_outer(near, pairs, after=()):
         got = dict(near)
         for dz in range(outer):
             low = dz & -dz
             if dz not in got:
-                got[dz] = moved(got[dz ^ low], low * inner, pairs)
+                block, *_ = lax.optimization_barrier((got[dz ^ low], *after))
+                got[dz] = moved(block, low * inner, pairs)
         return got
 
-    def handed_down(grad, turn):
+    def handed_down(grad, turn, after=()):
         own = moved(grad, 0, [(turn + 1, turn)])
         if turn % 2 == 0:
             near, side = spread(grad, [(turn + 1, turn)])
         else:
+            own, *_ = lax.optimization_barrier((own, *after))
             near, side = spread(own, [(turn, turn)])
         return {0: own, **near}, side
 
@@ -321,7 +322,8 @@
         for n in range(1, outer + 1):
             if n < outer:
                 dz = order[n]
-                ties = [totals[0]] + [blocks[order[max(0, n - 2)], dx] for dx in range(1, inner)]
+                ties = [totals[0] if n > 1 or turn < sections - 1 else matrix]
+                ties += [blocks[order[max(0, n - 2)], dx] for dx in range(1, inner)]
                 block, *_ = lax.optimization_barrier(
                     (got[dz], *ties, *(within if n == outer - 1 else []))
                 )
@@ -342,9 +344,9 @@
         parts = [dz * inner + dx for dz, dx in blocks]
         return stream_dot(at, turn, list(blocks.values()), out_cols, parts, jnp.bfloat16)
 
-    def rotate_begin(inputs, among, after=()):
+    def rotate_begin(inputs, among):
         pairs = [(a, a) for a in among]
-        own, *others = partials(at, among, inputs, basis_in[0], inner, after)
+        own, *others = partials(at, among, inputs, basis_in[0], inner)
         return own, others, [moved(other, 1 + n, pairs) for n, other in enumerate(others)]
 
     def summed(sums, among):
@@ -354,11 +356,11 @@
             own = own + moved(part, dz * inner, pairs).astype(jnp.float32)
         return own.astype(jnp.bfloat16)
 
-    def outer_columns(own, among, halves):
+    def outer_columns(own, among, halves, after=()):
         pairs = [(a, a) for a in among]
         powers = [1 << p for p in range(outer.bit_length() - 1)]
         near = {0: own, **{dz: moved(own, dz * inner, pairs) for dz in reversed(powers)}}
-        got = along_outer(near, pairs)
+        got = along_outer(near, pairs, after)
         return [jnp.stack([got[dz] for dz in some]) for some in halves]
 
     def all_columns(columns, among):
@@ -382,15 +384,13 @@
             sent = handed_down(grad, turn - 1)
             rot_outs[turn] = rotated(turn, blocks)
             before, within = [low], [rot_outs[turn]]
-    low = outer_columns(low, lower, halves)
-    grad, low = lax.optimization_barrier((grad, low))
-    sent = handed_down(grad, lower[0])
-    done = moved(grad[:16, :128], 0, [(upper[-1], a) for a in upper[:1]])
+    low = outer_columns(low, lower, halves, [grad])
+    sent = handed_down(grad, lower[0], low)
     low = all_columns(low, lower)
     rot_outs[upper[-1]] = rotated(upper[-1], blocks)
     inputs, *_ = lax.optimization_barrier((inputs, sent[0][0]))
     last_cols = resident(at, out_cols, 0)
-    high_own, _, high_arrived = rotate_begin(inputs, upper, [done])
+    high_own, _, high_arrived = rotate_begin(inputs, upper)
     before, within = [], [rot_outs[upper[-1]], *jax.tree.leaves(low)]
     for turn in lower:
         grad, blocks = relay(turn, sent, before, within, weights if turn else last_cols)

time: 230 us -> 207 us (0.900)
  the two profiles are of different devices: /device:TPU:22 before, /device:TPU:0 now
where the time goes in v9:
time: 207 us; the launch traced here: 206 us
  waiting for transfers between devices  92.9 us (45%)
  starting transfers between devices  66.5 us (32%)
  Pallas kernels  44.2 us (21%)
    ppermute x47, waiting for transfers between devices, moved(): return lax.ppermute(block, ('section', 'shard'), route)  92.9 us
    ppermute x47, starting transfers between devices, moved(): return lax.ppermute(block, ('section', 'shard'), route)  66.5 us
    pallas_call x16, Pallas kernels, block_dot(): pl.pallas_call(body, in_specs=[SMEM] + [VMEM] * (1 + count + (base is not...  12.4 us
    pallas_call x1, Pallas kernels, mean_square(): pl.pallas_call(body, in_specs=[SMEM] + [VMEM] * (sections + len(low) + le...  12.2 us
    pallas_call x2, Pallas kernels, resident(): pl.pallas_call(body, in_specs=[SMEM, HBM], out_specs=VMEM, out_shape=jax....  10.5 us
    pallas_call x2, Pallas kernels, partials(): pl.pallas_call(body, in_specs=[SMEM, HBM, VMEM], out_specs=[VMEM] * inner...  5.98 us
  transfers between devices with their start and end apart: 47, of which 12 were waited for; matrix products, arithmetic and copies ran while one was open for 0% of the time, Pallas kernels for 16%

profile of v9, /device:TPU:0, one launch (start us, length us, event | category | flops | bytes accessed | tf_op | source)
XLA Modules:
  0.0 206.3 jit_solution(16247206896682182795)
XLA Ops:
  2.7 5.4 %partials.2 = (f32[4,256,512]{2,1,0:T(8,128)S(1)}, bf16[4,256,512]{2,1,0:T(8,128)(2,1)S(1)}) custom-call(s32[9]{0:T(128)S(1)} %stack.69.at, bf16[1024,4096]{1,0:T(8,128)(2,1)} %bitcast.35, bf16[256,1024]{1,0:T(8,128)(2,1)S(1)} %bitcast.29), custom_call_target="tpu_custom_call" | custom-call | tf_op jit(solution)/shard_map/partials/pallas_call | solution.py:150
  8.0 4.8 %collective-permute-start.4 = (bf16[4,256,512]{2,1,0:T(8,128)(2,1)S(1)}, bf16[4,256,512]{2,1,0:T(8,128)(2,1)S(1)}, u32[]{:S(2)}, u32[]{:S(2)}) collective-permute-start(bf16[4,256,512]{2,1,0:T(8,128)(2,1)S(1)} %get-tuple-element.34), channel_id=1, source_target_pairs={{8,9},{9,8},{10,11},{11,10},{12,13},{13,12},{14,15},{15,14},{0,1},... | collective-permute-start | bytes 3145736 | tf_op jit(solution)/shard_map/ppermute | solution.py:281
  13.6 6.5 %resident.3.weights_ref = bf16[8,1024,1024]{2,1,0:T(8,128)(2,1)S(1)} custom-call(s32[9]{0:T(128)S(1)} %stack.69.at, bf16[8192,1024]{1,0:T(8,128)(2,1)} %bitcast.37), custom_call_target="tpu_custom_call" | custom-call | tf_op jit(solution)/shard_map/resident/pallas_call | solution.py:43
  22.8 13.3 %collective-permute-done.4.refs_0_ = bf16[4,256,512]{2,1,0:T(8,128)(2,1)S(1)} collective-permute-done((bf16[4,256,512]{2,1,0:T(8,128)(2,1)S(1)}, bf16[4,256,512]{2,1,0:T(8,128)(2,1)S(1)}, u32[]{:S(2)}, u32[]{:S(2)}) %collective-permute-start.4) | collective-permute-done | bytes 1048608 | tf_op jit(solution)/shard_map/ppermute | solution.py:281
  37.5 3.7 %collective-permute-start.11 = (bf16[256,512]{1,0:T(8,128)(2,1)S(1)}, bf16[256,512]{1,0:T(8,128)(2,1)S(1)}, u32[]{:S(2)}, u32[]{:S(2)}) collective-permute-start(bf16[256,512]{1,0:T(8,128)(2,1)S(1)} %get-tuple-element.39), channel_id=1, source_target_pairs={{8,10},{9,11},{10,8},{11,9},{12,14},{13,15},{14,12},{15,13},{0,2},... | collective-permute-start | bytes 786440 | tf_op jit(solution)/shard_map/ppermute | solution.py:281
  41.2 4.5 %collective-permute-start.12 = (bf16[256,512]{1,0:T(8,128)(2,1)S(1)}, bf16[256,512]{1,0:T(8,128)(2,1)S(1)}, u32[]{:S(2)}, u32[]{:S(2)}) collective-permute-start(bf16[256,512]{1,0:T(8,128)(2,1)S(1)} %get-tuple-element.40), channel_id=1, source_target_pairs={{8,12},{9,13},{10,14},{11,15},{12,8},{13,9},{14,10},{15,11},{0,4},... | collective-permute-start | bytes 786440 | tf_op jit(solution)/shard_map/ppermute | solution.py:281
  45.7 1.9 collective-permute-start.13
  51.5 12.6 %collective-permute-done.12 = bf16[256,512]{1,0:T(8,128)(2,1)S(1)} collective-permute-done((bf16[256,512]{1,0:T(8,128)(2,1)S(1)}, bf16[256,512]{1,0:T(8,128)(2,1)S(1)}, u32[]{:S(2)}, u32[]{:S(2)}) %collective-permute-start.12) | collective-permute-done | bytes 262176 | tf_op jit(solution)/shard_map/ppermute | solution.py:281
  69.0 7.2 %collective-permute-start.20 = (bf16[256,512]{1,0:T(8,128)(2,1)S(1)}, bf16[256,512]{1,0:T(8,128)(2,1)S(1)}, u32[]{:S(2)}, u32[]{:S(2)}) collective-permute-start(bf16[256,512]{1,0:T(8,128)(2,1)S(1)} %add_convert_fusion.1), channel_id=1, source_target_pairs={{8,12},{9,13},{10,14},{11,15},{12,8},{13,9},{14,10},{15,11},{0,4},... | collective-permute-start | bytes 786440 | tf_op jit(solution)/shard_map/ppermute | solution.py:281
  78.6 1.9 collective-permute-start.21
  80.5 6.2 %collective-permute-done.20 = bf16[256,512]{1,0:T(8,128)(2,1)S(1)} collective-permute-done((bf16[256,512]{1,0:T(8,128)(2,1)S(1)}, bf16[256,512]{1,0:T(8,128)(2,1)S(1)}, u32[]{:S(2)}, u32[]{:S(2)}) %collective-permute-start.20) | collective-permute-done | bytes 262176 | tf_op jit(solution)/shard_map/ppermute | solution.py:281
  86.8 1.9 collective-permute-start.22
  88.7 3.8 %collective-permute-done.21 = bf16[256,512]{1,0:T(8,128)(2,1)S(1)} collective-permute-done((bf16[256,512]{1,0:T(8,128)(2,1)S(1)}, bf16[256,512]{1,0:T(8,128)(2,1)S(1)}, u32[]{:S(2)}, u32[]{:S(2)}) %collective-permute-start.21) | collective-permute-done | bytes 262176 | tf_op jit(solution)/shard_map/ppermute | solution.py:281
  92.4 5.2 %collective-permute-done.22 = bf16[256,512]{1,0:T(8,128)(2,1)S(1)} collective-permute-done((bf16[256,512]{1,0:T(8,128)(2,1)S(1)}, bf16[256,512]{1,0:T(8,128)(2,1)S(1)}, u32[]{:S(2)}, u32[]{:S(2)}) %collective-permute-start.22) | collective-permute-done | bytes 262176 | tf_op jit(solution)/shard_map/ppermute | solution.py:281
  99.2 3.4 %collective-permute-start.27 = (bf16[4,256,512]{2,1,0:T(8,128)(2,1)S(1)}, bf16[4,256,512]{2,1,0:T(8,128)(2,1)S(1)}, u32[]{:S(2)}, u32[]{:S(2)}) collective-permute-start(bf16[4,256,512]{2,1,0:T(8,128)(2,1)S(1)} %pad_maximum_fusion.refs_4_), channel_id=1, source_target_pairs={{8,9},{9,8},{10,11},{11,10},{12,13},{13,12},{14,15},{15,14},{0,1},... | collective-permute-start | bytes 3145736 | tf_op jit(solution)/shard_map/ppermute | solution.py:281
  108.2 11.2 %collective-permute-done.27.refs_5_ = bf16[4,256,512]{2,1,0:T(8,128)(2,1)S(1)} collective-permute-done((bf16[4,256,512]{2,1,0:T(8,128)(2,1)S(1)}, bf16[4,256,512]{2,1,0:T(8,128)(2,1)S(1)}, u32[]{:S(2)}, u32[]{:S(2)}) %collective-permute-start.27) | collective-permute-done | bytes 1048608 | tf_op jit(solution)/shard_map/ppermute | solution.py:281
  127.0 1.3 collective-permute-start.31
  130.5 4.0 %resident.2.weights_ref = bf16[8,1024,512]{2,1,0:T(8,128)(2,1)S(1)} custom-call(s32[9]{0:T(128)S(1)} %stack.69.at, bf16[8192,512]{1,0:T(8,128)(2,1)} %bitcast.33), custom_call_target="tpu_custom_call" | custom-call | tf_op jit(solution)/shard_map/resident/pallas_call | solution.py:43
  134.6 20.7 %collective-permute-done.33.refs_0_ = bf16[256,1024]{1,0:T(8,128)(2,1)S(1)} collective-permute-done((bf16[256,1024]{1,0:T(8,128)(2,1)S(1)}, bf16[256,1024]{1,0:T(8,128)(2,1)S(1)}, u32[]{:S(2)}, u32[]{:S(2)}) %collective-permute-start.33) | collective-permute-done | bytes 524320 | tf_op jit(solution)/shard_map/ppermute | solution.py:281
  156.5 4.0 %collective-permute-done.34.refs_1_ = bf16[256,1024]{1,0:T(8,128)(2,1)S(1)} collective-permute-done((bf16[256,1024]{1,0:T(8,128)(2,1)S(1)}, bf16[256,1024]{1,0:T(8,128)(2,1)S(1)}, u32[]{:S(2)}, u32[]{:S(2)}) %collective-permute-start.34) | collective-permute-done | bytes 524320 | tf_op jit(solution)/shard_map/ppermute | solution.py:281
  160.5 1.4 block_dot.28.refs_2_
  161.9 5.3 %collective-permute-done.31.refs_0_ = bf16[256,1024]{1,0:T(8,128)(2,1)S(1)} collective-permute-done((bf16[256,1024]{1,0:T(8,128)(2,1)S(1)}, bf16[256,1024]{1,0:T(8,128)(2,1)S(1)}, u32[]{:S(2)}, u32[]{:S(2)}) %collective-permute-start.31) | collective-permute-done | bytes 524320 | tf_op jit(solution)/shard_map/ppermute | solution.py:281
  167.2 3.4 %collective-permute-start.35 = (bf16[256,1024]{1,0:T(8,128)(2,1)S(1)}, bf16[256,1024]{1,0:T(8,128)(2,1)S(1)}, u32[]{:S(2)}, u32[]{:S(2)}) collective-permute-start(bf16[256,1024]{1,0:T(8,128)(2,1)S(1)} %collective-permute-done.31.refs_0_), channel_id=1, source_target_pairs={{0,1},{1,0},{2,3},{3,2},{4,5},{5,4},{6,7},{7,6}} | collective-permute-start | bytes 1572872 | tf_op jit(solution)/shard_map/ppermute | solution.py:281
  170.6 1.9 collective-permute-start.32
  174.1 2.4 %collective-permute-start.38 = (bf16[256,1024]{1,0:T(8,128)(2,1)S(1)}, bf16[256,1024]{1,0:T(8,128)(2,1)S(1)}, u32[]{:S(2)}, u32[]{:S(2)}) collective-permute-start(bf16[256,1024]{1,0:T(8,128)(2,1)S(1)} %collective-permute-done.37.refs_0_), channel_id=1, source_target_pairs={{0,1},{1,0},{2,3},{3,2},{4,5},{5,4},{6,7},{7,6}} | collective-permute-start | bytes 1572872 | tf_op jit(solution)/shard_map/ppermute | solution.py:281
  176.5 1.7 collective-permute-done.35.refs_1_
  178.3 3.5 %collective-permute-done.32.refs_2_ = bf16[256,1024]{1,0:T(8,128)(2,1)S(1)} collective-permute-done((bf16[256,1024]{1,0:T(8,128)(2,1)S(1)}, bf16[256,1024]{1,0:T(8,128)(2,1)S(1)}, u32[]{:S(2)}, u32[]{:S(2)}) %collective-permute-start.32) | collective-permute-done | bytes 524320 | tf_op jit(solution)/shard_map/ppermute | solution.py:281
  181.7 2.4 %collective-permute-start.36 = (bf16[256,1024]{1,0:T(8,128)(2,1)S(1)}, bf16[256,1024]{1,0:T(8,128)(2,1)S(1)}, u32[]{:S(2)}, u32[]{:S(2)}) collective-permute-start(bf16[256,1024]{1,0:T(8,128)(2,1)S(1)} %collective-permute-done.32.refs_2_), channel_id=1, source_target_pairs={{0,1},{1,0},{2,3},{3,2},{4,5},{5,4},{6,7},{7,6}} | collective-permute-start | bytes 1572872 | tf_op jit(solution)/shard_map/ppermute | solution.py:281
  184.1 1.4 block_dot.29.refs_3_
  185.6 1.7 block_dot.30.refs_1_
  187.3 5.5 %collective-permute-done.36.refs_0_ = bf16[256,1024]{1,0:T(8,128)(2,1)S(1)} collective-permute-done((bf16[256,1024]{1,0:T(8,128)(2,1)S(1)}, bf16[256,1024]{1,0:T(8,128)(2,1)S(1)}, u32[]{:S(2)}, u32[]{:S(2)}) %collective-permute-start.36) | collective-permute-done | bytes 524320 | tf_op jit(solution)/shard_map/ppermute | solution.py:281
  194.0 12.2 %mean_square.1 = f32[512,4096]{1,0:T(8,128)} custom-call(s32[9]{0:T(128)S(1)} %stack.69.at, bf16[256,512]{1,0:T(8,128)(2,1)S(1)} %block_dot.31.refs_0_, bf16[256,512]{1,0:T(8,128)(2,1)S(1)} %stream_dot.5.refs_1_, bf16[256,512]{1,0:T(8,128)(2,1)S(1)} %stream_dot.4.refs_2_, bf16[256,512]{1,0:T(8,128)(2,1)S(1)} %stream_dot.3.refs_3_, ...), custom_call_target="tpu_custom_call" | custom-call | tf_op jit(solution)/shard_map/mean_square/pallas_call | solution.py:244
  (99 shorter events, 39.0 us)
Async XLA Ops:
  0.0 20.1 %collective-permute-start.2 = (bf16[256,1024]{1,0:T(8,128)(2,1)}, bf16[256,1024]{1,0:T(8,128)(2,1)S(1)}, u32[]{:S(2)}, u32[]{:S(2)}) collective-permute-start(bf16[256,1024]{1,0:T(8,128)(2,1)} %bitcast.23), channel_id=1, source_target_pairs={{24,25},{25,24},{26,27},{27,26},{28,29},{29,28},{30,31},{31,30}} | collective-permute-start | bytes 1572872 | tf_op jit(solution)/shard_map/ppermute | solution.py:281
  0.8 19.3 %collective-permute-start = (bf16[256,1024]{1,0:T(8,128)(2,1)}, bf16[256,1024]{1,0:T(8,128)(2,1)S(1)}, u32[]{:S(2)}, u32[]{:S(2)}) collective-permute-start(bf16[256,1024]{1,0:T(8,128)(2,1)} %bitcast.24), channel_id=1, source_target_pairs={{24,28},{25,29},{26,30},{27,31},{28,24},{29,25},{30,26},{31,27}} | collective-permute-start | bytes 1572872 | tf_op jit(solution)/shard_map/ppermute | solution.py:281
  8.0 28.0 %collective-permute-start.4 = (bf16[4,256,512]{2,1,0:T(8,128)(2,1)S(1)}, bf16[4,256,512]{2,1,0:T(8,128)(2,1)S(1)}, u32[]{:S(2)}, u32[]{:S(2)}) collective-permute-start(bf16[4,256,512]{2,1,0:T(8,128)(2,1)S(1)} %get-tuple-element.34), channel_id=1, source_target_pairs={{8,9},{9,8},{10,11},{11,10},{12,13},{13,12},{14,15},{15,14},{0,1},... | collective-permute-start | bytes 3145736 | tf_op jit(solution)/shard_map/ppermute | solution.py:281
  20.1 16.7 %collective-permute-start.3 = (bf16[256,1024]{1,0:T(8,128)(2,1)S(1)}, bf16[256,1024]{1,0:T(8,128)(2,1)S(1)}, u32[]{:S(2)}, u32[]{:S(2)}) collective-permute-start(bf16[256,1024]{1,0:T(8,128)(2,1)S(1)} %collective-permute-done.refs_0_.refs_2_), channel_id=1, source_target_pairs={{24,25},{25,24},{26,27},{27,26},{28,29},{29,28},{30,31},{31,30}} | collective-permute-start | bytes 1572872 | tf_op jit(solution)/shard_map/ppermute | solution.py:281
  20.8 16.0 %collective-permute-start.1 = (bf16[256,1024]{1,0:T(8,128)(2,1)S(1)}, bf16[256,1024]{1,0:T(8,128)(2,1)S(1)}, u32[]{:S(2)}, u32[]{:S(2)}) collective-permute-start(bf16[256,1024]{1,0:T(8,128)(2,1)S(1)} %collective-permute-done.refs_0_.refs_2_), channel_id=1, source_target_pairs={{24,26},{25,27},{26,24},{27,25},{28,30},{29,31},{30,28},{31,29}} | collective-permute-start | bytes 1572872 | tf_op jit(solution)/shard_map/ppermute | solution.py:281
  22.1 26.1 %collective-permute-start.7 = (bf16[256,1024]{1,0:T(8,128)(2,1)S(1)}, bf16[256,1024]{1,0:T(8,128)(2,1)S(1)}, u32[]{:S(2)}, u32[]{:S(2)}) collective-permute-start(bf16[256,1024]{1,0:T(8,128)(2,1)S(1)} %collective-permute-done.6.refs_0_.refs_4_), channel_id=1, source_target_pairs={{24,25},{25,24},{26,27},{27,26},{28,29},{29,28},{30,31},{31,30}} | collective-permute-start | bytes 1572872 | tf_op jit(solution)/shard_map/ppermute | solution.py:281
  36.8 12.0 %collective-permute-start.5 = (bf16[256,1024]{1,0:T(8,128)(2,1)S(1)}, bf16[256,1024]{1,0:T(8,128)(2,1)S(1)}, u32[]{:S(2)}, u32[]{:S(2)}) collective-permute-start(bf16[256,1024]{1,0:T(8,128)(2,1)S(1)} %collective-permute-done.1.refs_2_.refs_6_), channel_id=1, source_target_pairs={{24,25},{25,24},{26,27},{27,26},{28,29},{29,28},{30,31},{31,30}} | collective-permute-start | bytes 1572872 | tf_op jit(solution)/shard_map/ppermute | solution.py:281
  37.5 13.3 %collective-permute-start.11 = (bf16[256,512]{1,0:T(8,128)(2,1)S(1)}, bf16[256,512]{1,0:T(8,128)(2,1)S(1)}, u32[]{:S(2)}, u32[]{:S(2)}) collective-permute-start(bf16[256,512]{1,0:T(8,128)(2,1)S(1)} %get-tuple-element.39), channel_id=1, source_target_pairs={{8,10},{9,11},{10,8},{11,9},{12,14},{13,15},{14,12},{15,13},{0,2},... | collective-permute-start | bytes 786440 | tf_op jit(solution)/shard_map/ppermute | solution.py:281
  41.2 22.8 %collective-permute-start.12 = (bf16[256,512]{1,0:T(8,128)(2,1)S(1)}, bf16[256,512]{1,0:T(8,128)(2,1)S(1)}, u32[]{:S(2)}, u32[]{:S(2)}) collective-permute-start(bf16[256,512]{1,0:T(8,128)(2,1)S(1)} %get-tuple-element.40), channel_id=1, source_target_pairs={{8,12},{9,13},{10,14},{11,15},{12,8},{13,9},{14,10},{15,11},{0,4},... | collective-permute-start | bytes 786440 | tf_op jit(solution)/shard_map/ppermute | solution.py:281
  45.7 18.3 %collective-permute-start.13 = (bf16[256,512]{1,0:T(8,128)(2,1)S(1)}, bf16[256,512]{1,0:T(8,128)(2,1)S(1)}, u32[]{:S(2)}, u32[]{:S(2)}) collective-permute-start(bf16[256,512]{1,0:T(8,128)(2,1)S(1)} %get-tuple-element.41), channel_id=1, source_target_pairs={{8,14},{9,15},{10,12},{11,13},{12,10},{13,11},{14,8},{15,9},{0,6},... | collective-permute-start | bytes 786440 | tf_op jit(solution)/shard_map/ppermute | solution.py:281
  49.3 15.6 %collective-permute-start.10 = (bf16[256,1024]{1,0:T(8,128)(2,1)S(1)}, bf16[256,1024]{1,0:T(8,128)(2,1)S(1)}, u32[]{:S(2)}, u32[]{:S(2)}) collective-permute-start(bf16[256,1024]{1,0:T(8,128)(2,1)S(1)} %block_dot.19), channel_id=1, source_target_pairs={{24,16},{25,17},{26,18},{27,19},{28,20},{29,21},{30,22},{31,23}} | collective-permute-start | bytes 1572872 | tf_op jit(solution)/shard_map/ppermute | solution.py:281
  50.0 14.9 %collective-permute-start.14 = (bf16[256,1024]{1,0:T(8,128)(2,1)S(1)}, bf16[256,1024]{1,0:T(8,128)(2,1)S(1)}, u32[]{:S(2)}, u32[]{:S(2)}) collective-permute-start(bf16[256,1024]{1,0:T(8,128)(2,1)S(1)} %block_dot.19), channel_id=1, source_target_pairs={{24,17},{25,16},{26,19},{27,18},{28,21},{29,20},{30,23},{31,22}} | collective-permute-start | bytes 1572872 | tf_op jit(solution)/shard_map/ppermute | solution.py:281
  50.8 14.7 %collective-permute-start.8 = (bf16[256,1024]{1,0:T(8,128)(2,1)S(1)}, bf16[256,1024]{1,0:T(8,128)(2,1)S(1)}, u32[]{:S(2)}, u32[]{:S(2)}) collective-permute-start(bf16[256,1024]{1,0:T(8,128)(2,1)S(1)} %block_dot.19), channel_id=1, source_target_pairs={{24,20},{25,21},{26,22},{27,23},{28,16},{29,17},{30,18},{31,19}} | collective-permute-start | bytes 1572872 | tf_op jit(solution)/shard_map/ppermute | solution.py:281
  69.0 17.8 %collective-permute-start.20 = (bf16[256,512]{1,0:T(8,128)(2,1)S(1)}, bf16[256,512]{1,0:T(8,128)(2,1)S(1)}, u32[]{:S(2)}, u32[]{:S(2)}) collective-permute-start(bf16[256,512]{1,0:T(8,128)(2,1)S(1)} %add_convert_fusion.1), channel_id=1, source_target_pairs={{8,12},{9,13},{10,14},{11,15},{12,8},{13,9},{14,10},{15,11},{0,4},... | collective-permute-start | bytes 786440 | tf_op jit(solution)/shard_map/ppermute | solution.py:281
  77.9 19.9 %collective-permute-start.19 = (bf16[256,1024]{1,0:T(8,128)(2,1)S(1)}, bf16[256,1024]{1,0:T(8,128)(2,1)S(1)}, u32[]{:S(2)}, u32[]{:S(2)}) collective-permute-start(bf16[256,1024]{1,0:T(8,128)(2,1)S(1)} %block_dot.23), channel_id=1, source_target_pairs={{16,8},{17,9},{18,10},{19,11},{20,12},{21,13},{22,14},{23,15}} | collective-permute-start | bytes 1572872 | tf_op jit(solution)/shard_map/ppermute | solution.py:281
  78.6 13.8 %collective-permute-start.21 = (bf16[256,512]{1,0:T(8,128)(2,1)S(1)}, bf16[256,512]{1,0:T(8,128)(2,1)S(1)}, u32[]{:S(2)}, u32[]{:S(2)}) collective-permute-start(bf16[256,512]{1,0:T(8,128)(2,1)S(1)} %add_convert_fusion.1), channel_id=1, source_target_pairs={{8,10},{9,11},{10,8},{11,9},{12,14},{13,15},{14,12},{15,13},{0,2},... | collective-permute-start | bytes 786440 | tf_op jit(solution)/shard_map/ppermute | solution.py:281
  99.2 20.2 %collective-permute-start.27 = (bf16[4,256,512]{2,1,0:T(8,128)(2,1)S(1)}, bf16[4,256,512]{2,1,0:T(8,128)(2,1)S(1)}, u32[]{:S(2)}, u32[]{:S(2)}) collective-permute-start(bf16[4,256,512]{2,1,0:T(8,128)(2,1)S(1)} %pad_maximum_fusion.refs_4_), channel_id=1, source_target_pairs={{8,9},{9,8},{10,11},{11,10},{12,13},{13,12},{14,15},{15,14},{0,1},... | collective-permute-start | bytes 3145736 | tf_op jit(solution)/shard_map/ppermute | solution.py:281
  103.2 16.8 %collective-permute-start.39 = (bf16[4,256,512]{2,1,0:T(8,128)(2,1)S(1)}, bf16[4,256,512]{2,1,0:T(8,128)(2,1)S(1)}, u32[]{:S(2)}, u32[]{:S(2)}) collective-permute-start(bf16[4,256,512]{2,1,0:T(8,128)(2,1)S(1)} %get-tuple-element.58), channel_id=1, source_target_pairs={{24,25},{25,24},{26,27},{27,26},{28,29},{29,28},{30,31},{31,30},{1... | collective-permute-start | bytes 3145736 | tf_op jit(solution)/shard_map/ppermute | solution.py:281
  105.4 13.9 %collective-permute-start.26 = (bf16[256,1024]{1,0:T(8,128)(2,1)S(1)}, bf16[256,1024]{1,0:T(8,128)(2,1)S(1)}, u32[]{:S(2)}, u32[]{:S(2)}) collective-permute-start(bf16[256,1024]{1,0:T(8,128)(2,1)S(1)} %collective-permute-done.23.refs_0_.refs_2_), channel_id=1, source_target_pairs={{8,9},{9,8},{10,11},{11,10},{12,13},{13,12},{14,15},{15,14}} | collective-permute-start | bytes 1572872 | tf_op jit(solution)/shard_map/ppermute | solution.py:281
  106.1 13.2 %collective-permute-start.24 = (bf16[256,1024]{1,0:T(8,128)(2,1)S(1)}, bf16[256,1024]{1,0:T(8,128)(2,1)S(1)}, u32[]{:S(2)}, u32[]{:S(2)}) collective-permute-start(bf16[256,1024]{1,0:T(8,128)(2,1)S(1)} %collective-permute-done.23.refs_0_.refs_2_), channel_id=1, source_target_pairs={{8,10},{9,11},{10,8},{11,9},{12,14},{13,15},{14,12},{15,13}} | collective-permute-start | bytes 1572872 | tf_op jit(solution)/shard_map/ppermute | solution.py:281
  107.5 15.8 %collective-permute-start.30 = (bf16[256,1024]{1,0:T(8,128)(2,1)S(1)}, bf16[256,1024]{1,0:T(8,128)(2,1)S(1)}, u32[]{:S(2)}, u32[]{:S(2)}) collective-permute-start(bf16[256,1024]{1,0:T(8,128)(2,1)S(1)} %collective-permute-done.29.refs_0_.refs_4_), channel_id=1, source_target_pairs={{8,9},{9,8},{10,11},{11,10},{12,13},{13,12},{14,15},{15,14}} | collective-permute-start | bytes 1572872 | tf_op jit(solution)/shard_map/ppermute | solution.py:281
  124.4 36.1 %collective-permute-start.34 = (bf16[256,1024]{1,0:T(8,128)(2,1)S(1)}, bf16[256,1024]{1,0:T(8,128)(2,1)S(1)}, u32[]{:S(2)}, u32[]{:S(2)}) collective-permute-start(bf16[256,1024]{1,0:T(8,128)(2,1)S(1)} %block_dot.27), channel_id=1, source_target_pairs={{8,1},{9,0},{10,3},{11,2},{12,5},{13,4},{14,7},{15,6}} | collective-permute-start | bytes 1572872 | tf_op jit(solution)/shard_map/ppermute | solution.py:281
  125.7 29.5 %collective-permute-start.33 = (bf16[256,1024]{1,0:T(8,128)(2,1)S(1)}, bf16[256,1024]{1,0:T(8,128)(2,1)S(1)}, u32[]{:S(2)}, u32[]{:S(2)}) collective-permute-start(bf16[256,1024]{1,0:T(8,128)(2,1)S(1)} %block_dot.27), channel_id=1, source_target_pairs={{8,0},{9,1},{10,2},{11,3},{12,4},{13,5},{14,6},{15,7}} | collective-permute-start | bytes 1572872 | tf_op jit(solution)/shard_map/ppermute | solution.py:281
  127.0 40.2 %collective-permute-start.31 = (bf16[256,1024]{1,0:T(8,128)(2,1)S(1)}, bf16[256,1024]{1,0:T(8,128)(2,1)S(1)}, u32[]{:S(2)}, u32[]{:S(2)}) collective-permute-start(bf16[256,1024]{1,0:T(8,128)(2,1)S(1)} %block_dot.27), channel_id=1, source_target_pairs={{8,4},{9,5},{10,6},{11,7},{12,0},{13,1},{14,2},{15,3}} | collective-permute-start | bytes 1572872 | tf_op jit(solution)/shard_map/ppermute | solution.py:281
  129.1 43.4 %collective-permute-start.44 = (bf16[256,512]{1,0:T(8,128)(2,1)S(1)}, bf16[256,512]{1,0:T(8,128)(2,1)S(1)}, u32[]{:S(2)}, u32[]{:S(2)}) collective-permute-start(bf16[256,512]{1,0:T(8,128)(2,1)S(1)} %add_convert_fusion), channel_id=1, source_target_pairs={{24,26},{25,27},{26,24},{27,25},{28,30},{29,31},{30,28},{31,29},{1... | collective-permute-start | bytes 786440 | tf_op jit(solution)/shard_map/ppermute | solution.py:281
  129.8 42.8 %collective-permute-start.45 = (bf16[256,512]{1,0:T(8,128)(2,1)S(1)}, bf16[256,512]{1,0:T(8,128)(2,1)S(1)}, u32[]{:S(2)}, u32[]{:S(2)}) collective-permute-start(bf16[256,512]{1,0:T(8,128)(2,1)S(1)} %collective-permute-done.43), channel_id=1, source_target_pairs={{24,26},{25,27},{26,24},{27,25},{28,30},{29,31},{30,28},{31,29},{1... | collective-permute-start | bytes 786440 | tf_op jit(solution)/shard_map/ppermute | solution.py:281
  155.2 18.9 %collective-permute-start.37 = (bf16[256,1024]{1,0:T(8,128)(2,1)S(1)}, bf16[256,1024]{1,0:T(8,128)(2,1)S(1)}, u32[]{:S(2)}, u32[]{:S(2)}) collective-permute-start(bf16[256,1024]{1,0:T(8,128)(2,1)S(1)} %block_dot.27), channel_id=1, source_target_pairs={{8,2},{9,3},{10,0},{11,1},{12,6},{13,7},{14,4},{15,5}} | collective-permute-start | bytes 1572872 | tf_op jit(solution)/shard_map/ppermute | solution.py:281
  167.2 11.1 %collective-permute-start.35 = (bf16[256,1024]{1,0:T(8,128)(2,1)S(1)}, bf16[256,1024]{1,0:T(8,128)(2,1)S(1)}, u32[]{:S(2)}, u32[]{:S(2)}) collective-permute-start(bf16[256,1024]{1,0:T(8,128)(2,1)S(1)} %collective-permute-done.31.refs_0_), channel_id=1, source_target_pairs={{0,1},{1,0},{2,3},{3,2},{4,5},{5,4},{6,7},{7,6}} | collective-permute-start | bytes 1572872 | tf_op jit(solution)/shard_map/ppermute | solution.py:281
  170.6 11.1 %collective-permute-start.32 = (bf16[256,1024]{1,0:T(8,128)(2,1)S(1)}, bf16[256,1024]{1,0:T(8,128)(2,1)S(1)}, u32[]{:S(2)}, u32[]{:S(2)}) collective-permute-start(bf16[256,1024]{1,0:T(8,128)(2,1)S(1)} %collective-permute-done.31.refs_0_), channel_id=1, source_target_pairs={{0,2},{1,3},{2,0},{3,1},{4,6},{5,7},{6,4},{7,5}} | collective-permute-start | bytes 1572872 | tf_op jit(solution)/shard_map/ppermute | solution.py:281
  172.7 21.2 %collective-permute-start.46 = (bf16[4,256,512]{2,1,0:T(8,128)(2,1)S(1)}, bf16[4,256,512]{2,1,0:T(8,128)(2,1)S(1)}, u32[]{:S(2)}, u32[]{:S(2)}) collective-permute-start(bf16[4,256,512]{2,1,0:T(8,128)(2,1)S(1)} %pad_maximum_fusion.1.refs_6_), channel_id=1, source_target_pairs={{24,25},{25,24},{26,27},{27,26},{28,29},{29,28},{30,31},{31,30},{1... | collective-permute-start | bytes 3145736 | tf_op jit(solution)/shard_map/ppermute | solution.py:281
  174.1 11.5 %collective-permute-start.38 = (bf16[256,1024]{1,0:T(8,128)(2,1)S(1)}, bf16[256,1024]{1,0:T(8,128)(2,1)S(1)}, u32[]{:S(2)}, u32[]{:S(2)}) collective-permute-start(bf16[256,1024]{1,0:T(8,128)(2,1)S(1)} %collective-permute-done.37.refs_0_), channel_id=1, source_target_pairs={{0,1},{1,0},{2,3},{3,2},{4,5},{5,4},{6,7},{7,6}} | collective-permute-start | bytes 1572872 | tf_op jit(solution)/shard_map/ppermute | solution.py:281
  181.7 11.1 %collective-permute-start.36 = (bf16[256,1024]{1,0:T(8,128)(2,1)S(1)}, bf16[256,1024]{1,0:T(8,128)(2,1)S(1)}, u32[]{:S(2)}, u32[]{:S(2)}) collective-permute-start(bf16[256,1024]{1,0:T(8,128)(2,1)S(1)} %collective-permute-done.32.refs_2_), channel_id=1, source_target_pairs={{0,1},{1,0},{2,3},{3,2},{4,5},{5,4},{6,7},{7,6}} | collective-permute-start | bytes 1572872 | tf_op jit(solution)/shard_map/ppermute | solution.py:281
  (18 other events, 128.5 us)

commit v10 on v9

--- a/solution.py
+++ b/solution.py
@@ -164,11 +164,11 @@
     )(at, in_hbm(weights), inputs)
 
 
-def added(at, among, own, arrived):
+def added(at, among, own, arrived, old=()):
     count, rows, width = own.shape
 
     def body(at, own_ref, *refs):
-        arrived_refs, out_refs = refs[: len(arrived)], refs[len(arrived) :]
+        arrived_refs, out_refs = refs[: len(arrived)], refs[len(arrived) + len(old) :]
 
         @pl.when((at[0] >= min(among)) & (at[0] <= max(among)))
         def _():
@@ -180,7 +180,8 @@
 
     return pl.pallas_call(
         body,
-        in_specs=[SMEM] + [VMEM] * (1 + len(arrived)),
+        in_specs=[SMEM] + [VMEM] * (1 + len(arrived) + len(old)),
+        input_output_aliases={2 + len(arrived) + n: n for n in range(len(old))},
         out_specs=[VMEM] * count,
         out_shape=[
             jax.ShapeDtypeStruct((rows, width), jnp.bfloat16 if n else jnp.float32)
@@ -188,7 +189,7 @@
         ],
         compiler_params=params(4),
         name="added",
-    )(at, own, *arrived)
+    )(at, own, *arrived, *old)
 
 
 def mean_square(at, half, rot_outs, low, high, low_runs, high_runs, micro, seq):
@@ -371,26 +372,30 @@
     lower = list(range(half - 1, -1, -1))
     rot_outs = [None] * sections
 
-    low_own, low_others, low_arrived = rotate_begin(inputs, lower)
+    first = lower + upper[1:]
+    own, others, arrived = rotate_begin(inputs, first)
     near, side = spread(top, [(upper[0], upper[0])])
     weights = resident(at, weights)
     halves = [order]
-    sums = added(at, lower, low_own, low_arrived)
+    sums = added(at, lower, own, arrived)
     low = summed(sums, lower)
-    sent, before, within = ({0: top, **near}, side), low_others, sums
+    sent, before, within = ({0: top, **near}, side), others, sums
     for turn in upper:
         grad, blocks = relay(turn, sent, before, within, weights)
         if turn != upper[-1]:
             sent = handed_down(grad, turn - 1)
             rot_outs[turn] = rotated(turn, blocks)
             before, within = [low], [rot_outs[turn]]
+        if turn == upper[0]:
+            inputs, _ = lax.optimization_barrier((inputs, grad))
+            last_own, last_others, last_arrived = rotate_begin(inputs, upper[:1])
+            before, within = before + last_others, within + last_arrived
     low = outer_columns(low, lower, halves, [grad])
     sent = handed_down(grad, lower[0], low)
     low = all_columns(low, lower)
     rot_outs[upper[-1]] = rotated(upper[-1], blocks)
-    inputs, *_ = lax.optimization_barrier((inputs, sent[0][0]))
     last_cols = resident(at, out_cols, 0)
-    high_own, _, high_arrived = rotate_begin(inputs, upper)
+    own, last_own, _ = lax.optimization_barrier((own, last_own, sent[0][0]))
     before, within = [], [rot_outs[upper[-1]], *jax.tree.leaves(low)]
     for turn in lower:
         grad, blocks = relay(turn, sent, before, within, weights if turn else last_cols)
@@ -399,7 +404,7 @@
             rot_outs[turn] = rotated(turn, blocks)
             before, within = [], [rot_outs[turn]]
     rot_outs[0] = grad
-    sums = added(at, upper, high_own, high_arrived)
+    sums = added(at, upper[:1], last_own, last_arrived, added(at, upper[1:], own, arrived))
     high = all_columns(outer_columns(summed(sums, upper), upper, [order]), upper)
 
     def runs(parts):

time: 207 us -> 205 us (level)
  waiting for transfers between devices: 92.9 us -> 90.5 us
    ppermute x47, waiting for transfers between devices: 92.9 us -> 90.5 us  [moved(): return lax.ppermute(block, ('section', 'shard'), route)]
where the time goes in v10:
time: 205 us; the launch traced here: 204 us
  waiting for transfers between devices  90.5 us (44%)
  starting transfers between devices  66.3 us (32%)
  Pallas kernels  44.7 us (22%)
    ppermute x47, waiting for transfers between devices, moved(): return lax.ppermute(block, ('section', 'shard'), route)  90.5 us
    ppermute x47, starting transfers between devices, moved(): return lax.ppermute(block, ('section', 'shard'), route)  66.3 us
    pallas_call x16, Pallas kernels, block_dot(): pl.pallas_call(body, in_specs=[SMEM] + [VMEM] * (1 + count + (base is not...  12.4 us
    pallas_call x1, Pallas kernels, mean_square(): pl.pallas_call(body, in_specs=[SMEM] + [VMEM] * (sections + len(low) + le...  12.2 us
    pallas_call x2, Pallas kernels, resident(): pl.pallas_call(body, in_specs=[SMEM, HBM], out_specs=VMEM, out_shape=jax....  10.5 us
    pallas_call x2, Pallas kernels, partials(): pl.pallas_call(body, in_specs=[SMEM, HBM, VMEM], out_specs=[VMEM] * inner...  5.98 us
  transfers between devices with their start and end apart: 47, of which 12 were waited for; matrix products, arithmetic and copies ran while one was open for 0% of the time, Pallas kernels for 16%

profile of v10, /device:TPU:0, one launch (start us, length us, event | category | flops | bytes accessed | tf_op | source)
XLA Modules:
  0.0 204.3 jit_solution(7069523672828157437)
XLA Ops:
  2.7 5.4 %partials.2 = (f32[4,256,512]{2,1,0:T(8,128)S(1)}, bf16[4,256,512]{2,1,0:T(8,128)(2,1)S(1)}) custom-call(s32[9]{0:T(128)S(1)} %stack.69.at, bf16[1024,4096]{1,0:T(8,128)(2,1)} %bitcast.35, bf16[256,1024]{1,0:T(8,128)(2,1)S(1)} %bitcast.29), custom_call_target="tpu_custom_call" | custom-call | tf_op jit(solution)/shard_map/partials/pallas_call | solution.py:150
  8.0 4.8 %collective-permute-start.4 = (bf16[4,256,512]{2,1,0:T(8,128)(2,1)S(1)}, bf16[4,256,512]{2,1,0:T(8,128)(2,1)S(1)}, u32[]{:S(2)}, u32[]{:S(2)}) collective-permute-start(bf16[4,256,512]{2,1,0:T(8,128)(2,1)S(1)} %get-tuple-element.40), channel_id=1, source_target_pairs={{8,9},{9,8},{10,11},{11,10},{12,13},{13,12},{14,15},{15,14},{0,1},... | collective-permute-start | bytes 3145736 | tf_op jit(solution)/shard_map/ppermute | solution.py:282
  13.6 6.5 %resident.3.weights_ref = bf16[8,1024,1024]{2,1,0:T(8,128)(2,1)S(1)} custom-call(s32[9]{0:T(128)S(1)} %stack.69.at, bf16[8192,1024]{1,0:T(8,128)(2,1)} %bitcast.37), custom_call_target="tpu_custom_call" | custom-call | tf_op jit(solution)/shard_map/resident/pallas_call | solution.py:43
  22.8 13.3 %collective-permute-done.4.refs_0_ = bf16[4,256,512]{2,1,0:T(8,128)(2,1)S(1)} collective-permute-done((bf16[4,256,512]{2,1,0:T(8,128)(2,1)S(1)}, bf16[4,256,512]{2,1,0:T(8,128)(2,1)S(1)}, u32[]{:S(2)}, u32[]{:S(2)}) %collective-permute-start.4) | collective-permute-done | bytes 1048608 | tf_op jit(solution)/shard_map/ppermute | solution.py:282
  37.5 3.7 %collective-permute-start.11 = (bf16[256,512]{1,0:T(8,128)(2,1)S(1)}, bf16[256,512]{1,0:T(8,128)(2,1)S(1)}, u32[]{:S(2)}, u32[]{:S(2)}) collective-permute-start(bf16[256,512]{1,0:T(8,128)(2,1)S(1)} %get-tuple-element.45), channel_id=1, source_target_pairs={{8,10},{9,11},{10,8},{11,9},{12,14},{13,15},{14,12},{15,13},{0,2},... | collective-permute-start | bytes 786440 | tf_op jit(solution)/shard_map/ppermute | solution.py:282
  41.2 4.5 %collective-permute-start.12 = (bf16[256,512]{1,0:T(8,128)(2,1)S(1)}, bf16[256,512]{1,0:T(8,128)(2,1)S(1)}, u32[]{:S(2)}, u32[]{:S(2)}) collective-permute-start(bf16[256,512]{1,0:T(8,128)(2,1)S(1)} %get-tuple-element.46), channel_id=1, source_target_pairs={{8,12},{9,13},{10,14},{11,15},{12,8},{13,9},{14,10},{15,11},{0,4},... | collective-permute-start | bytes 786440 | tf_op jit(solution)/shard_map/ppermute | solution.py:282
  45.7 1.9 collective-permute-start.13
  52.1 12.0 %collective-permute-done.12 = bf16[256,512]{1,0:T(8,128)(2,1)S(1)} collective-permute-done((bf16[256,512]{1,0:T(8,128)(2,1)S(1)}, bf16[256,512]{1,0:T(8,128)(2,1)S(1)}, u32[]{:S(2)}, u32[]{:S(2)}) %collective-permute-start.12) | collective-permute-done | bytes 262176 | tf_op jit(solution)/shard_map/ppermute | solution.py:282
  69.7 6.5 %collective-permute-start.21 = (bf16[256,512]{1,0:T(8,128)(2,1)S(1)}, bf16[256,512]{1,0:T(8,128)(2,1)S(1)}, u32[]{:S(2)}, u32[]{:S(2)}) collective-permute-start(bf16[256,512]{1,0:T(8,128)(2,1)S(1)} %add_convert_fusion.1), channel_id=1, source_target_pairs={{8,12},{9,13},{10,14},{11,15},{12,8},{13,9},{14,10},{15,11},{0,4},... | collective-permute-start | bytes 786440 | tf_op jit(solution)/shard_map/ppermute | solution.py:282
  78.6 1.9 collective-permute-start.22
  80.5 6.2 %collective-permute-done.21 = bf16[256,512]{1,0:T(8,128)(2,1)S(1)} collective-permute-done((bf16[256,512]{1,0:T(8,128)(2,1)S(1)}, bf16[256,512]{1,0:T(8,128)(2,1)S(1)}, u32[]{:S(2)}, u32[]{:S(2)}) %collective-permute-start.21) | collective-permute-done | bytes 262176 | tf_op jit(solution)/shard_map/ppermute | solution.py:282
  86.8 1.9 collective-permute-start.23
  88.7 3.8 %collective-permute-done.22 = bf16[256,512]{1,0:T(8,128)(2,1)S(1)} collective-permute-done((bf16[256,512]{1,0:T(8,128)(2,1)S(1)}, bf16[256,512]{1,0:T(8,128)(2,1)S(1)}, u32[]{:S(2)}, u32[]{:S(2)}) %collective-permute-start.22) | collective-permute-done | bytes 262176 | tf_op jit(solution)/shard_map/ppermute | solution.py:282
  92.4 5.2 %collective-permute-done.23 = bf16[256,512]{1,0:T(8,128)(2,1)S(1)} collective-permute-done((bf16[256,512]{1,0:T(8,128)(2,1)S(1)}, bf16[256,512]{1,0:T(8,128)(2,1)S(1)}, u32[]{:S(2)}, u32[]{:S(2)}) %collective-permute-start.23) | collective-permute-done | bytes 262176 | tf_op jit(solution)/shard_map/ppermute | solution.py:282
  99.2 3.6 %collective-permute-start.28 = (bf16[4,256,512]{2,1,0:T(8,128)(2,1)S(1)}, bf16[4,256,512]{2,1,0:T(8,128)(2,1)S(1)}, u32[]{:S(2)}, u32[]{:S(2)}) collective-permute-start(bf16[4,256,512]{2,1,0:T(8,128)(2,1)S(1)} %pad_maximum_fusion.refs_4_), channel_id=1, source_target_pairs={{8,9},{9,8},{10,11},{11,10},{12,13},{13,12},{14,15},{15,14},{0,1},... | collective-permute-start | bytes 3145736 | tf_op jit(solution)/shard_map/ppermute | solution.py:282
  106.8 18.4 %collective-permute-done.28.refs_5_ = bf16[4,256,512]{2,1,0:T(8,128)(2,1)S(1)} collective-permute-done((bf16[4,256,512]{2,1,0:T(8,128)(2,1)S(1)}, bf16[4,256,512]{2,1,0:T(8,128)(2,1)S(1)}, u32[]{:S(2)}, u32[]{:S(2)}) %collective-permute-start.28) | collective-permute-done | bytes 1048608 | tf_op jit(solution)/shard_map/ppermute | solution.py:282
  130.8 1.3 collective-permute-start.35
  136.9 4.0 %resident.2.weights_ref = bf16[8,1024,512]{2,1,0:T(8,128)(2,1)S(1)} custom-call(s32[9]{0:T(128)S(1)} %stack.69.at, bf16[8192,512]{1,0:T(8,128)(2,1)} %bitcast.33), custom_call_target="tpu_custom_call" | custom-call | tf_op jit(solution)/shard_map/resident/pallas_call | solution.py:43
  141.0 14.7 %collective-permute-done.34.refs_0_ = bf16[256,1024]{1,0:T(8,128)(2,1)S(1)} collective-permute-done((bf16[256,1024]{1,0:T(8,128)(2,1)S(1)}, bf16[256,1024]{1,0:T(8,128)(2,1)S(1)}, u32[]{:S(2)}, u32[]{:S(2)}) %collective-permute-start.34) | collective-permute-done | bytes 524320 | tf_op jit(solution)/shard_map/ppermute | solution.py:282
  157.0 3.5 %collective-permute-done.35.refs_1_ = bf16[256,1024]{1,0:T(8,128)(2,1)S(1)} collective-permute-done((bf16[256,1024]{1,0:T(8,128)(2,1)S(1)}, bf16[256,1024]{1,0:T(8,128)(2,1)S(1)}, u32[]{:S(2)}, u32[]{:S(2)}) %collective-permute-start.35) | collective-permute-done | bytes 524320 | tf_op jit(solution)/shard_map/ppermute | solution.py:282
  160.5 1.5 block_dot.28.refs_2_
  161.9 3.8 %collective-permute-done.32.refs_0_ = bf16[256,1024]{1,0:T(8,128)(2,1)S(1)} collective-permute-done((bf16[256,1024]{1,0:T(8,128)(2,1)S(1)}, bf16[256,1024]{1,0:T(8,128)(2,1)S(1)}, u32[]{:S(2)}, u32[]{:S(2)}) %collective-permute-start.32) | collective-permute-done | bytes 524320 | tf_op jit(solution)/shard_map/ppermute | solution.py:282
  165.7 2.9 %collective-permute-start.36 = (bf16[256,1024]{1,0:T(8,128)(2,1)S(1)}, bf16[256,1024]{1,0:T(8,128)(2,1)S(1)}, u32[]{:S(2)}, u32[]{:S(2)}) collective-permute-start(bf16[256,1024]{1,0:T(8,128)(2,1)S(1)} %collective-permute-done.32.refs_0_), channel_id=1, source_target_pairs={{0,1},{1,0},{2,3},{3,2},{4,5},{5,4},{6,7},{7,6}} | collective-permute-start | bytes 1572872 | tf_op jit(solution)/shard_map/ppermute | solution.py:282
  168.6 1.9 collective-permute-start.33
  172.1 2.9 %collective-permute-start.39 = (bf16[256,1024]{1,0:T(8,128)(2,1)S(1)}, bf16[256,1024]{1,0:T(8,128)(2,1)S(1)}, u32[]{:S(2)}, u32[]{:S(2)}) collective-permute-start(bf16[256,1024]{1,0:T(8,128)(2,1)S(1)} %collective-permute-done.38.refs_0_), channel_id=1, source_target_pairs={{0,1},{1,0},{2,3},{3,2},{4,5},{5,4},{6,7},{7,6}} | collective-permute-start | bytes 1572872 | tf_op jit(solution)/shard_map/ppermute | solution.py:282
  175.0 1.7 collective-permute-done.36.refs_1_
  176.8 2.9 %collective-permute-done.33.refs_2_ = bf16[256,1024]{1,0:T(8,128)(2,1)S(1)} collective-permute-done((bf16[256,1024]{1,0:T(8,128)(2,1)S(1)}, bf16[256,1024]{1,0:T(8,128)(2,1)S(1)}, u32[]{:S(2)}, u32[]{:S(2)}) %collective-permute-start.33) | collective-permute-done | bytes 524320 | tf_op jit(solution)/shard_map/ppermute | solution.py:282
  179.7 2.9 %collective-permute-start.37 = (bf16[256,1024]{1,0:T(8,128)(2,1)S(1)}, bf16[256,1024]{1,0:T(8,128)(2,1)S(1)}, u32[]{:S(2)}, u32[]{:S(2)}) collective-permute-start(bf16[256,1024]{1,0:T(8,128)(2,1)S(1)} %collective-permute-done.33.refs_2_), channel_id=1, source_target_pairs={{0,1},{1,0},{2,3},{3,2},{4,5},{5,4},{6,7},{7,6}} | collective-permute-start | bytes 1572872 | tf_op jit(solution)/shard_map/ppermute | solution.py:282
  182.6 1.5 block_dot.29.refs_3_
  184.1 1.7 block_dot.30.refs_1_
  185.8 4.9 %collective-permute-done.37.refs_0_ = bf16[256,1024]{1,0:T(8,128)(2,1)S(1)} collective-permute-done((bf16[256,1024]{1,0:T(8,128)(2,1)S(1)}, bf16[256,1024]{1,0:T(8,128)(2,1)S(1)}, u32[]{:S(2)}, u32[]{:S(2)}) %collective-permute-start.37) | collective-permute-done | bytes 524320 | tf_op jit(solution)/shard_map/ppermute | solution.py:282
  191.9 12.2 %mean_square.1 = f32[512,4096]{1,0:T(8,128)} custom-call(s32[9]{0:T(128)S(1)} %stack.69.at, bf16[256,512]{1,0:T(8,128)(2,1)S(1)} %block_dot.31.refs_0_, bf16[256,512]{1,0:T(8,128)(2,1)S(1)} %stream_dot.5.refs_1_, bf16[256,512]{1,0:T(8,128)(2,1)S(1)} %stream_dot.4.refs_2_, bf16[256,512]{1,0:T(8,128)(2,1)S(1)} %stream_dot.3.refs_3_, ...), custom_call_target="tpu_custom_call" | custom-call | tf_op jit(solution)/shard_map/mean_square/pallas_call | solution.py:245
  (98 shorter events, 39.3 us)
Async XLA Ops:
  0.0 20.1 %collective-permute-start.2 = (bf16[256,1024]{1,0:T(8,128)(2,1)}, bf16[256,1024]{1,0:T(8,128)(2,1)S(1)}, u32[]{:S(2)}, u32[]{:S(2)}) collective-permute-start(bf16[256,1024]{1,0:T(8,128)(2,1)} %bitcast.23), channel_id=1, source_target_pairs={{24,25},{25,24},{26,27},{27,26},{28,29},{29,28},{30,31},{31,30}} | collective-permute-start | bytes 1572872 | tf_op jit(solution)/shard_map/ppermute | solution.py:282
  0.8 19.3 %collective-permute-start = (bf16[256,1024]{1,0:T(8,128)(2,1)}, bf16[256,1024]{1,0:T(8,128)(2,1)S(1)}, u32[]{:S(2)}, u32[]{:S(2)}) collective-permute-start(bf16[256,1024]{1,0:T(8,128)(2,1)} %bitcast.24), channel_id=1, source_target_pairs={{24,28},{25,29},{26,30},{27,31},{28,24},{29,25},{30,26},{31,27}} | collective-permute-start | bytes 1572872 | tf_op jit(solution)/shard_map/ppermute | solution.py:282
  8.0 28.0 %collective-permute-start.4 = (bf16[4,256,512]{2,1,0:T(8,128)(2,1)S(1)}, bf16[4,256,512]{2,1,0:T(8,128)(2,1)S(1)}, u32[]{:S(2)}, u32[]{:S(2)}) collective-permute-start(bf16[4,256,512]{2,1,0:T(8,128)(2,1)S(1)} %get-tuple-element.40), channel_id=1, source_target_pairs={{8,9},{9,8},{10,11},{11,10},{12,13},{13,12},{14,15},{15,14},{0,1},... | collective-permute-start | bytes 3145736 | tf_op jit(solution)/shard_map/ppermute | solution.py:282
  20.1 16.7 %collective-permute-start.3 = (bf16[256,1024]{1,0:T(8,128)(2,1)S(1)}, bf16[256,1024]{1,0:T(8,128)(2,1)S(1)}, u32[]{:S(2)}, u32[]{:S(2)}) collective-permute-start(bf16[256,1024]{1,0:T(8,128)(2,1)S(1)} %collective-permute-done.refs_0_.refs_2_), channel_id=1, source_target_pairs={{24,25},{25,24},{26,27},{27,26},{28,29},{29,28},{30,31},{31,30}} | collective-permute-start | bytes 1572872 | tf_op jit(solution)/shard_map/ppermute | solution.py:282
  20.8 16.0 %collective-permute-start.1 = (bf16[256,1024]{1,0:T(8,128)(2,1)S(1)}, bf16[256,1024]{1,0:T(8,128)(2,1)S(1)}, u32[]{:S(2)}, u32[]{:S(2)}) collective-permute-start(bf16[256,1024]{1,0:T(8,128)(2,1)S(1)} %collective-permute-done.refs_0_.refs_2_), channel_id=1, source_target_pairs={{24,26},{25,27},{26,24},{27,25},{28,30},{29,31},{30,28},{31,29}} | collective-permute-start | bytes 1572872 | tf_op jit(solution)/shard_map/ppermute | solution.py:282
  22.1 26.1 %collective-permute-start.7 = (bf16[256,1024]{1,0:T(8,128)(2,1)S(1)}, bf16[256,1024]{1,0:T(8,128)(2,1)S(1)}, u32[]{:S(2)}, u32[]{:S(2)}) collective-permute-start(bf16[256,1024]{1,0:T(8,128)(2,1)S(1)} %collective-permute-done.6.refs_0_.refs_4_), channel_id=1, source_target_pairs={{24,25},{25,24},{26,27},{27,26},{28,29},{29,28},{30,31},{31,30}} | collective-permute-start | bytes 1572872 | tf_op jit(solution)/shard_map/ppermute | solution.py:282
  36.8 12.0 %collective-permute-start.5 = (bf16[256,1024]{1,0:T(8,128)(2,1)S(1)}, bf16[256,1024]{1,0:T(8,128)(2,1)S(1)}, u32[]{:S(2)}, u32[]{:S(2)}) collective-permute-start(bf16[256,1024]{1,0:T(8,128)(2,1)S(1)} %collective-permute-done.1.refs_2_.refs_6_), channel_id=1, source_target_pairs={{24,25},{25,24},{26,27},{27,26},{28,29},{29,28},{30,31},{31,30}} | collective-permute-start | bytes 1572872 | tf_op jit(solution)/shard_map/ppermute | solution.py:282
  37.5 13.3 %collective-permute-start.11 = (bf16[256,512]{1,0:T(8,128)(2,1)S(1)}, bf16[256,512]{1,0:T(8,128)(2,1)S(1)}, u32[]{:S(2)}, u32[]{:S(2)}) collective-permute-start(bf16[256,512]{1,0:T(8,128)(2,1)S(1)} %get-tuple-element.45), channel_id=1, source_target_pairs={{8,10},{9,11},{10,8},{11,9},{12,14},{13,15},{14,12},{15,13},{0,2},... | collective-permute-start | bytes 786440 | tf_op jit(solution)/shard_map/ppermute | solution.py:282
  41.2 22.8 %collective-permute-start.12 = (bf16[256,512]{1,0:T(8,128)(2,1)S(1)}, bf16[256,512]{1,0:T(8,128)(2,1)S(1)}, u32[]{:S(2)}, u32[]{:S(2)}) collective-permute-start(bf16[256,512]{1,0:T(8,128)(2,1)S(1)} %get-tuple-element.46), channel_id=1, source_target_pairs={{8,12},{9,13},{10,14},{11,15},{12,8},{13,9},{14,10},{15,11},{0,4},... | collective-permute-start | bytes 786440 | tf_op jit(solution)/shard_map/ppermute | solution.py:282
  45.7 19.1 %collective-permute-start.13 = (bf16[256,512]{1,0:T(8,128)(2,1)S(1)}, bf16[256,512]{1,0:T(8,128)(2,1)S(1)}, u32[]{:S(2)}, u32[]{:S(2)}) collective-permute-start(bf16[256,512]{1,0:T(8,128)(2,1)S(1)} %get-tuple-element.47), channel_id=1, source_target_pairs={{8,14},{9,15},{10,12},{11,13},{12,10},{13,11},{14,8},{15,9},{0,6},... | collective-permute-start | bytes 786440 | tf_op jit(solution)/shard_map/ppermute | solution.py:282
  49.3 16.3 %collective-permute-start.10 = (bf16[256,1024]{1,0:T(8,128)(2,1)S(1)}, bf16[256,1024]{1,0:T(8,128)(2,1)S(1)}, u32[]{:S(2)}, u32[]{:S(2)}) collective-permute-start(bf16[256,1024]{1,0:T(8,128)(2,1)S(1)} %block_dot.19), channel_id=1, source_target_pairs={{24,16},{25,17},{26,18},{27,19},{28,20},{29,21},{30,22},{31,23}} | collective-permute-start | bytes 1572872 | tf_op jit(solution)/shard_map/ppermute | solution.py:282
  50.0 15.6 %collective-permute-start.14 = (bf16[256,1024]{1,0:T(8,128)(2,1)S(1)}, bf16[256,1024]{1,0:T(8,128)(2,1)S(1)}, u32[]{:S(2)}, u32[]{:S(2)}) collective-permute-start(bf16[256,1024]{1,0:T(8,128)(2,1)S(1)} %block_dot.19), channel_id=1, source_target_pairs={{24,17},{25,16},{26,19},{27,18},{28,21},{29,20},{30,23},{31,22}} | collective-permute-start | bytes 1572872 | tf_op jit(solution)/shard_map/ppermute | solution.py:282
  50.8 15.5 %collective-permute-start.8 = (bf16[256,1024]{1,0:T(8,128)(2,1)S(1)}, bf16[256,1024]{1,0:T(8,128)(2,1)S(1)}, u32[]{:S(2)}, u32[]{:S(2)}) collective-permute-start(bf16[256,1024]{1,0:T(8,128)(2,1)S(1)} %block_dot.19), channel_id=1, source_target_pairs={{24,20},{25,21},{26,22},{27,23},{28,16},{29,17},{30,18},{31,19}} | collective-permute-start | bytes 1572872 | tf_op jit(solution)/shard_map/ppermute | solution.py:282
  69.7 17.0 %collective-permute-start.21 = (bf16[256,512]{1,0:T(8,128)(2,1)S(1)}, bf16[256,512]{1,0:T(8,128)(2,1)S(1)}, u32[]{:S(2)}, u32[]{:S(2)}) collective-permute-start(bf16[256,512]{1,0:T(8,128)(2,1)S(1)} %add_convert_fusion.1), channel_id=1, source_target_pairs={{8,12},{9,13},{10,14},{11,15},{12,8},{13,9},{14,10},{15,11},{0,4},... | collective-permute-start | bytes 786440 | tf_op jit(solution)/shard_map/ppermute | solution.py:282
  77.9 19.9 %collective-permute-start.20 = (bf16[256,1024]{1,0:T(8,128)(2,1)S(1)}, bf16[256,1024]{1,0:T(8,128)(2,1)S(1)}, u32[]{:S(2)}, u32[]{:S(2)}) collective-permute-start(bf16[256,1024]{1,0:T(8,128)(2,1)S(1)} %block_dot.23), channel_id=1, source_target_pairs={{16,8},{17,9},{18,10},{19,11},{20,12},{21,13},{22,14},{23,15}} | collective-permute-start | bytes 1572872 | tf_op jit(solution)/shard_map/ppermute | solution.py:282
  78.6 13.8 %collective-permute-start.22 = (bf16[256,512]{1,0:T(8,128)(2,1)S(1)}, bf16[256,512]{1,0:T(8,128)(2,1)S(1)}, u32[]{:S(2)}, u32[]{:S(2)}) collective-permute-start(bf16[256,512]{1,0:T(8,128)(2,1)S(1)} %add_convert_fusion.1), channel_id=1, source_target_pairs={{8,10},{9,11},{10,8},{11,9},{12,14},{13,15},{14,12},{15,13},{0,2},... | collective-permute-start | bytes 786440 | tf_op jit(solution)/shard_map/ppermute | solution.py:282
  86.8 10.8 %collective-permute-start.23 = (bf16[256,512]{1,0:T(8,128)(2,1)S(1)}, bf16[256,512]{1,0:T(8,128)(2,1)S(1)}, u32[]{:S(2)}, u32[]{:S(2)}) collective-permute-start(bf16[256,512]{1,0:T(8,128)(2,1)S(1)} %collective-permute-done.21), channel_id=1, source_target_pairs={{8,10},{9,11},{10,8},{11,9},{12,14},{13,15},{14,12},{15,13},{0,2},... | collective-permute-start | bytes 786440 | tf_op jit(solution)/shard_map/ppermute | solution.py:282
  99.2 26.1 %collective-permute-start.28 = (bf16[4,256,512]{2,1,0:T(8,128)(2,1)S(1)}, bf16[4,256,512]{2,1,0:T(8,128)(2,1)S(1)}, u32[]{:S(2)}, u32[]{:S(2)}) collective-permute-start(bf16[4,256,512]{2,1,0:T(8,128)(2,1)S(1)} %pad_maximum_fusion.refs_4_), channel_id=1, source_target_pairs={{8,9},{9,8},{10,11},{11,10},{12,13},{13,12},{14,15},{15,14},{0,1},... | collective-permute-start | bytes 3145736 | tf_op jit(solution)/shard_map/ppermute | solution.py:282
  104.1 21.2 %collective-permute-start.27 = (bf16[256,1024]{1,0:T(8,128)(2,1)S(1)}, bf16[256,1024]{1,0:T(8,128)(2,1)S(1)}, u32[]{:S(2)}, u32[]{:S(2)}) collective-permute-start(bf16[256,1024]{1,0:T(8,128)(2,1)S(1)} %collective-permute-done.24.refs_0_.refs_2_), channel_id=1, source_target_pairs={{8,9},{9,8},{10,11},{11,10},{12,13},{13,12},{14,15},{15,14}} | collective-permute-start | bytes 1572872 | tf_op jit(solution)/shard_map/ppermute | solution.py:282
  104.8 20.5 %collective-permute-start.25 = (bf16[256,1024]{1,0:T(8,128)(2,1)S(1)}, bf16[256,1024]{1,0:T(8,128)(2,1)S(1)}, u32[]{:S(2)}, u32[]{:S(2)}) collective-permute-start(bf16[256,1024]{1,0:T(8,128)(2,1)S(1)} %collective-permute-done.24.refs_0_.refs_2_), channel_id=1, source_target_pairs={{8,10},{9,11},{10,8},{11,9},{12,14},{13,15},{14,12},{15,13}} | collective-permute-start | bytes 1572872 | tf_op jit(solution)/shard_map/ppermute | solution.py:282
  106.1 23.6 %collective-permute-start.31 = (bf16[256,1024]{1,0:T(8,128)(2,1)S(1)}, bf16[256,1024]{1,0:T(8,128)(2,1)S(1)}, u32[]{:S(2)}, u32[]{:S(2)}) collective-permute-start(bf16[256,1024]{1,0:T(8,128)(2,1)S(1)} %collective-permute-done.30.refs_0_.refs_4_), channel_id=1, source_target_pairs={{8,9},{9,8},{10,11},{11,10},{12,13},{13,12},{14,15},{15,14}} | collective-permute-start | bytes 1572872 | tf_op jit(solution)/shard_map/ppermute | solution.py:282
  130.8 29.7 %collective-permute-start.35 = (bf16[256,1024]{1,0:T(8,128)(2,1)S(1)}, bf16[256,1024]{1,0:T(8,128)(2,1)S(1)}, u32[]{:S(2)}, u32[]{:S(2)}) collective-permute-start(bf16[256,1024]{1,0:T(8,128)(2,1)S(1)} %block_dot.27), channel_id=1, source_target_pairs={{8,1},{9,0},{10,3},{11,2},{12,5},{13,4},{14,7},{15,6}} | collective-permute-start | bytes 1572872 | tf_op jit(solution)/shard_map/ppermute | solution.py:282
  132.1 23.6 %collective-permute-start.34 = (bf16[256,1024]{1,0:T(8,128)(2,1)S(1)}, bf16[256,1024]{1,0:T(8,128)(2,1)S(1)}, u32[]{:S(2)}, u32[]{:S(2)}) collective-permute-start(bf16[256,1024]{1,0:T(8,128)(2,1)S(1)} %block_dot.27), channel_id=1, source_target_pairs={{8,0},{9,1},{10,2},{11,3},{12,4},{13,5},{14,6},{15,7}} | collective-permute-start | bytes 1572872 | tf_op jit(solution)/shard_map/ppermute | solution.py:282
  133.4 32.3 %collective-permute-start.32 = (bf16[256,1024]{1,0:T(8,128)(2,1)S(1)}, bf16[256,1024]{1,0:T(8,128)(2,1)S(1)}, u32[]{:S(2)}, u32[]{:S(2)}) collective-permute-start(bf16[256,1024]{1,0:T(8,128)(2,1)S(1)} %block_dot.27), channel_id=1, source_target_pairs={{8,4},{9,5},{10,6},{11,7},{12,0},{13,1},{14,2},{15,3}} | collective-permute-start | bytes 1572872 | tf_op jit(solution)/shard_map/ppermute | solution.py:282
  135.6 35.0 %collective-permute-start.44 = (bf16[256,512]{1,0:T(8,128)(2,1)S(1)}, bf16[256,512]{1,0:T(8,128)(2,1)S(1)}, u32[]{:S(2)}, u32[]{:S(2)}) collective-permute-start(bf16[256,512]{1,0:T(8,128)(2,1)S(1)} %add_convert_fusion), channel_id=1, source_target_pairs={{24,26},{25,27},{26,24},{27,25},{28,30},{29,31},{30,28},{31,29},{1... | collective-permute-start | bytes 786440 | tf_op jit(solution)/shard_map/ppermute | solution.py:282
  136.3 34.3 %collective-permute-start.45 = (bf16[256,512]{1,0:T(8,128)(2,1)S(1)}, bf16[256,512]{1,0:T(8,128)(2,1)S(1)}, u32[]{:S(2)}, u32[]{:S(2)}) collective-permute-start(bf16[256,512]{1,0:T(8,128)(2,1)S(1)} %collective-permute-done.43), channel_id=1, source_target_pairs={{24,26},{25,27},{26,24},{27,25},{28,30},{29,31},{30,28},{31,29},{1... | collective-permute-start | bytes 786440 | tf_op jit(solution)/shard_map/ppermute | solution.py:282
  155.7 16.4 %collective-permute-start.38 = (bf16[256,1024]{1,0:T(8,128)(2,1)S(1)}, bf16[256,1024]{1,0:T(8,128)(2,1)S(1)}, u32[]{:S(2)}, u32[]{:S(2)}) collective-permute-start(bf16[256,1024]{1,0:T(8,128)(2,1)S(1)} %block_dot.27), channel_id=1, source_target_pairs={{8,2},{9,3},{10,0},{11,1},{12,6},{13,7},{14,4},{15,5}} | collective-permute-start | bytes 1572872 | tf_op jit(solution)/shard_map/ppermute | solution.py:282
  165.7 11.1 %collective-permute-start.36 = (bf16[256,1024]{1,0:T(8,128)(2,1)S(1)}, bf16[256,1024]{1,0:T(8,128)(2,1)S(1)}, u32[]{:S(2)}, u32[]{:S(2)}) collective-permute-start(bf16[256,1024]{1,0:T(8,128)(2,1)S(1)} %collective-permute-done.32.refs_0_), channel_id=1, source_target_pairs={{0,1},{1,0},{2,3},{3,2},{4,5},{5,4},{6,7},{7,6}} | collective-permute-start | bytes 1572872 | tf_op jit(solution)/shard_map/ppermute | solution.py:282
  168.6 11.1 %collective-permute-start.33 = (bf16[256,1024]{1,0:T(8,128)(2,1)S(1)}, bf16[256,1024]{1,0:T(8,128)(2,1)S(1)}, u32[]{:S(2)}, u32[]{:S(2)}) collective-permute-start(bf16[256,1024]{1,0:T(8,128)(2,1)S(1)} %collective-permute-done.32.refs_0_), channel_id=1, source_target_pairs={{0,2},{1,3},{2,0},{3,1},{4,6},{5,7},{6,4},{7,5}} | collective-permute-start | bytes 1572872 | tf_op jit(solution)/shard_map/ppermute | solution.py:282
  170.7 21.2 %collective-permute-start.46 = (bf16[4,256,512]{2,1,0:T(8,128)(2,1)S(1)}, bf16[4,256,512]{2,1,0:T(8,128)(2,1)S(1)}, u32[]{:S(2)}, u32[]{:S(2)}) collective-permute-start(bf16[4,256,512]{2,1,0:T(8,128)(2,1)S(1)} %pad_maximum_fusion.1.refs_6_), channel_id=1, source_target_pairs={{24,25},{25,24},{26,27},{27,26},{28,29},{29,28},{30,31},{31,30},{1... | collective-permute-start | bytes 3145736 | tf_op jit(solution)/shard_map/ppermute | solution.py:282
  172.1 12.0 %collective-permute-start.39 = (bf16[256,1024]{1,0:T(8,128)(2,1)S(1)}, bf16[256,1024]{1,0:T(8,128)(2,1)S(1)}, u32[]{:S(2)}, u32[]{:S(2)}) collective-permute-start(bf16[256,1024]{1,0:T(8,128)(2,1)S(1)} %collective-permute-done.38.refs_0_), channel_id=1, source_target_pairs={{0,1},{1,0},{2,3},{3,2},{4,5},{5,4},{6,7},{7,6}} | collective-permute-start | bytes 1572872 | tf_op jit(solution)/shard_map/ppermute | solution.py:282
  179.7 11.1 %collective-permute-start.37 = (bf16[256,1024]{1,0:T(8,128)(2,1)S(1)}, bf16[256,1024]{1,0:T(8,128)(2,1)S(1)}, u32[]{:S(2)}, u32[]{:S(2)}) collective-permute-start(bf16[256,1024]{1,0:T(8,128)(2,1)S(1)} %collective-permute-done.33.refs_2_), channel_id=1, source_target_pairs={{0,1},{1,0},{2,3},{3,2},{4,5},{5,4},{6,7},{7,6}} | collective-permute-start | bytes 1572872 | tf_op jit(solution)/shard_map/ppermute | solution.py:282
  (17 other events, 93.6 us)

commit v11 on v10

--- a/solution.py
+++ b/solution.py
@@ -392,17 +392,22 @@
             before, within = before + last_others, within + last_arrived
     low = outer_columns(low, lower, halves, [grad])
     sent = handed_down(grad, lower[0], low)
-    low = all_columns(low, lower)
+    if len(lower) == 1:
+        low = all_columns(low, lower)
     rot_outs[upper[-1]] = rotated(upper[-1], blocks)
     last_cols = resident(at, out_cols, 0)
     own, last_own, _ = lax.optimization_barrier((own, last_own, sent[0][0]))
-    before, within = [], [rot_outs[upper[-1]], *jax.tree.leaves(low)]
+    before, within = [], [rot_outs[upper[-1]]]
     for turn in lower:
         grad, blocks = relay(turn, sent, before, within, weights if turn else last_cols)
         if turn != 0:
             sent = handed_down(grad, turn - 1)
             rot_outs[turn] = rotated(turn, blocks)
             before, within = [], [rot_outs[turn]]
+        if turn == lower[0] and turn != 0:
+            low, _ = lax.optimization_barrier((low, sent[0][0]))
+            low = all_columns(low, lower)
+            within = within + jax.tree.leaves(low)
     rot_outs[0] = grad
     sums = added(at, upper[:1], last_own, last_arrived, added(at, upper[1:], own, arrived))
     high = all_columns(outer_columns(summed(sums, upper), upper, [order]), upper)

time: 205 us -> 210 us (1.024)
  waiting for transfers between devices: 90.5 us -> 95.9 us
    ppermute x47, waiting for transfers between devices: 90.5 us -> 95.9 us  [moved(): return lax.ppermute(block, ('section', 'shard'), route)]
  transfers between devices with their start and end apart: 47 -> 47, of which waited for: 12 -> 11; matrix products, arithmetic and copies ran while one was open for 0% -> 0% of each run, Pallas kernels for 16% -> 16%
where the time goes in v11:
time: 210 us; the launch traced here: 209 us
  waiting for transfers between devices  95.9 us (46%)
  starting transfers between devices  65.8 us (31%)
  Pallas kernels  44.7 us (21%)
    ppermute x47, waiting for transfers between devices, moved(): return lax.ppermute(block, ('section', 'shard'), route)  95.9 us
    ppermute x47, starting transfers between devices, moved(): return lax.ppermute(block, ('section', 'shard'), route)  65.8 us
    pallas_call x16, Pallas kernels, block_dot(): pl.pallas_call(body, in_specs=[SMEM] + [VMEM] * (1 + count + (base is not...  12.4 us
    pallas_call x1, Pallas kernels, mean_square(): pl.pallas_call(body, in_specs=[SMEM] + [VMEM] * (sections + len(low) + le...  12.2 us
    pallas_call x2, Pallas kernels, resident(): pl.pallas_call(body, in_specs=[SMEM, HBM], out_specs=VMEM, out_shape=jax....  10.5 us
    pallas_call x2, Pallas kernels, partials(): pl.pallas_call(body, in_specs=[SMEM, HBM, VMEM], out_specs=[VMEM] * inner...  5.98 us
  transfers between devices with their start and end apart: 47, of which 11 were waited for; matrix products, arithmetic and copies ran while one was open for 0% of the time, Pallas kernels for 16%

profile of v11, /device:TPU:0, one launch (start us, length us, event | category | flops | bytes accessed | tf_op | source)
XLA Modules:
  0.0 209.1 jit_solution(8208682395310584918)
XLA Ops:
  2.7 5.4 %partials.2 = (f32[4,256,512]{2,1,0:T(8,128)S(1)}, bf16[4,256,512]{2,1,0:T(8,128)(2,1)S(1)}) custom-call(s32[9]{0:T(128)S(1)} %stack.69.at, bf16[1024,4096]{1,0:T(8,128)(2,1)} %bitcast.35, bf16[256,1024]{1,0:T(8,128)(2,1)S(1)} %bitcast.29), custom_call_target="tpu_custom_call" | custom-call | tf_op jit(solution)/shard_map/partials/pallas_call | solution.py:150
  8.0 4.8 %collective-permute-start.4 = (bf16[4,256,512]{2,1,0:T(8,128)(2,1)S(1)}, bf16[4,256,512]{2,1,0:T(8,128)(2,1)S(1)}, u32[]{:S(2)}, u32[]{:S(2)}) collective-permute-start(bf16[4,256,512]{2,1,0:T(8,128)(2,1)S(1)} %get-tuple-element.41), channel_id=1, source_target_pairs={{8,9},{9,8},{10,11},{11,10},{12,13},{13,12},{14,15},{15,14},{0,1},... | collective-permute-start | bytes 3145736 | tf_op jit(solution)/shard_map/ppermute | solution.py:282
  13.6 6.5 %resident.3.weights_ref = bf16[8,1024,1024]{2,1,0:T(8,128)(2,1)S(1)} custom-call(s32[9]{0:T(128)S(1)} %stack.69.at, bf16[8192,1024]{1,0:T(8,128)(2,1)} %bitcast.37), custom_call_target="tpu_custom_call" | custom-call | tf_op jit(solution)/shard_map/resident/pallas_call | solution.py:43
  22.8 13.3 %collective-permute-done.4.refs_0_ = bf16[4,256,512]{2,1,0:T(8,128)(2,1)S(1)} collective-permute-done((bf16[4,256,512]{2,1,0:T(8,128)(2,1)S(1)}, bf16[4,256,512]{2,1,0:T(8,128)(2,1)S(1)}, u32[]{:S(2)}, u32[]{:S(2)}) %collective-permute-start.4) | collective-permute-done | bytes 1048608 | tf_op jit(solution)/shard_map/ppermute | solution.py:282
  37.5 3.7 %collective-permute-start.11 = (bf16[256,512]{1,0:T(8,128)(2,1)S(1)}, bf16[256,512]{1,0:T(8,128)(2,1)S(1)}, u32[]{:S(2)}, u32[]{:S(2)}) collective-permute-start(bf16[256,512]{1,0:T(8,128)(2,1)S(1)} %get-tuple-element.46), channel_id=1, source_target_pairs={{8,10},{9,11},{10,8},{11,9},{12,14},{13,15},{14,12},{15,13},{0,2},... | collective-permute-start | bytes 786440 | tf_op jit(solution)/shard_map/ppermute | solution.py:282
  41.2 4.5 %collective-permute-start.12 = (bf16[256,512]{1,0:T(8,128)(2,1)S(1)}, bf16[256,512]{1,0:T(8,128)(2,1)S(1)}, u32[]{:S(2)}, u32[]{:S(2)}) collective-permute-start(bf16[256,512]{1,0:T(8,128)(2,1)S(1)} %get-tuple-element.47), channel_id=1, source_target_pairs={{8,12},{9,13},{10,14},{11,15},{12,8},{13,9},{14,10},{15,11},{0,4},... | collective-permute-start | bytes 786440 | tf_op jit(solution)/shard_map/ppermute | solution.py:282
  45.7 1.9 collective-permute-start.13
  52.1 12.0 %collective-permute-done.12 = bf16[256,512]{1,0:T(8,128)(2,1)S(1)} collective-permute-done((bf16[256,512]{1,0:T(8,128)(2,1)S(1)}, bf16[256,512]{1,0:T(8,128)(2,1)S(1)}, u32[]{:S(2)}, u32[]{:S(2)}) %collective-permute-start.12) | collective-permute-done | bytes 262176 | tf_op jit(solution)/shard_map/ppermute | solution.py:282
  69.7 6.5 %collective-permute-start.21 = (bf16[256,512]{1,0:T(8,128)(2,1)S(1)}, bf16[256,512]{1,0:T(8,128)(2,1)S(1)}, u32[]{:S(2)}, u32[]{:S(2)}) collective-permute-start(bf16[256,512]{1,0:T(8,128)(2,1)S(1)} %add_convert_fusion.1), channel_id=1, source_target_pairs={{8,12},{9,13},{10,14},{11,15},{12,8},{13,9},{14,10},{15,11},{0,4},... | collective-permute-start | bytes 786440 | tf_op jit(solution)/shard_map/ppermute | solution.py:282
  78.6 1.9 collective-permute-start.22
  80.5 6.2 %collective-permute-done.21 = bf16[256,512]{1,0:T(8,128)(2,1)S(1)} collective-permute-done((bf16[256,512]{1,0:T(8,128)(2,1)S(1)}, bf16[256,512]{1,0:T(8,128)(2,1)S(1)}, u32[]{:S(2)}, u32[]{:S(2)}) %collective-permute-start.21) | collective-permute-done | bytes 262176 | tf_op jit(solution)/shard_map/ppermute | solution.py:282
  86.8 1.9 collective-permute-start.23
  88.7 3.8 %collective-permute-done.22 = bf16[256,512]{1,0:T(8,128)(2,1)S(1)} collective-permute-done((bf16[256,512]{1,0:T(8,128)(2,1)S(1)}, bf16[256,512]{1,0:T(8,128)(2,1)S(1)}, u32[]{:S(2)}, u32[]{:S(2)}) %collective-permute-start.22) | collective-permute-done | bytes 262176 | tf_op jit(solution)/shard_map/ppermute | solution.py:282
  92.4 5.2 %collective-permute-done.23 = bf16[256,512]{1,0:T(8,128)(2,1)S(1)} collective-permute-done((bf16[256,512]{1,0:T(8,128)(2,1)S(1)}, bf16[256,512]{1,0:T(8,128)(2,1)S(1)}, u32[]{:S(2)}, u32[]{:S(2)}) %collective-permute-start.23) | collective-permute-done | bytes 262176 | tf_op jit(solution)/shard_map/ppermute | solution.py:282
  109.0 1.3 collective-permute-start.33
  110.3 1.3 collective-permute-start.34
  111.6 1.3 collective-permute-start.31
  113.7 34.9 %collective-permute-done.33.refs_0_ = bf16[256,1024]{1,0:T(8,128)(2,1)S(1)} collective-permute-done((bf16[256,1024]{1,0:T(8,128)(2,1)S(1)}, bf16[256,1024]{1,0:T(8,128)(2,1)S(1)}, u32[]{:S(2)}, u32[]{:S(2)}) %collective-permute-start.33) | collective-permute-done | bytes 524320 | tf_op jit(solution)/shard_map/ppermute | solution.py:282
  148.6 3.1 %collective-permute-start.36 = (bf16[4,256,512]{2,1,0:T(8,128)(2,1)S(1)}, bf16[4,256,512]{2,1,0:T(8,128)(2,1)S(1)}, u32[]{:S(2)}, u32[]{:S(2)}) collective-permute-start(bf16[4,256,512]{2,1,0:T(8,128)(2,1)S(1)} %pad_maximum_fusion.refs_4_), channel_id=1, source_target_pairs={{8,9},{9,8},{10,11},{11,10},{12,13},{13,12},{14,15},{15,14},{0,1},... | collective-permute-start | bytes 3145736 | tf_op jit(solution)/shard_map/ppermute | solution.py:282
  153.2 4.0 %resident.2.weights_ref = bf16[8,1024,512]{2,1,0:T(8,128)(2,1)S(1)} custom-call(s32[9]{0:T(128)S(1)} %stack.69.at, bf16[8192,512]{1,0:T(8,128)(2,1)} %bitcast.33), custom_call_target="tpu_custom_call" | custom-call | tf_op jit(solution)/shard_map/resident/pallas_call | solution.py:43
  158.4 1.3 collective-permute-start.38
  159.7 1.4 block_dot.28.refs_2_
  162.4 3.0 %collective-permute-start.35 = (bf16[256,1024]{1,0:T(8,128)(2,1)S(1)}, bf16[256,1024]{1,0:T(8,128)(2,1)S(1)}, u32[]{:S(2)}, u32[]{:S(2)}) collective-permute-start(bf16[256,1024]{1,0:T(8,128)(2,1)S(1)} %collective-permute-done.31.refs_0_), channel_id=1, source_target_pairs={{0,1},{1,0},{2,3},{3,2},{4,5},{5,4},{6,7},{7,6}} | collective-permute-start | bytes 1572872 | tf_op jit(solution)/shard_map/ppermute | solution.py:282
  165.4 1.9 collective-permute-start.32
  168.9 2.8 %collective-permute-start.39 = (bf16[256,1024]{1,0:T(8,128)(2,1)S(1)}, bf16[256,1024]{1,0:T(8,128)(2,1)S(1)}, u32[]{:S(2)}, u32[]{:S(2)}) collective-permute-start(bf16[256,1024]{1,0:T(8,128)(2,1)S(1)} %collective-permute-done.38.refs_0_), channel_id=1, source_target_pairs={{0,1},{1,0},{2,3},{3,2},{4,5},{5,4},{6,7},{7,6}} | collective-permute-start | bytes 1572872 | tf_op jit(solution)/shard_map/ppermute | solution.py:282
  171.7 12.7 %collective-permute-done.35.refs_1_ = bf16[256,1024]{1,0:T(8,128)(2,1)S(1)} collective-permute-done((bf16[256,1024]{1,0:T(8,128)(2,1)S(1)}, bf16[256,1024]{1,0:T(8,128)(2,1)S(1)}, u32[]{:S(2)}, u32[]{:S(2)}) %collective-permute-start.35) | collective-permute-done | bytes 524320 | tf_op jit(solution)/shard_map/ppermute | solution.py:282
  184.4 2.7 %collective-permute-start.37 = (bf16[256,1024]{1,0:T(8,128)(2,1)S(1)}, bf16[256,1024]{1,0:T(8,128)(2,1)S(1)}, u32[]{:S(2)}, u32[]{:S(2)}) collective-permute-start(bf16[256,1024]{1,0:T(8,128)(2,1)S(1)} %collective-permute-done.32.refs_2_), channel_id=1, source_target_pairs={{0,1},{1,0},{2,3},{3,2},{4,5},{5,4},{6,7},{7,6}} | collective-permute-start | bytes 1572872 | tf_op jit(solution)/shard_map/ppermute | solution.py:282
  187.1 1.4 block_dot.29.refs_3_
  188.5 1.5 collective-permute-done.39.refs_1_
  190.0 1.7 block_dot.30.refs_1_
  191.7 3.9 %collective-permute-done.37.refs_0_ = bf16[256,1024]{1,0:T(8,128)(2,1)S(1)} collective-permute-done((bf16[256,1024]{1,0:T(8,128)(2,1)S(1)}, bf16[256,1024]{1,0:T(8,128)(2,1)S(1)}, u32[]{:S(2)}, u32[]{:S(2)}) %collective-permute-start.37) | collective-permute-done | bytes 524320 | tf_op jit(solution)/shard_map/ppermute | solution.py:282
  196.8 12.2 %mean_square.1 = f32[512,4096]{1,0:T(8,128)} custom-call(s32[9]{0:T(128)S(1)} %stack.69.at, bf16[256,512]{1,0:T(8,128)(2,1)S(1)} %block_dot.31.refs_0_, bf16[256,512]{1,0:T(8,128)(2,1)S(1)} %stream_dot.5.refs_1_, bf16[256,512]{1,0:T(8,128)(2,1)S(1)} %stream_dot.4.refs_2_, bf16[256,512]{1,0:T(8,128)(2,1)S(1)} %stream_dot.3.refs_3_, ...), custom_call_target="tpu_custom_call" | custom-call | tf_op jit(solution)/shard_map/mean_square/pallas_call | solution.py:245
  (98 shorter events, 38.1 us)
Async XLA Ops:
  0.0 20.1 %collective-permute-start.2 = (bf16[256,1024]{1,0:T(8,128)(2,1)}, bf16[256,1024]{1,0:T(8,128)(2,1)S(1)}, u32[]{:S(2)}, u32[]{:S(2)}) collective-permute-start(bf16[256,1024]{1,0:T(8,128)(2,1)} %bitcast.23), channel_id=1, source_target_pairs={{24,25},{25,24},{26,27},{27,26},{28,29},{29,28},{30,31},{31,30}} | collective-permute-start | bytes 1572872 | tf_op jit(solution)/shard_map/ppermute | solution.py:282
  0.8 19.3 %collective-permute-start = (bf16[256,1024]{1,0:T(8,128)(2,1)}, bf16[256,1024]{1,0:T(8,128)(2,1)S(1)}, u32[]{:S(2)}, u32[]{:S(2)}) collective-permute-start(bf16[256,1024]{1,0:T(8,128)(2,1)} %bitcast.24), channel_id=1, source_target_pairs={{24,28},{25,29},{26,30},{27,31},{28,24},{29,25},{30,26},{31,27}} | collective-permute-start | bytes 1572872 | tf_op jit(solution)/shard_map/ppermute | solution.py:282
  8.0 28.0 %collective-permute-start.4 = (bf16[4,256,512]{2,1,0:T(8,128)(2,1)S(1)}, bf16[4,256,512]{2,1,0:T(8,128)(2,1)S(1)}, u32[]{:S(2)}, u32[]{:S(2)}) collective-permute-start(bf16[4,256,512]{2,1,0:T(8,128)(2,1)S(1)} %get-tuple-element.41), channel_id=1, source_target_pairs={{8,9},{9,8},{10,11},{11,10},{12,13},{13,12},{14,15},{15,14},{0,1},... | collective-permute-start | bytes 3145736 | tf_op jit(solution)/shard_map/ppermute | solution.py:282
  12.9 9.2 %collective-permute-start.6 = (bf16[256,1024]{1,0:T(8,128)(2,1)S(1)}, bf16[256,1024]{1,0:T(8,128)(2,1)S(1)}, u32[]{:S(2)}, u32[]{:S(2)}) collective-permute-start(bf16[256,1024]{1,0:T(8,128)(2,1)S(1)} %bitcast.25), channel_id=1, source_target_pairs={{24,26},{25,27},{26,24},{27,25},{28,30},{29,31},{30,28},{31,29}} | collective-permute-start | bytes 1572872 | tf_op jit(solution)/shard_map/ppermute | solution.py:282
  20.1 16.7 %collective-permute-start.3 = (bf16[256,1024]{1,0:T(8,128)(2,1)S(1)}, bf16[256,1024]{1,0:T(8,128)(2,1)S(1)}, u32[]{:S(2)}, u32[]{:S(2)}) collective-permute-start(bf16[256,1024]{1,0:T(8,128)(2,1)S(1)} %collective-permute-done.refs_0_.refs_2_), channel_id=1, source_target_pairs={{24,25},{25,24},{26,27},{27,26},{28,29},{29,28},{30,31},{31,30}} | collective-permute-start | bytes 1572872 | tf_op jit(solution)/shard_map/ppermute | solution.py:282
  20.8 16.0 %collective-permute-start.1 = (bf16[256,1024]{1,0:T(8,128)(2,1)S(1)}, bf16[256,1024]{1,0:T(8,128)(2,1)S(1)}, u32[]{:S(2)}, u32[]{:S(2)}) collective-permute-start(bf16[256,1024]{1,0:T(8,128)(2,1)S(1)} %collective-permute-done.refs_0_.refs_2_), channel_id=1, source_target_pairs={{24,26},{25,27},{26,24},{27,25},{28,30},{29,31},{30,28},{31,29}} | collective-permute-start | bytes 1572872 | tf_op jit(solution)/shard_map/ppermute | solution.py:282
  22.1 26.1 %collective-permute-start.7 = (bf16[256,1024]{1,0:T(8,128)(2,1)S(1)}, bf16[256,1024]{1,0:T(8,128)(2,1)S(1)}, u32[]{:S(2)}, u32[]{:S(2)}) collective-permute-start(bf16[256,1024]{1,0:T(8,128)(2,1)S(1)} %collective-permute-done.6.refs_0_.refs_4_), channel_id=1, source_target_pairs={{24,25},{25,24},{26,27},{27,26},{28,29},{29,28},{30,31},{31,30}} | collective-permute-start | bytes 1572872 | tf_op jit(solution)/shard_map/ppermute | solution.py:282
  36.8 12.0 %collective-permute-start.5 = (bf16[256,1024]{1,0:T(8,128)(2,1)S(1)}, bf16[256,1024]{1,0:T(8,128)(2,1)S(1)}, u32[]{:S(2)}, u32[]{:S(2)}) collective-permute-start(bf16[256,1024]{1,0:T(8,128)(2,1)S(1)} %collective-permute-done.1.refs_2_.refs_6_), channel_id=1, source_target_pairs={{24,25},{25,24},{26,27},{27,26},{28,29},{29,28},{30,31},{31,30}} | collective-permute-start | bytes 1572872 | tf_op jit(solution)/shard_map/ppermute | solution.py:282
  37.5 13.3 %collective-permute-start.11 = (bf16[256,512]{1,0:T(8,128)(2,1)S(1)}, bf16[256,512]{1,0:T(8,128)(2,1)S(1)}, u32[]{:S(2)}, u32[]{:S(2)}) collective-permute-start(bf16[256,512]{1,0:T(8,128)(2,1)S(1)} %get-tuple-element.46), channel_id=1, source_target_pairs={{8,10},{9,11},{10,8},{11,9},{12,14},{13,15},{14,12},{15,13},{0,2},... | collective-permute-start | bytes 786440 | tf_op jit(solution)/shard_map/ppermute | solution.py:282
  41.2 22.8 %collective-permute-start.12 = (bf16[256,512]{1,0:T(8,128)(2,1)S(1)}, bf16[256,512]{1,0:T(8,128)(2,1)S(1)}, u32[]{:S(2)}, u32[]{:S(2)}) collective-permute-start(bf16[256,512]{1,0:T(8,128)(2,1)S(1)} %get-tuple-element.47), channel_id=1, source_target_pairs={{8,12},{9,13},{10,14},{11,15},{12,8},{13,9},{14,10},{15,11},{0,4},... | collective-permute-start | bytes 786440 | tf_op jit(solution)/shard_map/ppermute | solution.py:282
  45.7 19.1 %collective-permute-start.13 = (bf16[256,512]{1,0:T(8,128)(2,1)S(1)}, bf16[256,512]{1,0:T(8,128)(2,1)S(1)}, u32[]{:S(2)}, u32[]{:S(2)}) collective-permute-start(bf16[256,512]{1,0:T(8,128)(2,1)S(1)} %get-tuple-element.48), channel_id=1, source_target_pairs={{8,14},{9,15},{10,12},{11,13},{12,10},{13,11},{14,8},{15,9},{0,6},... | collective-permute-start | bytes 786440 | tf_op jit(solution)/shard_map/ppermute | solution.py:282
  49.3 16.3 %collective-permute-start.10 = (bf16[256,1024]{1,0:T(8,128)(2,1)S(1)}, bf16[256,1024]{1,0:T(8,128)(2,1)S(1)}, u32[]{:S(2)}, u32[]{:S(2)}) collective-permute-start(bf16[256,1024]{1,0:T(8,128)(2,1)S(1)} %block_dot.19), channel_id=1, source_target_pairs={{24,16},{25,17},{26,18},{27,19},{28,20},{29,21},{30,22},{31,23}} | collective-permute-start | bytes 1572872 | tf_op jit(solution)/shard_map/ppermute | solution.py:282
  50.0 15.6 %collective-permute-start.14 = (bf16[256,1024]{1,0:T(8,128)(2,1)S(1)}, bf16[256,1024]{1,0:T(8,128)(2,1)S(1)}, u32[]{:S(2)}, u32[]{:S(2)}) collective-permute-start(bf16[256,1024]{1,0:T(8,128)(2,1)S(1)} %block_dot.19), channel_id=1, source_target_pairs={{24,17},{25,16},{26,19},{27,18},{28,21},{29,20},{30,23},{31,22}} | collective-permute-start | bytes 1572872 | tf_op jit(solution)/shard_map/ppermute | solution.py:282
  50.8 15.5 %collective-permute-start.8 = (bf16[256,1024]{1,0:T(8,128)(2,1)S(1)}, bf16[256,1024]{1,0:T(8,128)(2,1)S(1)}, u32[]{:S(2)}, u32[]{:S(2)}) collective-permute-start(bf16[256,1024]{1,0:T(8,128)(2,1)S(1)} %block_dot.19), channel_id=1, source_target_pairs={{24,20},{25,21},{26,22},{27,23},{28,16},{29,17},{30,18},{31,19}} | collective-permute-start | bytes 1572872 | tf_op jit(solution)/shard_map/ppermute | solution.py:282
  68.3 8.5 %collective-permute-start.19 = (bf16[256,1024]{1,0:T(8,128)(2,1)S(1)}, bf16[256,1024]{1,0:T(8,128)(2,1)S(1)}, u32[]{:S(2)}, u32[]{:S(2)}) collective-permute-start(bf16[256,1024]{1,0:T(8,128)(2,1)S(1)} %collective-permute-done.18.refs_0_.refs_4_), channel_id=1, source_target_pairs={{16,17},{17,16},{18,19},{19,18},{20,21},{21,20},{22,23},{23,22}} | collective-permute-start | bytes 1572872 | tf_op jit(solution)/shard_map/ppermute | solution.py:282
  69.7 17.0 %collective-permute-start.21 = (bf16[256,512]{1,0:T(8,128)(2,1)S(1)}, bf16[256,512]{1,0:T(8,128)(2,1)S(1)}, u32[]{:S(2)}, u32[]{:S(2)}) collective-permute-start(bf16[256,512]{1,0:T(8,128)(2,1)S(1)} %add_convert_fusion.1), channel_id=1, source_target_pairs={{8,12},{9,13},{10,14},{11,15},{12,8},{13,9},{14,10},{15,11},{0,4},... | collective-permute-start | bytes 786440 | tf_op jit(solution)/shard_map/ppermute | solution.py:282
  77.9 19.9 %collective-permute-start.20 = (bf16[256,1024]{1,0:T(8,128)(2,1)S(1)}, bf16[256,1024]{1,0:T(8,128)(2,1)S(1)}, u32[]{:S(2)}, u32[]{:S(2)}) collective-permute-start(bf16[256,1024]{1,0:T(8,128)(2,1)S(1)} %block_dot.23), channel_id=1, source_target_pairs={{16,8},{17,9},{18,10},{19,11},{20,12},{21,13},{22,14},{23,15}} | collective-permute-start | bytes 1572872 | tf_op jit(solution)/shard_map/ppermute | solution.py:282
  78.6 13.8 %collective-permute-start.22 = (bf16[256,512]{1,0:T(8,128)(2,1)S(1)}, bf16[256,512]{1,0:T(8,128)(2,1)S(1)}, u32[]{:S(2)}, u32[]{:S(2)}) collective-permute-start(bf16[256,512]{1,0:T(8,128)(2,1)S(1)} %add_convert_fusion.1), channel_id=1, source_target_pairs={{8,10},{9,11},{10,8},{11,9},{12,14},{13,15},{14,12},{15,13},{0,2},... | collective-permute-start | bytes 786440 | tf_op jit(solution)/shard_map/ppermute | solution.py:282
  86.8 10.8 %collective-permute-start.23 = (bf16[256,512]{1,0:T(8,128)(2,1)S(1)}, bf16[256,512]{1,0:T(8,128)(2,1)S(1)}, u32[]{:S(2)}, u32[]{:S(2)}) collective-permute-start(bf16[256,512]{1,0:T(8,128)(2,1)S(1)} %collective-permute-done.21), channel_id=1, source_target_pairs={{8,10},{9,11},{10,8},{11,9},{12,14},{13,15},{14,12},{15,13},{0,2},... | collective-permute-start | bytes 786440 | tf_op jit(solution)/shard_map/ppermute | solution.py:282
  109.0 39.7 %collective-permute-start.33 = (bf16[256,1024]{1,0:T(8,128)(2,1)S(1)}, bf16[256,1024]{1,0:T(8,128)(2,1)S(1)}, u32[]{:S(2)}, u32[]{:S(2)}) collective-permute-start(bf16[256,1024]{1,0:T(8,128)(2,1)S(1)} %block_dot.27), channel_id=1, source_target_pairs={{8,0},{9,1},{10,2},{11,3},{12,4},{13,5},{14,6},{15,7}} | collective-permute-start | bytes 1572872 | tf_op jit(solution)/shard_map/ppermute | solution.py:282
  110.3 48.1 %collective-permute-start.34 = (bf16[256,1024]{1,0:T(8,128)(2,1)S(1)}, bf16[256,1024]{1,0:T(8,128)(2,1)S(1)}, u32[]{:S(2)}, u32[]{:S(2)}) collective-permute-start(bf16[256,1024]{1,0:T(8,128)(2,1)S(1)} %block_dot.27), channel_id=1, source_target_pairs={{8,1},{9,0},{10,3},{11,2},{12,5},{13,4},{14,7},{15,6}} | collective-permute-start | bytes 1572872 | tf_op jit(solution)/shard_map/ppermute | solution.py:282
  111.6 50.8 %collective-permute-start.31 = (bf16[256,1024]{1,0:T(8,128)(2,1)S(1)}, bf16[256,1024]{1,0:T(8,128)(2,1)S(1)}, u32[]{:S(2)}, u32[]{:S(2)}) collective-permute-start(bf16[256,1024]{1,0:T(8,128)(2,1)S(1)} %block_dot.27), channel_id=1, source_target_pairs={{8,4},{9,5},{10,6},{11,7},{12,0},{13,1},{14,2},{15,3}} | collective-permute-start | bytes 1572872 | tf_op jit(solution)/shard_map/ppermute | solution.py:282
  113.0 39.4 %collective-permute-start.43 = (bf16[256,512]{1,0:T(8,128)(2,1)S(1)}, bf16[256,512]{1,0:T(8,128)(2,1)S(1)}, u32[]{:S(2)}, u32[]{:S(2)}) collective-permute-start(bf16[256,512]{1,0:T(8,128)(2,1)S(1)} %add_convert_fusion), channel_id=1, source_target_pairs={{24,28},{25,29},{26,30},{27,31},{28,24},{29,25},{30,26},{31,27},{1... | collective-permute-start | bytes 786440 | tf_op jit(solution)/shard_map/ppermute | solution.py:282
  148.6 35.7 %collective-permute-start.36 = (bf16[4,256,512]{2,1,0:T(8,128)(2,1)S(1)}, bf16[4,256,512]{2,1,0:T(8,128)(2,1)S(1)}, u32[]{:S(2)}, u32[]{:S(2)}) collective-permute-start(bf16[4,256,512]{2,1,0:T(8,128)(2,1)S(1)} %pad_maximum_fusion.refs_4_), channel_id=1, source_target_pairs={{8,9},{9,8},{10,11},{11,10},{12,13},{13,12},{14,15},{15,14},{0,1},... | collective-permute-start | bytes 3145736 | tf_op jit(solution)/shard_map/ppermute | solution.py:282
  151.8 13.6 %collective-permute-start.44 = (bf16[256,512]{1,0:T(8,128)(2,1)S(1)}, bf16[256,512]{1,0:T(8,128)(2,1)S(1)}, u32[]{:S(2)}, u32[]{:S(2)}) collective-permute-start(bf16[256,512]{1,0:T(8,128)(2,1)S(1)} %add_convert_fusion), channel_id=1, source_target_pairs={{24,26},{25,27},{26,24},{27,25},{28,30},{29,31},{30,28},{31,29},{1... | collective-permute-start | bytes 786440 | tf_op jit(solution)/shard_map/ppermute | solution.py:282
  152.5 14.9 %collective-permute-start.45 = (bf16[256,512]{1,0:T(8,128)(2,1)S(1)}, bf16[256,512]{1,0:T(8,128)(2,1)S(1)}, u32[]{:S(2)}, u32[]{:S(2)}) collective-permute-start(bf16[256,512]{1,0:T(8,128)(2,1)S(1)} %collective-permute-done.43), channel_id=1, source_target_pairs={{24,26},{25,27},{26,24},{27,25},{28,30},{29,31},{30,28},{31,29},{1... | collective-permute-start | bytes 786440 | tf_op jit(solution)/shard_map/ppermute | solution.py:282
  158.4 10.5 %collective-permute-start.38 = (bf16[256,1024]{1,0:T(8,128)(2,1)S(1)}, bf16[256,1024]{1,0:T(8,128)(2,1)S(1)}, u32[]{:S(2)}, u32[]{:S(2)}) collective-permute-start(bf16[256,1024]{1,0:T(8,128)(2,1)S(1)} %block_dot.27), channel_id=1, source_target_pairs={{8,2},{9,3},{10,0},{11,1},{12,6},{13,7},{14,4},{15,5}} | collective-permute-start | bytes 1572872 | tf_op jit(solution)/shard_map/ppermute | solution.py:282
  162.4 22.0 %collective-permute-start.35 = (bf16[256,1024]{1,0:T(8,128)(2,1)S(1)}, bf16[256,1024]{1,0:T(8,128)(2,1)S(1)}, u32[]{:S(2)}, u32[]{:S(2)}) collective-permute-start(bf16[256,1024]{1,0:T(8,128)(2,1)S(1)} %collective-permute-done.31.refs_0_), channel_id=1, source_target_pairs={{0,1},{1,0},{2,3},{3,2},{4,5},{5,4},{6,7},{7,6}} | collective-permute-start | bytes 1572872 | tf_op jit(solution)/shard_map/ppermute | solution.py:282
  165.4 19.0 %collective-permute-start.32 = (bf16[256,1024]{1,0:T(8,128)(2,1)S(1)}, bf16[256,1024]{1,0:T(8,128)(2,1)S(1)}, u32[]{:S(2)}, u32[]{:S(2)}) collective-permute-start(bf16[256,1024]{1,0:T(8,128)(2,1)S(1)} %collective-permute-done.31.refs_0_), channel_id=1, source_target_pairs={{0,2},{1,3},{2,0},{3,1},{4,6},{5,7},{6,4},{7,5}} | collective-permute-start | bytes 1572872 | tf_op jit(solution)/shard_map/ppermute | solution.py:282
  167.5 29.3 %collective-permute-start.46 = (bf16[4,256,512]{2,1,0:T(8,128)(2,1)S(1)}, bf16[4,256,512]{2,1,0:T(8,128)(2,1)S(1)}, u32[]{:S(2)}, u32[]{:S(2)}) collective-permute-start(bf16[4,256,512]{2,1,0:T(8,128)(2,1)S(1)} %pad_maximum_fusion.1.refs_6_), channel_id=1, source_target_pairs={{24,25},{25,24},{26,27},{27,26},{28,29},{29,28},{30,31},{31,30},{1... | collective-permute-start | bytes 3145736 | tf_op jit(solution)/shard_map/ppermute | solution.py:282
  168.9 21.1 %collective-permute-start.39 = (bf16[256,1024]{1,0:T(8,128)(2,1)S(1)}, bf16[256,1024]{1,0:T(8,128)(2,1)S(1)}, u32[]{:S(2)}, u32[]{:S(2)}) collective-permute-start(bf16[256,1024]{1,0:T(8,128)(2,1)S(1)} %collective-permute-done.38.refs_0_), channel_id=1, source_target_pairs={{0,1},{1,0},{2,3},{3,2},{4,5},{5,4},{6,7},{7,6}} | collective-permute-start | bytes 1572872 | tf_op jit(solution)/shard_map/ppermute | solution.py:282
  184.4 11.2 %collective-permute-start.37 = (bf16[256,1024]{1,0:T(8,128)(2,1)S(1)}, bf16[256,1024]{1,0:T(8,128)(2,1)S(1)}, u32[]{:S(2)}, u32[]{:S(2)}) collective-permute-start(bf16[256,1024]{1,0:T(8,128)(2,1)S(1)} %collective-permute-done.32.refs_2_), channel_id=1, source_target_pairs={{0,1},{1,0},{2,3},{3,2},{4,5},{5,4},{6,7},{7,6}} | collective-permute-start | bytes 1572872 | tf_op jit(solution)/shard_map/ppermute | solution.py:282
  (17 other events, 77.9 us)

commit v12 on v10

--- a/solution.py
+++ b/solution.py
@@ -366,7 +366,11 @@
 
     def all_columns(columns, among):
         pairs = [(a, a) for a in among]
-        return [[c] + [moved(c, dx, pairs) for dx in range(1, inner)] for c in columns]
+        all_parts = []
+        for column in columns:
+            tied, *_ = lax.optimization_barrier((column, *(all_parts[-1][1:] if all_parts else [])))
+            all_parts.append([column] + [moved(tied, dx, pairs) for dx in range(1, inner)])
+        return all_parts
 
     upper = list(range(sections - 1, half - 1, -1))
     lower = list(range(half - 1, -1, -1))
@@ -376,7 +380,7 @@
     own, others, arrived = rotate_begin(inputs, first)
     near, side = spread(top, [(upper[0], upper[0])])
     weights = resident(at, weights)
-    halves = [order]
+    halves = [order[: outer // 2], order[outer // 2 :]] if outer > 1 else [order]
     sums = added(at, lower, own, arrived)
     low = summed(sums, lower)
     sent, before, within = ({0: top, **near}, side), others, sums
@@ -391,12 +395,12 @@
             last_own, last_others, last_arrived = rotate_begin(inputs, upper[:1])
             before, within = before + last_others, within + last_arrived
     low = outer_columns(low, lower, halves, [grad])
-    sent = handed_down(grad, lower[0], low)
-    low = all_columns(low, lower)
+    columns, low = low, all_columns(low, lower)
+    sent = handed_down(grad, lower[0], columns + low[0][1:])
     rot_outs[upper[-1]] = rotated(upper[-1], blocks)
     last_cols = resident(at, out_cols, 0)
     own, last_own, _ = lax.optimization_barrier((own, last_own, sent[0][0]))
-    before, within = [], [rot_outs[upper[-1]], *jax.tree.leaves(low)]
+    before, within = [], [rot_outs[upper[-1]], *low[-1][1:]]
     for turn in lower:
         grad, blocks = relay(turn, sent, before, within, weights if turn else last_cols)
         if turn != 0:

time: 205 us -> 206 us (level)
  starting transfers between devices: 66.3 us -> 70.2 us
  waiting for transfers between devices: 90.5 us -> 87.8 us
    ppermute x47 -> x48, starting transfers between devices: 66.3 us -> 70.2 us  [moved(): return lax.ppermute(block, ('section', 'shard'), route)]
    ppermute x47 -> x48, waiting for transfers between devices: 90.5 us -> 87.8 us  [moved(): return lax.ppermute(block, ('section', 'shard'), route)]
  transfers between devices with their start and end apart: 47 -> 48, of which waited for: 12 -> 12; matrix products, arithmetic and copies ran while one was open for 0% -> 0% of each run, Pallas kernels for 16% -> 16%
where the time goes in v12:
time: 206 us; the launch traced here: 205 us
  waiting for transfers between devices  87.8 us (43%)
  starting transfers between devices  70.2 us (34%)
  Pallas kernels  44.7 us (22%)
    ppermute x48, waiting for transfers between devices, moved(): return lax.ppermute(block, ('section', 'shard'), route)  87.8 us
    ppermute x48, starting transfers between devices, moved(): return lax.ppermute(block, ('section', 'shard'), route)  70.2 us
    pallas_call x16, Pallas kernels, block_dot(): pl.pallas_call(body, in_specs=[SMEM] + [VMEM] * (1 + count + (base is not...  12.4 us
    pallas_call x1, Pallas kernels, mean_square(): pl.pallas_call(body, in_specs=[SMEM] + [VMEM] * (sections + len(low) + le...  12.2 us
    pallas_call x2, Pallas kernels, resident(): pl.pallas_call(body, in_specs=[SMEM, HBM], out_specs=VMEM, out_shape=jax....  10.5 us
    pallas_call x2, Pallas kernels, partials(): pl.pallas_call(body, in_specs=[SMEM, HBM, VMEM], out_specs=[VMEM] * inner...  5.98 us
  transfers between devices with their start and end apart: 48, of which 12 were waited for; matrix products, arithmetic and copies ran while one was open for 0% of the time, Pallas kernels for 16%

profile of v12, /device:TPU:0, one launch (start us, length us, event | category | flops | bytes accessed | tf_op | source)
XLA Modules:
  0.0 205.5 jit_solution(16166845671704863745)
XLA Ops:
  2.7 5.4 %partials.2 = (f32[4,256,512]{2,1,0:T(8,128)S(1)}, bf16[4,256,512]{2,1,0:T(8,128)(2,1)S(1)}) custom-call(s32[9]{0:T(128)S(1)} %stack.72.at, bf16[1024,4096]{1,0:T(8,128)(2,1)} %bitcast.35, bf16[256,1024]{1,0:T(8,128)(2,1)S(1)} %bitcast.29), custom_call_target="tpu_custom_call" | custom-call | tf_op jit(solution)/shard_map/partials/pallas_call | solution.py:150
  8.0 4.8 %collective-permute-start.4 = (bf16[4,256,512]{2,1,0:T(8,128)(2,1)S(1)}, bf16[4,256,512]{2,1,0:T(8,128)(2,1)S(1)}, u32[]{:S(2)}, u32[]{:S(2)}) collective-permute-start(bf16[4,256,512]{2,1,0:T(8,128)(2,1)S(1)} %get-tuple-element.41), channel_id=1, source_target_pairs={{8,9},{9,8},{10,11},{11,10},{12,13},{13,12},{14,15},{15,14},{0,1},... | collective-permute-start | bytes 3145736 | tf_op jit(solution)/shard_map/ppermute | solution.py:282
  13.6 6.5 %resident.3.weights_ref = bf16[8,1024,1024]{2,1,0:T(8,128)(2,1)S(1)} custom-call(s32[9]{0:T(128)S(1)} %stack.72.at, bf16[8192,1024]{1,0:T(8,128)(2,1)} %bitcast.37), custom_call_target="tpu_custom_call" | custom-call | tf_op jit(solution)/shard_map/resident/pallas_call | solution.py:43
  22.8 13.3 %collective-permute-done.4.refs_0_ = bf16[4,256,512]{2,1,0:T(8,128)(2,1)S(1)} collective-permute-done((bf16[4,256,512]{2,1,0:T(8,128)(2,1)S(1)}, bf16[4,256,512]{2,1,0:T(8,128)(2,1)S(1)}, u32[]{:S(2)}, u32[]{:S(2)}) %collective-permute-start.4) | collective-permute-done | bytes 1048608 | tf_op jit(solution)/shard_map/ppermute | solution.py:282
  37.5 3.7 %collective-permute-start.11 = (bf16[256,512]{1,0:T(8,128)(2,1)S(1)}, bf16[256,512]{1,0:T(8,128)(2,1)S(1)}, u32[]{:S(2)}, u32[]{:S(2)}) collective-permute-start(bf16[256,512]{1,0:T(8,128)(2,1)S(1)} %get-tuple-element.46), channel_id=1, source_target_pairs={{8,10},{9,11},{10,8},{11,9},{12,14},{13,15},{14,12},{15,13},{0,2},... | collective-permute-start | bytes 786440 | tf_op jit(solution)/shard_map/ppermute | solution.py:282
  41.2 4.5 %collective-permute-start.12 = (bf16[256,512]{1,0:T(8,128)(2,1)S(1)}, bf16[256,512]{1,0:T(8,128)(2,1)S(1)}, u32[]{:S(2)}, u32[]{:S(2)}) collective-permute-start(bf16[256,512]{1,0:T(8,128)(2,1)S(1)} %get-tuple-element.47), channel_id=1, source_target_pairs={{8,12},{9,13},{10,14},{11,15},{12,8},{13,9},{14,10},{15,11},{0,4},... | collective-permute-start | bytes 786440 | tf_op jit(solution)/shard_map/ppermute | solution.py:282
  45.7 1.9 collective-permute-start.13
  52.1 12.0 %collective-permute-done.12 = bf16[256,512]{1,0:T(8,128)(2,1)S(1)} collective-permute-done((bf16[256,512]{1,0:T(8,128)(2,1)S(1)}, bf16[256,512]{1,0:T(8,128)(2,1)S(1)}, u32[]{:S(2)}, u32[]{:S(2)}) %collective-permute-start.12) | collective-permute-done | bytes 262176 | tf_op jit(solution)/shard_map/ppermute | solution.py:282
  69.7 6.5 %collective-permute-start.21 = (bf16[256,512]{1,0:T(8,128)(2,1)S(1)}, bf16[256,512]{1,0:T(8,128)(2,1)S(1)}, u32[]{:S(2)}, u32[]{:S(2)}) collective-permute-start(bf16[256,512]{1,0:T(8,128)(2,1)S(1)} %add_convert_fusion.1), channel_id=1, source_target_pairs={{8,12},{9,13},{10,14},{11,15},{12,8},{13,9},{14,10},{15,11},{0,4},... | collective-permute-start | bytes 786440 | tf_op jit(solution)/shard_map/ppermute | solution.py:282
  76.2 10.5 %collective-permute-done.21 = bf16[256,512]{1,0:T(8,128)(2,1)S(1)} collective-permute-done((bf16[256,512]{1,0:T(8,128)(2,1)S(1)}, bf16[256,512]{1,0:T(8,128)(2,1)S(1)}, u32[]{:S(2)}, u32[]{:S(2)}) %collective-permute-start.21) | collective-permute-done | bytes 262176 | tf_op jit(solution)/shard_map/ppermute | solution.py:282
  86.7 3.4 %collective-permute-start.24 = (bf16[2,256,512]{2,1,0:T(8,128)(2,1)S(1)}, bf16[2,256,512]{2,1,0:T(8,128)(2,1)S(1)}, u32[]{:S(2)}, u32[]{:S(2)}) collective-permute-start(bf16[2,256,512]{2,1,0:T(8,128)(2,1)S(1)} %pad_maximum_fusion.1.refs_4_), channel_id=1, source_target_pairs={{8,9},{9,8},{10,11},{11,10},{12,13},{13,12},{14,15},{15,14},{0,1},... | collective-permute-start | bytes 1572872 | tf_op jit(solution)/shard_map/ppermute | solution.py:282
  92.6 1.9 collective-permute-start.22
  94.5 3.9 %collective-permute-start.23 = (bf16[256,512]{1,0:T(8,128)(2,1)S(1)}, bf16[256,512]{1,0:T(8,128)(2,1)S(1)}, u32[]{:S(2)}, u32[]{:S(2)}) collective-permute-start(bf16[256,512]{1,0:T(8,128)(2,1)S(1)} %collective-permute-done.21), channel_id=1, source_target_pairs={{8,10},{9,11},{10,8},{11,9},{12,14},{13,15},{14,12},{15,13},{0,2},... | collective-permute-start | bytes 786440 | tf_op jit(solution)/shard_map/ppermute | solution.py:282
  98.4 5.3 %collective-permute-done.22 = bf16[256,512]{1,0:T(8,128)(2,1)S(1)} collective-permute-done((bf16[256,512]{1,0:T(8,128)(2,1)S(1)}, bf16[256,512]{1,0:T(8,128)(2,1)S(1)}, u32[]{:S(2)}, u32[]{:S(2)}) %collective-permute-start.22) | collective-permute-done | bytes 262176 | tf_op jit(solution)/shard_map/ppermute | solution.py:282
  103.7 4.0 %collective-permute-done.23 = bf16[256,512]{1,0:T(8,128)(2,1)S(1)} collective-permute-done((bf16[256,512]{1,0:T(8,128)(2,1)S(1)}, bf16[256,512]{1,0:T(8,128)(2,1)S(1)}, u32[]{:S(2)}, u32[]{:S(2)}) %collective-permute-start.23) | collective-permute-done | bytes 262176 | tf_op jit(solution)/shard_map/ppermute | solution.py:282
  109.1 2.6 %collective-permute-start.29 = (bf16[2,256,512]{2,1,0:T(8,128)(2,1)S(1)}, bf16[2,256,512]{2,1,0:T(8,128)(2,1)S(1)}, u32[]{:S(2)}, u32[]{:S(2)}) collective-permute-start(bf16[2,256,512]{2,1,0:T(8,128)(2,1)S(1)} %pad_maximum_fusion.2.refs_6_), channel_id=1, source_target_pairs={{8,9},{9,8},{10,11},{11,10},{12,13},{13,12},{14,15},{15,14},{0,1},... | collective-permute-start | bytes 1572872 | tf_op jit(solution)/shard_map/ppermute | solution.py:282
  115.8 10.3 %collective-permute-done.29.refs_7_ = bf16[2,256,512]{2,1,0:T(8,128)(2,1)S(1)} collective-permute-done((bf16[2,256,512]{2,1,0:T(8,128)(2,1)S(1)}, bf16[2,256,512]{2,1,0:T(8,128)(2,1)S(1)}, u32[]{:S(2)}, u32[]{:S(2)}) %collective-permute-start.29) | collective-permute-done | bytes 524320 | tf_op jit(solution)/shard_map/ppermute | solution.py:282
  137.8 4.0 %resident.2.weights_ref = bf16[8,1024,512]{2,1,0:T(8,128)(2,1)S(1)} custom-call(s32[9]{0:T(128)S(1)} %stack.72.at, bf16[8192,512]{1,0:T(8,128)(2,1)} %bitcast.33), custom_call_target="tpu_custom_call" | custom-call | tf_op jit(solution)/shard_map/resident/pallas_call | solution.py:43
  141.8 12.7 %collective-permute-done.35.refs_0_ = bf16[256,1024]{1,0:T(8,128)(2,1)S(1)} collective-permute-done((bf16[256,1024]{1,0:T(8,128)(2,1)S(1)}, bf16[256,1024]{1,0:T(8,128)(2,1)S(1)}, u32[]{:S(2)}, u32[]{:S(2)}) %collective-permute-start.35) | collective-permute-done | bytes 524320 | tf_op jit(solution)/shard_map/ppermute | solution.py:282
  155.8 4.0 %collective-permute-done.36.refs_1_ = bf16[256,1024]{1,0:T(8,128)(2,1)S(1)} collective-permute-done((bf16[256,1024]{1,0:T(8,128)(2,1)S(1)}, bf16[256,1024]{1,0:T(8,128)(2,1)S(1)}, u32[]{:S(2)}, u32[]{:S(2)}) %collective-permute-start.36) | collective-permute-done | bytes 524320 | tf_op jit(solution)/shard_map/ppermute | solution.py:282
  159.7 1.4 block_dot.28.refs_2_
  161.2 5.2 %collective-permute-done.33.refs_0_ = bf16[256,1024]{1,0:T(8,128)(2,1)S(1)} collective-permute-done((bf16[256,1024]{1,0:T(8,128)(2,1)S(1)}, bf16[256,1024]{1,0:T(8,128)(2,1)S(1)}, u32[]{:S(2)}, u32[]{:S(2)}) %collective-permute-start.33) | collective-permute-done | bytes 524320 | tf_op jit(solution)/shard_map/ppermute | solution.py:282
  166.4 3.4 %collective-permute-start.37 = (bf16[256,1024]{1,0:T(8,128)(2,1)S(1)}, bf16[256,1024]{1,0:T(8,128)(2,1)S(1)}, u32[]{:S(2)}, u32[]{:S(2)}) collective-permute-start(bf16[256,1024]{1,0:T(8,128)(2,1)S(1)} %collective-permute-done.33.refs_0_), channel_id=1, source_target_pairs={{0,1},{1,0},{2,3},{3,2},{4,5},{5,4},{6,7},{7,6}} | collective-permute-start | bytes 1572872 | tf_op jit(solution)/shard_map/ppermute | solution.py:282
  169.8 1.9 collective-permute-start.34
  173.3 2.4 %collective-permute-start.40 = (bf16[256,1024]{1,0:T(8,128)(2,1)S(1)}, bf16[256,1024]{1,0:T(8,128)(2,1)S(1)}, u32[]{:S(2)}, u32[]{:S(2)}) collective-permute-start(bf16[256,1024]{1,0:T(8,128)(2,1)S(1)} %collective-permute-done.39.refs_0_), channel_id=1, source_target_pairs={{0,1},{1,0},{2,3},{3,2},{4,5},{5,4},{6,7},{7,6}} | collective-permute-start | bytes 1572872 | tf_op jit(solution)/shard_map/ppermute | solution.py:282
  175.7 1.7 collective-permute-done.37.refs_1_
  177.5 3.4 %collective-permute-done.34.refs_2_ = bf16[256,1024]{1,0:T(8,128)(2,1)S(1)} collective-permute-done((bf16[256,1024]{1,0:T(8,128)(2,1)S(1)}, bf16[256,1024]{1,0:T(8,128)(2,1)S(1)}, u32[]{:S(2)}, u32[]{:S(2)}) %collective-permute-start.34) | collective-permute-done | bytes 524320 | tf_op jit(solution)/shard_map/ppermute | solution.py:282
  180.9 2.4 %collective-permute-start.38 = (bf16[256,1024]{1,0:T(8,128)(2,1)S(1)}, bf16[256,1024]{1,0:T(8,128)(2,1)S(1)}, u32[]{:S(2)}, u32[]{:S(2)}) collective-permute-start(bf16[256,1024]{1,0:T(8,128)(2,1)S(1)} %collective-permute-done.34.refs_2_), channel_id=1, source_target_pairs={{0,1},{1,0},{2,3},{3,2},{4,5},{5,4},{6,7},{7,6}} | collective-permute-start | bytes 1572872 | tf_op jit(solution)/shard_map/ppermute | solution.py:282
  183.3 1.4 block_dot.29.refs_3_
  184.8 1.7 block_dot.30.refs_1_
  186.5 5.5 %collective-permute-done.38.refs_0_ = bf16[256,1024]{1,0:T(8,128)(2,1)S(1)} collective-permute-done((bf16[256,1024]{1,0:T(8,128)(2,1)S(1)}, bf16[256,1024]{1,0:T(8,128)(2,1)S(1)}, u32[]{:S(2)}, u32[]{:S(2)}) %collective-permute-start.38) | collective-permute-done | bytes 524320 | tf_op jit(solution)/shard_map/ppermute | solution.py:282
  193.1 12.2 %mean_square.1 = f32[512,4096]{1,0:T(8,128)} custom-call(s32[9]{0:T(128)S(1)} %stack.72.at, bf16[256,512]{1,0:T(8,128)(2,1)S(1)} %block_dot.31.refs_0_, bf16[256,512]{1,0:T(8,128)(2,1)S(1)} %stream_dot.5.refs_1_, bf16[256,512]{1,0:T(8,128)(2,1)S(1)} %stream_dot.4.refs_2_, bf16[256,512]{1,0:T(8,128)(2,1)S(1)} %stream_dot.3.refs_3_, ...), custom_call_target="tpu_custom_call" | custom-call | tf_op jit(solution)/shard_map/mean_square/pallas_call | solution.py:245
  (101 shorter events, 40.6 us)
Async XLA Ops:
  0.0 20.1 %collective-permute-start.2 = (bf16[256,1024]{1,0:T(8,128)(2,1)}, bf16[256,1024]{1,0:T(8,128)(2,1)S(1)}, u32[]{:S(2)}, u32[]{:S(2)}) collective-permute-start(bf16[256,1024]{1,0:T(8,128)(2,1)} %bitcast.23), channel_id=1, source_target_pairs={{24,25},{25,24},{26,27},{27,26},{28,29},{29,28},{30,31},{31,30}} | collective-permute-start | bytes 1572872 | tf_op jit(solution)/shard_map/ppermute | solution.py:282
  0.8 19.3 %collective-permute-start = (bf16[256,1024]{1,0:T(8,128)(2,1)}, bf16[256,1024]{1,0:T(8,128)(2,1)S(1)}, u32[]{:S(2)}, u32[]{:S(2)}) collective-permute-start(bf16[256,1024]{1,0:T(8,128)(2,1)} %bitcast.24), channel_id=1, source_target_pairs={{24,28},{25,29},{26,30},{27,31},{28,24},{29,25},{30,26},{31,27}} | collective-permute-start | bytes 1572872 | tf_op jit(solution)/shard_map/ppermute | solution.py:282
  8.0 28.0 %collective-permute-start.4 = (bf16[4,256,512]{2,1,0:T(8,128)(2,1)S(1)}, bf16[4,256,512]{2,1,0:T(8,128)(2,1)S(1)}, u32[]{:S(2)}, u32[]{:S(2)}) collective-permute-start(bf16[4,256,512]{2,1,0:T(8,128)(2,1)S(1)} %get-tuple-element.41), channel_id=1, source_target_pairs={{8,9},{9,8},{10,11},{11,10},{12,13},{13,12},{14,15},{15,14},{0,1},... | collective-permute-start | bytes 3145736 | tf_op jit(solution)/shard_map/ppermute | solution.py:282
  20.1 16.7 %collective-permute-start.3 = (bf16[256,1024]{1,0:T(8,128)(2,1)S(1)}, bf16[256,1024]{1,0:T(8,128)(2,1)S(1)}, u32[]{:S(2)}, u32[]{:S(2)}) collective-permute-start(bf16[256,1024]{1,0:T(8,128)(2,1)S(1)} %collective-permute-done.refs_0_.refs_2_), channel_id=1, source_target_pairs={{24,25},{25,24},{26,27},{27,26},{28,29},{29,28},{30,31},{31,30}} | collective-permute-start | bytes 1572872 | tf_op jit(solution)/shard_map/ppermute | solution.py:282
  20.8 16.0 %collective-permute-start.1 = (bf16[256,1024]{1,0:T(8,128)(2,1)S(1)}, bf16[256,1024]{1,0:T(8,128)(2,1)S(1)}, u32[]{:S(2)}, u32[]{:S(2)}) collective-permute-start(bf16[256,1024]{1,0:T(8,128)(2,1)S(1)} %collective-permute-done.refs_0_.refs_2_), channel_id=1, source_target_pairs={{24,26},{25,27},{26,24},{27,25},{28,30},{29,31},{30,28},{31,29}} | collective-permute-start | bytes 1572872 | tf_op jit(solution)/shard_map/ppermute | solution.py:282
  22.1 26.1 %collective-permute-start.7 = (bf16[256,1024]{1,0:T(8,128)(2,1)S(1)}, bf16[256,1024]{1,0:T(8,128)(2,1)S(1)}, u32[]{:S(2)}, u32[]{:S(2)}) collective-permute-start(bf16[256,1024]{1,0:T(8,128)(2,1)S(1)} %collective-permute-done.6.refs_0_.refs_4_), channel_id=1, source_target_pairs={{24,25},{25,24},{26,27},{27,26},{28,29},{29,28},{30,31},{31,30}} | collective-permute-start | bytes 1572872 | tf_op jit(solution)/shard_map/ppermute | solution.py:282
  36.8 12.0 %collective-permute-start.5 = (bf16[256,1024]{1,0:T(8,128)(2,1)S(1)}, bf16[256,1024]{1,0:T(8,128)(2,1)S(1)}, u32[]{:S(2)}, u32[]{:S(2)}) collective-permute-start(bf16[256,1024]{1,0:T(8,128)(2,1)S(1)} %collective-permute-done.1.refs_2_.refs_6_), channel_id=1, source_target_pairs={{24,25},{25,24},{26,27},{27,26},{28,29},{29,28},{30,31},{31,30}} | collective-permute-start | bytes 1572872 | tf_op jit(solution)/shard_map/ppermute | solution.py:282
  37.5 13.3 %collective-permute-start.11 = (bf16[256,512]{1,0:T(8,128)(2,1)S(1)}, bf16[256,512]{1,0:T(8,128)(2,1)S(1)}, u32[]{:S(2)}, u32[]{:S(2)}) collective-permute-start(bf16[256,512]{1,0:T(8,128)(2,1)S(1)} %get-tuple-element.46), channel_id=1, source_target_pairs={{8,10},{9,11},{10,8},{11,9},{12,14},{13,15},{14,12},{15,13},{0,2},... | collective-permute-start | bytes 786440 | tf_op jit(solution)/shard_map/ppermute | solution.py:282
  41.2 22.8 %collective-permute-start.12 = (bf16[256,512]{1,0:T(8,128)(2,1)S(1)}, bf16[256,512]{1,0:T(8,128)(2,1)S(1)}, u32[]{:S(2)}, u32[]{:S(2)}) collective-permute-start(bf16[256,512]{1,0:T(8,128)(2,1)S(1)} %get-tuple-element.47), channel_id=1, source_target_pairs={{8,12},{9,13},{10,14},{11,15},{12,8},{13,9},{14,10},{15,11},{0,4},... | collective-permute-start | bytes 786440 | tf_op jit(solution)/shard_map/ppermute | solution.py:282
  45.7 19.1 %collective-permute-start.13 = (bf16[256,512]{1,0:T(8,128)(2,1)S(1)}, bf16[256,512]{1,0:T(8,128)(2,1)S(1)}, u32[]{:S(2)}, u32[]{:S(2)}) collective-permute-start(bf16[256,512]{1,0:T(8,128)(2,1)S(1)} %get-tuple-element.48), channel_id=1, source_target_pairs={{8,14},{9,15},{10,12},{11,13},{12,10},{13,11},{14,8},{15,9},{0,6},... | collective-permute-start | bytes 786440 | tf_op jit(solution)/shard_map/ppermute | solution.py:282
  49.3 16.3 %collective-permute-start.10 = (bf16[256,1024]{1,0:T(8,128)(2,1)S(1)}, bf16[256,1024]{1,0:T(8,128)(2,1)S(1)}, u32[]{:S(2)}, u32[]{:S(2)}) collective-permute-start(bf16[256,1024]{1,0:T(8,128)(2,1)S(1)} %block_dot.19), channel_id=1, source_target_pairs={{24,16},{25,17},{26,18},{27,19},{28,20},{29,21},{30,22},{31,23}} | collective-permute-start | bytes 1572872 | tf_op jit(solution)/shard_map/ppermute | solution.py:282
  50.0 15.6 %collective-permute-start.14 = (bf16[256,1024]{1,0:T(8,128)(2,1)S(1)}, bf16[256,1024]{1,0:T(8,128)(2,1)S(1)}, u32[]{:S(2)}, u32[]{:S(2)}) collective-permute-start(bf16[256,1024]{1,0:T(8,128)(2,1)S(1)} %block_dot.19), channel_id=1, source_target_pairs={{24,17},{25,16},{26,19},{27,18},{28,21},{29,20},{30,23},{31,22}} | collective-permute-start | bytes 1572872 | tf_op jit(solution)/shard_map/ppermute | solution.py:282
  50.8 15.5 %collective-permute-start.8 = (bf16[256,1024]{1,0:T(8,128)(2,1)S(1)}, bf16[256,1024]{1,0:T(8,128)(2,1)S(1)}, u32[]{:S(2)}, u32[]{:S(2)}) collective-permute-start(bf16[256,1024]{1,0:T(8,128)(2,1)S(1)} %block_dot.19), channel_id=1, source_target_pairs={{24,20},{25,21},{26,22},{27,23},{28,16},{29,17},{30,18},{31,19}} | collective-permute-start | bytes 1572872 | tf_op jit(solution)/shard_map/ppermute | solution.py:282
  68.3 22.4 %collective-permute-start.19 = (bf16[256,1024]{1,0:T(8,128)(2,1)S(1)}, bf16[256,1024]{1,0:T(8,128)(2,1)S(1)}, u32[]{:S(2)}, u32[]{:S(2)}) collective-permute-start(bf16[256,1024]{1,0:T(8,128)(2,1)S(1)} %collective-permute-done.18.refs_0_.refs_4_), channel_id=1, source_target_pairs={{16,17},{17,16},{18,19},{19,18},{20,21},{21,20},{22,23},{23,22}} | collective-permute-start | bytes 1572872 | tf_op jit(solution)/shard_map/ppermute | solution.py:282
  69.0 22.3 %collective-permute-start.17 = (bf16[256,1024]{1,0:T(8,128)(2,1)S(1)}, bf16[256,1024]{1,0:T(8,128)(2,1)S(1)}, u32[]{:S(2)}, u32[]{:S(2)}) collective-permute-start(bf16[256,1024]{1,0:T(8,128)(2,1)S(1)} %collective-permute-done.9.refs_2_.refs_6_), channel_id=1, source_target_pairs={{16,17},{17,16},{18,19},{19,18},{20,21},{21,20},{22,23},{23,22}} | collective-permute-start | bytes 1572872 | tf_op jit(solution)/shard_map/ppermute | solution.py:282
  69.7 16.9 %collective-permute-start.21 = (bf16[256,512]{1,0:T(8,128)(2,1)S(1)}, bf16[256,512]{1,0:T(8,128)(2,1)S(1)}, u32[]{:S(2)}, u32[]{:S(2)}) collective-permute-start(bf16[256,512]{1,0:T(8,128)(2,1)S(1)} %add_convert_fusion.1), channel_id=1, source_target_pairs={{8,12},{9,13},{10,14},{11,15},{12,8},{13,9},{14,10},{15,11},{0,4},... | collective-permute-start | bytes 786440 | tf_op jit(solution)/shard_map/ppermute | solution.py:282
  86.7 21.0 %collective-permute-start.24 = (bf16[2,256,512]{2,1,0:T(8,128)(2,1)S(1)}, bf16[2,256,512]{2,1,0:T(8,128)(2,1)S(1)}, u32[]{:S(2)}, u32[]{:S(2)}) collective-permute-start(bf16[2,256,512]{2,1,0:T(8,128)(2,1)S(1)} %pad_maximum_fusion.1.refs_4_), channel_id=1, source_target_pairs={{8,9},{9,8},{10,11},{11,10},{12,13},{13,12},{14,15},{15,14},{0,1},... | collective-permute-start | bytes 1572872 | tf_op jit(solution)/shard_map/ppermute | solution.py:282
  91.9 15.9 %collective-permute-start.20 = (bf16[256,1024]{1,0:T(8,128)(2,1)S(1)}, bf16[256,1024]{1,0:T(8,128)(2,1)S(1)}, u32[]{:S(2)}, u32[]{:S(2)}) collective-permute-start(bf16[256,1024]{1,0:T(8,128)(2,1)S(1)} %block_dot.23), channel_id=1, source_target_pairs={{16,8},{17,9},{18,10},{19,11},{20,12},{21,13},{22,14},{23,15}} | collective-permute-start | bytes 1572872 | tf_op jit(solution)/shard_map/ppermute | solution.py:282
  92.6 11.1 %collective-permute-start.22 = (bf16[256,512]{1,0:T(8,128)(2,1)S(1)}, bf16[256,512]{1,0:T(8,128)(2,1)S(1)}, u32[]{:S(2)}, u32[]{:S(2)}) collective-permute-start(bf16[256,512]{1,0:T(8,128)(2,1)S(1)} %add_convert_fusion.1), channel_id=1, source_target_pairs={{8,10},{9,11},{10,8},{11,9},{12,14},{13,15},{14,12},{15,13},{0,2},... | collective-permute-start | bytes 786440 | tf_op jit(solution)/shard_map/ppermute | solution.py:282
  94.5 13.2 %collective-permute-start.23 = (bf16[256,512]{1,0:T(8,128)(2,1)S(1)}, bf16[256,512]{1,0:T(8,128)(2,1)S(1)}, u32[]{:S(2)}, u32[]{:S(2)}) collective-permute-start(bf16[256,512]{1,0:T(8,128)(2,1)S(1)} %collective-permute-done.21), channel_id=1, source_target_pairs={{8,10},{9,11},{10,8},{11,9},{12,14},{13,15},{14,12},{15,13},{0,2},... | collective-permute-start | bytes 786440 | tf_op jit(solution)/shard_map/ppermute | solution.py:282
  109.1 16.9 %collective-permute-start.29 = (bf16[2,256,512]{2,1,0:T(8,128)(2,1)S(1)}, bf16[2,256,512]{2,1,0:T(8,128)(2,1)S(1)}, u32[]{:S(2)}, u32[]{:S(2)}) collective-permute-start(bf16[2,256,512]{2,1,0:T(8,128)(2,1)S(1)} %pad_maximum_fusion.2.refs_6_), channel_id=1, source_target_pairs={{8,9},{9,8},{10,11},{11,10},{12,13},{13,12},{14,15},{15,14},{0,1},... | collective-permute-start | bytes 1572872 | tf_op jit(solution)/shard_map/ppermute | solution.py:282
  113.0 13.0 %collective-permute-start.28 = (bf16[256,1024]{1,0:T(8,128)(2,1)S(1)}, bf16[256,1024]{1,0:T(8,128)(2,1)S(1)}, u32[]{:S(2)}, u32[]{:S(2)}) collective-permute-start(bf16[256,1024]{1,0:T(8,128)(2,1)S(1)} %collective-permute-done.25.refs_0_.refs_2_), channel_id=1, source_target_pairs={{8,9},{9,8},{10,11},{11,10},{12,13},{13,12},{14,15},{15,14}} | collective-permute-start | bytes 1572872 | tf_op jit(solution)/shard_map/ppermute | solution.py:282
  113.7 12.3 %collective-permute-start.26 = (bf16[256,1024]{1,0:T(8,128)(2,1)S(1)}, bf16[256,1024]{1,0:T(8,128)(2,1)S(1)}, u32[]{:S(2)}, u32[]{:S(2)}) collective-permute-start(bf16[256,1024]{1,0:T(8,128)(2,1)S(1)} %collective-permute-done.25.refs_0_.refs_2_), channel_id=1, source_target_pairs={{8,10},{9,11},{10,8},{11,9},{12,14},{13,15},{14,12},{15,13}} | collective-permute-start | bytes 1572872 | tf_op jit(solution)/shard_map/ppermute | solution.py:282
  115.1 15.4 %collective-permute-start.32 = (bf16[256,1024]{1,0:T(8,128)(2,1)S(1)}, bf16[256,1024]{1,0:T(8,128)(2,1)S(1)}, u32[]{:S(2)}, u32[]{:S(2)}) collective-permute-start(bf16[256,1024]{1,0:T(8,128)(2,1)S(1)} %collective-permute-done.31.refs_0_.refs_4_), channel_id=1, source_target_pairs={{8,9},{9,8},{10,11},{11,10},{12,13},{13,12},{14,15},{15,14}} | collective-permute-start | bytes 1572872 | tf_op jit(solution)/shard_map/ppermute | solution.py:282
  131.6 28.1 %collective-permute-start.36 = (bf16[256,1024]{1,0:T(8,128)(2,1)S(1)}, bf16[256,1024]{1,0:T(8,128)(2,1)S(1)}, u32[]{:S(2)}, u32[]{:S(2)}) collective-permute-start(bf16[256,1024]{1,0:T(8,128)(2,1)S(1)} %block_dot.27), channel_id=1, source_target_pairs={{8,1},{9,0},{10,3},{11,2},{12,5},{13,4},{14,7},{15,6}} | collective-permute-start | bytes 1572872 | tf_op jit(solution)/shard_map/ppermute | solution.py:282
  132.9 21.6 %collective-permute-start.35 = (bf16[256,1024]{1,0:T(8,128)(2,1)S(1)}, bf16[256,1024]{1,0:T(8,128)(2,1)S(1)}, u32[]{:S(2)}, u32[]{:S(2)}) collective-permute-start(bf16[256,1024]{1,0:T(8,128)(2,1)S(1)} %block_dot.27), channel_id=1, source_target_pairs={{8,0},{9,1},{10,2},{11,3},{12,4},{13,5},{14,6},{15,7}} | collective-permute-start | bytes 1572872 | tf_op jit(solution)/shard_map/ppermute | solution.py:282
  134.2 32.2 %collective-permute-start.33 = (bf16[256,1024]{1,0:T(8,128)(2,1)S(1)}, bf16[256,1024]{1,0:T(8,128)(2,1)S(1)}, u32[]{:S(2)}, u32[]{:S(2)}) collective-permute-start(bf16[256,1024]{1,0:T(8,128)(2,1)S(1)} %block_dot.27), channel_id=1, source_target_pairs={{8,4},{9,5},{10,6},{11,7},{12,0},{13,1},{14,2},{15,3}} | collective-permute-start | bytes 1572872 | tf_op jit(solution)/shard_map/ppermute | solution.py:282
  136.4 35.3 %collective-permute-start.45 = (bf16[256,512]{1,0:T(8,128)(2,1)S(1)}, bf16[256,512]{1,0:T(8,128)(2,1)S(1)}, u32[]{:S(2)}, u32[]{:S(2)}) collective-permute-start(bf16[256,512]{1,0:T(8,128)(2,1)S(1)} %add_convert_fusion), channel_id=1, source_target_pairs={{24,26},{25,27},{26,24},{27,25},{28,30},{29,31},{30,28},{31,29},{1... | collective-permute-start | bytes 786440 | tf_op jit(solution)/shard_map/ppermute | solution.py:282
  137.1 34.7 %collective-permute-start.46 = (bf16[256,512]{1,0:T(8,128)(2,1)S(1)}, bf16[256,512]{1,0:T(8,128)(2,1)S(1)}, u32[]{:S(2)}, u32[]{:S(2)}) collective-permute-start(bf16[256,512]{1,0:T(8,128)(2,1)S(1)} %collective-permute-done.44), channel_id=1, source_target_pairs={{24,26},{25,27},{26,24},{27,25},{28,30},{29,31},{30,28},{31,29},{1... | collective-permute-start | bytes 786440 | tf_op jit(solution)/shard_map/ppermute | solution.py:282
  154.5 18.8 %collective-permute-start.39 = (bf16[256,1024]{1,0:T(8,128)(2,1)S(1)}, bf16[256,1024]{1,0:T(8,128)(2,1)S(1)}, u32[]{:S(2)}, u32[]{:S(2)}) collective-permute-start(bf16[256,1024]{1,0:T(8,128)(2,1)S(1)} %block_dot.27), channel_id=1, source_target_pairs={{8,2},{9,3},{10,0},{11,1},{12,6},{13,7},{14,4},{15,5}} | collective-permute-start | bytes 1572872 | tf_op jit(solution)/shard_map/ppermute | solution.py:282
  171.9 21.2 %collective-permute-start.47 = (bf16[4,256,512]{2,1,0:T(8,128)(2,1)S(1)}, bf16[4,256,512]{2,1,0:T(8,128)(2,1)S(1)}, u32[]{:S(2)}, u32[]{:S(2)}) collective-permute-start(bf16[4,256,512]{2,1,0:T(8,128)(2,1)S(1)} %pad_maximum_fusion.refs_8_), channel_id=1, source_target_pairs={{24,25},{25,24},{26,27},{27,26},{28,29},{29,28},{30,31},{31,30},{1... | collective-permute-start | bytes 3145736 | tf_op jit(solution)/shard_map/ppermute | solution.py:282
  173.3 11.5 %collective-permute-start.40 = (bf16[256,1024]{1,0:T(8,128)(2,1)S(1)}, bf16[256,1024]{1,0:T(8,128)(2,1)S(1)}, u32[]{:S(2)}, u32[]{:S(2)}) collective-permute-start(bf16[256,1024]{1,0:T(8,128)(2,1)S(1)} %collective-permute-done.39.refs_0_), channel_id=1, source_target_pairs={{0,1},{1,0},{2,3},{3,2},{4,5},{5,4},{6,7},{7,6}} | collective-permute-start | bytes 1572872 | tf_op jit(solution)/shard_map/ppermute | solution.py:282
  (18 other events, 108.0 us)

commit v13 on v12

--- a/solution.py
+++ b/solution.py
@@ -380,7 +380,7 @@
     own, others, arrived = rotate_begin(inputs, first)
     near, side = spread(top, [(upper[0], upper[0])])
     weights = resident(at, weights)
-    halves = [order[: outer // 2], order[outer // 2 :]] if outer > 1 else [order]
+    halves = [[0, 1], [dz for dz in order if dz > 1]] if outer > 2 else [order]
     sums = added(at, lower, own, arrived)
     low = summed(sums, lower)
     sent, before, within = ({0: top, **near}, side), others, sums

time: 206 us -> 202 us (0.981)
  waiting for transfers between devices: 87.8 us -> 84.7 us
    ppermute x48, waiting for transfers between devices: 87.8 us -> 84.7 us  [moved(): return lax.ppermute(block, ('section', 'shard'), route)]
where the time goes in v13:
time: 202 us
  waiting for transfers between devices  84.7 us (42%)
  starting transfers between devices  69.4 us (34%)
  Pallas kernels  44.7 us (22%)
    ppermute x48, waiting for transfers between devices, moved(): return lax.ppermute(block, ('section', 'shard'), route)  84.7 us
    ppermute x48, starting transfers between devices, moved(): return lax.ppermute(block, ('section', 'shard'), route)  69.4 us
    pallas_call x16, Pallas kernels, block_dot(): pl.pallas_call(body, in_specs=[SMEM] + [VMEM] * (1 + count + (base is not...  12.4 us
    pallas_call x1, Pallas kernels, mean_square(): pl.pallas_call(body, in_specs=[SMEM] + [VMEM] * (sections + len(low) + le...  12.2 us
    pallas_call x2, Pallas kernels, resident(): pl.pallas_call(body, in_specs=[SMEM, HBM], out_specs=VMEM, out_shape=jax....  10.5 us
    pallas_call x2, Pallas kernels, partials(): pl.pallas_call(body, in_specs=[SMEM, HBM, VMEM], out_specs=[VMEM] * inner...  5.98 us
  transfers between devices with their start and end apart: 48, of which 12 were waited for; matrix products, arithmetic and copies ran while one was open for 0% of the time, Pallas kernels for 16%

profile of v13, /device:TPU:0, one launch (start us, length us, event | category | flops | bytes accessed | tf_op | source)
XLA Modules:
  0.0 201.6 jit_solution(6786436487044773429)
XLA Ops:
  2.7 5.4 %partials.2 = (f32[4,256,512]{2,1,0:T(8,128)S(1)}, bf16[4,256,512]{2,1,0:T(8,128)(2,1)S(1)}) custom-call(s32[9]{0:T(128)S(1)} %stack.72.at, bf16[1024,4096]{1,0:T(8,128)(2,1)} %bitcast.35, bf16[256,1024]{1,0:T(8,128)(2,1)S(1)} %bitcast.29), custom_call_target="tpu_custom_call" | custom-call | tf_op jit(solution)/shard_map/partials/pallas_call | solution.py:150
  8.0 4.8 %collective-permute-start.4 = (bf16[4,256,512]{2,1,0:T(8,128)(2,1)S(1)}, bf16[4,256,512]{2,1,0:T(8,128)(2,1)S(1)}, u32[]{:S(2)}, u32[]{:S(2)}) collective-permute-start(bf16[4,256,512]{2,1,0:T(8,128)(2,1)S(1)} %get-tuple-element.41), channel_id=1, source_target_pairs={{8,9},{9,8},{10,11},{11,10},{12,13},{13,12},{14,15},{15,14},{0,1},... | collective-permute-start | bytes 3145736 | tf_op jit(solution)/shard_map/ppermute | solution.py:282
  13.6 6.5 %resident.3.weights_ref = bf16[8,1024,1024]{2,1,0:T(8,128)(2,1)S(1)} custom-call(s32[9]{0:T(128)S(1)} %stack.72.at, bf16[8192,1024]{1,0:T(8,128)(2,1)} %bitcast.37), custom_call_target="tpu_custom_call" | custom-call | tf_op jit(solution)/shard_map/resident/pallas_call | solution.py:43
  22.8 13.3 %collective-permute-done.4.refs_0_ = bf16[4,256,512]{2,1,0:T(8,128)(2,1)S(1)} collective-permute-done((bf16[4,256,512]{2,1,0:T(8,128)(2,1)S(1)}, bf16[4,256,512]{2,1,0:T(8,128)(2,1)S(1)}, u32[]{:S(2)}, u32[]{:S(2)}) %collective-permute-start.4) | collective-permute-done | bytes 1048608 | tf_op jit(solution)/shard_map/ppermute | solution.py:282
  37.5 3.7 %collective-permute-start.11 = (bf16[256,512]{1,0:T(8,128)(2,1)S(1)}, bf16[256,512]{1,0:T(8,128)(2,1)S(1)}, u32[]{:S(2)}, u32[]{:S(2)}) collective-permute-start(bf16[256,512]{1,0:T(8,128)(2,1)S(1)} %get-tuple-element.46), channel_id=1, source_target_pairs={{8,10},{9,11},{10,8},{11,9},{12,14},{13,15},{14,12},{15,13},{0,2},... | collective-permute-start | bytes 786440 | tf_op jit(solution)/shard_map/ppermute | solution.py:282
  41.2 4.5 %collective-permute-start.12 = (bf16[256,512]{1,0:T(8,128)(2,1)S(1)}, bf16[256,512]{1,0:T(8,128)(2,1)S(1)}, u32[]{:S(2)}, u32[]{:S(2)}) collective-permute-start(bf16[256,512]{1,0:T(8,128)(2,1)S(1)} %get-tuple-element.47), channel_id=1, source_target_pairs={{8,12},{9,13},{10,14},{11,15},{12,8},{13,9},{14,10},{15,11},{0,4},... | collective-permute-start | bytes 786440 | tf_op jit(solution)/shard_map/ppermute | solution.py:282
  45.7 1.9 collective-permute-start.13
  52.1 12.0 %collective-permute-done.12 = bf16[256,512]{1,0:T(8,128)(2,1)S(1)} collective-permute-done((bf16[256,512]{1,0:T(8,128)(2,1)S(1)}, bf16[256,512]{1,0:T(8,128)(2,1)S(1)}, u32[]{:S(2)}, u32[]{:S(2)}) %collective-permute-start.12) | collective-permute-done | bytes 262176 | tf_op jit(solution)/shard_map/ppermute | solution.py:282
  69.7 5.5 %collective-permute-start.21 = (bf16[256,512]{1,0:T(8,128)(2,1)S(1)}, bf16[256,512]{1,0:T(8,128)(2,1)S(1)}, u32[]{:S(2)}, u32[]{:S(2)}) collective-permute-start(bf16[256,512]{1,0:T(8,128)(2,1)S(1)} %add_convert_fusion.1), channel_id=1, source_target_pairs={{8,10},{9,11},{10,8},{11,9},{12,14},{13,15},{14,12},{15,13},{0,2},... | collective-permute-start | bytes 786440 | tf_op jit(solution)/shard_map/ppermute | solution.py:282
  75.2 2.9 %collective-permute-start.22 = (bf16[256,512]{1,0:T(8,128)(2,1)S(1)}, bf16[256,512]{1,0:T(8,128)(2,1)S(1)}, u32[]{:S(2)}, u32[]{:S(2)}) collective-permute-start(bf16[256,512]{1,0:T(8,128)(2,1)S(1)} %add_convert_fusion.1), channel_id=1, source_target_pairs={{8,12},{9,13},{10,14},{11,15},{12,8},{13,9},{14,10},{15,11},{0,4},... | collective-permute-start | bytes 786440 | tf_op jit(solution)/shard_map/ppermute | solution.py:282
  78.1 4.1 %collective-permute-done.21 = bf16[256,512]{1,0:T(8,128)(2,1)S(1)} collective-permute-done((bf16[256,512]{1,0:T(8,128)(2,1)S(1)}, bf16[256,512]{1,0:T(8,128)(2,1)S(1)}, u32[]{:S(2)}, u32[]{:S(2)}) %collective-permute-start.21) | collective-permute-done | bytes 262176 | tf_op jit(solution)/shard_map/ppermute | solution.py:282
  82.2 3.4 %collective-permute-start.24 = (bf16[2,256,512]{2,1,0:T(8,128)(2,1)S(1)}, bf16[2,256,512]{2,1,0:T(8,128)(2,1)S(1)}, u32[]{:S(2)}, u32[]{:S(2)}) collective-permute-start(bf16[2,256,512]{2,1,0:T(8,128)(2,1)S(1)} %pad_maximum_fusion.1.refs_4_), channel_id=1, source_target_pairs={{8,9},{9,8},{10,11},{11,10},{12,13},{13,12},{14,15},{15,14},{0,1},... | collective-permute-start | bytes 1572872 | tf_op jit(solution)/shard_map/ppermute | solution.py:282
  88.1 1.7 collective-permute-done.22
  89.8 2.1 %collective-permute-start.23 = (bf16[256,512]{1,0:T(8,128)(2,1)S(1)}, bf16[256,512]{1,0:T(8,128)(2,1)S(1)}, u32[]{:S(2)}, u32[]{:S(2)}) collective-permute-start(bf16[256,512]{1,0:T(8,128)(2,1)S(1)} %collective-permute-done.22), channel_id=1, source_target_pairs={{8,10},{9,11},{10,8},{11,9},{12,14},{13,15},{14,12},{15,13},{0,2},... | collective-permute-start | bytes 786440 | tf_op jit(solution)/shard_map/ppermute | solution.py:282
  91.9 6.1 %collective-permute-done.23 = bf16[256,512]{1,0:T(8,128)(2,1)S(1)} collective-permute-done((bf16[256,512]{1,0:T(8,128)(2,1)S(1)}, bf16[256,512]{1,0:T(8,128)(2,1)S(1)}, u32[]{:S(2)}, u32[]{:S(2)}) %collective-permute-start.23) | collective-permute-done | bytes 262176 | tf_op jit(solution)/shard_map/ppermute | solution.py:282
  99.5 3.6 %collective-permute-start.29 = (bf16[2,256,512]{2,1,0:T(8,128)(2,1)S(1)}, bf16[2,256,512]{2,1,0:T(8,128)(2,1)S(1)}, u32[]{:S(2)}, u32[]{:S(2)}) collective-permute-start(bf16[2,256,512]{2,1,0:T(8,128)(2,1)S(1)} %pad_maximum_fusion.2.refs_6_), channel_id=1, source_target_pairs={{8,9},{9,8},{10,11},{11,10},{12,13},{13,12},{14,15},{15,14},{0,1},... | collective-permute-start | bytes 1572872 | tf_op jit(solution)/shard_map/ppermute | solution.py:282
  107.2 7.9 %collective-permute-done.29.refs_7_ = bf16[2,256,512]{2,1,0:T(8,128)(2,1)S(1)} collective-permute-done((bf16[2,256,512]{2,1,0:T(8,128)(2,1)S(1)}, bf16[2,256,512]{2,1,0:T(8,128)(2,1)S(1)}, u32[]{:S(2)}, u32[]{:S(2)}) %collective-permute-start.29) | collective-permute-done | bytes 524320 | tf_op jit(solution)/shard_map/ppermute | solution.py:282
  126.9 4.0 %resident.2.weights_ref = bf16[8,1024,512]{2,1,0:T(8,128)(2,1)S(1)} custom-call(s32[9]{0:T(128)S(1)} %stack.72.at, bf16[8192,512]{1,0:T(8,128)(2,1)} %bitcast.33), custom_call_target="tpu_custom_call" | custom-call | tf_op jit(solution)/shard_map/resident/pallas_call | solution.py:43
  130.9 19.1 %collective-permute-done.35.refs_0_ = bf16[256,1024]{1,0:T(8,128)(2,1)S(1)} collective-permute-done((bf16[256,1024]{1,0:T(8,128)(2,1)S(1)}, bf16[256,1024]{1,0:T(8,128)(2,1)S(1)}, u32[]{:S(2)}, u32[]{:S(2)}) %collective-permute-start.35) | collective-permute-done | bytes 524320 | tf_op jit(solution)/shard_map/ppermute | solution.py:282
  151.3 3.7 %collective-permute-done.36.refs_1_ = bf16[256,1024]{1,0:T(8,128)(2,1)S(1)} collective-permute-done((bf16[256,1024]{1,0:T(8,128)(2,1)S(1)}, bf16[256,1024]{1,0:T(8,128)(2,1)S(1)}, u32[]{:S(2)}, u32[]{:S(2)}) %collective-permute-start.36) | collective-permute-done | bytes 524320 | tf_op jit(solution)/shard_map/ppermute | solution.py:282
  154.9 1.4 block_dot.28.refs_2_
  156.4 6.1 %collective-permute-done.33.refs_0_ = bf16[256,1024]{1,0:T(8,128)(2,1)S(1)} collective-permute-done((bf16[256,1024]{1,0:T(8,128)(2,1)S(1)}, bf16[256,1024]{1,0:T(8,128)(2,1)S(1)}, u32[]{:S(2)}, u32[]{:S(2)}) %collective-permute-start.33) | collective-permute-done | bytes 524320 | tf_op jit(solution)/shard_map/ppermute | solution.py:282
  162.5 3.4 %collective-permute-start.37 = (bf16[256,1024]{1,0:T(8,128)(2,1)S(1)}, bf16[256,1024]{1,0:T(8,128)(2,1)S(1)}, u32[]{:S(2)}, u32[]{:S(2)}) collective-permute-start(bf16[256,1024]{1,0:T(8,128)(2,1)S(1)} %collective-permute-done.33.refs_0_), channel_id=1, source_target_pairs={{0,1},{1,0},{2,3},{3,2},{4,5},{5,4},{6,7},{7,6}} | collective-permute-start | bytes 1572872 | tf_op jit(solution)/shard_map/ppermute | solution.py:282
  165.9 1.9 collective-permute-start.34
  169.4 2.4 %collective-permute-start.40 = (bf16[256,1024]{1,0:T(8,128)(2,1)S(1)}, bf16[256,1024]{1,0:T(8,128)(2,1)S(1)}, u32[]{:S(2)}, u32[]{:S(2)}) collective-permute-start(bf16[256,1024]{1,0:T(8,128)(2,1)S(1)} %collective-permute-done.39.refs_0_), channel_id=1, source_target_pairs={{0,1},{1,0},{2,3},{3,2},{4,5},{5,4},{6,7},{7,6}} | collective-permute-start | bytes 1572872 | tf_op jit(solution)/shard_map/ppermute | solution.py:282
  171.8 1.7 collective-permute-done.37.refs_1_
  173.5 3.4 %collective-permute-done.34.refs_2_ = bf16[256,1024]{1,0:T(8,128)(2,1)S(1)} collective-permute-done((bf16[256,1024]{1,0:T(8,128)(2,1)S(1)}, bf16[256,1024]{1,0:T(8,128)(2,1)S(1)}, u32[]{:S(2)}, u32[]{:S(2)}) %collective-permute-start.34) | collective-permute-done | bytes 524320 | tf_op jit(solution)/shard_map/ppermute | solution.py:282
  177.0 2.4 %collective-permute-start.38 = (bf16[256,1024]{1,0:T(8,128)(2,1)S(1)}, bf16[256,1024]{1,0:T(8,128)(2,1)S(1)}, u32[]{:S(2)}, u32[]{:S(2)}) collective-permute-start(bf16[256,1024]{1,0:T(8,128)(2,1)S(1)} %collective-permute-done.34.refs_2_), channel_id=1, source_target_pairs={{0,1},{1,0},{2,3},{3,2},{4,5},{5,4},{6,7},{7,6}} | collective-permute-start | bytes 1572872 | tf_op jit(solution)/shard_map/ppermute | solution.py:282
  179.4 1.5 block_dot.29.refs_3_
  180.8 1.7 block_dot.30.refs_1_
  182.6 5.5 %collective-permute-done.38.refs_0_ = bf16[256,1024]{1,0:T(8,128)(2,1)S(1)} collective-permute-done((bf16[256,1024]{1,0:T(8,128)(2,1)S(1)}, bf16[256,1024]{1,0:T(8,128)(2,1)S(1)}, u32[]{:S(2)}, u32[]{:S(2)}) %collective-permute-start.38) | collective-permute-done | bytes 524320 | tf_op jit(solution)/shard_map/ppermute | solution.py:282
  189.2 12.2 %mean_square.1 = f32[512,4096]{1,0:T(8,128)} custom-call(s32[9]{0:T(128)S(1)} %stack.72.at, bf16[256,512]{1,0:T(8,128)(2,1)S(1)} %block_dot.31.refs_0_, bf16[256,512]{1,0:T(8,128)(2,1)S(1)} %stream_dot.5.refs_1_, bf16[256,512]{1,0:T(8,128)(2,1)S(1)} %stream_dot.4.refs_2_, bf16[256,512]{1,0:T(8,128)(2,1)S(1)} %stream_dot.3.refs_3_, ...), custom_call_target="tpu_custom_call" | custom-call | tf_op jit(solution)/shard_map/mean_square/pallas_call | solution.py:245
  (101 shorter events, 40.6 us)
Async XLA Ops:
  0.0 20.1 %collective-permute-start.2 = (bf16[256,1024]{1,0:T(8,128)(2,1)}, bf16[256,1024]{1,0:T(8,128)(2,1)S(1)}, u32[]{:S(2)}, u32[]{:S(2)}) collective-permute-start(bf16[256,1024]{1,0:T(8,128)(2,1)} %bitcast.23), channel_id=1, source_target_pairs={{24,25},{25,24},{26,27},{27,26},{28,29},{29,28},{30,31},{31,30}} | collective-permute-start | bytes 1572872 | tf_op jit(solution)/shard_map/ppermute | solution.py:282
  0.8 19.3 %collective-permute-start = (bf16[256,1024]{1,0:T(8,128)(2,1)}, bf16[256,1024]{1,0:T(8,128)(2,1)S(1)}, u32[]{:S(2)}, u32[]{:S(2)}) collective-permute-start(bf16[256,1024]{1,0:T(8,128)(2,1)} %bitcast.24), channel_id=1, source_target_pairs={{24,28},{25,29},{26,30},{27,31},{28,24},{29,25},{30,26},{31,27}} | collective-permute-start | bytes 1572872 | tf_op jit(solution)/shard_map/ppermute | solution.py:282
  8.0 28.0 %collective-permute-start.4 = (bf16[4,256,512]{2,1,0:T(8,128)(2,1)S(1)}, bf16[4,256,512]{2,1,0:T(8,128)(2,1)S(1)}, u32[]{:S(2)}, u32[]{:S(2)}) collective-permute-start(bf16[4,256,512]{2,1,0:T(8,128)(2,1)S(1)} %get-tuple-element.41), channel_id=1, source_target_pairs={{8,9},{9,8},{10,11},{11,10},{12,13},{13,12},{14,15},{15,14},{0,1},... | collective-permute-start | bytes 3145736 | tf_op jit(solution)/shard_map/ppermute | solution.py:282
  20.1 16.7 %collective-permute-start.3 = (bf16[256,1024]{1,0:T(8,128)(2,1)S(1)}, bf16[256,1024]{1,0:T(8,128)(2,1)S(1)}, u32[]{:S(2)}, u32[]{:S(2)}) collective-permute-start(bf16[256,1024]{1,0:T(8,128)(2,1)S(1)} %collective-permute-done.refs_0_.refs_2_), channel_id=1, source_target_pairs={{24,25},{25,24},{26,27},{27,26},{28,29},{29,28},{30,31},{31,30}} | collective-permute-start | bytes 1572872 | tf_op jit(solution)/shard_map/ppermute | solution.py:282
  20.8 16.0 %collective-permute-start.1 = (bf16[256,1024]{1,0:T(8,128)(2,1)S(1)}, bf16[256,1024]{1,0:T(8,128)(2,1)S(1)}, u32[]{:S(2)}, u32[]{:S(2)}) collective-permute-start(bf16[256,1024]{1,0:T(8,128)(2,1)S(1)} %collective-permute-done.refs_0_.refs_2_), channel_id=1, source_target_pairs={{24,26},{25,27},{26,24},{27,25},{28,30},{29,31},{30,28},{31,29}} | collective-permute-start | bytes 1572872 | tf_op jit(solution)/shard_map/ppermute | solution.py:282
  22.1 26.1 %collective-permute-start.7 = (bf16[256,1024]{1,0:T(8,128)(2,1)S(1)}, bf16[256,1024]{1,0:T(8,128)(2,1)S(1)}, u32[]{:S(2)}, u32[]{:S(2)}) collective-permute-start(bf16[256,1024]{1,0:T(8,128)(2,1)S(1)} %collective-permute-done.6.refs_0_.refs_4_), channel_id=1, source_target_pairs={{24,25},{25,24},{26,27},{27,26},{28,29},{29,28},{30,31},{31,30}} | collective-permute-start | bytes 1572872 | tf_op jit(solution)/shard_map/ppermute | solution.py:282
  36.8 12.0 %collective-permute-start.5 = (bf16[256,1024]{1,0:T(8,128)(2,1)S(1)}, bf16[256,1024]{1,0:T(8,128)(2,1)S(1)}, u32[]{:S(2)}, u32[]{:S(2)}) collective-permute-start(bf16[256,1024]{1,0:T(8,128)(2,1)S(1)} %collective-permute-done.1.refs_2_.refs_6_), channel_id=1, source_target_pairs={{24,25},{25,24},{26,27},{27,26},{28,29},{29,28},{30,31},{31,30}} | collective-permute-start | bytes 1572872 | tf_op jit(solution)/shard_map/ppermute | solution.py:282
  37.5 13.3 %collective-permute-start.11 = (bf16[256,512]{1,0:T(8,128)(2,1)S(1)}, bf16[256,512]{1,0:T(8,128)(2,1)S(1)}, u32[]{:S(2)}, u32[]{:S(2)}) collective-permute-start(bf16[256,512]{1,0:T(8,128)(2,1)S(1)} %get-tuple-element.46), channel_id=1, source_target_pairs={{8,10},{9,11},{10,8},{11,9},{12,14},{13,15},{14,12},{15,13},{0,2},... | collective-permute-start | bytes 786440 | tf_op jit(solution)/shard_map/ppermute | solution.py:282
  41.2 22.8 %collective-permute-start.12 = (bf16[256,512]{1,0:T(8,128)(2,1)S(1)}, bf16[256,512]{1,0:T(8,128)(2,1)S(1)}, u32[]{:S(2)}, u32[]{:S(2)}) collective-permute-start(bf16[256,512]{1,0:T(8,128)(2,1)S(1)} %get-tuple-element.47), channel_id=1, source_target_pairs={{8,12},{9,13},{10,14},{11,15},{12,8},{13,9},{14,10},{15,11},{0,4},... | collective-permute-start | bytes 786440 | tf_op jit(solution)/shard_map/ppermute | solution.py:282
  45.7 19.1 %collective-permute-start.13 = (bf16[256,512]{1,0:T(8,128)(2,1)S(1)}, bf16[256,512]{1,0:T(8,128)(2,1)S(1)}, u32[]{:S(2)}, u32[]{:S(2)}) collective-permute-start(bf16[256,512]{1,0:T(8,128)(2,1)S(1)} %get-tuple-element.48), channel_id=1, source_target_pairs={{8,14},{9,15},{10,12},{11,13},{12,10},{13,11},{14,8},{15,9},{0,6},... | collective-permute-start | bytes 786440 | tf_op jit(solution)/shard_map/ppermute | solution.py:282
  49.3 16.3 %collective-permute-start.10 = (bf16[256,1024]{1,0:T(8,128)(2,1)S(1)}, bf16[256,1024]{1,0:T(8,128)(2,1)S(1)}, u32[]{:S(2)}, u32[]{:S(2)}) collective-permute-start(bf16[256,1024]{1,0:T(8,128)(2,1)S(1)} %block_dot.19), channel_id=1, source_target_pairs={{24,16},{25,17},{26,18},{27,19},{28,20},{29,21},{30,22},{31,23}} | collective-permute-start | bytes 1572872 | tf_op jit(solution)/shard_map/ppermute | solution.py:282
  50.0 15.6 %collective-permute-start.14 = (bf16[256,1024]{1,0:T(8,128)(2,1)S(1)}, bf16[256,1024]{1,0:T(8,128)(2,1)S(1)}, u32[]{:S(2)}, u32[]{:S(2)}) collective-permute-start(bf16[256,1024]{1,0:T(8,128)(2,1)S(1)} %block_dot.19), channel_id=1, source_target_pairs={{24,17},{25,16},{26,19},{27,18},{28,21},{29,20},{30,23},{31,22}} | collective-permute-start | bytes 1572872 | tf_op jit(solution)/shard_map/ppermute | solution.py:282
  50.8 15.5 %collective-permute-start.8 = (bf16[256,1024]{1,0:T(8,128)(2,1)S(1)}, bf16[256,1024]{1,0:T(8,128)(2,1)S(1)}, u32[]{:S(2)}, u32[]{:S(2)}) collective-permute-start(bf16[256,1024]{1,0:T(8,128)(2,1)S(1)} %block_dot.19), channel_id=1, source_target_pairs={{24,20},{25,21},{26,22},{27,23},{28,16},{29,17},{30,18},{31,19}} | collective-permute-start | bytes 1572872 | tf_op jit(solution)/shard_map/ppermute | solution.py:282
  68.3 18.0 %collective-permute-start.19 = (bf16[256,1024]{1,0:T(8,128)(2,1)S(1)}, bf16[256,1024]{1,0:T(8,128)(2,1)S(1)}, u32[]{:S(2)}, u32[]{:S(2)}) collective-permute-start(bf16[256,1024]{1,0:T(8,128)(2,1)S(1)} %collective-permute-done.18.refs_0_.refs_4_), channel_id=1, source_target_pairs={{16,17},{17,16},{18,19},{19,18},{20,21},{21,20},{22,23},{23,22}} | collective-permute-start | bytes 1572872 | tf_op jit(solution)/shard_map/ppermute | solution.py:282
  69.0 17.8 %collective-permute-start.17 = (bf16[256,1024]{1,0:T(8,128)(2,1)S(1)}, bf16[256,1024]{1,0:T(8,128)(2,1)S(1)}, u32[]{:S(2)}, u32[]{:S(2)}) collective-permute-start(bf16[256,1024]{1,0:T(8,128)(2,1)S(1)} %collective-permute-done.9.refs_2_.refs_6_), channel_id=1, source_target_pairs={{16,17},{17,16},{18,19},{19,18},{20,21},{21,20},{22,23},{23,22}} | collective-permute-start | bytes 1572872 | tf_op jit(solution)/shard_map/ppermute | solution.py:282
  69.7 12.5 %collective-permute-start.21 = (bf16[256,512]{1,0:T(8,128)(2,1)S(1)}, bf16[256,512]{1,0:T(8,128)(2,1)S(1)}, u32[]{:S(2)}, u32[]{:S(2)}) collective-permute-start(bf16[256,512]{1,0:T(8,128)(2,1)S(1)} %add_convert_fusion.1), channel_id=1, source_target_pairs={{8,10},{9,11},{10,8},{11,9},{12,14},{13,15},{14,12},{15,13},{0,2},... | collective-permute-start | bytes 786440 | tf_op jit(solution)/shard_map/ppermute | solution.py:282
  75.2 14.6 %collective-permute-start.22 = (bf16[256,512]{1,0:T(8,128)(2,1)S(1)}, bf16[256,512]{1,0:T(8,128)(2,1)S(1)}, u32[]{:S(2)}, u32[]{:S(2)}) collective-permute-start(bf16[256,512]{1,0:T(8,128)(2,1)S(1)} %add_convert_fusion.1), channel_id=1, source_target_pairs={{8,12},{9,13},{10,14},{11,15},{12,8},{13,9},{14,10},{15,11},{0,4},... | collective-permute-start | bytes 786440 | tf_op jit(solution)/shard_map/ppermute | solution.py:282
  82.2 15.9 %collective-permute-start.24 = (bf16[2,256,512]{2,1,0:T(8,128)(2,1)S(1)}, bf16[2,256,512]{2,1,0:T(8,128)(2,1)S(1)}, u32[]{:S(2)}, u32[]{:S(2)}) collective-permute-start(bf16[2,256,512]{2,1,0:T(8,128)(2,1)S(1)} %pad_maximum_fusion.1.refs_4_), channel_id=1, source_target_pairs={{8,9},{9,8},{10,11},{11,10},{12,13},{13,12},{14,15},{15,14},{0,1},... | collective-permute-start | bytes 1572872 | tf_op jit(solution)/shard_map/ppermute | solution.py:282
  87.4 10.7 %collective-permute-start.20 = (bf16[256,1024]{1,0:T(8,128)(2,1)S(1)}, bf16[256,1024]{1,0:T(8,128)(2,1)S(1)}, u32[]{:S(2)}, u32[]{:S(2)}) collective-permute-start(bf16[256,1024]{1,0:T(8,128)(2,1)S(1)} %block_dot.23), channel_id=1, source_target_pairs={{16,8},{17,9},{18,10},{19,11},{20,12},{21,13},{22,14},{23,15}} | collective-permute-start | bytes 1572872 | tf_op jit(solution)/shard_map/ppermute | solution.py:282
  99.5 15.6 %collective-permute-start.29 = (bf16[2,256,512]{2,1,0:T(8,128)(2,1)S(1)}, bf16[2,256,512]{2,1,0:T(8,128)(2,1)S(1)}, u32[]{:S(2)}, u32[]{:S(2)}) collective-permute-start(bf16[2,256,512]{2,1,0:T(8,128)(2,1)S(1)} %pad_maximum_fusion.2.refs_6_), channel_id=1, source_target_pairs={{8,9},{9,8},{10,11},{11,10},{12,13},{13,12},{14,15},{15,14},{0,1},... | collective-permute-start | bytes 1572872 | tf_op jit(solution)/shard_map/ppermute | solution.py:282
  106.5 13.1 %collective-permute-start.32 = (bf16[256,1024]{1,0:T(8,128)(2,1)S(1)}, bf16[256,1024]{1,0:T(8,128)(2,1)S(1)}, u32[]{:S(2)}, u32[]{:S(2)}) collective-permute-start(bf16[256,1024]{1,0:T(8,128)(2,1)S(1)} %collective-permute-done.31.refs_0_.refs_4_), channel_id=1, source_target_pairs={{8,9},{9,8},{10,11},{11,10},{12,13},{13,12},{14,15},{15,14}} | collective-permute-start | bytes 1572872 | tf_op jit(solution)/shard_map/ppermute | solution.py:282
  120.7 34.2 %collective-permute-start.36 = (bf16[256,1024]{1,0:T(8,128)(2,1)S(1)}, bf16[256,1024]{1,0:T(8,128)(2,1)S(1)}, u32[]{:S(2)}, u32[]{:S(2)}) collective-permute-start(bf16[256,1024]{1,0:T(8,128)(2,1)S(1)} %block_dot.27), channel_id=1, source_target_pairs={{8,1},{9,0},{10,3},{11,2},{12,5},{13,4},{14,7},{15,6}} | collective-permute-start | bytes 1572872 | tf_op jit(solution)/shard_map/ppermute | solution.py:282
  122.0 28.0 %collective-permute-start.35 = (bf16[256,1024]{1,0:T(8,128)(2,1)S(1)}, bf16[256,1024]{1,0:T(8,128)(2,1)S(1)}, u32[]{:S(2)}, u32[]{:S(2)}) collective-permute-start(bf16[256,1024]{1,0:T(8,128)(2,1)S(1)} %block_dot.27), channel_id=1, source_target_pairs={{8,0},{9,1},{10,2},{11,3},{12,4},{13,5},{14,6},{15,7}} | collective-permute-start | bytes 1572872 | tf_op jit(solution)/shard_map/ppermute | solution.py:282
  123.3 39.1 %collective-permute-start.33 = (bf16[256,1024]{1,0:T(8,128)(2,1)S(1)}, bf16[256,1024]{1,0:T(8,128)(2,1)S(1)}, u32[]{:S(2)}, u32[]{:S(2)}) collective-permute-start(bf16[256,1024]{1,0:T(8,128)(2,1)S(1)} %block_dot.27), channel_id=1, source_target_pairs={{8,4},{9,5},{10,6},{11,7},{12,0},{13,1},{14,2},{15,3}} | collective-permute-start | bytes 1572872 | tf_op jit(solution)/shard_map/ppermute | solution.py:282
  125.5 42.3 %collective-permute-start.45 = (bf16[256,512]{1,0:T(8,128)(2,1)S(1)}, bf16[256,512]{1,0:T(8,128)(2,1)S(1)}, u32[]{:S(2)}, u32[]{:S(2)}) collective-permute-start(bf16[256,512]{1,0:T(8,128)(2,1)S(1)} %add_convert_fusion), channel_id=1, source_target_pairs={{24,26},{25,27},{26,24},{27,25},{28,30},{29,31},{30,28},{31,29},{1... | collective-permute-start | bytes 786440 | tf_op jit(solution)/shard_map/ppermute | solution.py:282
  126.2 41.7 %collective-permute-start.46 = (bf16[256,512]{1,0:T(8,128)(2,1)S(1)}, bf16[256,512]{1,0:T(8,128)(2,1)S(1)}, u32[]{:S(2)}, u32[]{:S(2)}) collective-permute-start(bf16[256,512]{1,0:T(8,128)(2,1)S(1)} %collective-permute-done.44), channel_id=1, source_target_pairs={{24,26},{25,27},{26,24},{27,25},{28,30},{29,31},{30,28},{31,29},{1... | collective-permute-start | bytes 786440 | tf_op jit(solution)/shard_map/ppermute | solution.py:282
  150.0 19.4 %collective-permute-start.39 = (bf16[256,1024]{1,0:T(8,128)(2,1)S(1)}, bf16[256,1024]{1,0:T(8,128)(2,1)S(1)}, u32[]{:S(2)}, u32[]{:S(2)}) collective-permute-start(bf16[256,1024]{1,0:T(8,128)(2,1)S(1)} %block_dot.27), channel_id=1, source_target_pairs={{8,2},{9,3},{10,0},{11,1},{12,6},{13,7},{14,4},{15,5}} | collective-permute-start | bytes 1572872 | tf_op jit(solution)/shard_map/ppermute | solution.py:282
  162.5 11.1 %collective-permute-start.37 = (bf16[256,1024]{1,0:T(8,128)(2,1)S(1)}, bf16[256,1024]{1,0:T(8,128)(2,1)S(1)}, u32[]{:S(2)}, u32[]{:S(2)}) collective-permute-start(bf16[256,1024]{1,0:T(8,128)(2,1)S(1)} %collective-permute-done.33.refs_0_), channel_id=1, source_target_pairs={{0,1},{1,0},{2,3},{3,2},{4,5},{5,4},{6,7},{7,6}} | collective-permute-start | bytes 1572872 | tf_op jit(solution)/shard_map/ppermute | solution.py:282
  165.9 11.1 %collective-permute-start.34 = (bf16[256,1024]{1,0:T(8,128)(2,1)S(1)}, bf16[256,1024]{1,0:T(8,128)(2,1)S(1)}, u32[]{:S(2)}, u32[]{:S(2)}) collective-permute-start(bf16[256,1024]{1,0:T(8,128)(2,1)S(1)} %collective-permute-done.33.refs_0_), channel_id=1, source_target_pairs={{0,2},{1,3},{2,0},{3,1},{4,6},{5,7},{6,4},{7,5}} | collective-permute-start | bytes 1572872 | tf_op jit(solution)/shard_map/ppermute | solution.py:282
  168.0 21.2 %collective-permute-start.47 = (bf16[4,256,512]{2,1,0:T(8,128)(2,1)S(1)}, bf16[4,256,512]{2,1,0:T(8,128)(2,1)S(1)}, u32[]{:S(2)}, u32[]{:S(2)}) collective-permute-start(bf16[4,256,512]{2,1,0:T(8,128)(2,1)S(1)} %pad_maximum_fusion.refs_8_), channel_id=1, source_target_pairs={{24,25},{25,24},{26,27},{27,26},{28,29},{29,28},{30,31},{31,30},{1... | collective-permute-start | bytes 3145736 | tf_op jit(solution)/shard_map/ppermute | solution.py:282
  169.4 11.5 %collective-permute-start.40 = (bf16[256,1024]{1,0:T(8,128)(2,1)S(1)}, bf16[256,1024]{1,0:T(8,128)(2,1)S(1)}, u32[]{:S(2)}, u32[]{:S(2)}) collective-permute-start(bf16[256,1024]{1,0:T(8,128)(2,1)S(1)} %collective-permute-done.39.refs_0_), channel_id=1, source_target_pairs={{0,1},{1,0},{2,3},{3,2},{4,5},{5,4},{6,7},{7,6}} | collective-permute-start | bytes 1572872 | tf_op jit(solution)/shard_map/ppermute | solution.py:282
  177.0 11.1 %collective-permute-start.38 = (bf16[256,1024]{1,0:T(8,128)(2,1)S(1)}, bf16[256,1024]{1,0:T(8,128)(2,1)S(1)}, u32[]{:S(2)}, u32[]{:S(2)}) collective-permute-start(bf16[256,1024]{1,0:T(8,128)(2,1)S(1)} %collective-permute-done.34.refs_2_), channel_id=1, source_target_pairs={{0,1},{1,0},{2,3},{3,2},{4,5},{5,4},{6,7},{7,6}} | collective-permute-start | bytes 1572872 | tf_op jit(solution)/shard_map/ppermute | solution.py:282
  (18 other events, 105.8 us)
